TPU v7x, 32 devices: a whole 2x2x4 slice. The times are simulated.
32 devices in a mesh: img: 4 (over x, core), exp: 8 (over z, y).
Axes of the slice: x: 2, y: 2, z: 4, core: 2. Of those that a mesh axis runs over, the one named last changes fastest.
Arguments:
- context: bfloat16 [64, 256, 1024], P(('img', 'exp')), may hold values from -1.5 to 1.5
- residual: bfloat16 [64, 256, 1024], P(('img', 'exp')), may hold values from -1.5 to 1.5
- cotangent: bfloat16 [64, 256, 1024], P(('img', 'exp')), may hold values from -6 to 6
- proj_weight: bfloat16 [1024, 1024], P('img'), may hold values from -0.1875 to 0.1875
- slot_params: bfloat16 [1024, 16], replicated, may hold values from -0.1875 to 0.1875
- expert_in: bfloat16 [16, 1024, 4096], P('exp', None, 'img'), may hold values from -0.1875 to 0.1875
- expert_out: bfloat16 [16, 4096, 1024], P('exp', 'img'), may hold values from -0.09375 to 0.09375
Outputs:
- grad_context: bfloat16 [64, 256, 1024], P(('img', 'exp'))
- grad_residual: bfloat16 [64, 256, 1024], P(('img', 'exp'))
- grad_proj: float32 [1024, 1024], P('img')
- grad_slots: float32 [1024, 16], replicated
- grad_expert_in: bfloat16 [16, 1024, 4096], P('exp', None, 'img')
- grad_expert_out: bfloat16 [16, 4096, 1024], P('exp', 'img')
All inputs are finite; a program needn't handle non-finite values.
Results may differ from a plain program's by a relative error of at most 0.025.
Values may be sent and summed in bfloat16 or wider, within the bound.
No kernel may reach another device: no remote copies, remote signals or barrier semaphores. Data moves between devices by JAX's collectives and lax.ppermute only.
A program may use at most 128 MiB of HBM per device.

v0:
```python
import math

import jax
import jax.numpy as jnp
from jax import lax
from jax.sharding import PartitionSpec as P

logit_scale = 48.0
epsilon = 1e-06


def gelu_back(pre, upstream):
    return jax.vjp(jax.nn.gelu, pre)[1](upstream)[0]


def shards(context, residual, cotangent, proj_weight, slot_params, expert_in, expert_out):
    images, tokens, width = context.shape
    rows = images * tokens
    factor = logit_scale / math.sqrt(width)
    flat_ctx = context.reshape(rows, width)
    mixed = jnp.dot(
        flat_ctx,
        lax.all_gather(proj_weight, "img", axis=0, tiled=True),
        preferred_element_type=jnp.float32,
    )
    stream = (residual.reshape(rows, width).astype(jnp.float32) + mixed).astype(jnp.bfloat16)
    stream32 = stream.astype(jnp.float32)
    inverse = lax.rsqrt(jnp.mean(stream32 * stream32, axis=-1, keepdims=True) + epsilon)
    normed32 = stream32 * inverse
    normed = normed32.astype(jnp.bfloat16)
    params32 = slot_params.astype(jnp.float32)
    slot_norm = jnp.sqrt(jnp.sum(params32 * params32, axis=0, keepdims=True) + epsilon)
    unit32 = params32 / slot_norm
    unit = unit32.astype(jnp.bfloat16)
    logits = factor * jnp.dot(normed, unit, preferred_element_type=jnp.float32)
    logits = logits.reshape(images, tokens, -1)
    expo = jnp.exp(logits)
    dispatch32 = expo / jnp.sum(expo, axis=1, keepdims=True)
    combine32 = expo / jnp.sum(expo, axis=2, keepdims=True)
    dispatch = dispatch32.astype(jnp.bfloat16)
    combine = combine32.astype(jnp.bfloat16)
    normed3 = normed.reshape(images, tokens, width)
    slot_in = jnp.einsum(
        "bms,bmd->bsd", dispatch, normed3, preferred_element_type=jnp.float32
    ).astype(jnp.bfloat16)
    sent = lax.all_to_all(slot_in, "exp", split_axis=1, concat_axis=0, tiled=True)
    slot_rows = lax.all_gather(sent, "img", axis=0, tiled=True)
    pre = jnp.einsum("gjd,jdf->gjf", slot_rows, expert_in, preferred_element_type=jnp.float32)
    act = jax.nn.gelu(pre).astype(jnp.bfloat16)
    piece = act
    summed = lax.psum_scatter(
        jnp.einsum("gjf,jfd->gjd", piece, expert_out, preferred_element_type=jnp.float32).astype(
            jnp.bfloat16
        ),
        "img",
        scatter_dimension=0,
        tiled=True,
    )
    slot_out = lax.all_to_all(summed, "exp", split_axis=0, concat_axis=1, tiled=True)
    grad_slot_out = jnp.einsum(
        "bms,bmd->bsd", combine, cotangent, preferred_element_type=jnp.float32
    ).astype(jnp.bfloat16)
    grad_sent = lax.all_to_all(grad_slot_out, "exp", split_axis=1, concat_axis=0, tiled=True)
    grad_gathered = lax.all_gather(grad_sent, "img", axis=0, tiled=True)
    grad_combine = jnp.einsum(
        "bmd,bsd->bms", cotangent, slot_out, preferred_element_type=jnp.float32
    )
    grad_act = jnp.einsum(
        "gjd,jfd->gjf", grad_gathered, expert_out, preferred_element_type=jnp.float32
    )
    grad_pre = gelu_back(pre, grad_act).astype(jnp.bfloat16)
    grad_expert_out = jnp.einsum(
        "gjf,gjd->jfd", act, grad_gathered, preferred_element_type=jnp.float32
    ).astype(jnp.bfloat16)
    grad_expert_in = jnp.einsum(
        "gjd,gjf->jdf", slot_rows, grad_pre, preferred_element_type=jnp.float32
    ).astype(jnp.bfloat16)
    piece = grad_pre
    grad_summed = lax.psum_scatter(
        jnp.einsum("gjf,jdf->gjd", piece, expert_in, preferred_element_type=jnp.float32).astype(
            jnp.bfloat16
        ),
        "img",
        scatter_dimension=0,
        tiled=True,
    )
    grad_slot_in = lax.all_to_all(grad_summed, "exp", split_axis=0, concat_axis=1, tiled=True)
    grad_dispatch = jnp.einsum(
        "bmd,bsd->bms", normed3, grad_slot_in, preferred_element_type=jnp.float32
    )
    grad_logits32 = combine32 * (
        grad_combine - jnp.sum(combine32 * grad_combine, axis=2, keepdims=True)
    )
    grad_logits32 = grad_logits32 + dispatch32 * (
        grad_dispatch - jnp.sum(dispatch32 * grad_dispatch, axis=1, keepdims=True)
    )
    grad_logits = grad_logits32.astype(jnp.bfloat16).reshape(rows, -1)
    grad_normed = jnp.einsum(
        "bms,bsd->bmd", dispatch, grad_slot_in, preferred_element_type=jnp.float32
    ).reshape(rows, width)
    grad_normed = grad_normed + factor * jnp.dot(
        grad_logits, unit.T, preferred_element_type=jnp.float32
    )
    local_unit = factor * jnp.dot(normed.T, grad_logits, preferred_element_type=jnp.float32)
    grad_unit = lax.psum(local_unit, ("img", "exp"))
    grad_slots = (
        grad_unit - unit32 * jnp.sum(unit32 * grad_unit, axis=0, keepdims=True)
    ) / slot_norm
    upstream = cotangent.reshape(rows, width).astype(jnp.float32)
    grad_stream = upstream + inverse * (
        grad_normed - normed32 * jnp.mean(normed32 * grad_normed, axis=-1, keepdims=True)
    )
    grad_residual = grad_stream.astype(jnp.bfloat16)
    grad_context = jnp.dot(
        grad_residual,
        lax.all_gather(proj_weight, "img", axis=0, tiled=True).T,
        preferred_element_type=jnp.float32,
    ).astype(jnp.bfloat16)
    whole_grad = jnp.dot(flat_ctx.T, grad_residual, preferred_element_type=jnp.float32)
    summed_grad = lax.psum(whole_grad.astype(jnp.bfloat16), "exp")
    grad_proj = lax.psum_scatter(summed_grad, "img", scatter_dimension=0, tiled=True).astype(
        jnp.float32
    )
    return (
        grad_context.reshape(images, tokens, width),
        grad_residual.reshape(images, tokens, width),
        grad_proj,
        grad_slots,
        grad_expert_in,
        grad_expert_out,
    )


def solution(mesh):
    placed = (
        P(("img", "exp"), None, None),
        P(("img", "exp"), None, None),
        P(("img", "exp"), None, None),
        P("img", None),
        P(),
        P("exp", None, "img"),
        P("exp", "img", None),
    )
    return jax.shard_map(
        shards,
        mesh=mesh,
        in_specs=placed,
        out_specs=(
            P(("img", "exp"), None, None),
            P(("img", "exp"), None, None),
            P("img", None),
            P(),
            P("exp", None, "img"),
            P("exp", "img", None),
        ),
        check_vma=False,
    )
```

profile of v0, /device:TPU:0, one launch (start us, length us, event | category | flops | bytes accessed | tf_op | source)
XLA Modules:
  0.0 388.9 jit_solution(11297163823382000506)
XLA Ops:
  8.8 26.1 %all-gather.2.cloned.1.call-done = bf16[1024,1024]{1,0:T(8,128)(2,1)} async-done(((bf16[256,1024]{1,0:T(8,128)(2,1)}), bf16[1024,1024]{1,0:T(8,128)(2,1)}) %all-gather.2.cloned.1.call-update) | async-done | bytes 2097168 | tf_op jit(solution)/shard_map/all_gather | solution.py:23
  34.9 3.2 fusion.10
  41.0 5.5 %all-to-all-start.1 = ((bf16[2,16,1024]{2,0,1:T(2,128)(2,1)}), bf16[2,16,1024]{2,0,1:T(2,128)(2,1)S(1)}, u32[]{:S(2)}, u32[]{:S(2)}) async-start(bf16[2,16,1024]{2,0,1:T(2,128)(2,1)} %copy.33), calls=%async_computation.1 | async-start | bytes 131072 | tf_op jit(solution)/shard_map/all_to_all | solution.py:46
  47.5 5.9 %all-to-all-done.1 = bf16[2,16,1024]{2,0,1:T(2,128)(2,1)S(1)} async-done(((bf16[2,16,1024]{2,0,1:T(2,128)(2,1)}), bf16[2,16,1024]{2,0,1:T(2,128)(2,1)S(1)}, u32[]{:S(2)}, u32[]{:S(2)}) %all-to-all-start.1) | async-done | bytes 65568 | tf_op jit(solution)/shard_map/all_to_all | solution.py:46
  53.4 3.4 all-to-all-start
  56.9 6.7 %all-to-all-done = bf16[2,16,1024]{2,0,1:T(2,128)(2,1)S(1)} async-done(((bf16[2,16,1024]{2,0,1:T(2,128)(2,1)}), bf16[2,16,1024]{2,0,1:T(2,128)(2,1)S(1)}, u32[]{:S(2)}, u32[]{:S(2)}) %all-to-all-start) | async-done | bytes 65568 | tf_op jit(solution)/shard_map/all_to_all | solution.py:63
  63.7 5.8 %all_gather.11 = bf16[64,2,1024]{2,0,1:T(8,128)(2,1)S(1)} all-gather(bf16[16,2,1024]{2,0,1:T(8,128)(2,1)S(1)} %all_to_all.55), channel_id=1, replica_groups=mesh['img'=4,'exp'=8] {'img'}, dimensions={0}, use_global_device_ids=true | all-gather | bytes 327680 | tf_op jit(solution)/shard_map/all_gather | solution.py:64
  69.5 5.8 %all_gather.12 = bf16[64,2,1024]{2,0,1:T(8,128)(2,1)S(1)} all-gather(bf16[16,2,1024]{2,0,1:T(8,128)(2,1)S(1)} %all_to_all.59), channel_id=1, replica_groups=mesh['img'=4,'exp'=8] {'img'}, dimensions={0}, use_global_device_ids=true | all-gather | bytes 327680 | tf_op jit(solution)/shard_map/all_gather | solution.py:47
  75.4 3.2 convolution_bitcast_fusion
  83.2 3.8 fusion.13
  87.0 12.9 %reduce-scatter.4.cloned.1.call-done = bf16[16,2,1024]{2,0,1:T(8,128)(2,1)} async-done(((bf16[64,2,1024]{2,0,1:T(8,128)(2,1)}), bf16[16,2,1024]{2,0,1:T(8,128)(2,1)}) %reduce-scatter.4.cloned.1.call-update) | async-done | bytes 65552 | tf_op jit(solution)/shard_map/reduce_scatter | solution.py:79
  101.4 5.5 %all-to-all-start.2 = ((bf16[16,2,1024]{2,1,0:T(2,128)(2,1)}), bf16[16,2,1024]{2,1,0:T(2,128)(2,1)S(1)}, u32[]{:S(2)}, u32[]{:S(2)}) async-start(bf16[16,2,1024]{2,1,0:T(2,128)(2,1)} %copy.35), calls=%async_computation.3 | async-start | bytes 131072 | tf_op jit(solution)/shard_map/all_to_all | solution.py:87
  106.9 16.2 %reduce-scatter.6.cloned.1.call-done = bf16[16,2,1024]{2,0,1:T(8,128)(2,1)} async-done(((bf16[64,2,1024]{2,0,1:T(8,128)(2,1)}), bf16[16,2,1024]{2,0,1:T(8,128)(2,1)}) %reduce-scatter.6.cloned.1.call-update) | async-done | bytes 65552 | tf_op jit(solution)/shard_map/reduce_scatter | solution.py:51
  124.7 5.5 %all-to-all-start.3 = ((bf16[16,2,1024]{2,1,0:T(2,128)(2,1)}), bf16[16,2,1024]{2,1,0:T(2,128)(2,1)}, u32[]{:S(2)}, u32[]{:S(2)}) async-start(bf16[16,2,1024]{2,1,0:T(2,128)(2,1)} %copy.37), calls=%async_computation.5 | async-start | bytes 131072 | tf_op jit(solution)/shard_map/all_to_all | solution.py:59
  134.9 2.3 all-to-all-done.3
  142.1 2.4 fusion.5
  146.1 2.6 convert_bitcast_fusion
  149.0 3.3 convolution_convert_fusion
  153.3 3.3 convolution_convert_fusion.1
  156.6 21.9 %reduce-scatter.8.cloned.1.call-done = bf16[256,1024]{0,1:T(8,128)(2,1)} async-done(((bf16[1024,1024]{0,1:T(8,128)(2,1)}), bf16[256,1024]{0,1:T(8,128)(2,1)}) %reduce-scatter.8.cloned.1.call-update) | async-done | bytes 524304 | tf_op jit(solution)/shard_map/reduce_scatter | solution.py:121
  178.6 3.8 convolution_convert_fusion.2
  182.4 120.6 %all-reduce.3.cloned.1.call-done = f32[1024,16]{0,1:T(8,128)} async-done(((f32[1024,16]{0,1:T(8,128)}), f32[1024,16]{0,1:T(8,128)}) %all-reduce.3.cloned.1.call-update) | async-done | bytes 65552 | tf_op jit(solution)/shard_map/psum | solution.py:105
  305.6 74.3 %all-reduce.5.cloned.1.call-done = bf16[256,1024]{0,1:T(8,128)(2,1)} async-done(((bf16[256,1024]{0,1:T(8,128)(2,1)}), bf16[256,1024]{0,1:T(8,128)(2,1)}) %all-reduce.5.cloned.1.call-update) | async-done | bytes 524304 | tf_op jit(solution)/shard_map/psum | solution.py:120
  379.9 2.2 copy.40
  (68 shorter events, 28.2 us)
Async XLA Ops:
  7.2 27.7 %copy-start = (bf16[2,256,1024]{2,1,0:T(8,128)(2,1)S(1)}, bf16[2,256,1024]{2,1,0:T(8,128)(2,1)}, u32[]{:S(2)}) copy-start(bf16[2,256,1024]{2,1,0:T(8,128)(2,1)} %param.7) | copy-start | bytes 3145732
  7.2 27.7 %all-gather.2.cloned.1.call-start = ((), (), s32[]{:S(2)}) async-start(), calls=%async_computation.7 | async-start | bytes 2621440 | tf_op jit(solution)/shard_map/all_gather | solution.py:23
  38.1 1.0 copy-start.4
  38.1 1.2 copy-start.9
  39.1 7.4 %copy-start.2 = (bf16[2,256,1024]{2,1,0:T(8,128)(2,1)S(1)}, bf16[2,256,1024]{2,1,0:T(8,128)(2,1)}, u32[]{:S(2)}) copy-start(bf16[2,256,1024]{2,1,0:T(8,128)(2,1)} %param.9) | copy-start | bytes 3145732
  41.0 12.4 %all-to-all-start.1 = ((bf16[2,16,1024]{2,0,1:T(2,128)(2,1)}), bf16[2,16,1024]{2,0,1:T(2,128)(2,1)S(1)}, u32[]{:S(2)}, u32[]{:S(2)}) async-start(bf16[2,16,1024]{2,0,1:T(2,128)(2,1)} %copy.33), calls=%async_computation.1 | async-start | bytes 131072 | tf_op jit(solution)/shard_map/all_to_all | solution.py:46
  53.4 10.2 %all-to-all-start = ((bf16[2,16,1024]{2,0,1:T(2,128)(2,1)}), bf16[2,16,1024]{2,0,1:T(2,128)(2,1)S(1)}, u32[]{:S(2)}, u32[]{:S(2)}) async-start(bf16[2,16,1024]{2,0,1:T(2,128)(2,1)} %copy.31), calls=%async_computation | async-start | bytes 131072 | tf_op jit(solution)/shard_map/all_to_all | solution.py:63
  56.8 43.1 %reduce-scatter.4.cloned.1.call-start = ((), (), s32[]{:S(2)}) async-start(), calls=%async_computation.8 | async-start | bytes 327680 | tf_op jit(solution)/shard_map/reduce_scatter | solution.py:79
  75.4 3.4 copy-start.6
  78.8 2.2 copy-start.1
  83.1 40.0 %reduce-scatter.6.cloned.1.call-start = ((), (), s32[]{:S(2)}) async-start(), calls=%async_computation.9 | async-start | bytes 327680 | tf_op jit(solution)/shard_map/reduce_scatter | solution.py:51
  101.4 23.3 %all-to-all-start.2 = ((bf16[16,2,1024]{2,1,0:T(2,128)(2,1)}), bf16[16,2,1024]{2,1,0:T(2,128)(2,1)S(1)}, u32[]{:S(2)}, u32[]{:S(2)}) async-start(bf16[16,2,1024]{2,1,0:T(2,128)(2,1)} %copy.35), calls=%async_computation.3 | async-start | bytes 131072 | tf_op jit(solution)/shard_map/all_to_all | solution.py:87
  124.7 12.5 %all-to-all-start.3 = ((bf16[16,2,1024]{2,1,0:T(2,128)(2,1)}), bf16[16,2,1024]{2,1,0:T(2,128)(2,1)}, u32[]{:S(2)}, u32[]{:S(2)}) async-start(bf16[16,2,1024]{2,1,0:T(2,128)(2,1)} %copy.37), calls=%async_computation.5 | async-start | bytes 131072 | tf_op jit(solution)/shard_map/all_to_all | solution.py:59
  130.2 48.3 %reduce-scatter.8.cloned.1.call-start = ((), (), s32[]{:S(2)}) async-start(), calls=%async_computation.11 | async-start | bytes 2621440 | tf_op jit(solution)/shard_map/reduce_scatter | solution.py:121
  139.6 2.5 copy-start.5
  142.1 2.4 copy-start.3
  145.1 1.0 copy-start.7
  148.8 154.3 %all-reduce.3.cloned.1.call-start = ((), (), s32[]{:S(2)}) async-start(), calls=%async_computation.10 | async-start | bytes 131072 | tf_op jit(solution)/shard_map/psum | solution.py:105
  153.2 25.3 %copy-start.8 = (bf16[512,1024]{1,0:T(8,128)(2,1)S(1)}, bf16[512,1024]{1,0:T(8,128)(2,1)}, u32[]{:S(2)}) copy-start(bf16[512,1024]{1,0:T(8,128)(2,1)} %copy-done.7) | copy-start | bytes 3145732
  153.2 226.6 %all-reduce.5.cloned.1.call-start = ((), (), s32[]{:S(2)}) async-start(), calls=%async_computation.12 | async-start | bytes 1048576 | tf_op jit(solution)/shard_map/psum | solution.py:120
Sparse Core Ops, SparseCore 0:
  9.6 25.2 all-gather.1
  83.2 16.5 reduce-scatter.3
  103.1 20.0 reduce-scatter.5
  148.9 29.5 reduce-scatter.7
  185.5 117.5 all-reduce.2
  306.7 73.1 all-reduce.4
where the time goes:
time: 390 us; the launch traced here: 389 us
  waiting for transfers between devices  288 us (74%)
  matrix products  35.9 us (9%)
  starting transfers between devices  20.3 us (5%)
  between operations  14.3 us (4%)
  local copies, waits for them, and re-layouts  13.8 us (4%)
  blocking collectives  11.6 us (3%)
  other arithmetic  5.21 us (1%)
    psum x1, waiting for transfers between devices, shards(): grad_unit = lax.psum(local_unit, ('img', 'exp'))  121 us
    psum x1, waiting for transfers between devices, shards(): summed_grad = lax.psum(whole_grad.astype(jnp.bfloat16), 'exp')  74.3 us
    all_gather x1, waiting for transfers between devices, shards(): lax.all_gather(proj_weight, 'img', axis=0, tiled=True)  26.1 us
    reduce_scatter x1, waiting for transfers between devices, shards(): lax.psum_scatter(summed_grad, 'img', scatter_dimension=0, tiled=True)  21.9 us
    reduce_scatter x1, waiting for transfers between devices, shards(): lax.psum_scatter(jnp.einsum('gjf,jfd->gjd', piece, expert_out, preferred_...  16.2 us
    reduce_scatter x1, waiting for transfers between devices, shards(): lax.psum_scatter(jnp.einsum('gjf,jdf->gjd', piece, expert_in, preferred_e...  12.9 us
  transfers between devices with their start and end apart: 10, of which 9 were waited for; matrix products, arithmetic and copies ran while one was open for 7% of the time, Pallas kernels for 0%

commit v1 on v0

v1 whole, which is shorter than its diff:
```python
import math

import jax
import jax.numpy as jnp
from jax import lax
from jax.sharding import PartitionSpec as P

logit_scale = 48.0
epsilon = 1e-06
f32 = jnp.float32
bf16 = jnp.bfloat16


def gelu_back(pre, upstream):
    return jax.vjp(jax.nn.gelu, pre)[1](upstream)[0]


def swap(x, axis, size, bit):
    return lax.ppermute(x, axis, [(i, i ^ bit) for i in range(size)])


def tree(parts):
    while len(parts) > 1:
        parts = [parts[k] + parts[k + 1] for k in range(0, len(parts), 2)]
    return parts[0]


def gather_rows(block, n_img):
    held = [block]
    bit = n_img // 2
    while bit:
        held = held + [swap(h, "img", n_img, bit) for h in held]
        bit //= 2
    return held


def shards(n_img, n_exp, context, residual, cotangent, proj_weight, slot_params, expert_in, expert_out):
    images, tokens, width = context.shape
    rows = images * tokens
    owned = expert_in.shape[0]
    factor = logit_scale / math.sqrt(width)
    me_img = lax.axis_index("img")
    me_exp = lax.axis_index("exp")
    flat_ctx = context.reshape(rows, width)
    flat_cot = cotangent.reshape(rows, width)

    near = swap(proj_weight, "img", n_img, 1)
    far = swap(proj_weight, "img", n_img, 2)
    far_near = swap(far, "img", n_img, 1)
    relative = [proj_weight, near, far, far_near]
    order = jnp.arange(n_img) ^ me_img
    blocks = jnp.stack(relative)
    whole_proj = jnp.take(blocks, order, axis=0).reshape(width, width)

    sub = width // (n_img * n_exp)
    ctx_t = flat_ctx.T.reshape(n_img, n_exp, sub, rows)
    ctx_t = jnp.take(ctx_t, order, axis=0)
    ctx_t = jnp.take(ctx_t, jnp.arange(n_exp) ^ me_exp, axis=1)
    ctx_t = ctx_t.reshape(2, 2, n_exp // 2, 2, sub, rows)
    left_p = ctx_t.transpose(1, 0, 3, 2, 4, 5).reshape(2, -1, rows)
    left_q = ctx_t.transpose(1, 3, 0, 2, 4, 5).reshape(2, -1, rows)

    mixed = jnp.dot(flat_ctx, whole_proj, preferred_element_type=f32)
    stream = (residual.reshape(rows, width).astype(f32) + mixed).astype(bf16)
    stream32 = stream.astype(f32)
    inverse = lax.rsqrt(jnp.mean(stream32 * stream32, axis=-1, keepdims=True) + epsilon)
    normed32 = stream32 * inverse
    normed = normed32.astype(bf16)
    params32 = slot_params.astype(f32)
    slot_norm = jnp.sqrt(jnp.sum(params32 * params32, axis=0, keepdims=True) + epsilon)
    unit32 = params32 / slot_norm
    unit = unit32.astype(bf16)
    logits = factor * jnp.dot(normed, unit, preferred_element_type=f32)
    logits = logits.reshape(images, tokens, -1)
    expo = jnp.exp(logits)
    dispatch32 = expo / jnp.sum(expo, axis=1, keepdims=True)
    combine32 = expo / jnp.sum(expo, axis=2, keepdims=True)
    dispatch = dispatch32.astype(bf16)
    combine = combine32.astype(bf16)
    normed3 = normed.reshape(images, tokens, width)
    slot_in = jnp.einsum("bms,bmd->sbd", dispatch, normed3, preferred_element_type=f32).astype(bf16)
    grad_slot_out = jnp.einsum(
        "bms,bmd->sbd", combine, cotangent, preferred_element_type=f32
    ).astype(bf16)

    out = jnp.stack([slot_in, grad_slot_out], axis=1).reshape(n_exp, owned * 2 * images, width)
    got = lax.all_to_all(out, "exp", split_axis=0, concat_axis=0, tiled=True)
    got = lax.all_gather(got, "img", axis=0, tiled=True)
    got = got.reshape(n_img * n_exp, owned, 2, images, width)
    slot_rows = got[:, :, 0].transpose(1, 0, 2, 3).reshape(owned, -1, width)
    grad_rows = got[:, :, 1].transpose(1, 0, 2, 3).reshape(owned, -1, width)

    pre = jnp.einsum("jgd,jdf->jgf", slot_rows, expert_in, preferred_element_type=f32)
    act = jax.nn.gelu(pre).astype(bf16)
    part_out = jnp.einsum("jgf,jfd->jgd", act, expert_out, preferred_element_type=f32)
    grad_act = jnp.einsum("jgd,jfd->jgf", grad_rows, expert_out, preferred_element_type=f32)
    grad_pre = gelu_back(pre, grad_act).astype(bf16)
    part_in = jnp.einsum("jgf,jdf->jgd", grad_pre, expert_in, preferred_element_type=f32)
    back = jnp.stack([part_out, part_in], axis=0).astype(bf16)
    back = back.reshape(2, owned, n_img * n_exp, images, width).transpose(2, 1, 0, 3, 4)
    back = back.reshape(n_img * n_exp, owned * 2 * images, width)
    back = lax.all_to_all(back, ("img", "exp"), split_axis=0, concat_axis=0, tiled=True)
    back = back.reshape(n_img, n_exp, owned, 2, images, width).astype(f32).sum(axis=0).astype(bf16)
    back = back.transpose(2, 3, 0, 1, 4).reshape(2, images, n_exp * owned, width)
    slot_out, grad_slot_in = back[0], back[1]

    grad_expert_out = jnp.einsum(
        "jgf,jgd->jfd", act, grad_rows, preferred_element_type=f32
    ).astype(bf16)
    grad_expert_in = jnp.einsum(
        "jgd,jgf->jdf", slot_rows, grad_pre, preferred_element_type=f32
    ).astype(bf16)

    grad_combine = jnp.einsum("bmd,bsd->bms", cotangent, slot_out, preferred_element_type=f32)
    grad_dispatch = jnp.einsum("bmd,bsd->bms", normed3, grad_slot_in, preferred_element_type=f32)
    grad_logits32 = combine32 * (
        grad_combine - jnp.sum(combine32 * grad_combine, axis=2, keepdims=True)
    )
    grad_logits32 = grad_logits32 + dispatch32 * (
        grad_dispatch - jnp.sum(dispatch32 * grad_dispatch, axis=1, keepdims=True)
    )
    grad_logits = grad_logits32.astype(bf16).reshape(rows, -1)
    grad_normed = jnp.einsum(
        "bms,bsd->bmd", dispatch, grad_slot_in, preferred_element_type=f32
    ).reshape(rows, width)
    grad_normed = grad_normed + factor * jnp.dot(grad_logits, unit.T, preferred_element_type=f32)
    local_unit = factor * jnp.dot(grad_logits.T, normed, preferred_element_type=f32)
    grad_stream = flat_cot.astype(f32) + inverse * (
        grad_normed - normed32 * jnp.mean(normed32 * grad_normed, axis=-1, keepdims=True)
    )
    grad_residual = grad_stream.astype(bf16)

    half = width // 2
    gr_p, gr_q = grad_residual[:, :half], grad_residual[:, half:]

    def product(k):
        p = jnp.dot(left_p[k], gr_p, preferred_element_type=f32).astype(bf16)
        q = jnp.dot(left_q[k], gr_q, preferred_element_type=f32).astype(bf16)
        return p, q

    def split(x):
        high = x.astype(bf16)
        low = (x - high.astype(f32)).astype(bf16)
        return jnp.concatenate([high, low], axis=0)

    def joined(x):
        n = x.shape[0] // 2
        return x[:n].astype(f32) + x[n:].astype(f32)

    def add(a, b):
        return (a.astype(f32) + b.astype(f32)).astype(bf16)

    def halves(x):
        n = x.shape[0] // 2
        return x[:n], x[n:]

    side = split(local_unit.reshape(-1, half))
    n_side = side.shape[0]
    send_p, send_q = product(1)
    n = send_p.shape[0]
    got = swap(jnp.concatenate([send_p, send_q, side]), "img", n_img, 1)
    keep_p, keep_q = product(0)
    p, q, other = got[:n], got[n : 2 * n], got[2 * n :]
    p0, p1 = halves(add(keep_p, p))
    q0, q1 = halves(add(keep_q, q))
    side = split(joined(side) + joined(other))
    n = p1.shape[0]
    got_p = swap(jnp.concatenate([p1, side]), "img", n_img, 2)
    got_q = swap(q1, "exp", n_exp, 1)
    p0, p1 = halves(add(p0, got_p[:n]))
    q0, q1 = halves(add(q0, got_q))
    side = split(joined(side) + joined(got_p[n:]))
    n = p1.shape[0]
    got_p = swap(jnp.concatenate([p1, side]), "exp", n_exp, 1)
    got_q = swap(q1, "img", n_img, 2)
    p, q = add(p0, got_p[:n]), add(q0, got_q)
    side = split(joined(side) + joined(got_p[n:]))
    groups = n_exp // 2
    p = p.reshape(groups, -1, half)
    q = q.reshape(groups, -1, half)
    n = p.shape[1]
    pq = jnp.concatenate([p, q], axis=1)
    got = [pq[0]]
    sides = [side]
    for m in range(1, groups):
        r = swap(jnp.concatenate([pq[m], side]), "exp", n_exp, 2 * m)
        got.append(r[: 2 * n])
        sides.append(r[2 * n :])
    own = tree([g.astype(f32) for g in got]).astype(bf16)
    grad_unit = tree([joined(s) for s in sides]).reshape(-1, width)
    held = jnp.stack([own] + [swap(own, "exp", n_exp, 2 * m) for m in range(1, groups)])
    held = jnp.stack([held, swap(held, "exp", n_exp, 1)], axis=1)
    held = held.reshape(n_exp, 2, n, half)
    bit = 1
    while bit < n_exp:
        view = held.reshape(n_exp // (2 * bit), 2, bit, 2, n, half)
        held = jnp.where((me_exp & bit) != 0, view[:, ::-1], view).reshape(n_exp, 2, n, half)
        bit *= 2
    grad_proj = held.astype(f32).transpose(0, 2, 1, 3).reshape(-1, width)

    unit_t = unit32.T
    grad_slots = (
        (grad_unit - unit_t * jnp.sum(unit_t * grad_unit, axis=1, keepdims=True)) / slot_norm.T
    ).T
    grad_context = jnp.dot(grad_residual, whole_proj.T, preferred_element_type=f32).astype(bf16)
    return (
        grad_context.reshape(images, tokens, width),
        grad_residual.reshape(images, tokens, width),
        grad_proj,
        grad_slots,
        grad_expert_in,
        grad_expert_out,
    )


def solution(mesh):
    n_img, n_exp = mesh.shape["img"], mesh.shape["exp"]
    placed = (
        P(("img", "exp"), None, None),
        P(("img", "exp"), None, None),
        P(("img", "exp"), None, None),
        P("img", None),
        P(),
        P("exp", None, "img"),
        P("exp", "img", None),
    )

    def run(*args):
        return shards(n_img, n_exp, *args)

    return jax.shard_map(
        run,
        mesh=mesh,
        in_specs=placed,
        out_specs=(
            P(("img", "exp"), None, None),
            P(("img", "exp"), None, None),
            P("img", None),
            P(),
            P("exp", None, "img"),
            P("exp", "img", None),
        ),
        check_vma=False,
    )
```

time: 390 us -> 172 us (0.44)
  waiting for transfers between devices: 288 us -> 48 us
  local copies, waits for them, and re-layouts: 13.8 us -> 37 us
  between operations: 14.3 us -> 1.23 us
  other arithmetic: 5.21 us -> 15 us
  starting transfers between devices: 20.3 us -> 26.4 us
  blocking collectives: 11.6 us -> 7.16 us
    psum x2 -> x0, waiting for transfers between devices: 195 us -> none  [the longest x1 121 us: shards(): grad_unit = lax.psum(local_unit, ('img', 'exp'))]
    reduce_scatter x3 -> x0, waiting for transfers between devices: 51 us -> none  [the longest x1 21.9 us: shards(): lax.psum_scatter(summed_grad, 'img', scatter_dimension=0, tiled=True)]
    ppermute x0 -> x15, waiting for transfers between devices: none -> 33.9 us  [swap(): return lax.ppermute(x, axis, [(i, i ^ bit) for i in range(size)])]
    all_gather x1 -> x0, waiting for transfers between devices: 26.1 us -> none  [shards(): lax.all_gather(proj_weight, 'img', axis=0, tiled=True)]
    ppermute x0 -> x15, starting transfers between devices: none -> 16.8 us  [swap(): return lax.ppermute(x, axis, [(i, i ^ bit) for i in range(size)])]
    all_to_all x4 -> x2, starting transfers between devices: 19.9 us -> 9.6 us  [the longest x1 6.08 us: shards(): got = lax.all_to_all(out, 'exp', split_axis=0, concat_axis=0, tiled=True)]
    reshape x1 -> x9, local copies, waits for them, and re-layouts: 0.01 us -> 7 us  [the longest x1 1.76 us: shards(): slot_rows = got[:, :, 0].transpose(1, 0, 2, 3).reshape(owned, -1, width)]
    gather x0 -> x3, local copies, waits for them, and re-layouts: none -> 6.66 us  [the longest x1 2.81 us: shards(): ctx_t = jnp.take(ctx_t, jnp.arange(n_exp) ^ me_exp, axis=1)]
  transfers between devices with their start and end apart: 10 -> 17, of which waited for: 9 -> 13; matrix products, arithmetic and copies ran while one was open for 7% -> 14% of each run, Pallas kernels for 0% -> 0%
where the time goes in v1:
time: 172 us; the launch traced here: 171 us
  waiting for transfers between devices  48 us (28%)
  local copies, waits for them, and re-layouts  37 us (22%)
  matrix products  35.7 us (21%)
  starting transfers between devices  26.4 us (15%)
  other arithmetic  15 us (9%)
  blocking collectives  7.16 us (4%)
    ppermute x15, waiting for transfers between devices, swap(): return lax.ppermute(x, axis, [(i, i ^ bit) for i in range(size)])  33.9 us
    ppermute x15, starting transfers between devices, swap(): return lax.ppermute(x, axis, [(i, i ^ bit) for i in range(size)])  16.8 us
    all_to_all x1, waiting for transfers between devices, shards(): lax.all_to_all(back, ('img', 'exp'), split_axis=0, concat_axis=0, tiled=T...  9.12 us
    all_gather x1, blocking collectives, shards(): got = lax.all_gather(got, 'img', axis=0, tiled=True)  7.16 us
    another operation x4, local copies, waits for them, and re-layouts, shards(): back = jnp.stack([part_out, part_in], axis=0).astype(bf16)  6.21 us
    unnamed x48, local copies, waits for them, and re-layouts  6.21 us
    all_to_all x1, starting transfers between devices, shards(): got = lax.all_to_all(out, 'exp', split_axis=0, concat_axis=0, tiled=True)  6.08 us
    all_to_all x1, waiting for transfers between devices, shards(): got = lax.all_to_all(out, 'exp', split_axis=0, concat_axis=0, tiled=True)  4.98 us
  transfers between devices with their start and end apart: 17, of which 13 were waited for; matrix products, arithmetic and copies ran while one was open for 14% of the time, Pallas kernels for 0%

profile of v1, /device:TPU:0, one launch (start us, length us, event | category | flops | bytes accessed | tf_op | source)
XLA Modules:
  0.0 170.6 jit_solution(15730823103642217373)
XLA Ops:
  0.6 3.0 %collective-permute-start.1 = (bf16[256,1024]{1,0:T(8,128)(2,1)}, bf16[256,1024]{1,0:T(8,128)(2,1)S(1)}, u32[]{:S(2)}, u32[]{:S(2)}) collective-permute-start(bf16[256,1024]{1,0:T(8,128)(2,1)} %param.10), channel_id=1, source_target_pairs={{0,16},{8,24},{16,0},{24,8},{1,17},{9,25},{17,1},{25,9},{2,18},{10... | collective-permute-start | bytes 1572872 | tf_op jit(solution)/shard_map/ppermute | solution.py:19
  6.8 9.0 %collective-permute-done.1 = bf16[256,1024]{1,0:T(8,128)(2,1)S(1)} collective-permute-done((bf16[256,1024]{1,0:T(8,128)(2,1)}, bf16[256,1024]{1,0:T(8,128)(2,1)S(1)}, u32[]{:S(2)}, u32[]{:S(2)}) %collective-permute-start.1) | collective-permute-done | bytes 524320 | tf_op jit(solution)/shard_map/ppermute | solution.py:19
  19.3 2.3 %gather_fusion = bf16[4,256,1024]{2,1,0:T(8,128)(2,1)S(1)} fusion(bf16[4,256,1024]{2,1,0:T(8,128)(2,1)} %pad_maximum_fusion, s32[1024]{0:T(1024)S(1)} %pad_clamp_fusion.1), kind=kCustom, calls=%fused_computation | custom fusion | bytes 4194320 | tf_op jit(solution)/shard_map/jit(_take)/gather | solution.py:53
  29.0 6.1 %all-to-all-start = ((bf16[8,8,1024]{2,1,0:T(8,128)(2,1)}), bf16[8,8,1024]{2,1,0:T(8,128)(2,1)S(1)}, u32[]{:S(2)}, u32[]{:S(2)}) async-start(bf16[8,8,1024]{2,1,0:T(8,128)(2,1)} %reshape.226), calls=%async_computation | async-start | bytes 262144 | tf_op jit(solution)/shard_map/all_to_all | solution.py:87
  35.1 2.4 %broadcast_select_fusion.1 = bf16[4,8,32,512]{3,2,1,0:T(8,128)(2,1)} fusion(bf16[4,8,32,512]{3,2,1,0:T(8,128)(2,1)} %gather_fusion.1, pred[4]{0:T(512)(128)(4,1)} %copy-done.19), kind=kLoop, calls=%fused_computation.53 | loop fusion | flops 524288 | bytes 2097156 | tf_op jit(solution)/shard_map/jit(_take)/select_n | solution.py:57
  37.5 5.0 %all-to-all-done = bf16[8,8,1024]{2,1,0:T(8,128)(2,1)S(1)} async-done(((bf16[8,8,1024]{2,1,0:T(8,128)(2,1)}), bf16[8,8,1024]{2,1,0:T(8,128)(2,1)S(1)}, u32[]{:S(2)}, u32[]{:S(2)}) %all-to-all-start) | async-done | bytes 131104 | tf_op jit(solution)/shard_map/all_to_all | solution.py:87
  42.4 7.2 %all_gather.3 = bf16[32,8,1024]{2,1,0:T(8,128)(2,1)S(1)} all-gather(bf16[8,8,1024]{2,1,0:T(8,128)(2,1)S(1)} %all-to-all-done), channel_id=1, replica_groups=mesh['img'=4,'exp'=8] {'img'}, dimensions={0}, use_global_device_ids=true | all-gather | bytes 655360 | tf_op jit(solution)/shard_map/all_gather | solution.py:88
  56.4 3.7 %fusion.86 = f32[2,64,1024]{2,1,0:T(8,128)S(1)} fusion(bf16[2,64,1024]{2,1,0:T(8,128)(2,1)S(1)} %reshape.229, bf16[2,1024,1024]{2,1,0:T(8,128)(2,1)} %param.13), kind=kOutput, calls=%fused_computation.167 | convolution fusion | flops 268435456 | bytes 4980736 | tf_op jit(solution)/shard_map/jgd,jfd->jgf/dot_general | solution.py:96
  68.3 3.9 %convolution_convert_fusion.8 = bf16[2,64,1024]{2,1,0:T(8,128)(2,1)} fusion(bf16[2,1024,1024]{2,1,0:T(8,128)(2,1)} %param.13, f32[2,64,1024]{2,1,0:T(8,128)} %get-tuple-element.35), kind=kOutput, calls=%fused_computation.32 | convolution fusion | flops 269746176 | bytes 4980736 | tf_op jit(solution)/shard_map/jgf,jfd->jgd/dot_general | solution.py:95
  77.0 3.5 %all-to-all-start.1 = ((bf16[32,8,1024]{2,1,0:T(8,128)(2,1)}), bf16[32,8,1024]{2,1,0:T(8,128)(2,1)}, u32[]{:S(2)}, u32[]{:S(2)}) async-start(bf16[32,8,1024]{2,1,0:T(8,128)(2,1)} %copy.48), calls=%async_computation.1 | async-start | bytes 1048576 | tf_op jit(solution)/shard_map/all_to_all | solution.py:102
  80.6 2.8 %gather_fusion.2 = bf16[8,4,32,512]{3,2,1,0:T(8,128)(2,1)} fusion(bf16[4,8,32,512]{3,2,1,0:T(8,128)(2,1)} %broadcast_select_fusion.1, s32[1024]{0:T(1024)S(1)} %pad_clamp_fusion), kind=kCustom, calls=%fused_computation.2 | custom fusion | bytes 2097184 | tf_op jit(solution)/shard_map/jit(_take)/gather | solution.py:58
  87.6 9.1 %all-to-all-done.1 = bf16[32,8,1024]{2,1,0:T(8,128)(2,1)} async-done(((bf16[32,8,1024]{2,1,0:T(8,128)(2,1)}), bf16[32,8,1024]{2,1,0:T(8,128)(2,1)}, u32[]{:S(2)}, u32[]{:S(2)}) %all-to-all-start.1) | async-done | bytes 524320 | tf_op jit(solution)/shard_map/all_to_all | solution.py:102
  109.1 2.8 %fusion.5 = (f32[512]{0:T(512)S(1)}, f32[512,1024]{1,0:T(8,128)S(1)}) fusion(bf16[512,1024]{1,0:T(8,128)(2,1)} %copy-done.1, f32[512]{0:T(512)S(1)} %add_rsqrt_fusion, bf16[512,16]{0,1:T(8,128)(2,1)S(1)} %bitcast.225, f32[16]{0:T(128)S(1)} %add_sqrt_fusion, bf16[1024,16]{0,1:T(8,128)(2,1)S(1)} %copy-done.13, f32[2,256,1024]{2,1,0:T(8,128)} %fusion.72), kind=kOutput, calls=%fused_computation.12 | convolution fusion | flops 19971584 | bytes 5296192 | tf_op jit(solution)/shard_map/dot_general | solution.py:126
  116.2 3.3 %convolution_convert_fusion = bf16[2,1024,1024]{2,1,0:T(8,128)(2,1)} fusion(bf16[2,64,1024]{2,1,0:T(8,128)(2,1)S(1)} %reshape.229, f32[2,64,1024]{2,1,0:T(8,128)S(1)} %copy-done.3), kind=kOutput, calls=%fused_computation.5 | convolution fusion | flops 271712256 | bytes 4980736 | tf_op jit(solution)/shard_map/jgf,jgd->jfd/dot_general | solution.py:107
  125.0 3.3 %convolution_convert_fusion.1 = bf16[2,1024,1024]{2,1,0:T(8,128)(2,1)} fusion(bf16[2,64,1024]{2,1,0:T(8,128)(2,1)S(1)} %copy-done.9, bf16[2,64,1024]{2,1,0:T(8,128)(2,1)S(1)} %copy-done.7), kind=kOutput, calls=%fused_computation.6 | convolution fusion | flops 270532608 | bytes 4718592 | tf_op jit(solution)/shard_map/jgd,jgf->jdf/dot_general | solution.py:110
  128.4 3.0 %collective-permute-done.6 = bf16[256,512]{1,0:T(8,128)(2,1)S(1)} collective-permute-done((bf16[256,512]{1,0:T(8,128)(2,1)S(1)}, bf16[256,512]{1,0:T(8,128)(2,1)S(1)}, u32[]{:S(2)}, u32[]{:S(2)}) %collective-permute-start.6) | collective-permute-done | bytes 262176 | tf_op jit(solution)/shard_map/ppermute | solution.py:19
  132.1 2.5 %collective-permute-done.4 = bf16[320,512]{1,0:T(8,128)(2,1)S(1)} collective-permute-done((bf16[320,512]{1,0:T(8,128)(2,1)S(1)}, bf16[320,512]{1,0:T(8,128)(2,1)S(1)}, u32[]{:S(2)}, u32[]{:S(2)}) %collective-permute-start.4) | collective-permute-done | bytes 327712 | tf_op jit(solution)/shard_map/ppermute | solution.py:19
  137.1 3.5 %collective-permute-done.5 = bf16[192,512]{1,0:T(8,128)(2,1)S(1)} collective-permute-done((bf16[192,512]{1,0:T(8,128)(2,1)S(1)}, bf16[192,512]{1,0:T(8,128)(2,1)S(1)}, u32[]{:S(2)}, u32[]{:S(2)}) %collective-permute-start.5) | collective-permute-done | bytes 196640 | tf_op jit(solution)/shard_map/ppermute | solution.py:19
  142.9 2.3 %collective-permute-start.10 = (bf16[128,512]{1,0:T(8,128)(2,1)S(1)}, bf16[128,512]{1,0:T(8,128)(2,1)S(1)}, u32[]{:S(2)}, u32[]{:S(2)}) collective-permute-start(bf16[128,512]{1,0:T(8,128)(2,1)S(1)} %get-tuple-element.29), channel_id=1, source_target_pairs={{0,6},{1,7},{2,4},{3,5},{4,2},{5,3},{6,0},{7,1},{8,14},{9,15},{10,... | collective-permute-start | bytes 393224 | tf_op jit(solution)/shard_map/ppermute | solution.py:19
  145.2 2.3 %convolution_convert_fusion.2 = bf16[512,1024]{1,0:T(8,128)(2,1)} fusion(bf16[512,1024]{1,0:T(8,128)(2,1)S(1)} %copy-done.12, bf16[1024,1024]{1,0:T(8,128)(2,1)S(1)} %bitcast_select_fusion), kind=kOutput, calls=%fused_computation.24 | convolution fusion | flops 1074266112 | bytes 4194304 | tf_op jit(solution)/shard_map/dot_general | solution.py:205
  147.5 5.1 %collective-permute-done.9 = bf16[128,512]{1,0:T(8,128)(2,1)S(1)} collective-permute-done((bf16[128,512]{1,0:T(8,128)(2,1)S(1)}, bf16[128,512]{1,0:T(8,128)(2,1)S(1)}, u32[]{:S(2)}, u32[]{:S(2)}) %collective-permute-start.9) | collective-permute-done | bytes 131104 | tf_op jit(solution)/shard_map/ppermute | solution.py:19
  153.8 3.0 %collective-permute-start.12 = (bf16[64,512]{1,0:T(8,128)(2,1)S(1)}, bf16[64,512]{1,0:T(8,128)(2,1)S(1)}, u32[]{:S(2)}, u32[]{:S(2)}) collective-permute-start(bf16[64,512]{1,0:T(8,128)(2,1)S(1)} %fusion.42), channel_id=1, source_target_pairs={{0,4},{1,5},{2,6},{3,7},{4,0},{5,1},{6,2},{7,3},{8,12},{9,13},{10,... | collective-permute-start | bytes 196616 | tf_op jit(solution)/shard_map/ppermute | solution.py:19
  158.7 2.1 %collective-permute-done.12 = bf16[64,512]{1,0:T(8,128)(2,1)S(1)} collective-permute-done((bf16[64,512]{1,0:T(8,128)(2,1)S(1)}, bf16[64,512]{1,0:T(8,128)(2,1)S(1)}, u32[]{:S(2)}, u32[]{:S(2)}) %collective-permute-start.12) | collective-permute-done | bytes 65568 | tf_op jit(solution)/shard_map/ppermute | solution.py:19
  163.5 4.5 %collective-permute-done.14 = bf16[4,64,512]{2,1,0:T(8,128)(2,1)S(1)} collective-permute-done((bf16[4,64,512]{2,1,0:T(8,128)(2,1)S(1)}, bf16[4,64,512]{2,1,0:T(8,128)(2,1)S(1)}, u32[]{:S(2)}, u32[]{:S(2)}) %collective-permute-start.14) | collective-permute-done | bytes 262176 | tf_op jit(solution)/shard_map/ppermute | solution.py:19
  (164 shorter events, 73.9 us)
Async XLA Ops:
  0.6 15.1 %collective-permute-start.1 = (bf16[256,1024]{1,0:T(8,128)(2,1)}, bf16[256,1024]{1,0:T(8,128)(2,1)S(1)}, u32[]{:S(2)}, u32[]{:S(2)}) collective-permute-start(bf16[256,1024]{1,0:T(8,128)(2,1)} %param.10), channel_id=1, source_target_pairs={{0,16},{8,24},{16,0},{24,8},{1,17},{9,25},{17,1},{25,9},{2,18},{10... | collective-permute-start | bytes 1572872 | tf_op jit(solution)/shard_map/ppermute | solution.py:19
  3.6 12.8 %collective-permute-start = (bf16[256,1024]{1,0:T(8,128)(2,1)}, bf16[256,1024]{1,0:T(8,128)(2,1)S(1)}, u32[]{:S(2)}, u32[]{:S(2)}) collective-permute-start(bf16[256,1024]{1,0:T(8,128)(2,1)} %param.10), channel_id=1, source_target_pairs={{0,8},{8,0},{16,24},{24,16},{1,9},{9,1},{17,25},{25,17},{2,10},{10... | collective-permute-start | bytes 1572872 | tf_op jit(solution)/shard_map/ppermute | solution.py:19
  3.6 12.7 %copy-start.13 = (bf16[1024,16]{0,1:T(8,128)(2,1)S(1)}, bf16[1024,16]{0,1:T(8,128)(2,1)}, u32[]{:S(2)}) copy-start(bf16[1024,16]{0,1:T(8,128)(2,1)} %param.11) | copy-start | bytes 98308
  3.6 14.0 %copy-start.17 = (bf16[256,1024]{1,0:T(8,128)(2,1)S(1)}, bf16[256,1024]{1,0:T(8,128)(2,1)}, u32[]{:S(2)}) copy-start(bf16[256,1024]{1,0:T(8,128)(2,1)} %param.10) | copy-start | bytes 1572868
  15.8 1.9 %collective-permute-start.2 = (bf16[256,1024]{1,0:T(8,128)(2,1)S(1)}, bf16[256,1024]{1,0:T(8,128)(2,1)S(1)}, u32[]{:S(2)}, u32[]{:S(2)}) collective-permute-start(bf16[256,1024]{1,0:T(8,128)(2,1)S(1)} %collective-permute-done.1), channel_id=1, source_target_pairs={{0,8},{8,0},{16,24},{24,16},{1,9},{9,1},{17,25},{25,17},{2,10},{10... | collective-permute-start | bytes 1572872 | tf_op jit(solution)/shard_map/ppermute | solution.py:19
  15.8 5.8 %copy-start.19 = (pred[4]{0:T(512)(128)(4,1)}, pred[4]{0:T(512)(128)(4,1)S(1)}, u32[]{:S(2)}) copy-start(pred[4]{0:T(512)(128)(4,1)S(1)} %compare_and_fusion.1) | copy-start | bytes 16
  29.0 13.4 %all-to-all-start = ((bf16[8,8,1024]{2,1,0:T(8,128)(2,1)}), bf16[8,8,1024]{2,1,0:T(8,128)(2,1)S(1)}, u32[]{:S(2)}, u32[]{:S(2)}) async-start(bf16[8,8,1024]{2,1,0:T(8,128)(2,1)} %reshape.226), calls=%async_computation | async-start | bytes 262144 | tf_op jit(solution)/shard_map/all_to_all | solution.py:87
  56.4 3.7 %copy-start.8 = (bf16[2,64,1024]{2,1,0:T(8,128)(2,1)S(1)}, bf16[2,64,1024]{2,1,0:T(8,128)(2,1)}, u32[]{:S(2)}) copy-start(bf16[2,64,1024]{2,1,0:T(8,128)(2,1)} %reshape.228) | copy-start | bytes 786436
  72.2 8.4 %copy-start.21 = (s32[8]{0:T(128)S(1)}, s32[8]{0:T(128)}, u32[]{:S(2)}) copy-start(s32[8]{0:T(128)} %fusion.76) | copy-start | bytes 100
  77.0 19.7 %all-to-all-start.1 = ((bf16[32,8,1024]{2,1,0:T(8,128)(2,1)}), bf16[32,8,1024]{2,1,0:T(8,128)(2,1)}, u32[]{:S(2)}, u32[]{:S(2)}) async-start(bf16[32,8,1024]{2,1,0:T(8,128)(2,1)} %copy.48), calls=%async_computation.1 | async-start | bytes 1048576 | tf_op jit(solution)/shard_map/all_to_all | solution.py:102
  115.0 4.5 %collective-permute-start.3 = (bf16[1088,512]{1,0:T(8,128)(2,1)}, bf16[1088,512]{1,0:T(8,128)(2,1)}, u32[]{:S(2)}, u32[]{:S(2)}) collective-permute-start(bf16[1088,512]{1,0:T(8,128)(2,1)} %pad_maximum_fusion.1), channel_id=1, source_target_pairs={{0,8},{8,0},{16,24},{24,16},{1,9},{9,1},{17,25},{25,17},{2,10},{10... | collective-permute-start | bytes 3342344 | tf_op jit(solution)/shard_map/ppermute | solution.py:19
  121.0 4.1 %copy-start.7 = (bf16[2,64,1024]{2,1,0:T(8,128)(2,1)S(1)}, bf16[2,64,1024]{2,1,0:T(8,128)(2,1)}, u32[]{:S(2)}) copy-start(bf16[2,64,1024]{2,1,0:T(8,128)(2,1)} %copy-done.6) | copy-start | bytes 786436
  121.0 4.1 %copy-start.9 = (bf16[2,64,1024]{2,1,0:T(8,128)(2,1)S(1)}, bf16[2,64,1024]{2,1,0:T(8,128)(2,1)}, u32[]{:S(2)}) copy-start(bf16[2,64,1024]{2,1,0:T(8,128)(2,1)} %reshape.228) | copy-start | bytes 786436
  122.6 8.8 %collective-permute-start.6 = (bf16[256,512]{1,0:T(8,128)(2,1)S(1)}, bf16[256,512]{1,0:T(8,128)(2,1)S(1)}, u32[]{:S(2)}, u32[]{:S(2)}) collective-permute-start(bf16[256,512]{1,0:T(8,128)(2,1)S(1)} %slice.217), channel_id=1, source_target_pairs={{0,1},{1,0},{2,3},{3,2},{4,5},{5,4},{6,7},{7,6},{8,9},{9,8},{10,11... | collective-permute-start | bytes 786440 | tf_op jit(solution)/shard_map/ppermute | solution.py:19
  124.4 10.2 %collective-permute-start.4 = (bf16[320,512]{1,0:T(8,128)(2,1)S(1)}, bf16[320,512]{1,0:T(8,128)(2,1)S(1)}, u32[]{:S(2)}, u32[]{:S(2)}) collective-permute-start(bf16[320,512]{1,0:T(8,128)(2,1)S(1)} %pad_maximum_fusion.4), channel_id=1, source_target_pairs={{0,16},{8,24},{16,0},{24,8},{1,17},{9,25},{17,1},{25,9},{2,18},{10... | collective-permute-start | bytes 983048 | tf_op jit(solution)/shard_map/ppermute | solution.py:19
  131.5 5.6 %collective-permute-start.7 = (bf16[128,512]{1,0:T(8,128)(2,1)S(1)}, bf16[128,512]{1,0:T(8,128)(2,1)S(1)}, u32[]{:S(2)}, u32[]{:S(2)}) collective-permute-start(bf16[128,512]{1,0:T(8,128)(2,1)S(1)} %slice.219), channel_id=1, source_target_pairs={{0,16},{8,24},{16,0},{24,8},{1,17},{9,25},{17,1},{25,9},{2,18},{10... | collective-permute-start | bytes 393224 | tf_op jit(solution)/shard_map/ppermute | solution.py:19
  134.8 5.8 %collective-permute-start.5 = (bf16[192,512]{1,0:T(8,128)(2,1)S(1)}, bf16[192,512]{1,0:T(8,128)(2,1)S(1)}, u32[]{:S(2)}, u32[]{:S(2)}) collective-permute-start(bf16[192,512]{1,0:T(8,128)(2,1)S(1)} %pad_maximum_fusion.12), channel_id=1, source_target_pairs={{0,1},{1,0},{2,3},{3,2},{4,5},{5,4},{6,7},{7,6},{8,9},{9,8},{10,11... | collective-permute-start | bytes 589832 | tf_op jit(solution)/shard_map/ppermute | solution.py:19
  140.7 6.7 %collective-permute-start.8 = (bf16[128,512]{1,0:T(8,128)(2,1)S(1)}, bf16[128,512]{1,0:T(8,128)(2,1)S(1)}, u32[]{:S(2)}, u32[]{:S(2)}) collective-permute-start(bf16[128,512]{1,0:T(8,128)(2,1)S(1)} %get-tuple-element.27), channel_id=1, source_target_pairs={{0,2},{1,3},{2,0},{3,1},{4,6},{5,7},{6,4},{7,5},{8,10},{9,11},{10,... | collective-permute-start | bytes 393224 | tf_op jit(solution)/shard_map/ppermute | solution.py:19
  141.3 11.3 %collective-permute-start.9 = (bf16[128,512]{1,0:T(8,128)(2,1)S(1)}, bf16[128,512]{1,0:T(8,128)(2,1)S(1)}, u32[]{:S(2)}, u32[]{:S(2)}) collective-permute-start(bf16[128,512]{1,0:T(8,128)(2,1)S(1)} %get-tuple-element.28), channel_id=1, source_target_pairs={{0,4},{1,5},{2,6},{3,7},{4,0},{5,1},{6,2},{7,3},{8,12},{9,13},{10,... | collective-permute-start | bytes 393224 | tf_op jit(solution)/shard_map/ppermute | solution.py:19
  142.9 9.6 %collective-permute-start.10 = (bf16[128,512]{1,0:T(8,128)(2,1)S(1)}, bf16[128,512]{1,0:T(8,128)(2,1)S(1)}, u32[]{:S(2)}, u32[]{:S(2)}) collective-permute-start(bf16[128,512]{1,0:T(8,128)(2,1)S(1)} %get-tuple-element.29), channel_id=1, source_target_pairs={{0,6},{1,7},{2,4},{3,5},{4,2},{5,3},{6,0},{7,1},{8,14},{9,15},{10,... | collective-permute-start | bytes 393224 | tf_op jit(solution)/shard_map/ppermute | solution.py:19
  152.6 6.2 %collective-permute-start.13 = (bf16[64,512]{1,0:T(8,128)(2,1)S(1)}, bf16[64,512]{1,0:T(8,128)(2,1)S(1)}, u32[]{:S(2)}, u32[]{:S(2)}) collective-permute-start(bf16[64,512]{1,0:T(8,128)(2,1)S(1)} %fusion.42), channel_id=1, source_target_pairs={{0,6},{1,7},{2,4},{3,5},{4,2},{5,3},{6,0},{7,1},{8,14},{9,15},{10,... | collective-permute-start | bytes 196616 | tf_op jit(solution)/shard_map/ppermute | solution.py:19
  153.8 7.0 %collective-permute-start.12 = (bf16[64,512]{1,0:T(8,128)(2,1)S(1)}, bf16[64,512]{1,0:T(8,128)(2,1)S(1)}, u32[]{:S(2)}, u32[]{:S(2)}) collective-permute-start(bf16[64,512]{1,0:T(8,128)(2,1)S(1)} %fusion.42), channel_id=1, source_target_pairs={{0,4},{1,5},{2,6},{3,7},{4,0},{5,1},{6,2},{7,3},{8,12},{9,13},{10,... | collective-permute-start | bytes 196616 | tf_op jit(solution)/shard_map/ppermute | solution.py:19
  156.8 4.7 %collective-permute-start.11 = (bf16[64,512]{1,0:T(8,128)(2,1)S(1)}, bf16[64,512]{1,0:T(8,128)(2,1)S(1)}, u32[]{:S(2)}, u32[]{:S(2)}) collective-permute-start(bf16[64,512]{1,0:T(8,128)(2,1)S(1)} %fusion.42), channel_id=1, source_target_pairs={{0,2},{1,3},{2,0},{3,1},{4,6},{5,7},{6,4},{7,5},{8,10},{9,11},{10,... | collective-permute-start | bytes 196616 | tf_op jit(solution)/shard_map/ppermute | solution.py:19
  161.6 6.4 %collective-permute-start.14 = (bf16[4,64,512]{2,1,0:T(8,128)(2,1)S(1)}, bf16[4,64,512]{2,1,0:T(8,128)(2,1)S(1)}, u32[]{:S(2)}, u32[]{:S(2)}) collective-permute-start(bf16[4,64,512]{2,1,0:T(8,128)(2,1)S(1)} %pad_maximum_fusion.5), channel_id=1, source_target_pairs={{0,1},{1,0},{2,3},{3,2},{4,5},{5,4},{6,7},{7,6},{8,9},{9,8},{10,11... | collective-permute-start | bytes 786440 | tf_op jit(solution)/shard_map/ppermute | solution.py:19
  (16 other events, 31.5 us)

commit v2 on v0

v2 whole, which is shorter than its diff:
```python
import functools
import math

import jax
import jax.numpy as jnp
import numpy as np
from jax import lax
from jax.experimental import pallas as pl
from jax.experimental.pallas import tpu as pltpu
from jax.sharding import PartitionSpec as P

logit_scale = 48.0
epsilon = 1e-06
f32 = jnp.float32
bf16 = jnp.bfloat16
vmem = pl.BlockSpec(memory_space=pltpu.VMEM)
smem = pl.BlockSpec(memory_space=pltpu.SMEM)
room = pltpu.CompilerParams(vmem_limit_bytes=48 * 1024 * 1024)


def swap(x, axis, size, bit):
    return lax.ppermute(x, axis, [(i, i ^ bit) for i in range(size)])


def tree(parts):
    while len(parts) > 1:
        parts = [parts[k] + parts[k + 1] for k in range(0, len(parts), 2)]
    return parts[0]


def dot(a, b):
    return jnp.dot(a, b, preferred_element_type=f32)


def dot_last(a, b):
    return lax.dot_general(a, b, (((1,), (1,)), ((), ())), preferred_element_type=f32)


def dot_first(a, b):
    return lax.dot_general(a, b, (((0,), (0,)), ((), ())), preferred_element_type=f32)


def one_hot(order):
    return (jnp.asarray(order, jnp.int32)[:, None] == jnp.arange(order.size)).astype(bf16)


def halves(x):
    n = x.shape[0] // 2
    return x[:n], x[n:]


def high_low(x):
    high = x.astype(bf16).astype(f32)
    return jnp.concatenate([high, (x - high).astype(bf16).astype(f32)], axis=0)


def joined(x):
    high, low = halves(x)
    return high + low


def gelu_both(pre):
    scale = math.sqrt(2.0 / math.pi)
    square = pre * pre
    bent = jnp.tanh(scale * (pre + 0.044715 * (square * pre)))
    cdf = 0.5 * (1.0 + bent)
    slope = 0.5 * (1.0 - bent * bent) * (scale * (1.0 + (3 * 0.044715) * square))
    return pre * cdf, cdf + pre * slope


def forward_kernel(images, factor, n_img, *refs):
    me, ctx, res, cot, unit, perm = refs[:6]
    blocks = refs[6 : 6 + n_img]
    stream_out, inverse_out, dispatch_out, combine_out, slots_out = refs[6 + n_img :]
    tokens = ctx.shape[0] // images
    deep = blocks[0].shape[0]
    slot_in, grad_out = [], []
    for b in range(images):
        at = pl.ds(b * tokens, tokens)
        mixed = res[at, :].astype(f32)
        for r in range(n_img):
            columns = pl.ds(pl.multiple_of((me[0] ^ r) * deep, deep), deep)
            mixed = mixed + dot(ctx[at, columns], blocks[r][...])
        stream = mixed.astype(bf16)
        stream_out[at, :] = stream
        stream32 = stream.astype(f32)
        inverse = lax.rsqrt(jnp.mean(stream32 * stream32, axis=-1, keepdims=True) + epsilon)
        inverse_out[at, :] = inverse
        normed = (stream32 * inverse).astype(bf16)
        expo = jnp.exp(factor * dot(normed, unit[...]))
        dispatch32 = expo / jnp.sum(expo, axis=0, keepdims=True)
        combine32 = expo / jnp.sum(expo, axis=1, keepdims=True)
        dispatch_out[at, :] = dispatch32
        combine_out[at, :] = combine32
        slot_in.append(dot_first(dispatch32.astype(bf16), normed).astype(bf16))
        grad_out.append(dot_first(combine32.astype(bf16), cot[at, :]).astype(bf16))
    parts = jnp.concatenate(slot_in + grad_out, axis=0)
    slots_out[...] = dot_first(perm[...], parts).astype(bf16)


def expert_kernel(got, perm, first, second, rows, act, grad_pre, back, sums, held):
    j, f = pl.program_id(0), pl.program_id(1)
    last = pl.num_programs(1) - 1

    @pl.when((j == 0) & (f == 0))
    def _():
        rows[...] = dot(perm[...], got[...]).astype(bf16).reshape(rows.shape)

    x, g = rows[2 * j], rows[2 * j + 1]
    first_w, second_w = first[0], second[0]
    pre = dot(x, first_w)
    value, slope = gelu_both(pre)
    value = value.astype(bf16)
    act[0] = value
    grad = (dot_last(g, second_w) * slope).astype(bf16)
    grad_pre[0] = grad
    part_out, part_in = dot(value, second_w), dot_last(grad, first_w)

    @pl.when(f == 0)
    def _():
        sums[0], sums[1] = part_out, part_in

    @pl.when(f > 0)
    def _():
        sums[0] += part_out
        sums[1] += part_in

    @pl.when(f == last)
    def _():
        held[2 * j] = sums[0].astype(bf16)
        held[2 * j + 1] = sums[1].astype(bf16)

    @pl.when((f == last) & (j == pl.num_programs(0) - 1))
    def _():
        parts = held[...].reshape(got.shape)
        back[...] = dot_first(perm[...], parts).astype(bf16)


def grads_kernel(rows, act, grad_pre, grad_first, grad_second):
    f = pl.program_id(1)
    deep = grad_second.shape[1]
    at = pl.ds(pl.multiple_of(f * deep, deep), deep)
    grad_second[0] = dot_first(act[0, :, at], rows[1]).astype(bf16)
    deep = grad_first.shape[1]
    at = pl.ds(pl.multiple_of(f * deep, deep), deep)
    grad_first[0] = dot_first(rows[0, :, at], grad_pre[0]).astype(bf16)


def backward_kernel(
    images, factor, me, back, perm, stream, inverse, cot, dispatch, combine, unit_t, left_p, left_q,
    grad_out, send, side_out,
):
    tokens = cot.shape[0] // images
    slots = unit_t.shape[0]
    half = send.shape[1]
    total = tree([back[r].astype(f32) for r in range(back.shape[0])]).astype(bf16)
    parts = dot(perm[...], total).astype(bf16)
    unit_sum = 0.0
    for b in range(images):
        at = pl.ds(b * tokens, tokens)
        slot_out = parts[b * slots : (b + 1) * slots]
        grad_slot_in = parts[(images + b) * slots : (images + b + 1) * slots]
        upstream = cot[at, :]
        inv = inverse[at, :]
        normed32 = stream[at, :].astype(f32) * inv
        normed = normed32.astype(bf16)
        dispatch32, combine32 = dispatch[at, :], combine[at, :]
        grad_combine = dot_last(upstream, slot_out)
        grad_dispatch = dot_last(normed, grad_slot_in)
        logits = combine32 * (
            grad_combine - jnp.sum(combine32 * grad_combine, axis=1, keepdims=True)
        ) + dispatch32 * (
            grad_dispatch - jnp.sum(dispatch32 * grad_dispatch, axis=0, keepdims=True)
        )
        logits = logits.astype(bf16)
        grad_normed = dot(dispatch32.astype(bf16), grad_slot_in) + factor * dot(logits, unit_t[...])
        unit_sum = unit_sum + dot_first(logits, normed)
        grad = upstream.astype(f32) + inv * (
            grad_normed - normed32 * jnp.mean(normed32 * grad_normed, axis=-1, keepdims=True)
        )
        grad_out[at, :] = grad.astype(bf16)
    n = left_p.shape[0]
    send[:n, :] = dot(left_p[...], grad_out[:, :half]).astype(bf16)
    send[n : 2 * n, :] = dot(left_q[...], grad_out[:, half:]).astype(bf16)
    low, high = halves(factor * unit_sum)
    mine = jnp.where((me[0] & 1) == 0, low, high)
    other = jnp.where((me[0] & 1) == 0, high, low)
    side_out[...] = jnp.concatenate([mine[:, :half], mine[:, half:]], axis=0)
    other = jnp.concatenate([other[:, :half], other[:, half:]], axis=0)
    send[2 * n :, :] = high_low(other).astype(bf16)


def keep_kernel(left_p, left_q, grad, out):
    half = out.shape[1]
    n = left_p.shape[0]
    out[:n, :] = dot(left_p[...], grad[:, :half]).astype(bf16)
    out[n:, :] = dot(left_q[...], grad[:, half:]).astype(bf16)


def first_kernel(me, keep, side, got, p_out, q_out, side_out, send_p, send_q):
    n = keep.shape[0] // 2
    p0, p1 = halves(keep[:n, :].astype(f32) + got[:n, :].astype(f32))
    q0, q1 = halves(keep[n:, :].astype(f32) + got[n : 2 * n, :].astype(f32))
    low, high = halves(side[...] + joined(got[2 * n :, :].astype(f32)))
    lower = (me[0] & 2) == 0
    side_out[...] = jnp.where(lower, low, high)
    p_out[...] = p0.astype(bf16)
    q_out[...] = q0.astype(bf16)
    other = high_low(jnp.where(lower, high, low))
    send_p[...] = jnp.concatenate([p1, other], axis=0).astype(bf16)
    send_q[...] = q1.astype(bf16)


def second_kernel(p_in, q_in, side, got_p, got_q, p_out, q_out, side_out, send_p, send_q):
    n = p_in.shape[0]
    got = got_p[...].astype(f32)
    p0, p1 = halves(p_in[...].astype(f32) + got[:n])
    q0, q1 = halves(q_in[...].astype(f32) + got_q[...].astype(f32))
    mine = high_low(side[...] + joined(got[n:]))
    side_out[...] = mine
    p_out[...] = p0.astype(bf16)
    q_out[...] = q0.astype(bf16)
    send_p[...] = jnp.concatenate([p1, mine], axis=0).astype(bf16)
    send_q[...] = q1.astype(bf16)


def third_kernel(p_in, q_in, side, got_p, got_q, keep, side_out, *sends):
    n = p_in.shape[0]
    got = got_p[...].astype(f32)
    p = p_in[...].astype(f32) + got[:n]
    q = q_in[...].astype(f32) + got_q[...].astype(f32)
    mine = high_low(joined(side[...]) + joined(got[n:]))
    side_out[...] = mine
    n = n // (len(sends) + 1)
    keep[...] = jnp.concatenate([p[:n], q[:n]], axis=0)
    for m, send in enumerate(sends, 1):
        at = slice(m * n, (m + 1) * n)
        send[...] = jnp.concatenate([p[at], q[at], mine], axis=0).astype(bf16)


def fourth_kernel(keep, side, *refs):
    gots, (own, side_out) = refs[:-2], refs[-2:]
    n = keep.shape[0]
    gots = [g[...].astype(f32) for g in gots]
    own[...] = tree([keep[...]] + [g[:n] for g in gots]).astype(bf16)
    total = tree([joined(side[...])] + [joined(g[n:]) for g in gots])
    side_out[...] = high_low(total).astype(bf16)


def last_kernel(me, near, far, out):
    n = near.shape[1] // 2
    half = near.shape[2]
    for z in range(near.shape[0]):
        for y, ref in enumerate((near, far)):
            block = ref[z].astype(f32)
            at = me[1] ^ (2 * z + y)
            out[at, :, :half] = block[:n]
            out[at, :, half:] = block[n:]


def shards(n_img, n_exp, context, residual, cotangent, proj_weight, slot_params, expert_in, expert_out):
    images, tokens, width = context.shape
    rows = images * tokens
    owned, _, hidden = expert_in.shape
    slots = slot_params.shape[1]
    half = width // 2
    factor = logit_scale / math.sqrt(width)
    me_img = lax.axis_index("img")
    me_exp = lax.axis_index("exp")
    me = jnp.stack([me_img, me_exp]).astype(jnp.int32)
    flat_ctx = context.reshape(rows, width)
    flat_cot = cotangent.reshape(rows, width)
    shape = jax.ShapeDtypeStruct

    near = swap(proj_weight, "img", n_img, 1)
    far = swap(proj_weight, "img", n_img, 2)
    far_near = swap(far, "img", n_img, 1)
    blocks = [proj_weight, near, far, far_near]
    order = jnp.arange(n_img) ^ me_img

    sub = width // (n_img * n_exp)
    ctx_t = flat_ctx.T.reshape(n_img, n_exp, sub, rows)
    ctx_t = jnp.take(ctx_t, order, axis=0)
    ctx_t = jnp.take(ctx_t, jnp.arange(n_exp) ^ me_exp, axis=1)
    ctx_t = ctx_t.reshape(2, 2, n_exp // 2, 2, sub, rows)
    left_p = ctx_t.transpose(1, 0, 3, 2, 4, 5).reshape(2, -1, rows)
    left_q = ctx_t.transpose(1, 3, 0, 2, 4, 5).reshape(2, -1, rows)

    params32 = slot_params.astype(f32)
    slot_norm = jnp.sqrt(jnp.sum(params32 * params32, axis=0, keepdims=True) + epsilon)
    unit32 = params32 / slot_norm
    unit = unit32.astype(bf16)
    unit_t32 = unit32.T
    unit_t = unit_t32.astype(bf16)

    perm = one_hot(
        np.arange(slots * 2 * images).reshape(slots, 2, images).transpose(1, 2, 0).reshape(-1)
    )
    stream, inverse, dispatch32, combine32, out = pl.pallas_call(
        functools.partial(forward_kernel, images, factor, n_img),
        in_specs=[smem] + [vmem] * (5 + n_img),
        out_specs=[vmem] * 5,
        out_shape=[
            shape((rows, width), bf16),
            shape((rows, 1), f32),
            shape((rows, slots), f32),
            shape((rows, slots), f32),
            shape((slots * 2 * images, width), bf16),
        ],
        compiler_params=room,
        name="forward",
    )(me, flat_ctx, residual.reshape(rows, width), flat_cot, unit, perm, *blocks)

    got = lax.all_to_all(
        out.reshape(n_exp, -1, width), "exp", split_axis=0, concat_axis=0, tiled=True
    )
    got = lax.all_gather(got, "img", axis=0, tiled=True).reshape(-1, width)

    sources = n_img * n_exp
    count = sources * images
    shuffle = one_hot(
        np.arange(count * owned * 2)
        .reshape(sources, owned, 2, images)
        .transpose(1, 2, 0, 3)
        .reshape(-1)
    )
    step = min(hidden, 512)
    whole = lambda s: pl.BlockSpec(s, lambda j, f: (0,) * len(s))
    act_spec = pl.BlockSpec((1, count, step), lambda j, f: (j, 0, f))
    slot_rows, act, grad_pre, back = pl.pallas_call(
        expert_kernel,
        grid=(owned, hidden // step),
        in_specs=[
            whole(got.shape),
            whole(shuffle.shape),
            pl.BlockSpec((1, width, step), lambda j, f: (j, 0, f)),
            pl.BlockSpec((1, step, width), lambda j, f: (j, f, 0)),
        ],
        out_specs=[whole((owned * 2, count, width)), act_spec, act_spec, whole(got.shape)],
        out_shape=[
            shape((owned * 2, count, width), bf16),
            shape((owned, count, hidden), bf16),
            shape((owned, count, hidden), bf16),
            shape(got.shape, bf16),
        ],
        scratch_shapes=[
            pltpu.VMEM((2, count, width), f32),
            pltpu.VMEM((owned * 2, count, width), bf16),
        ],
        compiler_params=room,
        name="experts",
    )(got, shuffle, expert_in, expert_out)

    back = lax.all_to_all(
        back.reshape(sources, -1, width), ("img", "exp"), split_axis=0, concat_axis=0, tiled=True
    )

    cuts = 4
    part = lambda s: pl.BlockSpec((1,) + s, lambda j, f: (j, 0, 0))
    grad_expert_in, grad_expert_out = pl.pallas_call(
        grads_kernel,
        grid=(owned, cuts),
        in_specs=[
            pl.BlockSpec((2, count, width), lambda j, f: (j, 0, 0)),
            part((count, hidden)),
            part((count, hidden)),
        ],
        out_specs=[
            pl.BlockSpec((1, width // cuts, hidden), lambda j, f: (j, f, 0)),
            pl.BlockSpec((1, hidden // cuts, width), lambda j, f: (j, f, 0)),
        ],
        out_shape=[shape(expert_in.shape, bf16), shape(expert_out.shape, bf16)],
        compiler_params=room,
        name="expert_grads",
    )(slot_rows, act, grad_pre)
    back, grad_expert_in, grad_expert_out = lax.optimization_barrier(
        (back, grad_expert_in, grad_expert_out)
    )

    n = left_p.shape[1]
    side_rows = 2 * slots
    grad_residual, send, side = pl.pallas_call(
        functools.partial(backward_kernel, images, factor),
        in_specs=[smem] + [vmem] * 10,
        out_specs=[vmem] * 3,
        out_shape=[
            shape((rows, width), bf16),
            shape((2 * n + side_rows, half), bf16),
            shape((slots, half), f32),
        ],
        compiler_params=room,
        name="backward",
    )(
        me, back.reshape(n_img, -1, width), perm, stream, inverse, flat_cot, dispatch32, combine32,
        unit_t, left_p[1], left_q[1],
    )

    got = swap(send, "img", n_img, 1)
    keep = pl.pallas_call(
        keep_kernel,
        in_specs=[vmem] * 3,
        out_specs=vmem,
        out_shape=shape((2 * n, half), bf16),
        compiler_params=room,
        name="keep",
    )(left_p[0], left_q[0], grad_residual)
    n, side_rows = n // 2, slots
    p, q, side, send_p, send_q = pl.pallas_call(
        first_kernel,
        in_specs=[smem] + [vmem] * 3,
        out_specs=[vmem] * 5,
        out_shape=[
            shape((n, half), bf16),
            shape((n, half), bf16),
            shape((slots // 2, half), f32),
            shape((n + slots, half), bf16),
            shape((n, half), bf16),
        ],
        compiler_params=room,
        name="first",
    )(me, keep, side, got)
    got_p = swap(send_p, "img", n_img, 2)
    got_q = swap(send_q, "exp", n_exp, 1)
    n = n // 2
    p, q, side, send_p, send_q = pl.pallas_call(
        second_kernel,
        in_specs=[vmem] * 5,
        out_specs=[vmem] * 5,
        out_shape=[
            shape((n, half), bf16),
            shape((n, half), bf16),
            shape((slots, half), f32),
            shape((n + slots, half), bf16),
            shape((n, half), bf16),
        ],
        compiler_params=room,
        name="second",
    )(p, q, side, got_p, got_q)
    got_p = swap(send_p, "exp", n_exp, 1)
    got_q = swap(send_q, "img", n_img, 2)
    groups = n_exp // 2
    n = n // groups
    keep, side, *sends = pl.pallas_call(
        third_kernel,
        in_specs=[vmem] * 5,
        out_specs=[vmem] * (1 + groups),
        out_shape=[shape((2 * n, half), f32), shape((slots, half), f32)]
        + [shape((2 * n + slots, half), bf16)] * (groups - 1),
        compiler_params=room,
        name="third",
    )(p, q, side, got_p, got_q)
    gots = [swap(s, "exp", n_exp, 2 * m) for m, s in enumerate(sends, 1)]
    own, side = pl.pallas_call(
        fourth_kernel,
        in_specs=[vmem] * (1 + groups),
        out_specs=[vmem] * 2,
        out_shape=[shape((2 * n, half), bf16), shape((slots, half), bf16)],
        compiler_params=room,
        name="fourth",
    )(keep, side, *gots)
    held = jnp.stack([own] + [swap(own, "exp", n_exp, 2 * m) for m in range(1, groups)])
    side = jnp.stack([side, swap(side, "img", n_img, 2)])
    other = swap(side, "img", n_img, 1)
    grad_proj = pl.pallas_call(
        last_kernel,
        in_specs=[smem, vmem, vmem],
        out_specs=vmem,
        out_shape=shape((n_exp, n, width), f32),
        compiler_params=room,
        name="last",
    )(me, held, swap(held, "exp", n_exp, 1)).reshape(-1, width)

    side = jnp.stack([side, other]).astype(f32).reshape(2, 2, 2, slots // 2, half).sum(axis=2)
    side = jnp.where((me_img & 1) == 0, side, side[::-1])
    side = jnp.where((me_img & 2) == 0, side, side[:, ::-1])
    grad_unit = side.transpose(0, 2, 1, 3).reshape(slots, width)
    grad_slots = (
        (grad_unit - unit_t32 * jnp.sum(unit_t32 * grad_unit, axis=1, keepdims=True)) / slot_norm.T
    ).T

    whole_proj = jnp.take(jnp.stack(blocks), order, axis=0).reshape(width, width)
    grad_context = dot_last(grad_residual, whole_proj).astype(bf16)
    return (
        grad_context.reshape(images, tokens, width),
        grad_residual.reshape(images, tokens, width),
        grad_proj,
        grad_slots,
        grad_expert_in,
        grad_expert_out,
    )


def solution(mesh):
    n_img, n_exp = mesh.shape["img"], mesh.shape["exp"]
    placed = (
        P(("img", "exp"), None, None),
        P(("img", "exp"), None, None),
        P(("img", "exp"), None, None),
        P("img", None),
        P(),
        P("exp", None, "img"),
        P("exp", "img", None),
    )
    return jax.shard_map(
        functools.partial(shards, n_img, n_exp),
        mesh=mesh,
        in_specs=placed,
        out_specs=(
            P(("img", "exp"), None, None),
            P(("img", "exp"), None, None),
            P("img", None),
            P(),
            P("exp", None, "img"),
            P("exp", "img", None),
        ),
        check_vma=False,
    )
```

time: 390 us -> 149 us (0.38)
  waiting for transfers between devices: 288 us -> 44.3 us
  matrix products: 35.9 us -> 2.26 us
  Pallas kernels: 0 us -> 27.2 us
  local copies, waits for them, and re-layouts: 13.8 us -> 29.9 us
  between operations: 14.3 us -> 1.09 us
  starting transfers between devices: 20.3 us -> 27.1 us
  blocking collectives: 11.6 us -> 7.16 us
    psum x2 -> x0, waiting for transfers between devices: 195 us -> none  [the longest x1 121 us: shards(): grad_unit = lax.psum(local_unit, ('img', 'exp'))]
    reduce_scatter x3 -> x0, waiting for transfers between devices: 51 us -> none  [the longest x1 21.9 us: shards(): lax.psum_scatter(summed_grad, 'img', scatter_dimension=0, tiled=True)]
    dot_general x16 -> x1, matrix products: 34.7 us -> 2.26 us  [dot_last(): lax.dot_general(a, b, (((1,), (1,)), ((), ())), preferred_element_type=f32)]
    ppermute x0 -> x17, waiting for transfers between devices: none -> 29.5 us  [swap(): return lax.ppermute(x, axis, [(i, i ^ bit) for i in range(size)])]
    pallas_call x0 -> x10, Pallas kernels: none -> 27.2 us  [the longest x1 8.3 us: shards(): pl.pallas_call(expert_kernel, grid=(owned, hidden // step), in_specs=[who...]
    all_gather x1 -> x0, waiting for transfers between devices: 26.1 us -> none  [shards(): lax.all_gather(proj_weight, 'img', axis=0, tiled=True)]
    ppermute x0 -> x17, starting transfers between devices: none -> 18.2 us  [swap(): return lax.ppermute(x, axis, [(i, i ^ bit) for i in range(size)])]
    all_to_all x4 -> x2, starting transfers between devices: 19.9 us -> 8.87 us  [the longest x1 6.08 us: shards(): lax.all_to_all(out.reshape(n_exp, -1, width), 'exp', split_axis=0, concat...]
  transfers between devices with their start and end apart: 10 -> 19, of which waited for: 9 -> 10; matrix products, arithmetic and copies ran while one was open for 7% -> 17% of each run, Pallas kernels for 0% -> 4%
where the time goes in v2:
time: 149 us; the launch traced here: 148 us
  waiting for transfers between devices  44.3 us (30%)
  local copies, waits for them, and re-layouts  29.9 us (20%)
  Pallas kernels  27.2 us (18%)
  starting transfers between devices  27.1 us (18%)
  other arithmetic  9.03 us (6%)
  blocking collectives  7.16 us (5%)
  matrix products  2.26 us (2%)
    ppermute x17, waiting for transfers between devices, swap(): return lax.ppermute(x, axis, [(i, i ^ bit) for i in range(size)])  29.5 us
    ppermute x17, starting transfers between devices, swap(): return lax.ppermute(x, axis, [(i, i ^ bit) for i in range(size)])  18.2 us
    unnamed x92, local copies, waits for them, and re-layouts  15.7 us
    pallas_call x1, Pallas kernels, shards(): pl.pallas_call(expert_kernel, grid=(owned, hidden // step), in_specs=[who...  8.3 us
    all_to_all x1, waiting for transfers between devices, shards(): lax.all_to_all(out.reshape(n_exp, -1, width), 'exp', split_axis=0, concat...  7.53 us
    all_to_all x1, waiting for transfers between devices, shards(): lax.all_to_all(back.reshape(sources, -1, width), ('img', 'exp'), split_ax...  7.31 us
    all_gather x1, blocking collectives, shards(): got = lax.all_gather(got, 'img', axis=0, tiled=True).reshape(-1, width)  7.16 us
    all_to_all x1, starting transfers between devices, shards(): lax.all_to_all(out.reshape(n_exp, -1, width), 'exp', split_axis=0, concat...  6.08 us
  transfers between devices with their start and end apart: 19, of which 10 were waited for; matrix products, arithmetic and copies ran while one was open for 17% of the time, Pallas kernels for 4%

profile of v2, /device:TPU:0, one launch (start us, length us, event | category | flops | bytes accessed | tf_op | source)
XLA Modules:
  0.0 148.0 jit_solution(4667041976334425424)
XLA Ops:
  0.6 3.0 %collective-permute-start.1 = (bf16[256,1024]{1,0:T(8,128)(2,1)}, bf16[256,1024]{1,0:T(8,128)(2,1)S(1)}, u32[]{:S(2)}, u32[]{:S(2)}) collective-permute-start(bf16[256,1024]{1,0:T(8,128)(2,1)} %refs_6_.1), channel_id=1, source_target_pairs={{0,16},{8,24},{16,0},{24,8},{1,17},{9,25},{17,1},{25,9},{2,18},{10... | collective-permute-start | bytes 1572872 | tf_op jit(solution)/shard_map/ppermute | solution.py:22
  5.4 10.3 %collective-permute-done.1.refs_8_ = bf16[256,1024]{1,0:T(8,128)(2,1)S(1)} collective-permute-done((bf16[256,1024]{1,0:T(8,128)(2,1)}, bf16[256,1024]{1,0:T(8,128)(2,1)S(1)}, u32[]{:S(2)}, u32[]{:S(2)}) %collective-permute-start.1) | collective-permute-done | bytes 524320 | tf_op jit(solution)/shard_map/ppermute | solution.py:22
  16.0 2.3 %copy.26 = bf16[1024,512]{1,0:T(8,128)(2,1)} copy(bf16[1024,512]{0,1:T(8,128)(2,1)} %bitcast.65) | data formatting | bytes 2097152 | tf_op jit(solution)/shard_map/transpose | solution.py:282
  18.3 2.9 %gather_fusion = bf16[4,8,32,512]{3,2,1,0:T(8,128)(2,1)} fusion(bf16[4,8,32,512]{3,2,1,0:T(8,128)(2,1)} %bitcast.83, s32[1024]{0:T(1024)S(1)} %pad_clamp_fusion.1), kind=kCustom, calls=%fused_computation | custom fusion | bytes 2097168 | tf_op jit(solution)/shard_map/jit(_take)/gather | solution.py:283
  21.4 2.4 %broadcast_select_fusion = bf16[4,8,32,512]{3,2,1,0:T(8,128)(2,1)} fusion(bf16[4,8,32,512]{3,2,1,0:T(8,128)(2,1)} %gather_fusion, pred[4]{0:T(512)(128)(4,1)S(1)} %compare_and_fusion), kind=kLoop, calls=%fused_computation.6 | loop fusion | flops 524288 | bytes 2097156 | tf_op jit(solution)/shard_map/jit(_take)/select_n | solution.py:283
  23.8 4.9 %forward.1 = (bf16[512,1024]{1,0:T(8,128)(2,1)S(1)}, f32[512,1]{1,0:T(8,128)S(1)}, f32[512,16]{1,0:T(8,128)S(1)}, f32[512,16]{1,0:T(8,128)S(1)}, bf16[64,1024]{1,0:T(8,128)(2,1)S(1)}) custom-call(s32[2]{0:T(128)S(1)} %pad_add_fusion.refs_0_.me, bf16[512,1024]{1,0:T(8,128)(2,1)S(1)} %bitcast.66, bf16[512,1024]{1,0:T(8,128)(2,1)} %bitcast.86, ...), custom_call_target="tpu_custom_call" | custom-call | tf_op jit(solution)/shard_map/forward/pallas_call | solution.py:299
  32.4 6.1 %all-to-all-start = ((bf16[8,8,1024]{2,1,0:T(8,128)(2,1)}), bf16[8,8,1024]{2,1,0:T(8,128)(2,1)S(1)}, u32[]{:S(2)}, u32[]{:S(2)}) async-start(bf16[8,8,1024]{2,1,0:T(8,128)(2,1)} %bitcast.78), calls=%async_computation | async-start | bytes 262144 | tf_op jit(solution)/shard_map/all_to_all | solution.py:314
  38.6 7.5 %all-to-all-done = bf16[8,8,1024]{2,1,0:T(8,128)(2,1)S(1)} async-done(((bf16[8,8,1024]{2,1,0:T(8,128)(2,1)}), bf16[8,8,1024]{2,1,0:T(8,128)(2,1)S(1)}, u32[]{:S(2)}, u32[]{:S(2)}) %all-to-all-start) | async-done | bytes 131104 | tf_op jit(solution)/shard_map/all_to_all | solution.py:314
  46.1 7.2 %all_gather.3 = bf16[32,8,1024]{2,1,0:T(8,128)(2,1)S(1)} all-gather(bf16[8,8,1024]{2,1,0:T(8,128)(2,1)S(1)} %all-to-all-done), channel_id=1, replica_groups=mesh['img'=4,'exp'=8] {'img'}, dimensions={0}, use_global_device_ids=true | all-gather | bytes 655360 | tf_op jit(solution)/shard_map/all_gather | solution.py:317
  53.3 8.3 %experts.1 = (bf16[4,64,1024]{2,1,0:T(8,128)(2,1)S(1)}, bf16[2,64,1024]{2,1,0:T(8,128)(2,1)S(1)}, bf16[2,64,1024]{2,1,0:T(8,128)(2,1)S(1)}, bf16[256,1024]{1,0:T(8,128)(2,1)}) custom-call(bf16[256,1024]{1,0:T(8,128)(2,1)S(1)} %bitcast.67, bf16[256,256]{1,0:T(8,128)(2,1)S(1)} %fusion.2.perm, bf16[2,1024,1024]{2,1,0:T(8,128)(2,1)} %first.2, ...), custom_call_target="tpu_custom_call" | custom-call | tf_op jit(solution)/shard_map/experts/pallas_call | solution.py:330
  63.8 2.8 %all-to-all-start.1 = ((bf16[32,8,1024]{2,1,0:T(8,128)(2,1)}), bf16[32,8,1024]{2,1,0:T(8,128)(2,1)S(1)}, u32[]{:S(2)}, u32[]{:S(2)}) async-start(bf16[32,8,1024]{2,1,0:T(8,128)(2,1)} %bitcast.7), calls=%async_computation.1 | async-start | bytes 1048576 | tf_op jit(solution)/shard_map/all_to_all | solution.py:354
  69.8 5.6 %expert_grads.1 = (bf16[2,1024,1024]{2,1,0:T(8,128)(2,1)}, bf16[2,1024,1024]{2,1,0:T(8,128)(2,1)}) custom-call(bf16[4,64,1024]{2,1,0:T(8,128)(2,1)S(1)} %copy-done.13, bf16[2,64,1024]{2,1,0:T(8,128)(2,1)S(1)} %copy-done.21, bf16[2,64,1024]{2,1,0:T(8,128)(2,1)S(1)} %copy-done.23), custom_call_target="tpu_custom_call" | custom-call | tf_op jit(solution)/shard_map/expert_grads/pallas_call | solution.py:360
  75.4 7.3 %all-to-all-done.1 = bf16[32,8,1024]{2,1,0:T(8,128)(2,1)S(1)} async-done(((bf16[32,8,1024]{2,1,0:T(8,128)(2,1)}), bf16[32,8,1024]{2,1,0:T(8,128)(2,1)S(1)}, u32[]{:S(2)}, u32[]{:S(2)}) %all-to-all-start.1) | async-done | bytes 524320 | tf_op jit(solution)/shard_map/all_to_all | solution.py:354
  85.9 3.9 %backward.1 = (bf16[512,1024]{1,0:T(8,128)(2,1)}, bf16[1056,512]{1,0:T(8,128)(2,1)S(1)}, f32[16,512]{1,0:T(8,128)S(1)}) custom-call(s32[2]{0:T(128)S(1)} %pad_add_fusion.refs_0_.me, bf16[4,64,1024]{2,1,0:T(8,128)(2,1)S(1)} %bitcast.68, bf16[64,64]{1,0:T(8,128)(2,1)S(1)} %fusion.8.refs_5_.perm, bf16[512,1024]{1,0:T(8,128)(2,1)S(1)} %copy-done.11, ...), custom_call_target="tpu_custom_call" | custom-call | tf_op jit(solution)/shard_map/backward/pallas_call | solution.py:382
  94.7 7.4 %collective-permute-done.5.got_q = bf16[256,512]{1,0:T(8,128)(2,1)S(1)} collective-permute-done((bf16[256,512]{1,0:T(8,128)(2,1)S(1)}, bf16[256,512]{1,0:T(8,128)(2,1)S(1)}, u32[]{:S(2)}, u32[]{:S(2)}) %collective-permute-start.5) | collective-permute-done | bytes 262176 | tf_op jit(solution)/shard_map/ppermute | solution.py:22
  116.0 3.1 %collective-permute-start.9 = (bf16[80,512]{1,0:T(8,128)(2,1)}, bf16[80,512]{1,0:T(8,128)(2,1)S(1)}, u32[]{:S(2)}, u32[]{:S(2)}) collective-permute-start(bf16[80,512]{1,0:T(8,128)(2,1)} %get-tuple-element.68), channel_id=1, source_target_pairs={{0,4},{1,5},{2,6},{3,7},{4,0},{5,1},{6,2},{7,3},{8,12},{9,13},{10,... | collective-permute-start | bytes 245768 | tf_op jit(solution)/shard_map/ppermute | solution.py:22
  119.0 1.6 %pad_maximum_fusion = bf16[4,256,1024]{2,1,0:T(8,128)(2,1)} fusion(bf16[1,256,1024]{2,1,0:T(8,128)(2,1)S(1)} %bitcast.76, bf16[1,256,1024]{2,1,0:T(8,128)(2,1)S(1)} %bitcast.74, bf16[1,256,1024]{2,1,0:T(8,128)(2,1)S(1)} %bitcast.75, bf16[1,256,1024]{2,1,0:T(8,128)(2,1)S(1)} %bitcast.73), kind=kLoop, calls=%fused_computation.3 | loop fusion | flops 3145728 | bytes 4194304 | tf_op jit(solution)/shard_map/stack | solution.py:481
  120.6 3.7 %gather_fusion.2 = bf16[4,256,1024]{2,1,0:T(8,128)(2,1)} fusion(bf16[4,256,1024]{2,1,0:T(8,128)(2,1)} %pad_maximum_fusion, s32[1024]{0:T(1024)} %copy-done.41), kind=kCustom, calls=%fused_computation.2 | custom fusion | bytes 4194320 | tf_op jit(solution)/shard_map/jit(_take)/gather | solution.py:481
  125.9 1.9 %bitcast_select_fusion = bf16[1024,1024]{1,0:T(8,128)(2,1)S(1)} fusion(bf16[4,256,1024]{2,1,0:T(8,128)(2,1)} %gather_fusion.2, pred[1024]{0:T(1024)(128)(4,1)S(1)} %copy-done.42), kind=kLoop, calls=%fused_computation.4 | loop fusion | flops 1048576 | bytes 4195328 | tf_op jit(solution)/shard_map/jit(_take)/select_n | solution.py:481
  128.3 2.3 %convolution_convert_fusion = bf16[512,1024]{1,0:T(8,128)(2,1)} fusion(bf16[512,1024]{1,0:T(8,128)(2,1)S(1)} %copy-done.9, bf16[1024,1024]{1,0:T(8,128)(2,1)S(1)} %bitcast_select_fusion), kind=kOutput, calls=%fused_computation.5 | convolution fusion | flops 1074266112 | bytes 4194304 | tf_op jit(solution)/shard_map/dot_general | solution.py:36
  130.6 1.9 %collective-permute-start.12 = (bf16[64,512]{1,0:T(8,128)(2,1)S(1)}, bf16[64,512]{1,0:T(8,128)(2,1)S(1)}, u32[]{:S(2)}, u32[]{:S(2)}) collective-permute-start(bf16[64,512]{1,0:T(8,128)(2,1)S(1)} %get-tuple-element.70), channel_id=1, source_target_pairs={{0,4},{1,5},{2,6},{3,7},{4,0},{5,1},{6,2},{7,3},{8,12},{9,13},{10,... | collective-permute-start | bytes 196616 | tf_op jit(solution)/shard_map/ppermute | solution.py:22
  132.5 2.5 %collective-permute-start.13 = (bf16[64,512]{1,0:T(8,128)(2,1)S(1)}, bf16[64,512]{1,0:T(8,128)(2,1)S(1)}, u32[]{:S(2)}, u32[]{:S(2)}) collective-permute-start(bf16[64,512]{1,0:T(8,128)(2,1)S(1)} %get-tuple-element.70), channel_id=1, source_target_pairs={{0,6},{1,7},{2,4},{3,5},{4,2},{5,3},{6,0},{7,1},{8,14},{9,15},{10,... | collective-permute-start | bytes 196616 | tf_op jit(solution)/shard_map/ppermute | solution.py:22
  136.2 3.0 %collective-permute-done.12 = bf16[64,512]{1,0:T(8,128)(2,1)S(1)} collective-permute-done((bf16[64,512]{1,0:T(8,128)(2,1)S(1)}, bf16[64,512]{1,0:T(8,128)(2,1)S(1)}, u32[]{:S(2)}, u32[]{:S(2)}) %collective-permute-start.12) | collective-permute-done | bytes 65568 | tf_op jit(solution)/shard_map/ppermute | solution.py:22
  141.6 4.9 %collective-permute-done.14.far = bf16[4,64,512]{2,1,0:T(8,128)(2,1)S(1)} collective-permute-done((bf16[4,64,512]{2,1,0:T(8,128)(2,1)S(1)}, bf16[4,64,512]{2,1,0:T(8,128)(2,1)S(1)}, u32[]{:S(2)}, u32[]{:S(2)}) %collective-permute-start.14) | collective-permute-done | bytes 262176 | tf_op jit(solution)/shard_map/ppermute | solution.py:22
  (155 shorter events, 40.3 us)
Async XLA Ops:
  0.6 15.1 %collective-permute-start.1 = (bf16[256,1024]{1,0:T(8,128)(2,1)}, bf16[256,1024]{1,0:T(8,128)(2,1)S(1)}, u32[]{:S(2)}, u32[]{:S(2)}) collective-permute-start(bf16[256,1024]{1,0:T(8,128)(2,1)} %refs_6_.1), channel_id=1, source_target_pairs={{0,16},{8,24},{16,0},{24,8},{1,17},{9,25},{17,1},{25,9},{2,18},{10... | collective-permute-start | bytes 1572872 | tf_op jit(solution)/shard_map/ppermute | solution.py:22
  3.6 20.1 %collective-permute-start = (bf16[256,1024]{1,0:T(8,128)(2,1)}, bf16[256,1024]{1,0:T(8,128)(2,1)S(1)}, u32[]{:S(2)}, u32[]{:S(2)}) collective-permute-start(bf16[256,1024]{1,0:T(8,128)(2,1)} %refs_6_.1), channel_id=1, source_target_pairs={{0,8},{8,0},{16,24},{24,16},{1,9},{9,1},{17,25},{25,17},{2,10},{10... | collective-permute-start | bytes 1572872 | tf_op jit(solution)/shard_map/ppermute | solution.py:22
  15.8 8.0 %collective-permute-start.2 = (bf16[256,1024]{1,0:T(8,128)(2,1)S(1)}, bf16[256,1024]{1,0:T(8,128)(2,1)S(1)}, u32[]{:S(2)}, u32[]{:S(2)}) collective-permute-start(bf16[256,1024]{1,0:T(8,128)(2,1)S(1)} %collective-permute-done.1.refs_8_), channel_id=1, source_target_pairs={{0,8},{8,0},{16,24},{24,16},{1,9},{9,1},{17,25},{25,17},{2,10},{10... | collective-permute-start | bytes 1572872 | tf_op jit(solution)/shard_map/ppermute | solution.py:22
  15.9 76.6 %copy-start.33 = (s32[2]{0:T(128)}, s32[2]{0:T(128)S(1)}, u32[]{:S(2)}) copy-start(s32[2]{0:T(128)S(1)} %pad_add_fusion.refs_0_.me) | copy-start | bytes 28
  32.4 13.7 %all-to-all-start = ((bf16[8,8,1024]{2,1,0:T(8,128)(2,1)}), bf16[8,8,1024]{2,1,0:T(8,128)(2,1)S(1)}, u32[]{:S(2)}, u32[]{:S(2)}) async-start(bf16[8,8,1024]{2,1,0:T(8,128)(2,1)} %bitcast.78), calls=%async_computation | async-start | bytes 262144 | tf_op jit(solution)/shard_map/all_to_all | solution.py:314
  63.8 19.0 %all-to-all-start.1 = ((bf16[32,8,1024]{2,1,0:T(8,128)(2,1)}), bf16[32,8,1024]{2,1,0:T(8,128)(2,1)S(1)}, u32[]{:S(2)}, u32[]{:S(2)}) async-start(bf16[32,8,1024]{2,1,0:T(8,128)(2,1)} %bitcast.7), calls=%async_computation.1 | async-start | bytes 1048576 | tf_op jit(solution)/shard_map/all_to_all | solution.py:354
  89.8 2.7 %collective-permute-start.3 = (bf16[1056,512]{1,0:T(8,128)(2,1)S(1)}, bf16[1056,512]{1,0:T(8,128)(2,1)S(1)}, u32[]{:S(2)}, u32[]{:S(2)}) collective-permute-start(bf16[1056,512]{1,0:T(8,128)(2,1)S(1)} %get-tuple-element.54), channel_id=1, source_target_pairs={{0,8},{8,0},{16,24},{24,16},{1,9},{9,1},{17,25},{25,17},{2,10},{10... | collective-permute-start | bytes 3244040 | tf_op jit(solution)/shard_map/ppermute | solution.py:22
  91.7 27.3 %copy-start.4 = (bf16[256,1024]{1,0:T(8,128)(2,1)S(1)}, bf16[256,1024]{1,0:T(8,128)(2,1)}, u32[]{:S(2)}) copy-start(bf16[256,1024]{1,0:T(8,128)(2,1)} %copy-done.3) | copy-start | bytes 1572868
  91.7 27.3 %copy-start.6 = (bf16[256,1024]{1,0:T(8,128)(2,1)S(1)}, bf16[256,1024]{1,0:T(8,128)(2,1)}, u32[]{:S(2)}) copy-start(bf16[256,1024]{1,0:T(8,128)(2,1)} %copy-done.5) | copy-start | bytes 1572868
  91.7 27.3 %copy-start.8 = (bf16[256,1024]{1,0:T(8,128)(2,1)S(1)}, bf16[256,1024]{1,0:T(8,128)(2,1)}, u32[]{:S(2)}) copy-start(bf16[256,1024]{1,0:T(8,128)(2,1)} %copy-done.7) | copy-start | bytes 1572868
  93.3 8.9 %collective-permute-start.4 = (bf16[272,512]{1,0:T(8,128)(2,1)S(1)}, bf16[272,512]{1,0:T(8,128)(2,1)S(1)}, u32[]{:S(2)}, u32[]{:S(2)}) collective-permute-start(bf16[272,512]{1,0:T(8,128)(2,1)S(1)} %get-tuple-element.58), channel_id=1, source_target_pairs={{0,16},{8,24},{16,0},{24,8},{1,17},{9,25},{17,1},{25,9},{2,18},{10... | collective-permute-start | bytes 835592 | tf_op jit(solution)/shard_map/ppermute | solution.py:22
  93.9 8.3 %collective-permute-start.5 = (bf16[256,512]{1,0:T(8,128)(2,1)S(1)}, bf16[256,512]{1,0:T(8,128)(2,1)S(1)}, u32[]{:S(2)}, u32[]{:S(2)}) collective-permute-start(bf16[256,512]{1,0:T(8,128)(2,1)S(1)} %get-tuple-element.59), channel_id=1, source_target_pairs={{0,1},{1,0},{2,3},{3,2},{4,5},{5,4},{6,7},{7,6},{8,9},{9,8},{10,11... | collective-permute-start | bytes 786440 | tf_op jit(solution)/shard_map/ppermute | solution.py:22
  104.2 6.6 %collective-permute-start.6 = (bf16[144,512]{1,0:T(8,128)(2,1)}, bf16[144,512]{1,0:T(8,128)(2,1)S(1)}, u32[]{:S(2)}, u32[]{:S(2)}) collective-permute-start(bf16[144,512]{1,0:T(8,128)(2,1)} %get-tuple-element.63), channel_id=1, source_target_pairs={{0,1},{1,0},{2,3},{3,2},{4,5},{5,4},{6,7},{7,6},{8,9},{9,8},{10,11... | collective-permute-start | bytes 442376 | tf_op jit(solution)/shard_map/ppermute | solution.py:22
  104.9 5.2 %collective-permute-start.7 = (bf16[128,512]{1,0:T(8,128)(2,1)}, bf16[128,512]{1,0:T(8,128)(2,1)S(1)}, u32[]{:S(2)}, u32[]{:S(2)}) collective-permute-start(bf16[128,512]{1,0:T(8,128)(2,1)} %get-tuple-element.64), channel_id=1, source_target_pairs={{0,16},{8,24},{16,0},{24,8},{1,17},{9,25},{17,1},{25,9},{2,18},{10... | collective-permute-start | bytes 393224 | tf_op jit(solution)/shard_map/ppermute | solution.py:22
  114.6 9.7 %collective-permute-start.10 = (bf16[80,512]{1,0:T(8,128)(2,1)}, bf16[80,512]{1,0:T(8,128)(2,1)S(1)}, u32[]{:S(2)}, u32[]{:S(2)}) collective-permute-start(bf16[80,512]{1,0:T(8,128)(2,1)} %get-tuple-element.69), channel_id=1, source_target_pairs={{0,6},{1,7},{2,4},{3,5},{4,2},{5,3},{6,0},{7,1},{8,14},{9,15},{10,... | collective-permute-start | bytes 245768 | tf_op jit(solution)/shard_map/ppermute | solution.py:22
  116.0 8.4 %collective-permute-start.8 = (bf16[80,512]{1,0:T(8,128)(2,1)}, bf16[80,512]{1,0:T(8,128)(2,1)S(1)}, u32[]{:S(2)}, u32[]{:S(2)}) collective-permute-start(bf16[80,512]{1,0:T(8,128)(2,1)} %get-tuple-element.67), channel_id=1, source_target_pairs={{0,2},{1,3},{2,0},{3,1},{4,6},{5,7},{6,4},{7,5},{8,10},{9,11},{10,... | collective-permute-start | bytes 245768 | tf_op jit(solution)/shard_map/ppermute | solution.py:22
  116.0 8.4 %collective-permute-start.9 = (bf16[80,512]{1,0:T(8,128)(2,1)}, bf16[80,512]{1,0:T(8,128)(2,1)S(1)}, u32[]{:S(2)}, u32[]{:S(2)}) collective-permute-start(bf16[80,512]{1,0:T(8,128)(2,1)} %get-tuple-element.68), channel_id=1, source_target_pairs={{0,4},{1,5},{2,6},{3,7},{4,0},{5,1},{6,2},{7,3},{8,12},{9,13},{10,... | collective-permute-start | bytes 245768 | tf_op jit(solution)/shard_map/ppermute | solution.py:22
  124.4 3.8 %collective-permute-start.15 = (bf16[16,512]{1,0:T(8,128)(2,1)S(1)}, bf16[16,512]{1,0:T(8,128)(2,1)S(1)}, u32[]{:S(2)}, u32[]{:S(2)}) collective-permute-start(bf16[16,512]{1,0:T(8,128)(2,1)S(1)} %get-tuple-element.71), channel_id=1, source_target_pairs={{0,16},{8,24},{16,0},{24,8},{1,17},{9,25},{17,1},{25,9},{2,18},{10... | collective-permute-start | bytes 49160 | tf_op jit(solution)/shard_map/ppermute | solution.py:22
  128.3 18.2 %copy-start.34 = (s32[2]{0:T(128)S(1)}, s32[2]{0:T(128)}, u32[]{:S(2)}) copy-start(s32[2]{0:T(128)} %copy-done.33) | copy-start | bytes 28
  128.3 6.7 %collective-permute-start.16 = (bf16[2,16,512]{2,1,0:T(8,128)(2,1)S(1)}, bf16[2,16,512]{2,1,0:T(8,128)(2,1)S(1)}, u32[]{:S(2)}, u32[]{:S(2)}) collective-permute-start(bf16[2,16,512]{2,1,0:T(8,128)(2,1)S(1)} %pad_maximum_fusion.2), channel_id=1, source_target_pairs={{0,8},{8,0},{16,24},{24,16},{1,9},{9,1},{17,25},{25,17},{2,10},{10... | collective-permute-start | bytes 98312 | tf_op jit(solution)/shard_map/ppermute | solution.py:22
  130.6 5.6 %collective-permute-start.11 = (bf16[64,512]{1,0:T(8,128)(2,1)S(1)}, bf16[64,512]{1,0:T(8,128)(2,1)S(1)}, u32[]{:S(2)}, u32[]{:S(2)}) collective-permute-start(bf16[64,512]{1,0:T(8,128)(2,1)S(1)} %get-tuple-element.70), channel_id=1, source_target_pairs={{0,2},{1,3},{2,0},{3,1},{4,6},{5,7},{6,4},{7,5},{8,10},{9,11},{10,... | collective-permute-start | bytes 196616 | tf_op jit(solution)/shard_map/ppermute | solution.py:22
  130.6 8.6 %collective-permute-start.12 = (bf16[64,512]{1,0:T(8,128)(2,1)S(1)}, bf16[64,512]{1,0:T(8,128)(2,1)S(1)}, u32[]{:S(2)}, u32[]{:S(2)}) collective-permute-start(bf16[64,512]{1,0:T(8,128)(2,1)S(1)} %get-tuple-element.70), channel_id=1, source_target_pairs={{0,4},{1,5},{2,6},{3,7},{4,0},{5,1},{6,2},{7,3},{8,12},{9,13},{10,... | collective-permute-start | bytes 196616 | tf_op jit(solution)/shard_map/ppermute | solution.py:22
  132.5 6.8 %collective-permute-start.13 = (bf16[64,512]{1,0:T(8,128)(2,1)S(1)}, bf16[64,512]{1,0:T(8,128)(2,1)S(1)}, u32[]{:S(2)}, u32[]{:S(2)}) collective-permute-start(bf16[64,512]{1,0:T(8,128)(2,1)S(1)} %get-tuple-element.70), channel_id=1, source_target_pairs={{0,6},{1,7},{2,4},{3,5},{4,2},{5,3},{6,0},{7,1},{8,14},{9,15},{10,... | collective-permute-start | bytes 196616 | tf_op jit(solution)/shard_map/ppermute | solution.py:22
  139.3 7.1 %collective-permute-start.14 = (bf16[4,64,512]{2,1,0:T(8,128)(2,1)S(1)}, bf16[4,64,512]{2,1,0:T(8,128)(2,1)S(1)}, u32[]{:S(2)}, u32[]{:S(2)}) collective-permute-start(bf16[4,64,512]{2,1,0:T(8,128)(2,1)S(1)} %pad_maximum_fusion.1.near), channel_id=1, source_target_pairs={{0,1},{1,0},{2,3},{3,2},{4,5},{5,4},{6,7},{7,6},{8,9},{9,8},{10,11... | collective-permute-start | bytes 786440 | tf_op jit(solution)/shard_map/ppermute | solution.py:22
  (41 other events, 195.4 us)

commit v3 on v2

v3 whole, which is shorter than its diff:
```python
import functools
import math

import jax
import jax.numpy as jnp
import numpy as np
from jax import lax
from jax.experimental import pallas as pl
from jax.experimental.pallas import tpu as pltpu
from jax.sharding import PartitionSpec as P

logit_scale = 48.0
epsilon = 1e-06
f32 = jnp.float32
bf16 = jnp.bfloat16
spaces = {"vmem": pltpu.VMEM, "hbm": pltpu.HBM, "smem": pltpu.SMEM, "free": pltpu.VMEM}


def call(kernel, name, mib, inputs, outputs, scratch=()):
    def held(where, x):
        fixed = where in ("vmem", "hbm")
        return pltpu.with_memory_space_constraint(x, spaces[where]) if fixed else x

    return pl.pallas_call(
        kernel,
        in_specs=[pl.BlockSpec(memory_space=spaces[where]) for where, _ in inputs],
        out_specs=[pl.BlockSpec(memory_space=spaces[where]) for where, _, _ in outputs],
        out_shape=[spaces[where](s, t) for where, s, t in outputs],
        scratch_shapes=list(scratch),
        compiler_params=pltpu.CompilerParams(vmem_limit_bytes=mib * 1024 * 1024),
        name=name,
    )(*[held(where, x) for where, x in inputs])


def swap(x, axis, size, bit):
    return lax.ppermute(x, axis, [(i, i ^ bit) for i in range(size)])


def tree(parts):
    while len(parts) > 1:
        parts = [parts[k] + parts[k + 1] for k in range(0, len(parts), 2)]
    return parts[0]


def dot(a, b):
    return jnp.dot(a, b, preferred_element_type=f32)


def dot_last(a, b):
    return lax.dot_general(a, b, (((1,), (1,)), ((), ())), preferred_element_type=f32)


def dot_first(a, b):
    return lax.dot_general(a, b, (((0,), (0,)), ((), ())), preferred_element_type=f32)


def one_hot(order):
    return (jnp.asarray(order, jnp.int32)[:, None] == jnp.arange(order.size)).astype(bf16)


def halves(x):
    n = x.shape[0] // 2
    return x[:n], x[n:]


def high_low(x):
    high = x.astype(bf16).astype(f32)
    return jnp.concatenate([high, (x - high).astype(bf16).astype(f32)], axis=0)


def joined(x):
    high, low = halves(x)
    return high + low


def gelu_both(pre):
    scale = math.sqrt(2.0 / math.pi)
    square = pre * pre
    bent = jnp.tanh(scale * (pre + 0.044715 * (square * pre)))
    cdf = 0.5 * (1.0 + bent)
    slope = 0.5 * (1.0 - bent * bent) * (scale * (1.0 + (3 * 0.044715) * square))
    return pre * cdf, cdf + pre * slope


class Mover:
    def __init__(self, sems):
        self.sems, self.used = sems, 0

    def start(self, source, target):
        copy = pltpu.make_async_copy(source, target, self.sems.at[self.used])
        self.used += 1
        copy.start()
        return copy


def prepare_kernel(n_img, n_exp, me, ctx_hbm, res_hbm, own_hbm, near, *refs):
    lefts, near_out, mixed = refs[:4], refs[4], refs[5]
    ctx, res, own, turned, kept, sems = refs[6:]
    mover = Mover(sems)
    get_ctx = mover.start(ctx_hbm, ctx)
    get_own = mover.start(own_hbm, own)
    get_res = mover.start(res_hbm, res)
    out = [mover.start(near, near_out)]
    sub = turned.shape[0] // (n_img * n_exp)
    get_ctx.wait()
    turned[...] = ctx[...].astype(f32).T
    for core in range(2):
        for x in range(2):
            for y in range(2):
                block = []
                for z in range(n_exp // 2):
                    at = ((me[0] ^ (2 * x + core)) * n_exp + (me[1] ^ (2 * z + y))) * sub
                    block.append(turned[pl.ds(pl.multiple_of(at, sub), sub), :])
                block = jnp.concatenate(block, axis=0).astype(bf16)
                n = block.shape[0]
                kept[2 * core, (2 * x + y) * n : (2 * x + y + 1) * n, :] = block
                kept[2 * core + 1, (2 * y + x) * n : (2 * y + x + 1) * n, :] = block
    out += [mover.start(kept.at[k], left) for k, left in enumerate(lefts)]
    get_own.wait()
    get_res.wait()
    deep = own.shape[0]
    first = pl.ds(pl.multiple_of(me[0] * deep, deep), deep)
    second = pl.ds(pl.multiple_of((me[0] ^ 1) * deep, deep), deep)
    mixed[...] = res[...].astype(f32) + dot(ctx[:, first], own[...]) + dot(ctx[:, second], near[...])
    for copy in out:
        copy.wait()


def partial_kernel(taken, me, ctx_hbm, start, block, block_out, total, ctx, sems):
    mover = Mover(sems)
    deep = block.shape[0]
    columns = pl.ds(pl.multiple_of((me[0] ^ taken) * deep, deep), deep)
    get = mover.start(ctx_hbm.at[:, columns], ctx)
    out = mover.start(block, block_out)
    get.wait()
    total[...] = start[...] + dot(ctx[...], block[...])
    out.wait()


def forward_kernel(images, factor, taken, me, ctx_hbm, start, cot_hbm, unit, perm, block, *refs):
    block_out, stream_hbm, inverse_hbm, dispatch_hbm, combine_hbm, slots_hbm = refs[:6]
    ctx, cot, stream_v, inverse_v, dispatch_v, combine_v, slots_v, sems = refs[6:]
    mover = Mover(sems)
    deep = block.shape[0]
    tokens = cot.shape[0] // images
    columns = pl.ds(pl.multiple_of((me[0] ^ taken) * deep, deep), deep)
    get = mover.start(ctx_hbm.at[:, columns], ctx)
    get_cot = mover.start(cot_hbm, cot)
    out = [mover.start(block, block_out)]
    get.wait()
    slot_in, grad_out = [], []
    for b in range(images):
        at = pl.ds(b * tokens, tokens)
        mixed = start[at, :] + dot(ctx[at, :], block[...])
        stream = mixed.astype(bf16)
        stream_v[at, :] = stream
        stream32 = stream.astype(f32)
        inverse = lax.rsqrt(jnp.mean(stream32 * stream32, axis=-1, keepdims=True) + epsilon)
        inverse_v[at, :] = inverse
        normed = (stream32 * inverse).astype(bf16)
        expo = jnp.exp(factor * dot(normed, unit[...]))
        dispatch32 = expo / jnp.sum(expo, axis=0, keepdims=True)
        combine32 = expo / jnp.sum(expo, axis=1, keepdims=True)
        dispatch_v[at, :] = dispatch32
        combine_v[at, :] = combine32
        slot_in.append(dot_first(dispatch32.astype(bf16), normed).astype(bf16))
        if b == 0:
            get_cot.wait()
        grad_out.append(dot_first(combine32.astype(bf16), cot[at, :]).astype(bf16))
    out.append(mover.start(stream_v, stream_hbm))
    out.append(mover.start(inverse_v, inverse_hbm))
    out.append(mover.start(dispatch_v, dispatch_hbm))
    out.append(mover.start(combine_v, combine_hbm))
    parts = jnp.concatenate(slot_in + grad_out, axis=0)
    slots_v[...] = dot_first(perm[...], parts).astype(bf16)
    out += [mover.start(slots_v, slots_hbm.at[r]) for r in range(slots_hbm.shape[0])]
    for copy in out:
        copy.wait()


def expert_kernel(step, got, perm, first_hbm, second_hbm, *refs):
    rows_hbm, act_hbm, grad_hbm, back_hbm = refs[:4]
    first, second, rows, act, grad_pre, held, back, sems = refs[4:]
    mover = Mover(sems)
    owned, _, hidden = first.shape
    cuts = [(j, slice(f, f + step)) for j in range(owned) for f in range(0, hidden, step)]
    gets = [
        (
            mover.start(first_hbm.at[j, :, at], first.at[j, :, at]),
            mover.start(second_hbm.at[j, at, :], second.at[j, at, :]),
        )
        for j, at in cuts
    ]
    rows[...] = dot(perm[...], got[...]).astype(bf16).reshape(rows.shape)
    out = [mover.start(rows, rows_hbm)]
    for j in range(owned):
        x, g = rows[2 * j], rows[2 * j + 1]
        part_out = part_in = 0.0
        for (of, at), get in zip(cuts, gets, strict=True):
            if of != j:
                continue
            get[0].wait()
            first_w = first[j, :, at]
            value, slope = gelu_both(dot(x, first_w))
            value = value.astype(bf16)
            act[j, :, at] = value
            get[1].wait()
            second_w = second[j, at, :]
            grad = (dot_last(g, second_w) * slope).astype(bf16)
            grad_pre[j, :, at] = grad
            part_out = part_out + dot(value, second_w)
            part_in = part_in + dot_last(grad, first_w)
        held[2 * j] = part_out.astype(bf16)
        held[2 * j + 1] = part_in.astype(bf16)
    out.append(mover.start(act, act_hbm))
    out.append(mover.start(grad_pre, grad_hbm))
    back[...] = dot_first(perm[...], held[...].reshape(back.shape)).astype(bf16)
    out.append(mover.start(back, back_hbm))
    for copy in out:
        copy.wait()


def grads_kernel(rows, act, grad_pre, grad_first, grad_second):
    f = pl.program_id(1)
    deep = grad_second.shape[1]
    at = pl.ds(pl.multiple_of(f * deep, deep), deep)
    grad_second[0] = dot_first(act[0, :, at], rows[1]).astype(bf16)
    deep = grad_first.shape[1]
    at = pl.ds(pl.multiple_of(f * deep, deep), deep)
    grad_first[0] = dot_first(rows[0, :, at], grad_pre[0]).astype(bf16)


def backward_kernel(images, factor, back, perm, unit_t, *refs):
    hbm, (grad_hbm, send, side_out), scratch = refs[:7], refs[7:10], refs[10:]
    stream, inverse, dispatch, combine, cot, left_p, left_q, grad_v, sems = scratch
    mover = Mover(sems)
    gets = [mover.start(source, target) for source, target in zip(hbm, scratch[:7], strict=True)]
    tokens = cot.shape[0] // images
    slots = unit_t.shape[0]
    half = send.shape[1]
    total = tree([back[r].astype(f32) for r in range(back.shape[0])]).astype(bf16)
    parts = dot(perm[...], total).astype(bf16)
    for get in gets[:5]:
        get.wait()
    unit_sum = 0.0
    out = []
    for b in range(images):
        at = pl.ds(b * tokens, tokens)
        slot_out = parts[b * slots : (b + 1) * slots]
        grad_slot_in = parts[(images + b) * slots : (images + b + 1) * slots]
        upstream = cot[at, :]
        inv = inverse[at, :]
        normed32 = stream[at, :].astype(f32) * inv
        normed = normed32.astype(bf16)
        dispatch32, combine32 = dispatch[at, :], combine[at, :]
        grad_combine = dot_last(upstream, slot_out)
        grad_dispatch = dot_last(normed, grad_slot_in)
        logits = combine32 * (
            grad_combine - jnp.sum(combine32 * grad_combine, axis=1, keepdims=True)
        ) + dispatch32 * (
            grad_dispatch - jnp.sum(dispatch32 * grad_dispatch, axis=0, keepdims=True)
        )
        logits = logits.astype(bf16)
        grad_normed = dot(dispatch32.astype(bf16), grad_slot_in) + factor * dot(logits, unit_t[...])
        unit_sum = unit_sum + dot_first(logits, normed)
        grad = upstream.astype(f32) + inv * (
            grad_normed - normed32 * jnp.mean(normed32 * grad_normed, axis=-1, keepdims=True)
        )
        grad_v[at, :] = grad.astype(bf16)
        out.append(mover.start(grad_v.at[at, :], grad_hbm.at[at, :]))
    for get in gets[5:]:
        get.wait()
    n = left_p.shape[0]
    send[:n, :] = dot(left_p[...], grad_v[:, :half]).astype(bf16)
    send[n : 2 * n, :] = dot(left_q[...], grad_v[:, half:]).astype(bf16)
    unit_sum = factor * unit_sum
    side = high_low(jnp.concatenate([unit_sum[:, :half], unit_sum[:, half:]], axis=0))
    send[2 * n :, :] = side.astype(bf16)
    side_out[...] = joined(side)
    for copy in out:
        copy.wait()


def keep_kernel(left_p_hbm, left_q_hbm, grad_hbm, out, left_p, left_q, grad, sems):
    mover = Mover(sems)
    gets = [
        mover.start(grad_hbm, grad),
        mover.start(left_p_hbm, left_p),
        mover.start(left_q_hbm, left_q),
    ]
    half = out.shape[1]
    n = left_p.shape[0]
    gets[0].wait()
    gets[1].wait()
    out[:n, :] = dot(left_p[...], grad[:, :half]).astype(bf16)
    gets[2].wait()
    out[n:, :] = dot(left_q[...], grad[:, half:]).astype(bf16)


def chosen(bit, low, high):
    return jnp.where(bit == 0, low, high)


def first_kernel(me, keep, side, got, p_out, q_out, side_out, send_p, send_q):
    n = keep.shape[0] // 2
    p0, p1 = halves(keep[:n, :].astype(f32) + got[:n, :].astype(f32))
    q0, q1 = halves(keep[n:, :].astype(f32) + got[n : 2 * n, :].astype(f32))
    low, high = halves(side[...] + joined(got[2 * n :, :].astype(f32)))
    bit = me[1] & 1
    side_out[...] = chosen(bit, low, high)
    p_out[...] = p0.astype(bf16)
    q_out[...] = q0.astype(bf16)
    send_p[...] = p1.astype(bf16)
    other = high_low(chosen(bit, high, low))
    send_q[...] = jnp.concatenate([q1, other], axis=0).astype(bf16)


def second_kernel(p_in, q_in, side, got_p, got_q, p_out, q_out, side_out, send_p, send_q):
    n = p_in.shape[0]
    got = got_q[...].astype(f32)
    p0, p1 = halves(p_in[...].astype(f32) + got_p[...].astype(f32))
    q0, q1 = halves(q_in[...].astype(f32) + got[:n])
    mine = high_low(side[...] + joined(got[n:]))
    side_out[...] = joined(mine)
    p_out[...] = p0.astype(bf16)
    q_out[...] = q0.astype(bf16)
    send_p[...] = p1.astype(bf16)
    send_q[...] = jnp.concatenate([q1, mine], axis=0).astype(bf16)


def side_rows(piece):
    piece = high_low(piece)
    short = -piece.shape[0] % 16
    if short:
        piece = jnp.concatenate([piece, jnp.zeros((short, piece.shape[1]), f32)], axis=0)
    return piece


def third_kernel(me, p_in, q_in, side, got_p, got_q, keep, side_out, *sends):
    n = p_in.shape[0]
    groups = len(sends) + 1
    got = got_q[...].astype(f32)
    p = p_in[...].astype(f32) + got_p[...].astype(f32)
    q = q_in[...].astype(f32) + got[:n]
    total = side[...] + joined(got[n:])
    deep = total.shape[0] // groups
    pieces = [total[m * deep : (m + 1) * deep] for m in range(groups)]
    bit = 1
    while bit < groups:
        flip = me[1] & (2 * bit)
        pieces = [chosen(flip, pieces[m], pieces[m ^ bit]) for m in range(groups)]
        bit *= 2
    side_out[...] = pieces[0]
    n = n // groups
    keep[...] = jnp.concatenate([p[:n], q[:n]], axis=0)
    for m, send in enumerate(sends, 1):
        at = slice(m * n, (m + 1) * n)
        send[...] = jnp.concatenate([p[at], q[at], side_rows(pieces[m])], axis=0).astype(bf16)


def fourth_kernel(keep, side, *refs):
    gots, own = refs[:-1], refs[-1]
    n, deep = keep.shape[0], side.shape[0]
    gots = [g[...].astype(f32) for g in gots]
    total = tree([side[...]] + [joined(g[n : n + 2 * deep]) for g in gots])
    total = jnp.concatenate([tree([keep[...]] + [g[:n] for g in gots]), side_rows(total)], axis=0)
    own[...] = total.astype(bf16)


def join_kernel(*refs):
    for k, ref in enumerate(refs[:-1]):
        refs[-1][k] = ref[...]


def context_kernel(me, grad_hbm, own_hbm, near_hbm, far_hbm, far_near_hbm, out_hbm, grad, blocks, out, sems):
    mover = Mover(sems)
    deep = blocks.shape[1]
    get = mover.start(grad_hbm, grad)
    sources = (own_hbm, near_hbm, far_hbm, far_near_hbm)
    gets = [mover.start(source, blocks.at[r]) for r, source in enumerate(sources)]
    get.wait()
    puts = []
    for r, get in enumerate(gets):
        get.wait()
        columns = pl.ds(pl.multiple_of((me[0] ^ r) * deep, deep), deep)
        out[r] = dot_last(grad[...], blocks[r]).astype(bf16)
        puts.append(mover.start(out.at[r], out_hbm.at[:, columns]))
    for put in puts:
        put.wait()


def last_kernel(deep, me, near, far, unit_t, slot_norm, grad_hbm, slots_hbm, *scratch):
    grad, side, slots_out, sems = scratch
    mover = Mover(sems)
    n, half = grad.shape[1], near.shape[2]
    puts = []
    for z in range(near.shape[0]):
        for y, ref in enumerate((near, far)):
            block = ref[z].astype(f32)
            at = me[1] ^ (2 * z + y)
            k = 2 * z + y
            grad[k, :, :half] = block[:n]
            grad[k, :, half:] = block[n : 2 * n]
            puts.append(mover.start(grad.at[k], grad_hbm.at[at]))
            side[(at & 1) * near.shape[0] + (at >> 1)] = joined(block[2 * n : 2 * n + 2 * deep])
    total = jnp.concatenate([side[k] for k in range(side.shape[0])], axis=0)
    total = jnp.concatenate(halves(total), axis=1)
    unit = unit_t[...]
    along = jnp.sum(unit * total, axis=1, keepdims=True)
    slots_out[...] = (total - unit * along) / slot_norm[...]
    puts.append(mover.start(slots_out, slots_hbm))
    for put in puts:
        put.wait()


def shards(n_img, n_exp, context, residual, cotangent, proj_weight, slot_params, expert_in, expert_out):
    images, tokens, width = context.shape
    rows = images * tokens
    owned, _, hidden = expert_in.shape
    slots = slot_params.shape[1]
    half = width // 2
    factor = logit_scale / math.sqrt(width)
    me_img = lax.axis_index("img")
    me_exp = lax.axis_index("exp")
    me = jnp.stack([me_img, me_exp]).astype(jnp.int32)
    flat_ctx = context.reshape(rows, width)
    flat_cot = cotangent.reshape(rows, width)
    flat_res = residual.reshape(rows, width)
    dma = pltpu.SemaphoreType.DMA
    own = ("smem", me)

    far = swap(proj_weight, "img", n_img, 2)
    near = swap(proj_weight, "img", n_img, 1)
    deep = proj_weight.shape[0]
    block = (deep, width)
    left = (width // 2, rows)
    *lefts, near_copy, mixed = call(
        functools.partial(prepare_kernel, n_img, n_exp),
        "prepare",
        16,
        [own, ("hbm", flat_ctx), ("hbm", flat_res), ("hbm", proj_weight), ("vmem", near)],
        [("hbm", left, bf16)] * 4 + [("hbm", block, bf16), ("vmem", (rows, width), f32)],
        [
            pltpu.VMEM((rows, width), bf16),
            pltpu.VMEM((rows, width), bf16),
            pltpu.VMEM(block, bf16),
            pltpu.VMEM((width, rows), f32),
            pltpu.VMEM((4,) + left, bf16),
            dma((8,)),
        ],
    )
    params32 = slot_params.astype(f32).T
    slot_norm = jnp.sqrt(jnp.sum(params32 * params32, axis=1, keepdims=True) + epsilon)
    unit_t32 = params32 / slot_norm
    unit_t = unit_t32.astype(bf16)
    unit = unit_t.T
    perm = one_hot(
        np.arange(slots * 2 * images).reshape(slots, 2, images).transpose(1, 2, 0).reshape(-1)
    )
    sources = n_img * n_exp
    count = sources * images
    shuffle = one_hot(
        np.arange(count * owned * 2)
        .reshape(sources, owned, 2, images)
        .transpose(1, 2, 0, 3)
        .reshape(-1)
    )
    far, mixed, unit, unit_t, perm, shuffle = lax.optimization_barrier(
        (far, mixed, unit, unit_t, perm, shuffle)
    )
    keep_left, send_left = lefts[:2], lefts[2:]
    far_near = swap(far, "img", n_img, 1)
    far_copy, mixed = call(
        functools.partial(partial_kernel, 2),
        "partial",
        6,
        [own, ("hbm", flat_ctx), ("vmem", mixed), ("vmem", far)],
        [("hbm", block, bf16), ("vmem", (rows, width), f32)],
        [pltpu.VMEM((rows, deep), bf16), dma((2,))],
    )
    stats = [((rows, width), bf16), ((rows, 1), f32), ((rows, slots), f32), ((rows, slots), f32)]
    message = slots * 2 * images
    far_near_copy, *stats_hbm, out = call(
        functools.partial(forward_kernel, images, factor, 3),
        "forward",
        20,
        [
            own, ("hbm", flat_ctx), ("vmem", mixed), ("hbm", flat_cot), ("free", unit),
            ("free", perm), ("vmem", far_near),
        ],
        [("hbm", block, bf16)]
        + [("hbm", *s) for s in stats]
        + [("hbm", (n_img, message, width), bf16)],
        [
            pltpu.VMEM((rows, deep), bf16),
            pltpu.VMEM((rows, width), bf16),
            *[pltpu.VMEM(*s) for s in stats],
            pltpu.VMEM((message, width), bf16),
            dma((7 + n_img,)),
        ],
    )

    both = ("img", "exp")
    got = out.reshape(sources, -1, width)
    got = lax.all_to_all(got, both, split_axis=0, concat_axis=0, tiled=True).reshape(-1, width)

    step = min(hidden, 512)
    kept = [((owned * 2, count, width), bf16)] + [((owned, count, hidden), bf16)] * 2
    slot_rows, act, grad_pre, back = call(
        functools.partial(expert_kernel, step),
        "experts",
        28,
        [("vmem", got), ("free", shuffle), ("hbm", expert_in), ("hbm", expert_out)],
        [("hbm", *s) for s in kept] + [("hbm", got.shape, bf16)],
        [
            pltpu.VMEM(expert_in.shape, bf16),
            pltpu.VMEM(expert_out.shape, bf16),
            *[pltpu.VMEM(*s) for s in kept],
            pltpu.VMEM((owned * 2, count, width), bf16),
            pltpu.VMEM(got.shape, bf16),
            dma((2 * owned * (hidden // step) + 4,)),
        ],
    )
    back = back.reshape(sources, -1, width)
    back = lax.all_to_all(back, both, split_axis=0, concat_axis=0, tiled=True)

    cuts = 4
    fixed = lambda x: pltpu.with_memory_space_constraint(x, pltpu.HBM)
    part = lambda s: pl.BlockSpec((1,) + s, lambda j, f: (j, 0, 0))
    grad_expert_in, grad_expert_out = pl.pallas_call(
        grads_kernel,
        grid=(owned, cuts),
        in_specs=[
            pl.BlockSpec((2, count, width), lambda j, f: (j, 0, 0)),
            part((count, hidden)),
            part((count, hidden)),
        ],
        out_specs=[
            pl.BlockSpec((1, width // cuts, hidden), lambda j, f: (j, f, 0)),
            pl.BlockSpec((1, hidden // cuts, width), lambda j, f: (j, f, 0)),
        ],
        out_shape=[pltpu.HBM(expert_in.shape, bf16), pltpu.HBM(expert_out.shape, bf16)],
        compiler_params=pltpu.CompilerParams(vmem_limit_bytes=14 * 1024 * 1024),
        name="expert_grads",
    )(fixed(slot_rows), fixed(act), fixed(grad_pre))
    back, grad_expert_in, grad_expert_out = lax.optimization_barrier(
        (back, grad_expert_in, grad_expert_out)
    )

    n = width // 2
    grad_residual, send, side = call(
        functools.partial(backward_kernel, images, factor),
        "backward",
        24,
        [("vmem", back.reshape(n_img, -1, width)), ("free", perm), ("free", unit_t)]
        + [("hbm", x) for x in (*stats_hbm, flat_cot, *send_left)],
        [
            ("hbm", (rows, width), bf16),
            ("vmem", (2 * n + 4 * slots, half), bf16),
            ("vmem", (2 * slots, half), f32),
        ],
        [
            *[pltpu.VMEM(*s) for s in stats],
            pltpu.VMEM((rows, width), bf16),
            pltpu.VMEM(left, bf16),
            pltpu.VMEM(left, bf16),
            pltpu.VMEM((rows, width), bf16),
            dma((7 + images,)),
        ],
    )

    got = swap(send, "img", n_img, 1)
    (keep,) = call(
        keep_kernel,
        "keep",
        8,
        [("hbm", x) for x in (*keep_left, grad_residual)],
        [("vmem", (2 * n, half), bf16)],
        [pltpu.VMEM(left, bf16), pltpu.VMEM(left, bf16), pltpu.VMEM((rows, width), bf16), dma((3,))],
    )

    def after(n):
        rest = (("vmem", (n, half), bf16),) * 2 + (("vmem", (slots, half), f32),)
        return [*rest, ("vmem", (n, half), bf16), ("vmem", (n + 2 * slots, half), bf16)]

    n = n // 2
    p, q, side, send_p, send_q = call(
        first_kernel,
        "first",
        6,
        [own, ("vmem", keep), ("vmem", side), ("vmem", got)],
        after(n),
    )
    got_p = swap(send_p, "img", n_img, 2)
    got_q = swap(send_q, "exp", n_exp, 1)
    projection = (proj_weight, near_copy, far_copy, far_near_copy)
    (grad_context,) = call(
        context_kernel,
        "context",
        12,
        [own] + [("hbm", x) for x in (grad_residual, *projection)],
        [("hbm", (rows, width), bf16)],
        [
            pltpu.VMEM((rows, width), bf16),
            pltpu.VMEM((n_img,) + block, bf16),
            pltpu.VMEM((n_img, rows, deep), bf16),
            dma((1 + 2 * n_img,)),
        ],
    )
    got_p, got_q, grad_context = lax.optimization_barrier((got_p, got_q, grad_context))
    n = n // 2
    p, q, side, send_p, send_q = call(
        second_kernel, "second", 4, [("vmem", x) for x in (p, q, side, got_p, got_q)], after(n)
    )
    got_p = swap(send_p, "exp", n_exp, 1)
    got_q = swap(send_q, "img", n_img, 2)
    groups = n_exp // 2
    n = n // groups
    piece = slots // groups
    tail = -(-2 * piece // 16) * 16
    block = (2 * n + tail, half)
    keep, side, *sends = call(
        third_kernel,
        "third",
        4,
        [own] + [("vmem", x) for x in (p, q, side, got_p, got_q)],
        [("vmem", (2 * n, half), f32), ("vmem", (piece, half), f32)]
        + [("vmem", block, bf16)] * (groups - 1),
    )
    gots = [swap(s, "exp", n_exp, 2 * m) for m, s in enumerate(sends, 1)]
    (held,) = call(
        fourth_kernel,
        "fourth",
        4,
        [("vmem", x) for x in (keep, side, *gots)],
        [("vmem", block, bf16)],
    )
    held = [held] + [swap(held, "exp", n_exp, 2 * m) for m in range(1, groups)]
    (held,) = call(
        join_kernel, "join", 4, [("vmem", x) for x in held], [("vmem", (groups,) + block, bf16)]
    )
    others = swap(held, "exp", n_exp, 1)
    grad_proj, grad_slots = call(
        functools.partial(last_kernel, piece),
        "last",
        6,
        [own, ("vmem", held), ("vmem", others), ("free", unit_t32), ("free", slot_norm)],
        [("hbm", (n_exp, n, width), f32), ("hbm", (slots, width), f32)],
        [
            pltpu.VMEM((n_exp, n, width), f32),
            pltpu.VMEM((n_exp, piece, half), f32),
            pltpu.VMEM((slots, width), f32),
            dma((n_exp + 1,)),
        ],
    )
    return (
        grad_context.reshape(images, tokens, width),
        grad_residual.reshape(images, tokens, width),
        grad_proj.reshape(-1, width),
        grad_slots.T,
        grad_expert_in,
        grad_expert_out,
    )


def solution(mesh):
    n_img, n_exp = mesh.shape["img"], mesh.shape["exp"]
    placed = (
        P(("img", "exp"), None, None),
        P(("img", "exp"), None, None),
        P(("img", "exp"), None, None),
        P("img", None),
        P(),
        P("exp", None, "img"),
        P("exp", "img", None),
    )
    return jax.shard_map(
        functools.partial(shards, n_img, n_exp),
        mesh=mesh,
        in_specs=placed,
        out_specs=(
            P(("img", "exp"), None, None),
            P(("img", "exp"), None, None),
            P("img", None),
            P(),
            P("exp", None, "img"),
            P("exp", "img", None),
        ),
        check_vma=False,
    )
```

time: 149 us -> 125 us (0.84)
  local copies, waits for them, and re-layouts: 29.9 us -> 1.67 us
  blocking collectives: 7.16 us -> 22.6 us
  Pallas kernels: 27.2 us -> 42.1 us
  waiting for transfers between devices: 44.3 us -> 33.7 us
  starting transfers between devices: 27.1 us -> 19.3 us
  other arithmetic: 9.03 us -> 4.49 us
  matrix products: 2.26 us -> 0 us
    all_to_all x0 -> x1, blocking collectives: none -> 22.6 us  [shards(): lax.all_to_all(got, both, split_axis=0, concat_axis=0, tiled=True)]
    unnamed x92 -> x10, local copies, waits for them, and re-layouts: 15.7 us -> 0.67 us
    pallas_call x9 -> x13, Pallas kernels: 21.6 us -> 34.7 us  [call(): pl.pallas_call(kernel, in_specs=[pl.BlockSpec(memory_space=spaces[where])...]
    gather x4 -> x0, local copies, waits for them, and re-layouts: 7.38 us -> none  [the longest x1 3.74 us: shards(): jnp.take(jnp.stack(blocks), order, axis=0).reshape(width, width)]
    all_gather x1 -> x0, blocking collectives: 7.16 us -> none  [shards(): got = lax.all_gather(got, 'img', axis=0, tiled=True).reshape(-1, width)]
    all_to_all x2 -> x1, starting transfers between devices: 8.87 us -> 2.8 us  [shards(): back = lax.all_to_all(back, both, split_axis=0, concat_axis=0, tiled=True)]
    all_to_all x2 -> x1, waiting for transfers between devices: 14.8 us -> 8.78 us  [shards(): back = lax.all_to_all(back, both, split_axis=0, concat_axis=0, tiled=True)]
    ppermute x17 -> x15, waiting for transfers between devices: 29.5 us -> 24.9 us  [swap(): return lax.ppermute(x, axis, [(i, i ^ bit) for i in range(size)])]
  transfers between devices with their start and end apart: 19 -> 16, of which waited for: 10 -> 12; matrix products, arithmetic and copies ran while one was open for 17% -> 4% of each run, Pallas kernels for 4% -> 17%
where the time goes in v3:
time: 125 us
  Pallas kernels  42.1 us (34%)
  waiting for transfers between devices  33.7 us (27%)
  blocking collectives  22.6 us (18%)
  starting transfers between devices  19.3 us (15%)
  other arithmetic  4.49 us (4%)
  local copies, waits for them, and re-layouts  1.67 us (1%)
    pallas_call x13, Pallas kernels, call(): pl.pallas_call(kernel, in_specs=[pl.BlockSpec(memory_space=spaces[where])...  34.7 us
    ppermute x15, waiting for transfers between devices, swap(): return lax.ppermute(x, axis, [(i, i ^ bit) for i in range(size)])  24.9 us
    all_to_all x1, blocking collectives, shards(): lax.all_to_all(got, both, split_axis=0, concat_axis=0, tiled=True)  22.6 us
    ppermute x15, starting transfers between devices, swap(): return lax.ppermute(x, axis, [(i, i ^ bit) for i in range(size)])  16.5 us
    all_to_all x1, waiting for transfers between devices, shards(): back = lax.all_to_all(back, both, split_axis=0, concat_axis=0, tiled=True)  8.78 us
    pallas_call x1, Pallas kernels, shards(): pl.pallas_call(grads_kernel, grid=(owned, cuts), in_specs=[pl.BlockSpec((...  7.39 us
    all_to_all x1, starting transfers between devices, shards(): back = lax.all_to_all(back, both, split_axis=0, concat_axis=0, tiled=True)  2.8 us
  transfers between devices with their start and end apart: 16, of which 12 were waited for; matrix products, arithmetic and copies ran while one was open for 4% of the time, Pallas kernels for 17%

profile of v3, /device:TPU:0, one launch (start us, length us, event | category | flops | bytes accessed | tf_op | source)
XLA Modules:
  0.0 124.7 jit_solution(17247653111813136063)
XLA Ops:
  1.1 2.6 %collective-permute-start.1 = (bf16[256,1024]{1,0:T(8,128)(2,1)}, bf16[256,1024]{1,0:T(8,128)(2,1)S(1)}, u32[]{:S(2)}, u32[]{:S(2)}) collective-permute-start(bf16[256,1024]{1,0:T(8,128)(2,1)} %own_hbm.3), channel_id=1, source_target_pairs={{0,16},{8,24},{16,0},{24,8},{1,17},{9,25},{17,1},{25,9},{2,18},{10... | collective-permute-start | bytes 1572872 | tf_op jit(solution)/shard_map/ppermute | solution.py:36
  6.7 1.5 %fusion.2 = (f32[16,1024]{1,0:T(8,128)}, bf16[16,1024]{1,0:T(8,128)(2,1)}, bf16[1024,16]{0,1:T(8,128)(2,1)}) fusion(bf16[1024,16]{0,1:T(8,128)(2,1)} %param.13, f32[16]{0:T(128)S(1)} %get-tuple-element.114), kind=kLoop, calls=%fused_computation.5 | loop fusion | flops 65536 | bytes 163904 | tf_op jit(solution)/shard_map/div | solution.py:454
  8.2 3.9 %prepare.1 = (bf16[512,512]{1,0:T(8,128)(2,1)}, bf16[512,512]{1,0:T(8,128)(2,1)}, bf16[512,512]{1,0:T(8,128)(2,1)}, bf16[512,512]{1,0:T(8,128)(2,1)}, bf16[256,1...) custom-call(s32[2]{0:T(128)S(1)} %pad_add_fusion.me, bf16[512,1024]{1,0:T(8,128)(2,1)} %bitcast.21, bf16[512,1024]{1,0:T(8,128)(2,1)} %bitcast.28, ...), custom_call_target="tpu_custom_call" | custom-call | tf_op jit(solution)/shard_map/prepare/pallas_call | solution.py:24
  12.1 4.3 %collective-permute-done.1.block = bf16[256,1024]{1,0:T(8,128)(2,1)S(1)} collective-permute-done((bf16[256,1024]{1,0:T(8,128)(2,1)}, bf16[256,1024]{1,0:T(8,128)(2,1)S(1)}, u32[]{:S(2)}, u32[]{:S(2)}) %collective-permute-start.1) | collective-permute-done | bytes 524320 | tf_op jit(solution)/shard_map/ppermute | solution.py:36
  16.4 2.1 %partial.1 = (bf16[256,1024]{1,0:T(8,128)(2,1)}, f32[512,1024]{1,0:T(8,128)S(1)}) custom-call(s32[2]{0:T(128)S(1)} %pad_add_fusion.me, bf16[512,1024]{1,0:T(8,128)(2,1)} %bitcast.22, f32[512,1024]{1,0:T(8,128)S(1)} %get-tuple-element.61.start, bf16[256,1024]{1,0:T(8,128)(2,1)S(1)} %collective-permute-done.1.block), custom_call_target="tpu_custom_call" | custom-call | tf_op jit(solution)/shard_map/partial/pallas_call | solution.py:24
  20.2 5.0 %forward.1 = (bf16[256,1024]{1,0:T(8,128)(2,1)}, bf16[512,1024]{1,0:T(8,128)(2,1)}, f32[512,1]{1,0:T(8,128)}, f32[512,16]{1,0:T(8,128)}, f32[512,16]{1,0:T(8,128)}, /*index=5*/bf16[4,64,1024]{2,1,0:T(8,128)(2,1)}) custom-call(s32[2]{0:T(128)S(1)} %copy-done.3, bf16[512,1024]{1,0:T(8,128)(2,1)} %bitcast.23, f32[512,1024]{1,0:T(8,128)S(1)} %get-tuple-element.63.start, ...), custom_call_target="tpu_custom_call" | custom-call | tf_op jit(solution)/shard_map/forward/pallas_call | solution.py:24
  25.2 22.6 %all_to_all.10 = bf16[32,8,1024]{2,1,0:T(8,128)(2,1)S(1)} all-to-all(bf16[32,8,1024]{2,1,0:T(8,128)(2,1)} %bitcast.30), channel_id=1, replica_groups=mesh['img'=4,'exp'=8] {'img','exp'}, dimensions={0} | all-to-all | bytes 1048576 | tf_op jit(solution)/shard_map/all_to_all | solution.py:505
  47.8 7.8 %experts.1 = (bf16[4,64,1024]{2,1,0:T(8,128)(2,1)}, bf16[2,64,1024]{2,1,0:T(8,128)(2,1)}, bf16[2,64,1024]{2,1,0:T(8,128)(2,1)}, bf16[256,1024]{1,0:T(8,128)(2,1)}) custom-call(bf16[256,1024]{1,0:T(8,128)(2,1)S(1)} %bitcast.20, bf16[256,256]{1,0:T(8,128)(2,1)S(1)} %fusion.perm, bf16[2,1024,1024]{2,1,0:T(8,128)(2,1)} %first_hbm.1, ...), custom_call_target="tpu_custom_call" | custom-call | tf_op jit(solution)/shard_map/experts/pallas_call | solution.py:24
  55.7 2.8 %all-to-all-start.1 = ((bf16[32,8,1024]{2,1,0:T(8,128)(2,1)}), bf16[32,8,1024]{2,1,0:T(8,128)(2,1)S(1)}, u32[]{:S(2)}, u32[]{:S(2)}) async-start(bf16[32,8,1024]{2,1,0:T(8,128)(2,1)} %bitcast.29), calls=%async_computation.1 | async-start | bytes 1048576 | tf_op jit(solution)/shard_map/all_to_all | solution.py:525
  58.5 7.4 %expert_grads.1 = (bf16[2,1024,1024]{2,1,0:T(8,128)(2,1)}, bf16[2,1024,1024]{2,1,0:T(8,128)(2,1)}) custom-call(bf16[4,64,1024]{2,1,0:T(8,128)(2,1)} %get-tuple-element.69.rows, bf16[2,64,1024]{2,1,0:T(8,128)(2,1)} %get-tuple-element.70.act, bf16[2,64,1024]{2,1,0:T(8,128)(2,1)} %get-tuple-element.71.grad_pre), custom_call_target="tpu_custom_call" | custom-call | tf_op jit(solution)/shard_map/expert_grads/pallas_call | solution.py:530
  65.9 8.8 %all-to-all-done.1 = bf16[32,8,1024]{2,1,0:T(8,128)(2,1)S(1)} async-done(((bf16[32,8,1024]{2,1,0:T(8,128)(2,1)}), bf16[32,8,1024]{2,1,0:T(8,128)(2,1)S(1)}, u32[]{:S(2)}, u32[]{:S(2)}) %all-to-all-start.1) | async-done | bytes 524320 | tf_op jit(solution)/shard_map/all_to_all | solution.py:525
  74.6 4.7 %backward.1 = (bf16[512,1024]{1,0:T(8,128)(2,1)}, bf16[1088,512]{1,0:T(8,128)(2,1)S(1)}, f32[32,512]{1,0:T(8,128)S(1)}) custom-call(bf16[4,64,1024]{2,1,0:T(8,128)(2,1)S(1)} %bitcast.19, bf16[64,64]{1,0:T(8,128)(2,1)S(1)} %fusion.4.perm, bf16[16,1024]{1,0:T(8,128)(2,1)S(1)} %copy-done.1, bf16[512,1024]{1,0:T(8,128)(2,1)} %get-tuple-element.76.refs_0_, ...), custom_call_target="tpu_custom_call" | custom-call | tf_op jit(solution)/shard_map/backward/pallas_call | solution.py:24
  79.5 2.3 %keep.1 = bf16[1024,512]{1,0:T(8,128)(2,1)S(1)} custom-call(bf16[512,512]{1,0:T(8,128)(2,1)} %get-tuple-element.58.left_p_hbm, bf16[512,512]{1,0:T(8,128)(2,1)} %get-tuple-element.59.left_q_hbm, bf16[512,1024]{1,0:T(8,128)(2,1)} %get-tuple-element.82.grad_hbm), custom_call_target="tpu_custom_call" | custom-call | tf_op jit(solution)/shard_map/keep/pallas_call | solution.py:24
  84.4 5.6 %context.1 = bf16[512,1024]{1,0:T(8,128)(2,1)} custom-call(s32[2]{0:T(128)S(1)} %copy-done.3, bf16[512,1024]{1,0:T(8,128)(2,1)} %get-tuple-element.82.grad_hbm, bf16[256,1024]{1,0:T(8,128)(2,1)} %own_hbm.3, bf16[256,1024]{1,0:T(8,128)(2,1)} %get-tuple-element.87.near_hbm, bf16[256,1024]{1,0:T(8,128)(2,1)} %get-tuple-element.88.far_hbm, ...), custom_call_target="tpu_custom_call" | custom-call | tf_op jit(solution)/shard_map/context/pallas_call | solution.py:24
  90.0 1.9 %collective-permute-done.4.got_p = bf16[256,512]{1,0:T(8,128)(2,1)S(1)} collective-permute-done((bf16[256,512]{1,0:T(8,128)(2,1)S(1)}, bf16[256,512]{1,0:T(8,128)(2,1)S(1)}, u32[]{:S(2)}, u32[]{:S(2)}) %collective-permute-start.4) | collective-permute-done | bytes 262176 | tf_op jit(solution)/shard_map/ppermute | solution.py:36
  94.1 3.9 %collective-permute-done.6.got_p = bf16[128,512]{1,0:T(8,128)(2,1)S(1)} collective-permute-done((bf16[128,512]{1,0:T(8,128)(2,1)S(1)}, bf16[128,512]{1,0:T(8,128)(2,1)S(1)}, u32[]{:S(2)}, u32[]{:S(2)}) %collective-permute-start.6) | collective-permute-done | bytes 131104 | tf_op jit(solution)/shard_map/ppermute | solution.py:36
  98.7 1.7 %collective-permute-start.10 = (bf16[80,512]{1,0:T(8,128)(2,1)S(1)}, bf16[80,512]{1,0:T(8,128)(2,1)S(1)}, u32[]{:S(2)}, u32[]{:S(2)}) collective-permute-start(bf16[80,512]{1,0:T(8,128)(2,1)S(1)} %get-tuple-element.105), channel_id=1, source_target_pairs={{0,6},{1,7},{2,4},{3,5},{4,2},{5,3},{6,0},{7,1},{8,14},{9,15},{10,... | collective-permute-start | bytes 245768 | tf_op jit(solution)/shard_map/ppermute | solution.py:36
  100.4 2.7 %collective-permute-start.9 = (bf16[80,512]{1,0:T(8,128)(2,1)S(1)}, bf16[80,512]{1,0:T(8,128)(2,1)S(1)}, u32[]{:S(2)}, u32[]{:S(2)}) collective-permute-start(bf16[80,512]{1,0:T(8,128)(2,1)S(1)} %get-tuple-element.104), channel_id=1, source_target_pairs={{0,4},{1,5},{2,6},{3,7},{4,0},{5,1},{6,2},{7,3},{8,12},{9,13},{10,... | collective-permute-start | bytes 245768 | tf_op jit(solution)/shard_map/ppermute | solution.py:36
  103.1 2.1 %collective-permute-done.10.refs_2_ = bf16[80,512]{1,0:T(8,128)(2,1)S(1)} collective-permute-done((bf16[80,512]{1,0:T(8,128)(2,1)S(1)}, bf16[80,512]{1,0:T(8,128)(2,1)S(1)}, u32[]{:S(2)}, u32[]{:S(2)}) %collective-permute-start.10) | collective-permute-done | bytes 81952 | tf_op jit(solution)/shard_map/ppermute | solution.py:36
  107.9 1.4 %collective-permute-start.12 = (bf16[80,512]{1,0:T(8,128)(2,1)S(1)}, bf16[80,512]{1,0:T(8,128)(2,1)S(1)}, u32[]{:S(2)}, u32[]{:S(2)}) collective-permute-start(bf16[80,512]{1,0:T(8,128)(2,1)S(1)} %fourth.1.refs_0_), channel_id=1, source_target_pairs={{0,4},{1,5},{2,6},{3,7},{4,0},{5,1},{6,2},{7,3},{8,12},{9,13},{10,... | collective-permute-start | bytes 245768 | tf_op jit(solution)/shard_map/ppermute | solution.py:36
  109.4 2.7 %collective-permute-start.13 = (bf16[80,512]{1,0:T(8,128)(2,1)S(1)}, bf16[80,512]{1,0:T(8,128)(2,1)S(1)}, u32[]{:S(2)}, u32[]{:S(2)}) collective-permute-start(bf16[80,512]{1,0:T(8,128)(2,1)S(1)} %fourth.1.refs_0_), channel_id=1, source_target_pairs={{0,6},{1,7},{2,4},{3,5},{4,2},{5,3},{6,0},{7,1},{8,14},{9,15},{10,... | collective-permute-start | bytes 245768 | tf_op jit(solution)/shard_map/ppermute | solution.py:36
  112.5 3.2 %collective-permute-done.12.refs_2_ = bf16[80,512]{1,0:T(8,128)(2,1)S(1)} collective-permute-done((bf16[80,512]{1,0:T(8,128)(2,1)S(1)}, bf16[80,512]{1,0:T(8,128)(2,1)S(1)}, u32[]{:S(2)}, u32[]{:S(2)}) %collective-permute-start.12) | collective-permute-done | bytes 81952 | tf_op jit(solution)/shard_map/ppermute | solution.py:36
  117.0 6.0 %collective-permute-done.14.far = bf16[4,80,512]{2,1,0:T(8,128)(2,1)S(1)} collective-permute-done((bf16[4,80,512]{2,1,0:T(8,128)(2,1)S(1)}, bf16[4,80,512]{2,1,0:T(8,128)(2,1)S(1)}, u32[]{:S(2)}, u32[]{:S(2)}) %collective-permute-start.14) | collective-permute-done | bytes 327712 | tf_op jit(solution)/shard_map/ppermute | solution.py:36
  123.0 1.6 %last.1 = (f32[8,32,1024]{2,1,0:T(8,128)}, f32[16,1024]{1,0:T(8,128)}) custom-call(s32[2]{0:T(128)S(1)} %copy-done.3, bf16[4,80,512]{2,1,0:T(8,128)(2,1)S(1)} %join.1.near, bf16[4,80,512]{2,1,0:T(8,128)(2,1)S(1)} %collective-permute-done.14.far, f32[16,1024]{1,0:T(8,128)S(1)} %copy-done, f32[16,1]{1,0:T(8,128)S(1)} %copy.16.slot_norm), custom_call_target="tpu_custom_call" | custom-call | tf_op jit(solution)/shard_map/last/pallas_call | solution.py:24
  (41 shorter events, 15.0 us)
Async XLA Ops:
  0.6 7.6 %collective-permute-start = (bf16[256,1024]{1,0:T(8,128)(2,1)}, bf16[256,1024]{1,0:T(8,128)(2,1)S(1)}, u32[]{:S(2)}, u32[]{:S(2)}) collective-permute-start(bf16[256,1024]{1,0:T(8,128)(2,1)} %own_hbm.3), channel_id=1, source_target_pairs={{0,8},{8,0},{16,24},{24,16},{1,9},{9,1},{17,25},{25,17},{2,10},{10... | collective-permute-start | bytes 1572872 | tf_op jit(solution)/shard_map/ppermute | solution.py:36
  1.1 15.3 %collective-permute-start.1 = (bf16[256,1024]{1,0:T(8,128)(2,1)}, bf16[256,1024]{1,0:T(8,128)(2,1)S(1)}, u32[]{:S(2)}, u32[]{:S(2)}) collective-permute-start(bf16[256,1024]{1,0:T(8,128)(2,1)} %own_hbm.3), channel_id=1, source_target_pairs={{0,16},{8,24},{16,0},{24,8},{1,17},{9,25},{17,1},{25,9},{2,18},{10... | collective-permute-start | bytes 1572872 | tf_op jit(solution)/shard_map/ppermute | solution.py:36
  5.9 10.5 %copy-start.2 = (s32[2]{0:T(128)}, s32[2]{0:T(128)S(1)}, u32[]{:S(2)}) copy-start(s32[2]{0:T(128)S(1)} %pad_add_fusion.me) | copy-start | bytes 28
  16.4 3.1 %collective-permute-start.2 = (bf16[256,1024]{1,0:T(8,128)(2,1)S(1)}, bf16[256,1024]{1,0:T(8,128)(2,1)S(1)}, u32[]{:S(2)}, u32[]{:S(2)}) collective-permute-start(bf16[256,1024]{1,0:T(8,128)(2,1)S(1)} %collective-permute-done.1.block), channel_id=1, source_target_pairs={{0,8},{8,0},{16,24},{24,16},{1,9},{9,1},{17,25},{25,17},{2,10},{10... | collective-permute-start | bytes 1572872 | tf_op jit(solution)/shard_map/ppermute | solution.py:36
  19.5 0.7 copy-start.3
  47.8 26.8 %copy-start.1 = (bf16[16,1024]{1,0:T(8,128)(2,1)S(1)}, bf16[16,1024]{1,0:T(8,128)(2,1)}, u32[]{:S(2)}) copy-start(bf16[16,1024]{1,0:T(8,128)(2,1)} %get-tuple-element.75.unit_t) | copy-start | bytes 98308
  55.7 19.0 %all-to-all-start.1 = ((bf16[32,8,1024]{2,1,0:T(8,128)(2,1)}), bf16[32,8,1024]{2,1,0:T(8,128)(2,1)S(1)}, u32[]{:S(2)}, u32[]{:S(2)}) async-start(bf16[32,8,1024]{2,1,0:T(8,128)(2,1)} %bitcast.29), calls=%async_computation.1 | async-start | bytes 1048576 | tf_op jit(solution)/shard_map/all_to_all | solution.py:525
  79.4 2.8 %collective-permute-start.3 = (bf16[1088,512]{1,0:T(8,128)(2,1)S(1)}, bf16[1088,512]{1,0:T(8,128)(2,1)S(1)}, u32[]{:S(2)}, u32[]{:S(2)}) collective-permute-start(bf16[1088,512]{1,0:T(8,128)(2,1)S(1)} %get-tuple-element.84), channel_id=1, source_target_pairs={{0,8},{8,0},{16,24},{24,16},{1,9},{9,1},{17,25},{25,17},{2,10},{10... | collective-permute-start | bytes 3342344 | tf_op jit(solution)/shard_map/ppermute | solution.py:36
  82.2 34.7 %copy-start.4 = (f32[16,1]{0,1:T(1,128)S(1)}, f32[16,1]{0,1:T(1,128)}, u32[]{:S(2)}) copy-start(f32[16,1]{0,1:T(1,128)} %get-tuple-element.113) | copy-start | bytes 196
  82.2 40.8 %copy-start = (f32[16,1024]{1,0:T(8,128)S(1)}, f32[16,1024]{1,0:T(8,128)}, u32[]{:S(2)}) copy-start(f32[16,1024]{1,0:T(8,128)} %get-tuple-element.110.unit_t) | copy-start | bytes 196612
  83.0 9.1 %collective-permute-start.5 = (bf16[288,512]{1,0:T(8,128)(2,1)S(1)}, bf16[288,512]{1,0:T(8,128)(2,1)S(1)}, u32[]{:S(2)}, u32[]{:S(2)}) collective-permute-start(bf16[288,512]{1,0:T(8,128)(2,1)S(1)} %get-tuple-element.86), channel_id=1, source_target_pairs={{0,1},{1,0},{2,3},{3,2},{4,5},{5,4},{6,7},{7,6},{8,9},{9,8},{10,11... | collective-permute-start | bytes 884744 | tf_op jit(solution)/shard_map/ppermute | solution.py:36
  83.9 8.1 %collective-permute-start.4 = (bf16[256,512]{1,0:T(8,128)(2,1)S(1)}, bf16[256,512]{1,0:T(8,128)(2,1)S(1)}, u32[]{:S(2)}, u32[]{:S(2)}) collective-permute-start(bf16[256,512]{1,0:T(8,128)(2,1)S(1)} %get-tuple-element.85), channel_id=1, source_target_pairs={{0,16},{8,24},{16,0},{24,8},{1,17},{9,25},{17,1},{25,9},{2,18},{10... | collective-permute-start | bytes 786440 | tf_op jit(solution)/shard_map/ppermute | solution.py:36
  92.3 5.8 %collective-permute-start.7 = (bf16[160,512]{1,0:T(8,128)(2,1)S(1)}, bf16[160,512]{1,0:T(8,128)(2,1)S(1)}, u32[]{:S(2)}, u32[]{:S(2)}) collective-permute-start(bf16[160,512]{1,0:T(8,128)(2,1)S(1)} %get-tuple-element.100), channel_id=1, source_target_pairs={{0,16},{8,24},{16,0},{24,8},{1,17},{9,25},{17,1},{25,9},{2,18},{10... | collective-permute-start | bytes 491528 | tf_op jit(solution)/shard_map/ppermute | solution.py:36
  93.1 5.0 %collective-permute-start.6 = (bf16[128,512]{1,0:T(8,128)(2,1)S(1)}, bf16[128,512]{1,0:T(8,128)(2,1)S(1)}, u32[]{:S(2)}, u32[]{:S(2)}) collective-permute-start(bf16[128,512]{1,0:T(8,128)(2,1)S(1)} %get-tuple-element.99), channel_id=1, source_target_pairs={{0,1},{1,0},{2,3},{3,2},{4,5},{5,4},{6,7},{7,6},{8,9},{9,8},{10,11... | collective-permute-start | bytes 393224 | tf_op jit(solution)/shard_map/ppermute | solution.py:36
  98.7 6.5 %collective-permute-start.10 = (bf16[80,512]{1,0:T(8,128)(2,1)S(1)}, bf16[80,512]{1,0:T(8,128)(2,1)S(1)}, u32[]{:S(2)}, u32[]{:S(2)}) collective-permute-start(bf16[80,512]{1,0:T(8,128)(2,1)S(1)} %get-tuple-element.105), channel_id=1, source_target_pairs={{0,6},{1,7},{2,4},{3,5},{4,2},{5,3},{6,0},{7,1},{8,14},{9,15},{10,... | collective-permute-start | bytes 245768 | tf_op jit(solution)/shard_map/ppermute | solution.py:36
  100.4 6.2 %collective-permute-start.8 = (bf16[80,512]{1,0:T(8,128)(2,1)S(1)}, bf16[80,512]{1,0:T(8,128)(2,1)S(1)}, u32[]{:S(2)}, u32[]{:S(2)}) collective-permute-start(bf16[80,512]{1,0:T(8,128)(2,1)S(1)} %get-tuple-element.103), channel_id=1, source_target_pairs={{0,2},{1,3},{2,0},{3,1},{4,6},{5,7},{6,4},{7,5},{8,10},{9,11},{10,... | collective-permute-start | bytes 245768 | tf_op jit(solution)/shard_map/ppermute | solution.py:36
  100.4 7.3 %collective-permute-start.9 = (bf16[80,512]{1,0:T(8,128)(2,1)S(1)}, bf16[80,512]{1,0:T(8,128)(2,1)S(1)}, u32[]{:S(2)}, u32[]{:S(2)}) collective-permute-start(bf16[80,512]{1,0:T(8,128)(2,1)S(1)} %get-tuple-element.104), channel_id=1, source_target_pairs={{0,4},{1,5},{2,6},{3,7},{4,0},{5,1},{6,2},{7,3},{8,12},{9,13},{10,... | collective-permute-start | bytes 245768 | tf_op jit(solution)/shard_map/ppermute | solution.py:36
  107.7 4.8 %collective-permute-start.11 = (bf16[80,512]{1,0:T(8,128)(2,1)S(1)}, bf16[80,512]{1,0:T(8,128)(2,1)S(1)}, u32[]{:S(2)}, u32[]{:S(2)}) collective-permute-start(bf16[80,512]{1,0:T(8,128)(2,1)S(1)} %fourth.1.refs_0_), channel_id=1, source_target_pairs={{0,2},{1,3},{2,0},{3,1},{4,6},{5,7},{6,4},{7,5},{8,10},{9,11},{10,... | collective-permute-start | bytes 245768 | tf_op jit(solution)/shard_map/ppermute | solution.py:36
  107.9 7.7 %collective-permute-start.12 = (bf16[80,512]{1,0:T(8,128)(2,1)S(1)}, bf16[80,512]{1,0:T(8,128)(2,1)S(1)}, u32[]{:S(2)}, u32[]{:S(2)}) collective-permute-start(bf16[80,512]{1,0:T(8,128)(2,1)S(1)} %fourth.1.refs_0_), channel_id=1, source_target_pairs={{0,4},{1,5},{2,6},{3,7},{4,0},{5,1},{6,2},{7,3},{8,12},{9,13},{10,... | collective-permute-start | bytes 245768 | tf_op jit(solution)/shard_map/ppermute | solution.py:36
  109.4 6.3 %collective-permute-start.13 = (bf16[80,512]{1,0:T(8,128)(2,1)S(1)}, bf16[80,512]{1,0:T(8,128)(2,1)S(1)}, u32[]{:S(2)}, u32[]{:S(2)}) collective-permute-start(bf16[80,512]{1,0:T(8,128)(2,1)S(1)} %fourth.1.refs_0_), channel_id=1, source_target_pairs={{0,6},{1,7},{2,4},{3,5},{4,2},{5,3},{6,0},{7,1},{8,14},{9,15},{10,... | collective-permute-start | bytes 245768 | tf_op jit(solution)/shard_map/ppermute | solution.py:36
  115.7 7.2 %collective-permute-start.14 = (bf16[4,80,512]{2,1,0:T(8,128)(2,1)S(1)}, bf16[4,80,512]{2,1,0:T(8,128)(2,1)S(1)}, u32[]{:S(2)}, u32[]{:S(2)}) collective-permute-start(bf16[4,80,512]{2,1,0:T(8,128)(2,1)S(1)} %join.1.near), channel_id=1, source_target_pairs={{0,1},{1,0},{2,3},{3,2},{4,5},{5,4},{6,7},{7,6},{8,9},{9,8},{10,11... | collective-permute-start | bytes 983048 | tf_op jit(solution)/shard_map/ppermute | solution.py:36

commit v4 on v3

--- a/solution.py
+++ b/solution.py
@@ -13,7 +13,7 @@
 epsilon = 1e-06
 f32 = jnp.float32
 bf16 = jnp.bfloat16
-spaces = {"vmem": pltpu.VMEM, "hbm": pltpu.HBM, "smem": pltpu.SMEM, "free": pltpu.VMEM}
+spaces = {"vmem": pltpu.VMEM, "hbm": pltpu.HBM, "free": pltpu.VMEM}
 
 
 def call(kernel, name, mib, inputs, outputs, scratch=()):
@@ -93,14 +93,14 @@
         return copy
 
 
-def prepare_kernel(n_img, n_exp, me, ctx_hbm, res_hbm, own_hbm, near, *refs):
-    lefts, near_out, mixed = refs[:4], refs[4], refs[5]
-    ctx, res, own, turned, kept, sems = refs[6:]
+def prepare_kernel(n_img, n_exp, ctx_hbm, res_hbm, cot_hbm, own_hbm, near, *refs):
+    lefts, near_out, mixed, ctx, cot = refs[:4], *refs[4:8]
+    res, own, turned, kept, sems = refs[8:]
     mover = Mover(sems)
     get_ctx = mover.start(ctx_hbm, ctx)
     get_own = mover.start(own_hbm, own)
     get_res = mover.start(res_hbm, res)
-    out = [mover.start(near, near_out)]
+    out = [mover.start(near, near_out), mover.start(cot_hbm, cot)]
     sub = turned.shape[0] // (n_img * n_exp)
     get_ctx.wait()
     turned[...] = ctx[...].astype(f32).T
@@ -109,7 +109,7 @@
             for y in range(2):
                 block = []
                 for z in range(n_exp // 2):
-                    at = ((me[0] ^ (2 * x + core)) * n_exp + (me[1] ^ (2 * z + y))) * sub
+                    at = ((lax.axis_index("img") ^ (2 * x + core)) * n_exp + (lax.axis_index("exp") ^ (2 * z + y))) * sub
                     block.append(turned[pl.ds(pl.multiple_of(at, sub), sub), :])
                 block = jnp.concatenate(block, axis=0).astype(bf16)
                 n = block.shape[0]
@@ -119,99 +119,93 @@
     get_own.wait()
     get_res.wait()
     deep = own.shape[0]
-    first = pl.ds(pl.multiple_of(me[0] * deep, deep), deep)
-    second = pl.ds(pl.multiple_of((me[0] ^ 1) * deep, deep), deep)
+    first = pl.ds(pl.multiple_of(lax.axis_index("img") * deep, deep), deep)
+    second = pl.ds(pl.multiple_of((lax.axis_index("img") ^ 1) * deep, deep), deep)
     mixed[...] = res[...].astype(f32) + dot(ctx[:, first], own[...]) + dot(ctx[:, second], near[...])
     for copy in out:
         copy.wait()
 
 
-def partial_kernel(taken, me, ctx_hbm, start, block, block_out, total, ctx, sems):
-    mover = Mover(sems)
+def partial_kernel(taken, ctx, start, block, block_out, total, sems):
     deep = block.shape[0]
-    columns = pl.ds(pl.multiple_of((me[0] ^ taken) * deep, deep), deep)
-    get = mover.start(ctx_hbm.at[:, columns], ctx)
-    out = mover.start(block, block_out)
-    get.wait()
-    total[...] = start[...] + dot(ctx[...], block[...])
+    columns = pl.ds(pl.multiple_of((lax.axis_index("img") ^ taken) * deep, deep), deep)
+    out = Mover(sems).start(block, block_out)
+    total[...] = start[...] + dot(ctx[:, columns], block[...])
     out.wait()
 
 
-def forward_kernel(images, factor, taken, me, ctx_hbm, start, cot_hbm, unit, perm, block, *refs):
-    block_out, stream_hbm, inverse_hbm, dispatch_hbm, combine_hbm, slots_hbm = refs[:6]
-    ctx, cot, stream_v, inverse_v, dispatch_v, combine_v, slots_v, sems = refs[6:]
+def forward_kernel(images, factor, taken, ctx, start, cot, unit, perm, block, *refs):
+    block_out, stream_v, stats_v, slots_hbm, slots_v, sems = refs
     mover = Mover(sems)
     deep = block.shape[0]
     tokens = cot.shape[0] // images
-    columns = pl.ds(pl.multiple_of((me[0] ^ taken) * deep, deep), deep)
-    get = mover.start(ctx_hbm.at[:, columns], ctx)
-    get_cot = mover.start(cot_hbm, cot)
+    columns = pl.ds(pl.multiple_of((lax.axis_index("img") ^ taken) * deep, deep), deep)
     out = [mover.start(block, block_out)]
-    get.wait()
     slot_in, grad_out = [], []
     for b in range(images):
         at = pl.ds(b * tokens, tokens)
-        mixed = start[at, :] + dot(ctx[at, :], block[...])
+        mixed = start[at, :] + dot(ctx[at, columns], block[...])
         stream = mixed.astype(bf16)
         stream_v[at, :] = stream
         stream32 = stream.astype(f32)
         inverse = lax.rsqrt(jnp.mean(stream32 * stream32, axis=-1, keepdims=True) + epsilon)
-        inverse_v[at, :] = inverse
         normed = (stream32 * inverse).astype(bf16)
-        expo = jnp.exp(factor * dot(normed, unit[...]))
+        expo = jnp.exp(factor * dot_last(normed, unit[...]))
         dispatch32 = expo / jnp.sum(expo, axis=0, keepdims=True)
         combine32 = expo / jnp.sum(expo, axis=1, keepdims=True)
-        dispatch_v[at, :] = dispatch32
-        combine_v[at, :] = combine32
+        slots = dispatch32.shape[1]
+        stats_v[at, :slots] = dispatch32
+        stats_v[at, slots : 2 * slots] = combine32
+        stats_v[at, 2 * slots : 2 * slots + 1] = inverse
         slot_in.append(dot_first(dispatch32.astype(bf16), normed).astype(bf16))
-        if b == 0:
-            get_cot.wait()
         grad_out.append(dot_first(combine32.astype(bf16), cot[at, :]).astype(bf16))
-    out.append(mover.start(stream_v, stream_hbm))
-    out.append(mover.start(inverse_v, inverse_hbm))
-    out.append(mover.start(dispatch_v, dispatch_hbm))
-    out.append(mover.start(combine_v, combine_hbm))
     parts = jnp.concatenate(slot_in + grad_out, axis=0)
     slots_v[...] = dot_first(perm[...], parts).astype(bf16)
-    out += [mover.start(slots_v, slots_hbm.at[r]) for r in range(slots_hbm.shape[0])]
+    out.append(mover.start(slots_v, slots_hbm))
     for copy in out:
         copy.wait()
 
 
-def expert_kernel(step, got, perm, first_hbm, second_hbm, *refs):
+def expert_kernel(step, ahead, got, perm, first_hbm, second_hbm, *refs):
     rows_hbm, act_hbm, grad_hbm, back_hbm = refs[:4]
     first, second, rows, act, grad_pre, held, back, sems = refs[4:]
     mover = Mover(sems)
     owned, _, hidden = first.shape
-    cuts = [(j, slice(f, f + step)) for j in range(owned) for f in range(0, hidden, step)]
-    gets = [
-        (
-            mover.start(first_hbm.at[j, :, at], first.at[j, :, at]),
-            mover.start(second_hbm.at[j, at, :], second.at[j, at, :]),
-        )
-        for j, at in cuts
-    ]
+    steps = [(j, slice(f, f + step)) for j in range(owned) for f in range(0, hidden, step)]
+    pieces = []
+    for j, at in steps:
+        pieces.append((first_hbm.at[j, :, at], first.at[j, :, at]))
+        pieces.append((second_hbm.at[j, at, :], second.at[j, at, :]))
+    coming = [mover.start(*piece) for piece in pieces[:ahead]]
+
+    def arrive():
+        if len(coming) < len(pieces):
+            coming.append(mover.start(*pieces[len(coming)]))
+
     rows[...] = dot(perm[...], got[...]).astype(bf16).reshape(rows.shape)
     out = [mover.start(rows, rows_hbm)]
-    for j in range(owned):
+    part_out = part_in = None
+    for k, (j, at) in enumerate(steps):
         x, g = rows[2 * j], rows[2 * j + 1]
-        part_out = part_in = 0.0
-        for (of, at), get in zip(cuts, gets, strict=True):
-            if of != j:
-                continue
-            get[0].wait()
-            first_w = first[j, :, at]
-            value, slope = gelu_both(dot(x, first_w))
-            value = value.astype(bf16)
-            act[j, :, at] = value
-            get[1].wait()
-            second_w = second[j, at, :]
-            grad = (dot_last(g, second_w) * slope).astype(bf16)
-            grad_pre[j, :, at] = grad
-            part_out = part_out + dot(value, second_w)
-            part_in = part_in + dot_last(grad, first_w)
-        held[2 * j] = part_out.astype(bf16)
-        held[2 * j + 1] = part_in.astype(bf16)
+        coming[2 * k].wait()
+        arrive()
+        first_w = first[j, :, at]
+        value, slope = gelu_both(dot(x, first_w))
+        value = value.astype(bf16)
+        act[j, :, at] = value
+        coming[2 * k + 1].wait()
+        arrive()
+        second_w = second[j, at, :]
+        grad = (dot_last(g, second_w) * slope).astype(bf16)
+        grad_pre[j, :, at] = grad
+        more_out, more_in = dot(value, second_w), dot_last(grad, first_w)
+        if at.start == 0:
+            part_out, part_in = more_out, more_in
+        else:
+            part_out, part_in = part_out + more_out, part_in + more_in
+        if at.stop == hidden:
+            held[2 * j] = part_out.astype(bf16)
+            held[2 * j + 1] = part_in.astype(bf16)
     out.append(mover.start(act, act_hbm))
     out.append(mover.start(grad_pre, grad_hbm))
     back[...] = dot_first(perm[...], held[...].reshape(back.shape)).astype(bf16)
@@ -231,17 +225,15 @@
 
 
 def backward_kernel(images, factor, back, perm, unit_t, *refs):
-    hbm, (grad_hbm, send, side_out), scratch = refs[:7], refs[7:10], refs[10:]
-    stream, inverse, dispatch, combine, cot, left_p, left_q, grad_v, sems = scratch
+    stream, stats, cot, left_p_hbm, left_q_hbm, grad_hbm, send, side_out = refs[:8]
+    left_p, left_q, grad_v, sems = refs[8:]
     mover = Mover(sems)
-    gets = [mover.start(source, target) for source, target in zip(hbm, scratch[:7], strict=True)]
+    gets = [mover.start(left_p_hbm, left_p), mover.start(left_q_hbm, left_q)]
     tokens = cot.shape[0] // images
     slots = unit_t.shape[0]
     half = send.shape[1]
     total = tree([back[r].astype(f32) for r in range(back.shape[0])]).astype(bf16)
     parts = dot(perm[...], total).astype(bf16)
-    for get in gets[:5]:
-        get.wait()
     unit_sum = 0.0
     out = []
     for b in range(images):
@@ -249,10 +241,10 @@
         slot_out = parts[b * slots : (b + 1) * slots]
         grad_slot_in = parts[(images + b) * slots : (images + b + 1) * slots]
         upstream = cot[at, :]
-        inv = inverse[at, :]
+        inv = stats[at, 2 * slots : 2 * slots + 1]
         normed32 = stream[at, :].astype(f32) * inv
         normed = normed32.astype(bf16)
-        dispatch32, combine32 = dispatch[at, :], combine[at, :]
+        dispatch32, combine32 = stats[at, :slots], stats[at, slots : 2 * slots]
         grad_combine = dot_last(upstream, slot_out)
         grad_dispatch = dot_last(normed, grad_slot_in)
         logits = combine32 * (
@@ -268,7 +260,7 @@
         )
         grad_v[at, :] = grad.astype(bf16)
         out.append(mover.start(grad_v.at[at, :], grad_hbm.at[at, :]))
-    for get in gets[5:]:
+    for get in gets:
         get.wait()
     n = left_p.shape[0]
     send[:n, :] = dot(left_p[...], grad_v[:, :half]).astype(bf16)
@@ -301,12 +293,12 @@
     return jnp.where(bit == 0, low, high)
 
 
-def first_kernel(me, keep, side, got, p_out, q_out, side_out, send_p, send_q):
+def first_kernel(keep, side, got, p_out, q_out, side_out, send_p, send_q):
     n = keep.shape[0] // 2
     p0, p1 = halves(keep[:n, :].astype(f32) + got[:n, :].astype(f32))
     q0, q1 = halves(keep[n:, :].astype(f32) + got[n : 2 * n, :].astype(f32))
     low, high = halves(side[...] + joined(got[2 * n :, :].astype(f32)))
-    bit = me[1] & 1
+    bit = lax.axis_index("exp") & 1
     side_out[...] = chosen(bit, low, high)
     p_out[...] = p0.astype(bf16)
     q_out[...] = q0.astype(bf16)
@@ -330,13 +322,13 @@
 
 def side_rows(piece):
     piece = high_low(piece)
-    short = -piece.shape[0] % 16
+    short = -piece.shape[0] % 8
     if short:
         piece = jnp.concatenate([piece, jnp.zeros((short, piece.shape[1]), f32)], axis=0)
     return piece
 
 
-def third_kernel(me, p_in, q_in, side, got_p, got_q, keep, side_out, *sends):
+def third_kernel(p_in, q_in, side, got_p, got_q, keep, side_out, *sends):
     n = p_in.shape[0]
     groups = len(sends) + 1
     got = got_q[...].astype(f32)
@@ -347,7 +339,7 @@
     pieces = [total[m * deep : (m + 1) * deep] for m in range(groups)]
     bit = 1
     while bit < groups:
-        flip = me[1] & (2 * bit)
+        flip = lax.axis_index("exp") & (2 * bit)
         pieces = [chosen(flip, pieces[m], pieces[m ^ bit]) for m in range(groups)]
         bit *= 2
     side_out[...] = pieces[0]
@@ -367,12 +359,7 @@
     own[...] = total.astype(bf16)
 
 
-def join_kernel(*refs):
-    for k, ref in enumerate(refs[:-1]):
-        refs[-1][k] = ref[...]
-
-
-def context_kernel(me, grad_hbm, own_hbm, near_hbm, far_hbm, far_near_hbm, out_hbm, grad, blocks, out, sems):
+def context_kernel(grad_hbm, own_hbm, near_hbm, far_hbm, far_near_hbm, out_hbm, grad, blocks, out, sems):
     mover = Mover(sems)
     deep = blocks.shape[1]
     get = mover.start(grad_hbm, grad)
@@ -382,27 +369,29 @@
     puts = []
     for r, get in enumerate(gets):
         get.wait()
-        columns = pl.ds(pl.multiple_of((me[0] ^ r) * deep, deep), deep)
+        columns = pl.ds(pl.multiple_of((lax.axis_index("img") ^ r) * deep, deep), deep)
         out[r] = dot_last(grad[...], blocks[r]).astype(bf16)
         puts.append(mover.start(out.at[r], out_hbm.at[:, columns]))
     for put in puts:
         put.wait()
 
 
-def last_kernel(deep, me, near, far, unit_t, slot_norm, grad_hbm, slots_hbm, *scratch):
-    grad, side, slots_out, sems = scratch
+def last_kernel(deep, *refs):
+    blocks, refs = refs[:-8], refs[-8:]
+    unit_t, slot_norm, grad_hbm, slots_hbm, grad, side, slots_out, sems = refs
     mover = Mover(sems)
-    n, half = grad.shape[1], near.shape[2]
+    groups = len(blocks) // 2
+    n, half = grad.shape[1], blocks[0].shape[1]
     puts = []
-    for z in range(near.shape[0]):
-        for y, ref in enumerate((near, far)):
-            block = ref[z].astype(f32)
-            at = me[1] ^ (2 * z + y)
+    for y in range(2):
+        for z in range(groups):
+            block = blocks[y * groups + z][...].astype(f32)
+            at = lax.axis_index("exp") ^ (2 * z + y)
             k = 2 * z + y
             grad[k, :, :half] = block[:n]
             grad[k, :, half:] = block[n : 2 * n]
             puts.append(mover.start(grad.at[k], grad_hbm.at[at]))
-            side[(at & 1) * near.shape[0] + (at >> 1)] = joined(block[2 * n : 2 * n + 2 * deep])
+            side[(at & 1) * groups + (at >> 1)] = joined(block[2 * n : 2 * n + 2 * deep])
     total = jnp.concatenate([side[k] for k in range(side.shape[0])], axis=0)
     total = jnp.concatenate(halves(total), axis=1)
     unit = unit_t[...]
@@ -420,40 +409,36 @@
     slots = slot_params.shape[1]
     half = width // 2
     factor = logit_scale / math.sqrt(width)
-    me_img = lax.axis_index("img")
-    me_exp = lax.axis_index("exp")
-    me = jnp.stack([me_img, me_exp]).astype(jnp.int32)
     flat_ctx = context.reshape(rows, width)
     flat_cot = cotangent.reshape(rows, width)
     flat_res = residual.reshape(rows, width)
     dma = pltpu.SemaphoreType.DMA
-    own = ("smem", me)
 
     far = swap(proj_weight, "img", n_img, 2)
     near = swap(proj_weight, "img", n_img, 1)
     deep = proj_weight.shape[0]
     block = (deep, width)
     left = (width // 2, rows)
-    *lefts, near_copy, mixed = call(
+    *lefts, near_copy, mixed, ctx, cot = call(
         functools.partial(prepare_kernel, n_img, n_exp),
         "prepare",
         16,
-        [own, ("hbm", flat_ctx), ("hbm", flat_res), ("hbm", proj_weight), ("vmem", near)],
-        [("hbm", left, bf16)] * 4 + [("hbm", block, bf16), ("vmem", (rows, width), f32)],
-        [
-            pltpu.VMEM((rows, width), bf16),
+        [("hbm", x) for x in (flat_ctx, flat_res, flat_cot, proj_weight)] + [("vmem", near)],
+        [("hbm", left, bf16)] * 4
+        + [("hbm", block, bf16), ("vmem", (rows, width), f32)]
+        + [("vmem", (rows, width), bf16)] * 2,
+        [
             pltpu.VMEM((rows, width), bf16),
             pltpu.VMEM(block, bf16),
             pltpu.VMEM((width, rows), f32),
             pltpu.VMEM((4,) + left, bf16),
-            dma((8,)),
+            dma((9,)),
         ],
     )
     params32 = slot_params.astype(f32).T
     slot_norm = jnp.sqrt(jnp.sum(params32 * params32, axis=1, keepdims=True) + epsilon)
     unit_t32 = params32 / slot_norm
     unit_t = unit_t32.astype(bf16)
-    unit = unit_t.T
     perm = one_hot(
         np.arange(slots * 2 * images).reshape(slots, 2, images).transpose(1, 2, 0).reshape(-1)
     )
@@ -465,8 +450,8 @@
         .transpose(1, 2, 0, 3)
         .reshape(-1)
     )
-    far, mixed, unit, unit_t, perm, shuffle = lax.optimization_barrier(
-        (far, mixed, unit, unit_t, perm, shuffle)
+    far, mixed, unit_t, perm, shuffle = lax.optimization_barrier(
+        (far, mixed, unit_t, perm, shuffle)
     )
     keep_left, send_left = lefts[:2], lefts[2:]
     far_near = swap(far, "img", n_img, 1)
@@ -474,40 +459,38 @@
         functools.partial(partial_kernel, 2),
         "partial",
         6,
-        [own, ("hbm", flat_ctx), ("vmem", mixed), ("vmem", far)],
+        [("vmem", ctx), ("vmem", mixed), ("vmem", far)],
         [("hbm", block, bf16), ("vmem", (rows, width), f32)],
-        [pltpu.VMEM((rows, deep), bf16), dma((2,))],
-    )
-    stats = [((rows, width), bf16), ((rows, 1), f32), ((rows, slots), f32), ((rows, slots), f32)]
+        [dma((1,))],
+    )
+    stats = [((rows, width), bf16), ((rows, -(-(2 * slots + 1) // 128) * 128), f32)]
     message = slots * 2 * images
-    far_near_copy, *stats_hbm, out = call(
+    far_near_copy, *kept_stats, out = call(
         functools.partial(forward_kernel, images, factor, 3),
         "forward",
         20,
         [
-            own, ("hbm", flat_ctx), ("vmem", mixed), ("hbm", flat_cot), ("free", unit),
-            ("free", perm), ("vmem", far_near),
+            ("vmem", ctx), ("vmem", mixed), ("vmem", cot), ("free", unit_t), ("free", perm),
+            ("vmem", far_near),
         ],
         [("hbm", block, bf16)]
-        + [("hbm", *s) for s in stats]
-        + [("hbm", (n_img, message, width), bf16)],
-        [
-            pltpu.VMEM((rows, deep), bf16),
-            pltpu.VMEM((rows, width), bf16),
-            *[pltpu.VMEM(*s) for s in stats],
+        + [("vmem", *s) for s in stats]
+        + [("hbm", (message, width), bf16)],
+        [
             pltpu.VMEM((message, width), bf16),
-            dma((7 + n_img,)),
+            dma((2,)),
         ],
     )
 
     both = ("img", "exp")
-    got = out.reshape(sources, -1, width)
-    got = lax.all_to_all(got, both, split_axis=0, concat_axis=0, tiled=True).reshape(-1, width)
+    got = out.reshape(n_exp, -1, width)
+    got = lax.all_to_all(got, "exp", split_axis=0, concat_axis=0, tiled=True)
+    got = lax.all_gather(got, "img", axis=0, tiled=True).reshape(-1, width)
 
     step = min(hidden, 512)
     kept = [((owned * 2, count, width), bf16)] + [((owned, count, hidden), bf16)] * 2
     slot_rows, act, grad_pre, back = call(
-        functools.partial(expert_kernel, step),
+        functools.partial(expert_kernel, step, 3),
         "experts",
         28,
         [("vmem", got), ("free", shuffle), ("hbm", expert_in), ("hbm", expert_out)],
@@ -553,19 +536,18 @@
         "backward",
         24,
         [("vmem", back.reshape(n_img, -1, width)), ("free", perm), ("free", unit_t)]
-        + [("hbm", x) for x in (*stats_hbm, flat_cot, *send_left)],
+        + [("vmem", x) for x in (*kept_stats, cot)]
+        + [("hbm", x) for x in send_left],
         [
             ("hbm", (rows, width), bf16),
             ("vmem", (2 * n + 4 * slots, half), bf16),
             ("vmem", (2 * slots, half), f32),
         ],
         [
-            *[pltpu.VMEM(*s) for s in stats],
-            pltpu.VMEM((rows, width), bf16),
             pltpu.VMEM(left, bf16),
             pltpu.VMEM(left, bf16),
             pltpu.VMEM((rows, width), bf16),
-            dma((7 + images,)),
+            dma((2 + images,)),
         ],
     )
 
@@ -588,7 +570,7 @@
         first_kernel,
         "first",
         6,
-        [own, ("vmem", keep), ("vmem", side), ("vmem", got)],
+        [("vmem", keep), ("vmem", side), ("vmem", got)],
         after(n),
     )
     got_p = swap(send_p, "img", n_img, 2)
@@ -598,7 +580,7 @@
         context_kernel,
         "context",
         12,
-        [own] + [("hbm", x) for x in (grad_residual, *projection)],
+        [("hbm", x) for x in (grad_residual, *projection)],
         [("hbm", (rows, width), bf16)],
         [
             pltpu.VMEM((rows, width), bf16),
@@ -617,13 +599,13 @@
     groups = n_exp // 2
     n = n // groups
     piece = slots // groups
-    tail = -(-2 * piece // 16) * 16
+    tail = -(-2 * piece // 8) * 8
     block = (2 * n + tail, half)
     keep, side, *sends = call(
         third_kernel,
         "third",
         4,
-        [own] + [("vmem", x) for x in (p, q, side, got_p, got_q)],
+        [("vmem", x) for x in (p, q, side, got_p, got_q)],
         [("vmem", (2 * n, half), f32), ("vmem", (piece, half), f32)]
         + [("vmem", block, bf16)] * (groups - 1),
     )
@@ -636,15 +618,12 @@
         [("vmem", block, bf16)],
     )
     held = [held] + [swap(held, "exp", n_exp, 2 * m) for m in range(1, groups)]
-    (held,) = call(
-        join_kernel, "join", 4, [("vmem", x) for x in held], [("vmem", (groups,) + block, bf16)]
-    )
-    others = swap(held, "exp", n_exp, 1)
+    others = [swap(x, "exp", n_exp, 1) for x in held]
     grad_proj, grad_slots = call(
         functools.partial(last_kernel, piece),
         "last",
         6,
-        [own, ("vmem", held), ("vmem", others), ("free", unit_t32), ("free", slot_norm)],
+        [("vmem", x) for x in (*held, *others)] + [("free", unit_t32), ("free", slot_norm)],
         [("hbm", (n_exp, n, width), f32), ("hbm", (slots, width), f32)],
         [
             pltpu.VMEM((n_exp, n, width), f32),

time: 125 us -> 114 us (0.912)
  Pallas kernels: 42.1 us -> 35.7 us
  starting transfers between devices: 19.3 us -> 22.4 us
  waiting for transfers between devices: 33.7 us -> 30.8 us
  blocking collectives: 22.6 us -> 20.6 us
  local copies, waits for them, and re-layouts: 1.67 us -> 0.08 us
  other arithmetic: 4.49 us -> 3.24 us
    all_to_all x1, blocking collectives: 22.6 us -> 13.4 us  [shards(): got = lax.all_to_all(got, 'exp', split_axis=0, concat_axis=0, tiled=True)]
    all_gather x0 -> x1, blocking collectives: none -> 7.16 us  [shards(): got = lax.all_gather(got, 'img', axis=0, tiled=True).reshape(-1, width)]
    pallas_call x13 -> x12, Pallas kernels: 34.7 us -> 28.3 us  [call(): pl.pallas_call(kernel, in_specs=[pl.BlockSpec(memory_space=spaces[where])...]
    ppermute x15 -> x18, starting transfers between devices: 16.5 us -> 19.6 us  [swap(): return lax.ppermute(x, axis, [(i, i ^ bit) for i in range(size)])]
    ppermute x15 -> x18, waiting for transfers between devices: 24.9 us -> 22 us  [swap(): return lax.ppermute(x, axis, [(i, i ^ bit) for i in range(size)])]
  transfers between devices with their start and end apart: 16 -> 19, of which waited for: 12 -> 14; matrix products, arithmetic and copies ran while one was open for 4% -> 3% of each run, Pallas kernels for 17% -> 17%
where the time goes in v4:
time: 114 us
  Pallas kernels  35.7 us (31%)
  waiting for transfers between devices  30.8 us (27%)
  starting transfers between devices  22.4 us (20%)
  blocking collectives  20.6 us (18%)
  other arithmetic  3.24 us (3%)
    pallas_call x12, Pallas kernels, call(): pl.pallas_call(kernel, in_specs=[pl.BlockSpec(memory_space=spaces[where])...  28.3 us
    ppermute x18, waiting for transfers between devices, swap(): return lax.ppermute(x, axis, [(i, i ^ bit) for i in range(size)])  22 us
    ppermute x18, starting transfers between devices, swap(): return lax.ppermute(x, axis, [(i, i ^ bit) for i in range(size)])  19.6 us
    all_to_all x1, blocking collectives, shards(): got = lax.all_to_all(got, 'exp', split_axis=0, concat_axis=0, tiled=True)  13.4 us
    all_to_all x1, waiting for transfers between devices, shards(): back = lax.all_to_all(back, both, split_axis=0, concat_axis=0, tiled=True)  8.78 us
    pallas_call x1, Pallas kernels, shards(): pl.pallas_call(grads_kernel, grid=(owned, cuts), in_specs=[pl.BlockSpec((...  7.39 us
    all_gather x1, blocking collectives, shards(): got = lax.all_gather(got, 'img', axis=0, tiled=True).reshape(-1, width)  7.16 us
    all_to_all x1, starting transfers between devices, shards(): back = lax.all_to_all(back, both, split_axis=0, concat_axis=0, tiled=True)  2.8 us
  transfers between devices with their start and end apart: 19, of which 14 were waited for; matrix products, arithmetic and copies ran while one was open for 3% of the time, Pallas kernels for 17%

profile of v4, /device:TPU:0, one launch (start us, length us, event | category | flops | bytes accessed | tf_op | source)
XLA Modules:
  0.0 113.7 jit_solution(18049121095460444639)
XLA Ops:
  1.1 2.6 %collective-permute-start.1 = (bf16[256,1024]{1,0:T(8,128)(2,1)}, bf16[256,1024]{1,0:T(8,128)(2,1)S(1)}, u32[]{:S(2)}, u32[]{:S(2)}) collective-permute-start(bf16[256,1024]{1,0:T(8,128)(2,1)} %own_hbm.3), channel_id=1, source_target_pairs={{0,16},{8,24},{16,0},{24,8},{1,17},{9,25},{17,1},{25,9},{2,18},{10... | collective-permute-start | bytes 1572872 | tf_op jit(solution)/shard_map/ppermute | solution.py:36
  7.0 3.4 %prepare.1 = (bf16[512,512]{1,0:T(8,128)(2,1)}, bf16[512,512]{1,0:T(8,128)(2,1)}, bf16[512,512]{1,0:T(8,128)(2,1)}, bf16[512,512]{1,0:T(8,128)(2,1)}, bf16[256,1...) custom-call(bf16[512,1024]{1,0:T(8,128)(2,1)} %bitcast.20, ...), custom_call_target="tpu_custom_call" | custom-call | tf_op jit(solution)/shard_map/prepare/pallas_call | solution.py:24
  10.3 6.1 %collective-permute-done.1.block = bf16[256,1024]{1,0:T(8,128)(2,1)S(1)} collective-permute-done((bf16[256,1024]{1,0:T(8,128)(2,1)}, bf16[256,1024]{1,0:T(8,128)(2,1)S(1)}, u32[]{:S(2)}, u32[]{:S(2)}) %collective-permute-start.1) | collective-permute-done | bytes 524320 | tf_op jit(solution)/shard_map/ppermute | solution.py:36
  18.4 3.1 %forward.1 = (bf16[256,1024]{1,0:T(8,128)(2,1)}, bf16[512,1024]{1,0:T(8,128)(2,1)S(1)}, f32[512,128]{1,0:T(8,128)S(1)}, bf16[64,1024]{1,0:T(8,128)(2,1)}) custom-call(bf16[512,1024]{1,0:T(8,128)(2,1)S(1)} %get-tuple-element.59.ctx, f32[512,1024]{1,0:T(8,128)S(1)} %get-tuple-element.63.start, bf16[512,1024]{1,0:T(8,128)(2,1)S(1)} %get-tuple-element.64.cot.refs_2_, ...), custom_call_target="tpu_custom_call" | custom-call | tf_op jit(solution)/shard_map/forward/pallas_call | solution.py:24
  21.5 13.4 %all_to_all.10 = bf16[8,8,1024]{2,1,0:T(8,128)(2,1)S(1)} all-to-all(bf16[8,8,1024]{2,1,0:T(8,128)(2,1)} %bitcast.25), channel_id=1, replica_groups=mesh['img'=4,'exp'=8] {'exp'}, dimensions={0} | all-to-all | bytes 262144 | tf_op jit(solution)/shard_map/all_to_all | solution.py:487
  34.9 7.2 %all_gather.3 = bf16[32,8,1024]{2,1,0:T(8,128)(2,1)S(1)} all-gather(bf16[8,8,1024]{2,1,0:T(8,128)(2,1)S(1)} %all_to_all.10), channel_id=1, replica_groups=mesh['img'=4,'exp'=8] {'img'}, dimensions={0}, use_global_device_ids=true | all-gather | bytes 655360 | tf_op jit(solution)/shard_map/all_gather | solution.py:488
  42.1 7.9 %experts.1 = (bf16[4,64,1024]{2,1,0:T(8,128)(2,1)}, bf16[2,64,1024]{2,1,0:T(8,128)(2,1)}, bf16[2,64,1024]{2,1,0:T(8,128)(2,1)}, bf16[256,1024]{1,0:T(8,128)(2,1)}) custom-call(bf16[256,1024]{1,0:T(8,128)(2,1)S(1)} %bitcast.17, bf16[256,256]{1,0:T(8,128)(2,1)S(1)} %fusion.perm, bf16[2,1024,1024]{2,1,0:T(8,128)(2,1)} %first_hbm.1, ...), custom_call_target="tpu_custom_call" | custom-call | tf_op jit(solution)/shard_map/experts/pallas_call | solution.py:24
  50.0 2.8 %all-to-all-start.1 = ((bf16[32,8,1024]{2,1,0:T(8,128)(2,1)}), bf16[32,8,1024]{2,1,0:T(8,128)(2,1)S(1)}, u32[]{:S(2)}, u32[]{:S(2)}) async-start(bf16[32,8,1024]{2,1,0:T(8,128)(2,1)} %bitcast.24), calls=%async_computation.1 | async-start | bytes 1048576 | tf_op jit(solution)/shard_map/all_to_all | solution.py:508
  52.8 7.4 %expert_grads.1 = (bf16[2,1024,1024]{2,1,0:T(8,128)(2,1)}, bf16[2,1024,1024]{2,1,0:T(8,128)(2,1)}) custom-call(bf16[4,64,1024]{2,1,0:T(8,128)(2,1)} %get-tuple-element.70.rows, bf16[2,64,1024]{2,1,0:T(8,128)(2,1)} %get-tuple-element.71.act, bf16[2,64,1024]{2,1,0:T(8,128)(2,1)} %get-tuple-element.72.grad_pre), custom_call_target="tpu_custom_call" | custom-call | tf_op jit(solution)/shard_map/expert_grads/pallas_call | solution.py:513
  60.2 8.8 %all-to-all-done.1 = bf16[32,8,1024]{2,1,0:T(8,128)(2,1)S(1)} async-done(((bf16[32,8,1024]{2,1,0:T(8,128)(2,1)}), bf16[32,8,1024]{2,1,0:T(8,128)(2,1)S(1)}, u32[]{:S(2)}, u32[]{:S(2)}) %all-to-all-start.1) | async-done | bytes 524320 | tf_op jit(solution)/shard_map/all_to_all | solution.py:508
  69.0 4.2 %backward.1 = (bf16[512,1024]{1,0:T(8,128)(2,1)}, bf16[1088,512]{1,0:T(8,128)(2,1)S(1)}, f32[32,512]{1,0:T(8,128)S(1)}) custom-call(bf16[4,64,1024]{2,1,0:T(8,128)(2,1)S(1)} %bitcast.18, bf16[64,64]{1,0:T(8,128)(2,1)S(1)} %fusion.3.perm, bf16[16,1024]{1,0:T(8,128)(2,1)S(1)} %get-tuple-element.65.unit.unit_t, ...), custom_call_target="tpu_custom_call" | custom-call | tf_op jit(solution)/shard_map/backward/pallas_call | solution.py:24
  73.3 2.3 %keep.1 = bf16[1024,512]{1,0:T(8,128)(2,1)S(1)} custom-call(bf16[512,512]{1,0:T(8,128)(2,1)} %get-tuple-element.57.left_p_hbm, bf16[512,512]{1,0:T(8,128)(2,1)} %get-tuple-element.58.left_q_hbm, bf16[512,1024]{1,0:T(8,128)(2,1)} %get-tuple-element.80.grad_hbm), custom_call_target="tpu_custom_call" | custom-call | tf_op jit(solution)/shard_map/keep/pallas_call | solution.py:24
  77.7 5.0 %context.1 = bf16[512,1024]{1,0:T(8,128)(2,1)} custom-call(bf16[512,1024]{1,0:T(8,128)(2,1)} %get-tuple-element.80.grad_hbm, bf16[256,1024]{1,0:T(8,128)(2,1)} %own_hbm.3, bf16[256,1024]{1,0:T(8,128)(2,1)} %get-tuple-element.85.near_hbm, bf16[256,1024]{1,0:T(8,128)(2,1)} %get-tuple-element.86.far_hbm, bf16[256,1024]{1,0:T(8,128)(2,1)} %get-tuple-element.87.far_near_hbm), custom_call_target="tpu_custom_call" | custom-call | tf_op jit(solution)/shard_map/context/pallas_call | solution.py:24
  82.7 2.5 %collective-permute-done.4.got_p = bf16[256,512]{1,0:T(8,128)(2,1)S(1)} collective-permute-done((bf16[256,512]{1,0:T(8,128)(2,1)S(1)}, bf16[256,512]{1,0:T(8,128)(2,1)S(1)}, u32[]{:S(2)}, u32[]{:S(2)}) %collective-permute-start.4) | collective-permute-done | bytes 262176 | tf_op jit(solution)/shard_map/ppermute | solution.py:36
  87.3 3.9 %collective-permute-done.6.got_p = bf16[128,512]{1,0:T(8,128)(2,1)S(1)} collective-permute-done((bf16[128,512]{1,0:T(8,128)(2,1)S(1)}, bf16[128,512]{1,0:T(8,128)(2,1)S(1)}, u32[]{:S(2)}, u32[]{:S(2)}) %collective-permute-start.6) | collective-permute-done | bytes 131104 | tf_op jit(solution)/shard_map/ppermute | solution.py:36
  91.3 1.7 %collective-permute-start.10 = (bf16[72,512]{1,0:T(8,128)(2,1)S(1)}, bf16[72,512]{1,0:T(8,128)(2,1)S(1)}, u32[]{:S(2)}, u32[]{:S(2)}) collective-permute-start(bf16[72,512]{1,0:T(8,128)(2,1)S(1)} %get-tuple-element.103), channel_id=1, source_target_pairs={{0,6},{1,7},{2,4},{3,5},{4,2},{5,3},{6,0},{7,1},{8,14},{9,15},{10,... | collective-permute-start | bytes 221192 | tf_op jit(solution)/shard_map/ppermute | solution.py:36
  93.1 2.7 %collective-permute-start.9 = (bf16[72,512]{1,0:T(8,128)(2,1)S(1)}, bf16[72,512]{1,0:T(8,128)(2,1)S(1)}, u32[]{:S(2)}, u32[]{:S(2)}) collective-permute-start(bf16[72,512]{1,0:T(8,128)(2,1)S(1)} %get-tuple-element.102), channel_id=1, source_target_pairs={{0,4},{1,5},{2,6},{3,7},{4,0},{5,1},{6,2},{7,3},{8,12},{9,13},{10,... | collective-permute-start | bytes 221192 | tf_op jit(solution)/shard_map/ppermute | solution.py:36
  95.8 1.9 %collective-permute-done.10.refs_2_ = bf16[72,512]{1,0:T(8,128)(2,1)S(1)} collective-permute-done((bf16[72,512]{1,0:T(8,128)(2,1)S(1)}, bf16[72,512]{1,0:T(8,128)(2,1)S(1)}, u32[]{:S(2)}, u32[]{:S(2)}) %collective-permute-start.10) | collective-permute-done | bytes 73760 | tf_op jit(solution)/shard_map/ppermute | solution.py:36
  97.7 1.7 %collective-permute-done.8.refs_0_ = bf16[72,512]{1,0:T(8,128)(2,1)S(1)} collective-permute-done((bf16[72,512]{1,0:T(8,128)(2,1)S(1)}, bf16[72,512]{1,0:T(8,128)(2,1)S(1)}, u32[]{:S(2)}, u32[]{:S(2)}) %collective-permute-start.8) | collective-permute-done | bytes 73760 | tf_op jit(solution)/shard_map/ppermute | solution.py:36
  100.5 1.5 %collective-permute-start.12 = (bf16[72,512]{1,0:T(8,128)(2,1)S(1)}, bf16[72,512]{1,0:T(8,128)(2,1)S(1)}, u32[]{:S(2)}, u32[]{:S(2)}) collective-permute-start(bf16[72,512]{1,0:T(8,128)(2,1)S(1)} %fourth.1.refs_0_), channel_id=1, source_target_pairs={{0,4},{1,5},{2,6},{3,7},{4,0},{5,1},{6,2},{7,3},{8,12},{9,13},{10,... | collective-permute-start | bytes 221192 | tf_op jit(solution)/shard_map/ppermute | solution.py:36
  101.9 1.9 %collective-permute-start.13 = (bf16[72,512]{1,0:T(8,128)(2,1)S(1)}, bf16[72,512]{1,0:T(8,128)(2,1)S(1)}, u32[]{:S(2)}, u32[]{:S(2)}) collective-permute-start(bf16[72,512]{1,0:T(8,128)(2,1)S(1)} %fourth.1.refs_0_), channel_id=1, source_target_pairs={{0,6},{1,7},{2,4},{3,5},{4,2},{5,3},{6,0},{7,1},{8,14},{9,15},{10,... | collective-permute-start | bytes 221192 | tf_op jit(solution)/shard_map/ppermute | solution.py:36
  106.5 1.3 %collective-permute-start.16 = (bf16[72,512]{1,0:T(8,128)(2,1)S(1)}, bf16[72,512]{1,0:T(8,128)(2,1)S(1)}, u32[]{:S(2)}, u32[]{:S(2)}) collective-permute-start(bf16[72,512]{1,0:T(8,128)(2,1)S(1)} %collective-permute-done.12.refs_2_), channel_id=1, source_target_pairs={{0,1},{1,0},{2,3},{3,2},{4,5},{5,4},{6,7},{7,6},{8,9},{9,8},{10,11... | collective-permute-start | bytes 221192 | tf_op jit(solution)/shard_map/ppermute | solution.py:36
  109.3 1.6 %collective-permute-done.16.refs_6_ = bf16[72,512]{1,0:T(8,128)(2,1)S(1)} collective-permute-done((bf16[72,512]{1,0:T(8,128)(2,1)S(1)}, bf16[72,512]{1,0:T(8,128)(2,1)S(1)}, u32[]{:S(2)}, u32[]{:S(2)}) %collective-permute-start.16) | collective-permute-done | bytes 73760 | tf_op jit(solution)/shard_map/ppermute | solution.py:36
  110.9 1.6 %collective-permute-done.17.refs_7_ = bf16[72,512]{1,0:T(8,128)(2,1)S(1)} collective-permute-done((bf16[72,512]{1,0:T(8,128)(2,1)S(1)}, bf16[72,512]{1,0:T(8,128)(2,1)S(1)}, u32[]{:S(2)}, u32[]{:S(2)}) %collective-permute-start.17) | collective-permute-done | bytes 73760 | tf_op jit(solution)/shard_map/ppermute | solution.py:36
  (35 shorter events, 16.4 us)
Async XLA Ops:
  0.6 6.3 %collective-permute-start = (bf16[256,1024]{1,0:T(8,128)(2,1)}, bf16[256,1024]{1,0:T(8,128)(2,1)S(1)}, u32[]{:S(2)}, u32[]{:S(2)}) collective-permute-start(bf16[256,1024]{1,0:T(8,128)(2,1)} %own_hbm.3), channel_id=1, source_target_pairs={{0,8},{8,0},{16,24},{24,16},{1,9},{9,1},{17,25},{25,17},{2,10},{10... | collective-permute-start | bytes 1572872 | tf_op jit(solution)/shard_map/ppermute | solution.py:36
  1.1 15.3 %collective-permute-start.1 = (bf16[256,1024]{1,0:T(8,128)(2,1)}, bf16[256,1024]{1,0:T(8,128)(2,1)S(1)}, u32[]{:S(2)}, u32[]{:S(2)}) collective-permute-start(bf16[256,1024]{1,0:T(8,128)(2,1)} %own_hbm.3), channel_id=1, source_target_pairs={{0,16},{8,24},{16,0},{24,8},{1,17},{9,25},{17,1},{25,9},{2,18},{10... | collective-permute-start | bytes 1572872 | tf_op jit(solution)/shard_map/ppermute | solution.py:36
  16.4 1.9 %collective-permute-start.2 = (bf16[256,1024]{1,0:T(8,128)(2,1)S(1)}, bf16[256,1024]{1,0:T(8,128)(2,1)S(1)}, u32[]{:S(2)}, u32[]{:S(2)}) collective-permute-start(bf16[256,1024]{1,0:T(8,128)(2,1)S(1)} %collective-permute-done.1.block), channel_id=1, source_target_pairs={{0,8},{8,0},{16,24},{24,16},{1,9},{9,1},{17,25},{25,17},{2,10},{10... | collective-permute-start | bytes 1572872 | tf_op jit(solution)/shard_map/ppermute | solution.py:36
  50.0 19.0 %all-to-all-start.1 = ((bf16[32,8,1024]{2,1,0:T(8,128)(2,1)}), bf16[32,8,1024]{2,1,0:T(8,128)(2,1)S(1)}, u32[]{:S(2)}, u32[]{:S(2)}) async-start(bf16[32,8,1024]{2,1,0:T(8,128)(2,1)} %bitcast.24), calls=%async_computation.1 | async-start | bytes 1048576 | tf_op jit(solution)/shard_map/all_to_all | solution.py:508
  73.2 2.8 %collective-permute-start.3 = (bf16[1088,512]{1,0:T(8,128)(2,1)S(1)}, bf16[1088,512]{1,0:T(8,128)(2,1)S(1)}, u32[]{:S(2)}, u32[]{:S(2)}) collective-permute-start(bf16[1088,512]{1,0:T(8,128)(2,1)S(1)} %get-tuple-element.82), channel_id=1, source_target_pairs={{0,8},{8,0},{16,24},{24,16},{1,9},{9,1},{17,25},{25,17},{2,10},{10... | collective-permute-start | bytes 3342344 | tf_op jit(solution)/shard_map/ppermute | solution.py:36
  76.3 9.1 %collective-permute-start.5 = (bf16[288,512]{1,0:T(8,128)(2,1)S(1)}, bf16[288,512]{1,0:T(8,128)(2,1)S(1)}, u32[]{:S(2)}, u32[]{:S(2)}) collective-permute-start(bf16[288,512]{1,0:T(8,128)(2,1)S(1)} %get-tuple-element.84), channel_id=1, source_target_pairs={{0,1},{1,0},{2,3},{3,2},{4,5},{5,4},{6,7},{7,6},{8,9},{9,8},{10,11... | collective-permute-start | bytes 884744 | tf_op jit(solution)/shard_map/ppermute | solution.py:36
  77.2 8.1 %collective-permute-start.4 = (bf16[256,512]{1,0:T(8,128)(2,1)S(1)}, bf16[256,512]{1,0:T(8,128)(2,1)S(1)}, u32[]{:S(2)}, u32[]{:S(2)}) collective-permute-start(bf16[256,512]{1,0:T(8,128)(2,1)S(1)} %get-tuple-element.83), channel_id=1, source_target_pairs={{0,16},{8,24},{16,0},{24,8},{1,17},{9,25},{17,1},{25,9},{2,18},{10... | collective-permute-start | bytes 786440 | tf_op jit(solution)/shard_map/ppermute | solution.py:36
  85.5 5.7 %collective-permute-start.7 = (bf16[160,512]{1,0:T(8,128)(2,1)S(1)}, bf16[160,512]{1,0:T(8,128)(2,1)S(1)}, u32[]{:S(2)}, u32[]{:S(2)}) collective-permute-start(bf16[160,512]{1,0:T(8,128)(2,1)S(1)} %get-tuple-element.98), channel_id=1, source_target_pairs={{0,16},{8,24},{16,0},{24,8},{1,17},{9,25},{17,1},{25,9},{2,18},{10... | collective-permute-start | bytes 491528 | tf_op jit(solution)/shard_map/ppermute | solution.py:36
  86.3 5.0 %collective-permute-start.6 = (bf16[128,512]{1,0:T(8,128)(2,1)S(1)}, bf16[128,512]{1,0:T(8,128)(2,1)S(1)}, u32[]{:S(2)}, u32[]{:S(2)}) collective-permute-start(bf16[128,512]{1,0:T(8,128)(2,1)S(1)} %get-tuple-element.97), channel_id=1, source_target_pairs={{0,1},{1,0},{2,3},{3,2},{4,5},{5,4},{6,7},{7,6},{8,9},{9,8},{10,11... | collective-permute-start | bytes 393224 | tf_op jit(solution)/shard_map/ppermute | solution.py:36
  91.3 6.3 %collective-permute-start.10 = (bf16[72,512]{1,0:T(8,128)(2,1)S(1)}, bf16[72,512]{1,0:T(8,128)(2,1)S(1)}, u32[]{:S(2)}, u32[]{:S(2)}) collective-permute-start(bf16[72,512]{1,0:T(8,128)(2,1)S(1)} %get-tuple-element.103), channel_id=1, source_target_pairs={{0,6},{1,7},{2,4},{3,5},{4,2},{5,3},{6,0},{7,1},{8,14},{9,15},{10,... | collective-permute-start | bytes 221192 | tf_op jit(solution)/shard_map/ppermute | solution.py:36
  93.1 6.3 %collective-permute-start.8 = (bf16[72,512]{1,0:T(8,128)(2,1)S(1)}, bf16[72,512]{1,0:T(8,128)(2,1)S(1)}, u32[]{:S(2)}, u32[]{:S(2)}) collective-permute-start(bf16[72,512]{1,0:T(8,128)(2,1)S(1)} %get-tuple-element.101), channel_id=1, source_target_pairs={{0,2},{1,3},{2,0},{3,1},{4,6},{5,7},{6,4},{7,5},{8,10},{9,11},{10,... | collective-permute-start | bytes 221192 | tf_op jit(solution)/shard_map/ppermute | solution.py:36
  93.1 6.3 %collective-permute-start.9 = (bf16[72,512]{1,0:T(8,128)(2,1)S(1)}, bf16[72,512]{1,0:T(8,128)(2,1)S(1)}, u32[]{:S(2)}, u32[]{:S(2)}) collective-permute-start(bf16[72,512]{1,0:T(8,128)(2,1)S(1)} %get-tuple-element.102), channel_id=1, source_target_pairs={{0,4},{1,5},{2,6},{3,7},{4,0},{5,1},{6,2},{7,3},{8,12},{9,13},{10,... | collective-permute-start | bytes 221192 | tf_op jit(solution)/shard_map/ppermute | solution.py:36
  99.4 5.3 %collective-permute-start.11 = (bf16[72,512]{1,0:T(8,128)(2,1)S(1)}, bf16[72,512]{1,0:T(8,128)(2,1)S(1)}, u32[]{:S(2)}, u32[]{:S(2)}) collective-permute-start(bf16[72,512]{1,0:T(8,128)(2,1)S(1)} %fourth.1.refs_0_), channel_id=1, source_target_pairs={{0,2},{1,3},{2,0},{3,1},{4,6},{5,7},{6,4},{7,5},{8,10},{9,11},{10,... | collective-permute-start | bytes 221192 | tf_op jit(solution)/shard_map/ppermute | solution.py:36
  100.5 6.0 %collective-permute-start.12 = (bf16[72,512]{1,0:T(8,128)(2,1)S(1)}, bf16[72,512]{1,0:T(8,128)(2,1)S(1)}, u32[]{:S(2)}, u32[]{:S(2)}) collective-permute-start(bf16[72,512]{1,0:T(8,128)(2,1)S(1)} %fourth.1.refs_0_), channel_id=1, source_target_pairs={{0,4},{1,5},{2,6},{3,7},{4,0},{5,1},{6,2},{7,3},{8,12},{9,13},{10,... | collective-permute-start | bytes 221192 | tf_op jit(solution)/shard_map/ppermute | solution.py:36
  101.9 6.2 %collective-permute-start.13 = (bf16[72,512]{1,0:T(8,128)(2,1)S(1)}, bf16[72,512]{1,0:T(8,128)(2,1)S(1)}, u32[]{:S(2)}, u32[]{:S(2)}) collective-permute-start(bf16[72,512]{1,0:T(8,128)(2,1)S(1)} %fourth.1.refs_0_), channel_id=1, source_target_pairs={{0,6},{1,7},{2,4},{3,5},{4,2},{5,3},{6,0},{7,1},{8,14},{9,15},{10,... | collective-permute-start | bytes 221192 | tf_op jit(solution)/shard_map/ppermute | solution.py:36
  103.8 5.3 %collective-permute-start.14 = (bf16[72,512]{1,0:T(8,128)(2,1)S(1)}, bf16[72,512]{1,0:T(8,128)(2,1)S(1)}, u32[]{:S(2)}, u32[]{:S(2)}) collective-permute-start(bf16[72,512]{1,0:T(8,128)(2,1)S(1)} %fourth.1.refs_0_), channel_id=1, source_target_pairs={{0,1},{1,0},{2,3},{3,2},{4,5},{5,4},{6,7},{7,6},{8,9},{9,8},{10,11... | collective-permute-start | bytes 221192 | tf_op jit(solution)/shard_map/ppermute | solution.py:36
  104.7 4.6 %collective-permute-start.15 = (bf16[72,512]{1,0:T(8,128)(2,1)S(1)}, bf16[72,512]{1,0:T(8,128)(2,1)S(1)}, u32[]{:S(2)}, u32[]{:S(2)}) collective-permute-start(bf16[72,512]{1,0:T(8,128)(2,1)S(1)} %collective-permute-done.11.refs_1_), channel_id=1, source_target_pairs={{0,1},{1,0},{2,3},{3,2},{4,5},{5,4},{6,7},{7,6},{8,9},{9,8},{10,11... | collective-permute-start | bytes 221192 | tf_op jit(solution)/shard_map/ppermute | solution.py:36
  106.5 4.4 %collective-permute-start.16 = (bf16[72,512]{1,0:T(8,128)(2,1)S(1)}, bf16[72,512]{1,0:T(8,128)(2,1)S(1)}, u32[]{:S(2)}, u32[]{:S(2)}) collective-permute-start(bf16[72,512]{1,0:T(8,128)(2,1)S(1)} %collective-permute-done.12.refs_2_), channel_id=1, source_target_pairs={{0,1},{1,0},{2,3},{3,2},{4,5},{5,4},{6,7},{7,6},{8,9},{9,8},{10,11... | collective-permute-start | bytes 221192 | tf_op jit(solution)/shard_map/ppermute | solution.py:36
  108.1 4.4 %collective-permute-start.17 = (bf16[72,512]{1,0:T(8,128)(2,1)S(1)}, bf16[72,512]{1,0:T(8,128)(2,1)S(1)}, u32[]{:S(2)}, u32[]{:S(2)}) collective-permute-start(bf16[72,512]{1,0:T(8,128)(2,1)S(1)} %collective-permute-done.13.refs_3_), channel_id=1, source_target_pairs={{0,1},{1,0},{2,3},{3,2},{4,5},{5,4},{6,7},{7,6},{8,9},{9,8},{10,11... | collective-permute-start | bytes 221192 | tf_op jit(solution)/shard_map/ppermute | solution.py:36

commit v5 on v4

--- a/solution.py
+++ b/solution.py
@@ -30,6 +30,14 @@
         compiler_params=pltpu.CompilerParams(vmem_limit_bytes=mib * 1024 * 1024),
         name=name,
     )(*[held(where, x) for where, x in inputs])
+
+
+def fetch_kernel(*refs):
+    n = len(refs) // 2
+    mover = Mover(refs[-1])
+    pairs = zip(refs[:n], refs[n : 2 * n], strict=True)
+    for copy in [mover.start(x.at[pl.ds(0, y.shape[0])], y) for x, y in pairs]:
+        copy.wait()
 
 
 def swap(x, axis, size, bit):
@@ -134,8 +142,17 @@
     out.wait()
 
 
+def inverse_of(stream32):
+    return lax.rsqrt(jnp.mean(stream32 * stream32, axis=-1, keepdims=True) + epsilon)
+
+
+def softmaxes(expo):
+    dispatch32 = expo / jnp.sum(expo, axis=0, keepdims=True)
+    return dispatch32, expo / jnp.sum(expo, axis=1, keepdims=True)
+
+
 def forward_kernel(images, factor, taken, ctx, start, cot, unit, perm, block, *refs):
-    block_out, stream_v, stats_v, slots_hbm, slots_v, sems = refs
+    block_out, stream_v, expo_v, slots_hbm, slots_v, sems = refs
     mover = Mover(sems)
     deep = block.shape[0]
     tokens = cot.shape[0] // images
@@ -148,15 +165,11 @@
         stream = mixed.astype(bf16)
         stream_v[at, :] = stream
         stream32 = stream.astype(f32)
-        inverse = lax.rsqrt(jnp.mean(stream32 * stream32, axis=-1, keepdims=True) + epsilon)
+        inverse = inverse_of(stream32)
         normed = (stream32 * inverse).astype(bf16)
         expo = jnp.exp(factor * dot_last(normed, unit[...]))
-        dispatch32 = expo / jnp.sum(expo, axis=0, keepdims=True)
-        combine32 = expo / jnp.sum(expo, axis=1, keepdims=True)
-        slots = dispatch32.shape[1]
-        stats_v[at, :slots] = dispatch32
-        stats_v[at, slots : 2 * slots] = combine32
-        stats_v[at, 2 * slots : 2 * slots + 1] = inverse
+        dispatch32, combine32 = softmaxes(expo)
+        expo_v[at, :] = expo
         slot_in.append(dot_first(dispatch32.astype(bf16), normed).astype(bf16))
         grad_out.append(dot_first(combine32.astype(bf16), cot[at, :]).astype(bf16))
     parts = jnp.concatenate(slot_in + grad_out, axis=0)
@@ -166,52 +179,40 @@
         copy.wait()
 
 
-def expert_kernel(step, ahead, got, perm, first_hbm, second_hbm, *refs):
-    rows_hbm, act_hbm, grad_hbm, back_hbm = refs[:4]
-    first, second, rows, act, grad_pre, held, back, sems = refs[4:]
-    mover = Mover(sems)
-    owned, _, hidden = first.shape
-    steps = [(j, slice(f, f + step)) for j in range(owned) for f in range(0, hidden, step)]
-    pieces = []
-    for j, at in steps:
-        pieces.append((first_hbm.at[j, :, at], first.at[j, :, at]))
-        pieces.append((second_hbm.at[j, at, :], second.at[j, at, :]))
-    coming = [mover.start(*piece) for piece in pieces[:ahead]]
-
-    def arrive():
-        if len(coming) < len(pieces):
-            coming.append(mover.start(*pieces[len(coming)]))
-
-    rows[...] = dot(perm[...], got[...]).astype(bf16).reshape(rows.shape)
+def expert_kernel(own, near, across, diagonal, perm, first, second, *refs):
+    rows_hbm, act_hbm, grad_hbm, keep, send = refs[:5]
+    rows, act, grad_pre, held, sems = refs[5:]
+    mover = Mover(sems)
+    owned = first.shape[0]
+    got = jnp.concatenate([own[...], across[...], near[...], diagonal[...]], axis=0)
+    rows[...] = dot(perm[...], got).astype(bf16).reshape(rows.shape)
     out = [mover.start(rows, rows_hbm)]
-    part_out = part_in = None
-    for k, (j, at) in enumerate(steps):
-        x, g = rows[2 * j], rows[2 * j + 1]
-        coming[2 * k].wait()
-        arrive()
-        first_w = first[j, :, at]
-        value, slope = gelu_both(dot(x, first_w))
+    for j in range(owned):
+        first_w, second_w = first[j], second[j]
+        value, slope = gelu_both(dot(rows[2 * j], first_w))
         value = value.astype(bf16)
-        act[j, :, at] = value
-        coming[2 * k + 1].wait()
-        arrive()
-        second_w = second[j, at, :]
-        grad = (dot_last(g, second_w) * slope).astype(bf16)
-        grad_pre[j, :, at] = grad
-        more_out, more_in = dot(value, second_w), dot_last(grad, first_w)
-        if at.start == 0:
-            part_out, part_in = more_out, more_in
-        else:
-            part_out, part_in = part_out + more_out, part_in + more_in
-        if at.stop == hidden:
-            held[2 * j] = part_out.astype(bf16)
-            held[2 * j + 1] = part_in.astype(bf16)
+        act[j] = value
+        grad = (dot_last(rows[2 * j + 1], second_w) * slope).astype(bf16)
+        grad_pre[j] = grad
+        held[2 * j] = dot(value, second_w).astype(bf16)
+        held[2 * j + 1] = dot_last(grad, first_w).astype(bf16)
     out.append(mover.start(act, act_hbm))
     out.append(mover.start(grad_pre, grad_hbm))
-    back[...] = dot_first(perm[...], held[...].reshape(back.shape)).astype(bf16)
-    out.append(mover.start(back, back_hbm))
+    back = dot_first(perm[...], held[...].reshape(got.shape)).astype(bf16)
+    keep[...], send[...] = halves(back)
     for copy in out:
         copy.wait()
+
+
+def pair_kernel(keep, got, out_hbm, out, sems):
+    mover = Mover(sems)
+    total = (keep[...].astype(f32) + got[...].astype(f32)).astype(bf16)
+    puts = []
+    for x, block in enumerate(halves(total)):
+        out[x] = block
+        puts.append(mover.start(out.at[x], out_hbm.at[(lax.axis_index("img") >> 1) ^ x]))
+    for put in puts:
+        put.wait()
 
 
 def grads_kernel(rows, act, grad_pre, grad_first, grad_second):
@@ -225,10 +226,9 @@
 
 
 def backward_kernel(images, factor, back, perm, unit_t, *refs):
-    stream, stats, cot, left_p_hbm, left_q_hbm, grad_hbm, send, side_out = refs[:8]
-    left_p, left_q, grad_v, sems = refs[8:]
-    mover = Mover(sems)
-    gets = [mover.start(left_p_hbm, left_p), mover.start(left_q_hbm, left_q)]
+    stream, expo, cot, left_p, left_q_hbm, grad_hbm, send, side_out, left_q, grad_v, sems = refs
+    mover = Mover(sems)
+    get = mover.start(left_q_hbm, left_q)
     tokens = cot.shape[0] // images
     slots = unit_t.shape[0]
     half = send.shape[1]
@@ -241,10 +241,11 @@
         slot_out = parts[b * slots : (b + 1) * slots]
         grad_slot_in = parts[(images + b) * slots : (images + b + 1) * slots]
         upstream = cot[at, :]
-        inv = stats[at, 2 * slots : 2 * slots + 1]
-        normed32 = stream[at, :].astype(f32) * inv
+        stream32 = stream[at, :].astype(f32)
+        inv = inverse_of(stream32)
+        normed32 = stream32 * inv
         normed = normed32.astype(bf16)
-        dispatch32, combine32 = stats[at, :slots], stats[at, slots : 2 * slots]
+        dispatch32, combine32 = softmaxes(expo[at, :])
         grad_combine = dot_last(upstream, slot_out)
         grad_dispatch = dot_last(normed, grad_slot_in)
         logits = combine32 * (
@@ -260,10 +261,9 @@
         )
         grad_v[at, :] = grad.astype(bf16)
         out.append(mover.start(grad_v.at[at, :], grad_hbm.at[at, :]))
-    for get in gets:
-        get.wait()
     n = left_p.shape[0]
     send[:n, :] = dot(left_p[...], grad_v[:, :half]).astype(bf16)
+    get.wait()
     send[n : 2 * n, :] = dot(left_q[...], grad_v[:, half:]).astype(bf16)
     unit_sum = factor * unit_sum
     side = high_low(jnp.concatenate([unit_sum[:, :half], unit_sum[:, half:]], axis=0))
@@ -415,7 +415,11 @@
     dma = pltpu.SemaphoreType.DMA
 
     far = swap(proj_weight, "img", n_img, 2)
-    near = swap(proj_weight, "img", n_img, 1)
+    perm = one_hot(
+        np.arange(slots * 2 * images).reshape(slots, 2, images).transpose(1, 2, 0).reshape(-1)
+    )
+    proj_again, perm = lax.optimization_barrier((proj_weight, perm))
+    near = swap(proj_again, "img", n_img, 1)
     deep = proj_weight.shape[0]
     block = (deep, width)
     left = (width // 2, rows)
@@ -439,10 +443,8 @@
     slot_norm = jnp.sqrt(jnp.sum(params32 * params32, axis=1, keepdims=True) + epsilon)
     unit_t32 = params32 / slot_norm
     unit_t = unit_t32.astype(bf16)
-    perm = one_hot(
-        np.arange(slots * 2 * images).reshape(slots, 2, images).transpose(1, 2, 0).reshape(-1)
-    )
     sources = n_img * n_exp
+    far_img = n_img // 2
     count = sources * images
     shuffle = one_hot(
         np.arange(count * owned * 2)
@@ -463,7 +465,7 @@
         [("hbm", block, bf16), ("vmem", (rows, width), f32)],
         [dma((1,))],
     )
-    stats = [((rows, width), bf16), ((rows, -(-(2 * slots + 1) // 128) * 128), f32)]
+    stats = [((rows, width), bf16), ((rows, slots), f32)]
     message = slots * 2 * images
     far_near_copy, *kept_stats, out = call(
         functools.partial(forward_kernel, images, factor, 3),
@@ -482,30 +484,53 @@
         ],
     )
 
-    both = ("img", "exp")
-    got = out.reshape(n_exp, -1, width)
-    got = lax.all_to_all(got, "exp", split_axis=0, concat_axis=0, tiled=True)
-    got = lax.all_gather(got, "img", axis=0, tiled=True).reshape(-1, width)
-
-    step = min(hidden, 512)
+    got = lax.all_to_all(out.reshape(n_exp, -1, width), "exp", 0, 0, tiled=True)
+    got = got.reshape(-1, width)
+    got, first, second = lax.optimization_barrier((got, expert_in, expert_out))
+    across = swap(got, "img", n_img, 2)
+    near = swap(got, "img", n_img, 1)
+    first, second = call(
+        fetch_kernel,
+        "weights",
+        4,
+        [("hbm", first), ("hbm", second)],
+        [("vmem", first.shape, bf16), ("vmem", second.shape, bf16)],
+        [dma((2,))],
+    )
+    across, first, second = lax.optimization_barrier((across, first, second))
+    diagonal = swap(across, "img", n_img, 1)
+
     kept = [((owned * 2, count, width), bf16)] + [((owned, count, hidden), bf16)] * 2
-    slot_rows, act, grad_pre, back = call(
-        functools.partial(expert_kernel, step, 3),
+    returned = (far_img * got.shape[0], width)
+    slot_rows, act, grad_pre, keep, send = call(
+        expert_kernel,
         "experts",
-        28,
-        [("vmem", got), ("free", shuffle), ("hbm", expert_in), ("hbm", expert_out)],
-        [("hbm", *s) for s in kept] + [("hbm", got.shape, bf16)],
-        [
-            pltpu.VMEM(expert_in.shape, bf16),
-            pltpu.VMEM(expert_out.shape, bf16),
+        16,
+        [("vmem", x) for x in (got, near, across, diagonal)]
+        + [("free", shuffle), ("vmem", first), ("vmem", second)],
+        [("hbm", *s) for s in kept] + [("vmem", returned, bf16)] * 2,
+        [
             *[pltpu.VMEM(*s) for s in kept],
             pltpu.VMEM((owned * 2, count, width), bf16),
-            pltpu.VMEM(got.shape, bf16),
-            dma((2 * owned * (hidden // step) + 4,)),
-        ],
-    )
-    back = back.reshape(sources, -1, width)
-    back = lax.all_to_all(back, both, split_axis=0, concat_axis=0, tiled=True)
+            dma((3,)),
+        ],
+    )
+    groups = [
+        [(2 * x + c) * n_exp + e for x in range(far_img) for e in range(n_exp)] for c in range(2)
+    ]
+    near = swap(send, "img", n_img, 1)
+    (back,) = call(
+        pair_kernel,
+        "pair",
+        4,
+        [("vmem", keep), ("vmem", near)],
+        [("hbm", (far_img,) + got.shape, bf16)],
+        [pltpu.VMEM((far_img,) + got.shape, bf16), dma((far_img,))],
+    )
+    back = back.reshape(far_img * n_exp, -1, width)
+    back = lax.all_to_all(
+        back, ("img", "exp"), 0, 0, axis_index_groups=groups, tiled=True
+    )
 
     cuts = 4
     fixed = lambda x: pltpu.with_memory_space_constraint(x, pltpu.HBM)
@@ -526,8 +551,11 @@
         compiler_params=pltpu.CompilerParams(vmem_limit_bytes=14 * 1024 * 1024),
         name="expert_grads",
     )(fixed(slot_rows), fixed(act), fixed(grad_pre))
-    back, grad_expert_in, grad_expert_out = lax.optimization_barrier(
-        (back, grad_expert_in, grad_expert_out)
+    (left_p,) = call(
+        fetch_kernel, "left", 4, [("hbm", send_left[0])], [("vmem", left, bf16)], [dma((1,))]
+    )
+    back, grad_expert_in, grad_expert_out, left_p = lax.optimization_barrier(
+        (back, grad_expert_in, grad_expert_out, left_p)
     )
 
     n = width // 2
@@ -535,9 +563,9 @@
         functools.partial(backward_kernel, images, factor),
         "backward",
         24,
-        [("vmem", back.reshape(n_img, -1, width)), ("free", perm), ("free", unit_t)]
-        + [("vmem", x) for x in (*kept_stats, cot)]
-        + [("hbm", x) for x in send_left],
+        [("vmem", back.reshape(far_img, -1, width)), ("free", perm), ("free", unit_t)]
+        + [("vmem", x) for x in (*kept_stats, cot, left_p)]
+        + [("hbm", send_left[1])],
         [
             ("hbm", (rows, width), bf16),
             ("vmem", (2 * n + 4 * slots, half), bf16),
@@ -545,9 +573,8 @@
         ],
         [
             pltpu.VMEM(left, bf16),
-            pltpu.VMEM(left, bf16),
             pltpu.VMEM((rows, width), bf16),
-            dma((2 + images,)),
+            dma((1 + images,)),
         ],
     )
 

time: 114 us -> 108 us (0.947)
  blocking collectives: 20.6 us -> 13.4 us
  waiting for transfers between devices: 30.8 us -> 26.4 us
  starting transfers between devices: 22.4 us -> 26.1 us
  Pallas kernels: 35.7 us -> 36.9 us
    all_gather x1 -> x0, blocking collectives: 7.16 us -> none  [shards(): got = lax.all_gather(got, 'img', axis=0, tiled=True).reshape(-1, width)]
    all_to_all x1, waiting for transfers between devices: 8.78 us -> 1.99 us  [shards(): lax.all_to_all(back, ('img', 'exp'), 0, 0, axis_index_groups=groups, tile...]
    ppermute x18 -> x22, starting transfers between devices: 19.6 us -> 22.4 us  [swap(): return lax.ppermute(x, axis, [(i, i ^ bit) for i in range(size)])]
    ppermute x18 -> x22, waiting for transfers between devices: 22 us -> 24.4 us  [swap(): return lax.ppermute(x, axis, [(i, i ^ bit) for i in range(size)])]
    pallas_call x12 -> x15, Pallas kernels: 28.3 us -> 29.5 us  [call(): pl.pallas_call(kernel, in_specs=[pl.BlockSpec(memory_space=spaces[where])...]
  transfers between devices with their start and end apart: 19 -> 23, of which waited for: 14 -> 15; matrix products, arithmetic and copies ran while one was open for 3% -> 3% of each run, Pallas kernels for 17% -> 22%
where the time goes in v5:
time: 108 us; the launch traced here: 107 us
  Pallas kernels  36.9 us (34%)
  waiting for transfers between devices  26.4 us (24%)
  starting transfers between devices  26.1 us (24%)
  blocking collectives  13.4 us (12%)
  other arithmetic  3.24 us (3%)
    pallas_call x15, Pallas kernels, call(): pl.pallas_call(kernel, in_specs=[pl.BlockSpec(memory_space=spaces[where])...  29.5 us
    ppermute x22, waiting for transfers between devices, swap(): return lax.ppermute(x, axis, [(i, i ^ bit) for i in range(size)])  24.4 us
    ppermute x22, starting transfers between devices, swap(): return lax.ppermute(x, axis, [(i, i ^ bit) for i in range(size)])  22.4 us
    all_to_all x1, blocking collectives, shards(): got = lax.all_to_all(out.reshape(n_exp, -1, width), 'exp', 0, 0, tiled=True)  13.4 us
    pallas_call x1, Pallas kernels, shards(): pl.pallas_call(grads_kernel, grid=(owned, cuts), in_specs=[pl.BlockSpec((...  7.39 us
    all_to_all x1, starting transfers between devices, shards(): lax.all_to_all(back, ('img', 'exp'), 0, 0, axis_index_groups=groups, tile...  3.74 us
  transfers between devices with their start and end apart: 23, of which 15 were waited for; matrix products, arithmetic and copies ran while one was open for 3% of the time, Pallas kernels for 22%

profile of v5, /device:TPU:0, one launch (start us, length us, event | category | flops | bytes accessed | tf_op | source)
XLA Modules:
  0.0 107.2 jit_solution(17688178066492784013)
XLA Ops:
  0.6 3.0 %collective-permute-start.1 = (bf16[256,1024]{1,0:T(8,128)(2,1)}, bf16[256,1024]{1,0:T(8,128)(2,1)S(1)}, u32[]{:S(2)}, u32[]{:S(2)}) collective-permute-start(bf16[256,1024]{1,0:T(8,128)(2,1)} %own_hbm.3), channel_id=1, source_target_pairs={{0,16},{8,24},{16,0},{24,8},{1,17},{9,25},{17,1},{25,9},{2,18},{10... | collective-permute-start | bytes 1572872 | tf_op jit(solution)/shard_map/ppermute | solution.py:44
  7.0 3.3 %prepare.1 = (bf16[512,512]{1,0:T(8,128)(2,1)}, bf16[512,512]{1,0:T(8,128)(2,1)}, bf16[512,512]{1,0:T(8,128)(2,1)}, bf16[512,512]{1,0:T(8,128)(2,1)}, bf16[256,1...) custom-call(bf16[512,1024]{1,0:T(8,128)(2,1)} %bitcast.23, ...), custom_call_target="tpu_custom_call" | custom-call | tf_op jit(solution)/shard_map/prepare/pallas_call | solution.py:24
  10.3 5.5 %collective-permute-done.1.block = bf16[256,1024]{1,0:T(8,128)(2,1)S(1)} collective-permute-done((bf16[256,1024]{1,0:T(8,128)(2,1)}, bf16[256,1024]{1,0:T(8,128)(2,1)S(1)}, u32[]{:S(2)}, u32[]{:S(2)}) %collective-permute-start.1) | collective-permute-done | bytes 524320 | tf_op jit(solution)/shard_map/ppermute | solution.py:44
  17.7 3.1 %forward.1 = (bf16[256,1024]{1,0:T(8,128)(2,1)}, bf16[512,1024]{1,0:T(8,128)(2,1)S(1)}, f32[512,16]{1,0:T(8,128)S(1)}, bf16[64,1024]{1,0:T(8,128)(2,1)}) custom-call(bf16[512,1024]{1,0:T(8,128)(2,1)S(1)} %get-tuple-element.72.ctx, f32[512,1024]{1,0:T(8,128)S(1)} %get-tuple-element.77.start, bf16[512,1024]{1,0:T(8,128)(2,1)S(1)} %get-tuple-element.78.cot.refs_2_, ...), custom_call_target="tpu_custom_call" | custom-call | tf_op jit(solution)/shard_map/forward/pallas_call | solution.py:24
  20.8 13.4 %all_to_all.10 = bf16[8,8,1024]{2,1,0:T(8,128)(2,1)S(1)} all-to-all(bf16[8,8,1024]{2,1,0:T(8,128)(2,1)} %bitcast.27), channel_id=1, replica_groups=mesh['img'=4,'exp'=8] {'exp'}, dimensions={0} | all-to-all | bytes 262144 | tf_op jit(solution)/shard_map/all_to_all | solution.py:487
  34.3 1.5 %collective-permute-start.4 = (bf16[64,1024]{1,0:T(8,128)(2,1)S(1)}, bf16[64,1024]{1,0:T(8,128)(2,1)S(1)}, u32[]{:S(2)}, u32[]{:S(2)}) collective-permute-start(bf16[64,1024]{1,0:T(8,128)(2,1)S(1)} %bitcast.18), channel_id=1, source_target_pairs={{0,16},{8,24},{16,0},{24,8},{1,17},{9,25},{17,1},{25,9},{2,18},{10... | collective-permute-start | bytes 393224 | tf_op jit(solution)/shard_map/ppermute | solution.py:44
  35.8 3.5 %weights.1 = (bf16[2,1024,1024]{2,1,0:T(8,128)(2,1)S(1)}, bf16[2,1024,1024]{2,1,0:T(8,128)(2,1)S(1)}) custom-call(bf16[2,1024,1024]{2,1,0:T(8,128)(2,1)} %refs_0_, bf16[2,1024,1024]{2,1,0:T(8,128)(2,1)} %refs_1_), custom_call_target="tpu_custom_call" | custom-call | tf_op jit(solution)/shard_map/weights/pallas_call | solution.py:24
  40.8 4.9 %experts.1 = (bf16[4,64,1024]{2,1,0:T(8,128)(2,1)}, bf16[2,64,1024]{2,1,0:T(8,128)(2,1)}, bf16[2,64,1024]{2,1,0:T(8,128)(2,1)}, bf16[128,1024]{1,0:T(8,128)(2,1)S(1)}, bf16[128,1024]{1,0:T(8,128)(2,1)S(1)}) custom-call(bf16[64,1024]{1,0:T(8,128)(2,1)S(1)} %bitcast.20, bf16[64,1024]{1,0:T(8,128)(2,1)S(1)} %collective-permute-done.3.near, ...), custom_call_target="tpu_custom_call" | custom-call | tf_op jit(solution)/shard_map/experts/pallas_call | solution.py:24
  46.2 1.2 %collective-permute-done.6.got = bf16[128,1024]{1,0:T(8,128)(2,1)S(1)} collective-permute-done((bf16[128,1024]{1,0:T(8,128)(2,1)S(1)}, bf16[128,1024]{1,0:T(8,128)(2,1)S(1)}, u32[]{:S(2)}, u32[]{:S(2)}) %collective-permute-start.6) | collective-permute-done | bytes 262176 | tf_op jit(solution)/shard_map/ppermute | solution.py:44
  48.1 3.7 %all-to-all-start.1 = ((bf16[16,8,1024]{2,1,0:T(8,128)(2,1)}), bf16[16,8,1024]{2,1,0:T(8,128)(2,1)S(1)}, u32[]{:S(2)}, u32[]{:S(2)}) async-start(bf16[16,8,1024]{2,1,0:T(8,128)(2,1)} %bitcast.22), calls=%async_computation.1 | async-start | bytes 524288 | tf_op jit(solution)/shard_map/all_to_all | solution.py:531
  52.9 7.4 %expert_grads.1 = (bf16[2,1024,1024]{2,1,0:T(8,128)(2,1)}, bf16[2,1024,1024]{2,1,0:T(8,128)(2,1)}) custom-call(bf16[4,64,1024]{2,1,0:T(8,128)(2,1)} %get-tuple-element.93.rows, bf16[2,64,1024]{2,1,0:T(8,128)(2,1)} %get-tuple-element.94.act, bf16[2,64,1024]{2,1,0:T(8,128)(2,1)} %get-tuple-element.95.grad_pre), custom_call_target="tpu_custom_call" | custom-call | tf_op jit(solution)/shard_map/expert_grads/pallas_call | solution.py:538
  60.3 2.0 %all-to-all-done.1 = bf16[16,8,1024]{2,1,0:T(8,128)(2,1)S(1)} async-done(((bf16[16,8,1024]{2,1,0:T(8,128)(2,1)}), bf16[16,8,1024]{2,1,0:T(8,128)(2,1)S(1)}, u32[]{:S(2)}, u32[]{:S(2)}) %all-to-all-start.1) | async-done | bytes 262176 | tf_op jit(solution)/shard_map/all_to_all | solution.py:531
  62.3 3.1 %backward.1 = (bf16[512,1024]{1,0:T(8,128)(2,1)}, bf16[1088,512]{1,0:T(8,128)(2,1)S(1)}, f32[32,512]{1,0:T(8,128)S(1)}) custom-call(bf16[2,64,1024]{2,1,0:T(8,128)(2,1)S(1)} %bitcast.17, bf16[64,64]{1,0:T(8,128)(2,1)S(1)} %fusion.3.perm, bf16[16,1024]{1,0:T(8,128)(2,1)S(1)} %get-tuple-element.79.unit.unit_t, ...), custom_call_target="tpu_custom_call" | custom-call | tf_op jit(solution)/shard_map/backward/pallas_call | solution.py:24
  65.4 2.3 %keep.1 = bf16[1024,512]{1,0:T(8,128)(2,1)S(1)} custom-call(bf16[512,512]{1,0:T(8,128)(2,1)} %get-tuple-element.70.left_p_hbm, bf16[512,512]{1,0:T(8,128)(2,1)} %get-tuple-element.71.left_q_hbm, bf16[512,1024]{1,0:T(8,128)(2,1)} %get-tuple-element.104.grad_hbm), custom_call_target="tpu_custom_call" | custom-call | tf_op jit(solution)/shard_map/keep/pallas_call | solution.py:24
  70.1 5.0 %context.1 = bf16[512,1024]{1,0:T(8,128)(2,1)} custom-call(bf16[512,1024]{1,0:T(8,128)(2,1)} %get-tuple-element.104.grad_hbm, bf16[256,1024]{1,0:T(8,128)(2,1)} %own_hbm.3, bf16[256,1024]{1,0:T(8,128)(2,1)} %get-tuple-element.109.near_hbm, bf16[256,1024]{1,0:T(8,128)(2,1)} %get-tuple-element.110.far_hbm, bf16[256,1024]{1,0:T(8,128)(2,1)} %get-tuple-element.111.far_near_hbm), custom_call_target="tpu_custom_call" | custom-call | tf_op jit(solution)/shard_map/context/pallas_call | solution.py:24
  75.2 2.2 %collective-permute-done.8.got_p = bf16[256,512]{1,0:T(8,128)(2,1)S(1)} collective-permute-done((bf16[256,512]{1,0:T(8,128)(2,1)S(1)}, bf16[256,512]{1,0:T(8,128)(2,1)S(1)}, u32[]{:S(2)}, u32[]{:S(2)}) %collective-permute-start.8) | collective-permute-done | bytes 262176 | tf_op jit(solution)/shard_map/ppermute | solution.py:44
  79.9 3.9 %collective-permute-done.10.got_p = bf16[128,512]{1,0:T(8,128)(2,1)S(1)} collective-permute-done((bf16[128,512]{1,0:T(8,128)(2,1)S(1)}, bf16[128,512]{1,0:T(8,128)(2,1)S(1)}, u32[]{:S(2)}, u32[]{:S(2)}) %collective-permute-start.10) | collective-permute-done | bytes 131104 | tf_op jit(solution)/shard_map/ppermute | solution.py:44
  84.7 2.3 %collective-permute-start.13 = (bf16[72,512]{1,0:T(8,128)(2,1)S(1)}, bf16[72,512]{1,0:T(8,128)(2,1)S(1)}, u32[]{:S(2)}, u32[]{:S(2)}) collective-permute-start(bf16[72,512]{1,0:T(8,128)(2,1)S(1)} %get-tuple-element.126), channel_id=1, source_target_pairs={{0,4},{1,5},{2,6},{3,7},{4,0},{5,1},{6,2},{7,3},{8,12},{9,13},{10,... | collective-permute-start | bytes 221192 | tf_op jit(solution)/shard_map/ppermute | solution.py:44
  87.0 1.4 %collective-permute-start.14 = (bf16[72,512]{1,0:T(8,128)(2,1)S(1)}, bf16[72,512]{1,0:T(8,128)(2,1)S(1)}, u32[]{:S(2)}, u32[]{:S(2)}) collective-permute-start(bf16[72,512]{1,0:T(8,128)(2,1)S(1)} %get-tuple-element.127), channel_id=1, source_target_pairs={{0,6},{1,7},{2,4},{3,5},{4,2},{5,3},{6,0},{7,1},{8,14},{9,15},{10,... | collective-permute-start | bytes 221192 | tf_op jit(solution)/shard_map/ppermute | solution.py:44
  88.4 2.9 %collective-permute-done.13.refs_1_ = bf16[72,512]{1,0:T(8,128)(2,1)S(1)} collective-permute-done((bf16[72,512]{1,0:T(8,128)(2,1)S(1)}, bf16[72,512]{1,0:T(8,128)(2,1)S(1)}, u32[]{:S(2)}, u32[]{:S(2)}) %collective-permute-start.13) | collective-permute-done | bytes 73760 | tf_op jit(solution)/shard_map/ppermute | solution.py:44
  91.3 2.5 %collective-permute-done.14.refs_2_ = bf16[72,512]{1,0:T(8,128)(2,1)S(1)} collective-permute-done((bf16[72,512]{1,0:T(8,128)(2,1)S(1)}, bf16[72,512]{1,0:T(8,128)(2,1)S(1)}, u32[]{:S(2)}, u32[]{:S(2)}) %collective-permute-start.14) | collective-permute-done | bytes 73760 | tf_op jit(solution)/shard_map/ppermute | solution.py:44
  93.9 1.4 %collective-permute-start.16 = (bf16[72,512]{1,0:T(8,128)(2,1)S(1)}, bf16[72,512]{1,0:T(8,128)(2,1)S(1)}, u32[]{:S(2)}, u32[]{:S(2)}) collective-permute-start(bf16[72,512]{1,0:T(8,128)(2,1)S(1)} %fourth.1.refs_0_), channel_id=1, source_target_pairs={{0,4},{1,5},{2,6},{3,7},{4,0},{5,1},{6,2},{7,3},{8,12},{9,13},{10,... | collective-permute-start | bytes 221192 | tf_op jit(solution)/shard_map/ppermute | solution.py:44
  95.3 3.0 %collective-permute-start.17 = (bf16[72,512]{1,0:T(8,128)(2,1)S(1)}, bf16[72,512]{1,0:T(8,128)(2,1)S(1)}, u32[]{:S(2)}, u32[]{:S(2)}) collective-permute-start(bf16[72,512]{1,0:T(8,128)(2,1)S(1)} %fourth.1.refs_0_), channel_id=1, source_target_pairs={{0,6},{1,7},{2,4},{3,5},{4,2},{5,3},{6,0},{7,1},{8,14},{9,15},{10,... | collective-permute-start | bytes 221192 | tf_op jit(solution)/shard_map/ppermute | solution.py:44
  104.7 1.2 %collective-permute-done.21.refs_7_ = bf16[72,512]{1,0:T(8,128)(2,1)S(1)} collective-permute-done((bf16[72,512]{1,0:T(8,128)(2,1)S(1)}, bf16[72,512]{1,0:T(8,128)(2,1)S(1)}, u32[]{:S(2)}, u32[]{:S(2)}) %collective-permute-start.21) | collective-permute-done | bytes 73760 | tf_op jit(solution)/shard_map/ppermute | solution.py:44
  (45 shorter events, 22.5 us)
Async XLA Ops:
  0.6 15.1 %collective-permute-start.1 = (bf16[256,1024]{1,0:T(8,128)(2,1)}, bf16[256,1024]{1,0:T(8,128)(2,1)S(1)}, u32[]{:S(2)}, u32[]{:S(2)}) collective-permute-start(bf16[256,1024]{1,0:T(8,128)(2,1)} %own_hbm.3), channel_id=1, source_target_pairs={{0,16},{8,24},{16,0},{24,8},{1,17},{9,25},{17,1},{25,9},{2,18},{10... | collective-permute-start | bytes 1572872 | tf_op jit(solution)/shard_map/ppermute | solution.py:44
  4.4 2.6 %collective-permute-start = (bf16[256,1024]{1,0:T(8,128)(2,1)}, bf16[256,1024]{1,0:T(8,128)(2,1)S(1)}, u32[]{:S(2)}, u32[]{:S(2)}) collective-permute-start(bf16[256,1024]{1,0:T(8,128)(2,1)} %own_hbm.3), channel_id=1, source_target_pairs={{0,8},{8,0},{16,24},{24,16},{1,9},{9,1},{17,25},{25,17},{2,10},{10... | collective-permute-start | bytes 1572872 | tf_op jit(solution)/shard_map/ppermute | solution.py:44
  15.8 1.9 %collective-permute-start.2 = (bf16[256,1024]{1,0:T(8,128)(2,1)S(1)}, bf16[256,1024]{1,0:T(8,128)(2,1)S(1)}, u32[]{:S(2)}, u32[]{:S(2)}) collective-permute-start(bf16[256,1024]{1,0:T(8,128)(2,1)S(1)} %collective-permute-done.1.block), channel_id=1, source_target_pairs={{0,8},{8,0},{16,24},{24,16},{1,9},{9,1},{17,25},{25,17},{2,10},{10... | collective-permute-start | bytes 1572872 | tf_op jit(solution)/shard_map/ppermute | solution.py:44
  34.3 5.0 %collective-permute-start.4 = (bf16[64,1024]{1,0:T(8,128)(2,1)S(1)}, bf16[64,1024]{1,0:T(8,128)(2,1)S(1)}, u32[]{:S(2)}, u32[]{:S(2)}) collective-permute-start(bf16[64,1024]{1,0:T(8,128)(2,1)S(1)} %bitcast.18), channel_id=1, source_target_pairs={{0,16},{8,24},{16,0},{24,8},{1,17},{9,25},{17,1},{25,9},{2,18},{10... | collective-permute-start | bytes 393224 | tf_op jit(solution)/shard_map/ppermute | solution.py:44
  35.7 4.1 %collective-permute-start.3 = (bf16[64,1024]{1,0:T(8,128)(2,1)S(1)}, bf16[64,1024]{1,0:T(8,128)(2,1)S(1)}, u32[]{:S(2)}, u32[]{:S(2)}) collective-permute-start(bf16[64,1024]{1,0:T(8,128)(2,1)S(1)} %bitcast.19), channel_id=1, source_target_pairs={{0,8},{8,0},{16,24},{24,16},{1,9},{9,1},{17,25},{25,17},{2,10},{10... | collective-permute-start | bytes 393224 | tf_op jit(solution)/shard_map/ppermute | solution.py:44
  39.3 1.6 %collective-permute-start.5 = (bf16[64,1024]{1,0:T(8,128)(2,1)S(1)}, bf16[64,1024]{1,0:T(8,128)(2,1)S(1)}, u32[]{:S(2)}, u32[]{:S(2)}) collective-permute-start(bf16[64,1024]{1,0:T(8,128)(2,1)S(1)} %collective-permute-done.4.across), channel_id=1, source_target_pairs={{0,8},{8,0},{16,24},{24,16},{1,9},{9,1},{17,25},{25,17},{2,10},{10... | collective-permute-start | bytes 393224 | tf_op jit(solution)/shard_map/ppermute | solution.py:44
  45.7 1.6 %collective-permute-start.6 = (bf16[128,1024]{1,0:T(8,128)(2,1)S(1)}, bf16[128,1024]{1,0:T(8,128)(2,1)S(1)}, u32[]{:S(2)}, u32[]{:S(2)}) collective-permute-start(bf16[128,1024]{1,0:T(8,128)(2,1)S(1)} %get-tuple-element.92), channel_id=1, source_target_pairs={{0,8},{8,0},{16,24},{24,16},{1,9},{9,1},{17,25},{25,17},{2,10},{10... | collective-permute-start | bytes 786440 | tf_op jit(solution)/shard_map/ppermute | solution.py:44
  48.1 14.2 %all-to-all-start.1 = ((bf16[16,8,1024]{2,1,0:T(8,128)(2,1)}), bf16[16,8,1024]{2,1,0:T(8,128)(2,1)S(1)}, u32[]{:S(2)}, u32[]{:S(2)}) async-start(bf16[16,8,1024]{2,1,0:T(8,128)(2,1)} %bitcast.22), calls=%async_computation.1 | async-start | bytes 524288 | tf_op jit(solution)/shard_map/all_to_all | solution.py:531
  65.4 2.8 %collective-permute-start.7 = (bf16[1088,512]{1,0:T(8,128)(2,1)S(1)}, bf16[1088,512]{1,0:T(8,128)(2,1)S(1)}, u32[]{:S(2)}, u32[]{:S(2)}) collective-permute-start(bf16[1088,512]{1,0:T(8,128)(2,1)S(1)} %get-tuple-element.106), channel_id=1, source_target_pairs={{0,8},{8,0},{16,24},{24,16},{1,9},{9,1},{17,25},{25,17},{2,10},{10... | collective-permute-start | bytes 3342344 | tf_op jit(solution)/shard_map/ppermute | solution.py:44
  68.4 9.1 %collective-permute-start.9 = (bf16[288,512]{1,0:T(8,128)(2,1)S(1)}, bf16[288,512]{1,0:T(8,128)(2,1)S(1)}, u32[]{:S(2)}, u32[]{:S(2)}) collective-permute-start(bf16[288,512]{1,0:T(8,128)(2,1)S(1)} %get-tuple-element.108), channel_id=1, source_target_pairs={{0,1},{1,0},{2,3},{3,2},{4,5},{5,4},{6,7},{7,6},{8,9},{9,8},{10,11... | collective-permute-start | bytes 884744 | tf_op jit(solution)/shard_map/ppermute | solution.py:44
  69.3 8.1 %collective-permute-start.8 = (bf16[256,512]{1,0:T(8,128)(2,1)S(1)}, bf16[256,512]{1,0:T(8,128)(2,1)S(1)}, u32[]{:S(2)}, u32[]{:S(2)}) collective-permute-start(bf16[256,512]{1,0:T(8,128)(2,1)S(1)} %get-tuple-element.107), channel_id=1, source_target_pairs={{0,16},{8,24},{16,0},{24,8},{1,17},{9,25},{17,1},{25,9},{2,18},{10... | collective-permute-start | bytes 786440 | tf_op jit(solution)/shard_map/ppermute | solution.py:44
  77.7 6.1 %collective-permute-start.11 = (bf16[160,512]{1,0:T(8,128)(2,1)S(1)}, bf16[160,512]{1,0:T(8,128)(2,1)S(1)}, u32[]{:S(2)}, u32[]{:S(2)}) collective-permute-start(bf16[160,512]{1,0:T(8,128)(2,1)S(1)} %get-tuple-element.122), channel_id=1, source_target_pairs={{0,16},{8,24},{16,0},{24,8},{1,17},{9,25},{17,1},{25,9},{2,18},{10... | collective-permute-start | bytes 491528 | tf_op jit(solution)/shard_map/ppermute | solution.py:44
  78.9 5.0 %collective-permute-start.10 = (bf16[128,512]{1,0:T(8,128)(2,1)S(1)}, bf16[128,512]{1,0:T(8,128)(2,1)S(1)}, u32[]{:S(2)}, u32[]{:S(2)}) collective-permute-start(bf16[128,512]{1,0:T(8,128)(2,1)S(1)} %get-tuple-element.121), channel_id=1, source_target_pairs={{0,1},{1,0},{2,3},{3,2},{4,5},{5,4},{6,7},{7,6},{8,9},{9,8},{10,11... | collective-permute-start | bytes 393224 | tf_op jit(solution)/shard_map/ppermute | solution.py:44
  83.9 4.5 %collective-permute-start.12 = (bf16[72,512]{1,0:T(8,128)(2,1)S(1)}, bf16[72,512]{1,0:T(8,128)(2,1)S(1)}, u32[]{:S(2)}, u32[]{:S(2)}) collective-permute-start(bf16[72,512]{1,0:T(8,128)(2,1)S(1)} %get-tuple-element.125), channel_id=1, source_target_pairs={{0,2},{1,3},{2,0},{3,1},{4,6},{5,7},{6,4},{7,5},{8,10},{9,11},{10,... | collective-permute-start | bytes 221192 | tf_op jit(solution)/shard_map/ppermute | solution.py:44
  84.7 6.6 %collective-permute-start.13 = (bf16[72,512]{1,0:T(8,128)(2,1)S(1)}, bf16[72,512]{1,0:T(8,128)(2,1)S(1)}, u32[]{:S(2)}, u32[]{:S(2)}) collective-permute-start(bf16[72,512]{1,0:T(8,128)(2,1)S(1)} %get-tuple-element.126), channel_id=1, source_target_pairs={{0,4},{1,5},{2,6},{3,7},{4,0},{5,1},{6,2},{7,3},{8,12},{9,13},{10,... | collective-permute-start | bytes 221192 | tf_op jit(solution)/shard_map/ppermute | solution.py:44
  87.0 6.8 %collective-permute-start.14 = (bf16[72,512]{1,0:T(8,128)(2,1)S(1)}, bf16[72,512]{1,0:T(8,128)(2,1)S(1)}, u32[]{:S(2)}, u32[]{:S(2)}) collective-permute-start(bf16[72,512]{1,0:T(8,128)(2,1)S(1)} %get-tuple-element.127), channel_id=1, source_target_pairs={{0,6},{1,7},{2,4},{3,5},{4,2},{5,3},{6,0},{7,1},{8,14},{9,15},{10,... | collective-permute-start | bytes 221192 | tf_op jit(solution)/shard_map/ppermute | solution.py:44
  93.8 5.4 %collective-permute-start.15 = (bf16[72,512]{1,0:T(8,128)(2,1)S(1)}, bf16[72,512]{1,0:T(8,128)(2,1)S(1)}, u32[]{:S(2)}, u32[]{:S(2)}) collective-permute-start(bf16[72,512]{1,0:T(8,128)(2,1)S(1)} %fourth.1.refs_0_), channel_id=1, source_target_pairs={{0,2},{1,3},{2,0},{3,1},{4,6},{5,7},{6,4},{7,5},{8,10},{9,11},{10,... | collective-permute-start | bytes 221192 | tf_op jit(solution)/shard_map/ppermute | solution.py:44
  93.9 6.4 %collective-permute-start.16 = (bf16[72,512]{1,0:T(8,128)(2,1)S(1)}, bf16[72,512]{1,0:T(8,128)(2,1)S(1)}, u32[]{:S(2)}, u32[]{:S(2)}) collective-permute-start(bf16[72,512]{1,0:T(8,128)(2,1)S(1)} %fourth.1.refs_0_), channel_id=1, source_target_pairs={{0,4},{1,5},{2,6},{3,7},{4,0},{5,1},{6,2},{7,3},{8,12},{9,13},{10,... | collective-permute-start | bytes 221192 | tf_op jit(solution)/shard_map/ppermute | solution.py:44
  95.3 6.2 %collective-permute-start.17 = (bf16[72,512]{1,0:T(8,128)(2,1)S(1)}, bf16[72,512]{1,0:T(8,128)(2,1)S(1)}, u32[]{:S(2)}, u32[]{:S(2)}) collective-permute-start(bf16[72,512]{1,0:T(8,128)(2,1)S(1)} %fourth.1.refs_0_), channel_id=1, source_target_pairs={{0,6},{1,7},{2,4},{3,5},{4,2},{5,3},{6,0},{7,1},{8,14},{9,15},{10,... | collective-permute-start | bytes 221192 | tf_op jit(solution)/shard_map/ppermute | solution.py:44
  98.3 4.4 %collective-permute-start.18 = (bf16[72,512]{1,0:T(8,128)(2,1)S(1)}, bf16[72,512]{1,0:T(8,128)(2,1)S(1)}, u32[]{:S(2)}, u32[]{:S(2)}) collective-permute-start(bf16[72,512]{1,0:T(8,128)(2,1)S(1)} %fourth.1.refs_0_), channel_id=1, source_target_pairs={{0,1},{1,0},{2,3},{3,2},{4,5},{5,4},{6,7},{7,6},{8,9},{9,8},{10,11... | collective-permute-start | bytes 221192 | tf_op jit(solution)/shard_map/ppermute | solution.py:44
  99.2 4.4 %collective-permute-start.19 = (bf16[72,512]{1,0:T(8,128)(2,1)S(1)}, bf16[72,512]{1,0:T(8,128)(2,1)S(1)}, u32[]{:S(2)}, u32[]{:S(2)}) collective-permute-start(bf16[72,512]{1,0:T(8,128)(2,1)S(1)} %collective-permute-done.15.refs_1_), channel_id=1, source_target_pairs={{0,1},{1,0},{2,3},{3,2},{4,5},{5,4},{6,7},{7,6},{8,9},{9,8},{10,11... | collective-permute-start | bytes 221192 | tf_op jit(solution)/shard_map/ppermute | solution.py:44
  100.3 4.4 %collective-permute-start.20 = (bf16[72,512]{1,0:T(8,128)(2,1)S(1)}, bf16[72,512]{1,0:T(8,128)(2,1)S(1)}, u32[]{:S(2)}, u32[]{:S(2)}) collective-permute-start(bf16[72,512]{1,0:T(8,128)(2,1)S(1)} %collective-permute-done.16.refs_2_), channel_id=1, source_target_pairs={{0,1},{1,0},{2,3},{3,2},{4,5},{5,4},{6,7},{7,6},{8,9},{9,8},{10,11... | collective-permute-start | bytes 221192 | tf_op jit(solution)/shard_map/ppermute | solution.py:44
  101.6 4.4 %collective-permute-start.21 = (bf16[72,512]{1,0:T(8,128)(2,1)S(1)}, bf16[72,512]{1,0:T(8,128)(2,1)S(1)}, u32[]{:S(2)}, u32[]{:S(2)}) collective-permute-start(bf16[72,512]{1,0:T(8,128)(2,1)S(1)} %collective-permute-done.17.refs_3_), channel_id=1, source_target_pairs={{0,1},{1,0},{2,3},{3,2},{4,5},{5,4},{6,7},{7,6},{8,9},{9,8},{10,11... | collective-permute-start | bytes 221192 | tf_op jit(solution)/shard_map/ppermute | solution.py:44

commit v6 on v5

--- a/solution.py
+++ b/solution.py
@@ -16,7 +16,7 @@
 spaces = {"vmem": pltpu.VMEM, "hbm": pltpu.HBM, "free": pltpu.VMEM}
 
 
-def call(kernel, name, mib, inputs, outputs, scratch=()):
+def call(kernel, name, mib, inputs, outputs, scratch=(), aliases=()):
     def held(where, x):
         fixed = where in ("vmem", "hbm")
         return pltpu.with_memory_space_constraint(x, spaces[where]) if fixed else x
@@ -27,6 +27,7 @@
         out_specs=[pl.BlockSpec(memory_space=spaces[where]) for where, _, _ in outputs],
         out_shape=[spaces[where](s, t) for where, s, t in outputs],
         scratch_shapes=list(scratch),
+        input_output_aliases=dict(aliases),
         compiler_params=pltpu.CompilerParams(vmem_limit_bytes=mib * 1024 * 1024),
         name=name,
     )(*[held(where, x) for where, x in inputs])
@@ -36,7 +37,8 @@
     n = len(refs) // 2
     mover = Mover(refs[-1])
     pairs = zip(refs[:n], refs[n : 2 * n], strict=True)
-    for copy in [mover.start(x.at[pl.ds(0, y.shape[0])], y) for x, y in pairs]:
+    tails = [(x.at[pl.ds(x.shape[0] - y.shape[0], y.shape[0])], y) for x, y in pairs]
+    for copy in [mover.start(x, y) for x, y in tails]:
         copy.wait()
 
 
@@ -101,9 +103,9 @@
         return copy
 
 
-def prepare_kernel(n_img, n_exp, ctx_hbm, res_hbm, cot_hbm, own_hbm, near, *refs):
-    lefts, near_out, mixed, ctx, cot = refs[:4], *refs[4:8]
-    res, own, turned, kept, sems = refs[8:]
+def prepare_kernel(n_img, n_exp, ctx_hbm, res_hbm, cot_hbm, own_hbm, first_hbm, near, *refs):
+    lefts, near_out, mixed, ctx, cot, early = refs[:4], *refs[4:9]
+    res, own, turned, kept, sems = refs[9:]
     mover = Mover(sems)
     get_ctx = mover.start(ctx_hbm, ctx)
     get_own = mover.start(own_hbm, own)
@@ -130,6 +132,7 @@
     first = pl.ds(pl.multiple_of(lax.axis_index("img") * deep, deep), deep)
     second = pl.ds(pl.multiple_of((lax.axis_index("img") ^ 1) * deep, deep), deep)
     mixed[...] = res[...].astype(f32) + dot(ctx[:, first], own[...]) + dot(ctx[:, second], near[...])
+    out.append(mover.start(first_hbm.at[pl.ds(0, early.shape[0])], early))
     for copy in out:
         copy.wait()
 
@@ -152,7 +155,7 @@
 
 
 def forward_kernel(images, factor, taken, ctx, start, cot, unit, perm, block, *refs):
-    block_out, stream_v, expo_v, slots_hbm, slots_v, sems = refs
+    block_out, stream_v, expo_v, slots_v, sems = refs
     mover = Mover(sems)
     deep = block.shape[0]
     tokens = cot.shape[0] // images
@@ -174,21 +177,22 @@
         grad_out.append(dot_first(combine32.astype(bf16), cot[at, :]).astype(bf16))
     parts = jnp.concatenate(slot_in + grad_out, axis=0)
     slots_v[...] = dot_first(perm[...], parts).astype(bf16)
-    out.append(mover.start(slots_v, slots_hbm))
     for copy in out:
         copy.wait()
 
 
-def expert_kernel(own, near, across, diagonal, perm, first, second, *refs):
+def expert_kernel(own, near, across, diagonal, perm, early, first, second, *refs):
     rows_hbm, act_hbm, grad_hbm, keep, send = refs[:5]
     rows, act, grad_pre, held, sems = refs[5:]
     mover = Mover(sems)
-    owned = first.shape[0]
+    owned = second.shape[0]
+    early_count = early.shape[0]
     got = jnp.concatenate([own[...], across[...], near[...], diagonal[...]], axis=0)
     rows[...] = dot(perm[...], got).astype(bf16).reshape(rows.shape)
     out = [mover.start(rows, rows_hbm)]
     for j in range(owned):
-        first_w, second_w = first[j], second[j]
+        first_w = early[j] if j < early_count else first[j - early_count]
+        second_w = second[j]
         value, slope = gelu_both(dot(rows[2 * j], first_w))
         value = value.astype(bf16)
         act[j] = value
@@ -204,25 +208,34 @@
         copy.wait()
 
 
-def pair_kernel(keep, got, out_hbm, out, sems):
+def pair_kernel(keep, got, out):
+    n = out.shape[1]
+    for x in range(out.shape[0]):
+        at = pl.ds(x * n, n)
+        total = keep[at, :].astype(f32) + got[at, :].astype(f32)
+        out[(lax.axis_index("img") >> 1) ^ x] = total.astype(bf16)
+
+
+def grads_kernel(cuts, rows_hbm, act_hbm, grad_hbm, left_hbm, cot_hbm, *refs):
+    first_hbm, second_hbm, left, cot = refs[:4]
+    refs = refs[4:]
+    rows, act, grad_pre, first, second, sems = refs
     mover = Mover(sems)
-    total = (keep[...].astype(f32) + got[...].astype(f32)).astype(bf16)
-    puts = []
-    for x, block in enumerate(halves(total)):
-        out[x] = block
-        puts.append(mover.start(out.at[x], out_hbm.at[(lax.axis_index("img") >> 1) ^ x]))
-    for put in puts:
-        put.wait()
-
-
-def grads_kernel(rows, act, grad_pre, grad_first, grad_second):
-    f = pl.program_id(1)
-    deep = grad_second.shape[1]
-    at = pl.ds(pl.multiple_of(f * deep, deep), deep)
-    grad_second[0] = dot_first(act[0, :, at], rows[1]).astype(bf16)
-    deep = grad_first.shape[1]
-    at = pl.ds(pl.multiple_of(f * deep, deep), deep)
-    grad_first[0] = dot_first(rows[0, :, at], grad_pre[0]).astype(bf16)
+    sources = (rows_hbm, act_hbm, grad_hbm)
+    gets = [mover.start(x, y) for x, y in zip(sources, refs[:3], strict=True)]
+    out = [mover.start(left_hbm, left), mover.start(cot_hbm, cot)]
+    for get in gets:
+        get.wait()
+    for j in range(first.shape[0]):
+        pairs = ((second, second_hbm, act[j], rows[2 * j + 1]), (first, first_hbm, rows[2 * j], grad_pre[j]))
+        for made, made_hbm, a, b in pairs:
+            deep = made.shape[1] // cuts
+            for k in range(cuts):
+                at = slice(k * deep, (k + 1) * deep)
+                made[j, at, :] = dot_first(a[:, at], b).astype(bf16)
+                out.append(mover.start(made.at[j, at, :], made_hbm.at[j, at, :]))
+    for copy in out:
+        copy.wait()
 
 
 def backward_kernel(images, factor, back, perm, unit_t, *refs):
@@ -376,22 +389,32 @@
         put.wait()
 
 
-def last_kernel(deep, *refs):
-    blocks, refs = refs[:-8], refs[-8:]
-    unit_t, slot_norm, grad_hbm, slots_hbm, grad, side, slots_out, sems = refs
-    mover = Mover(sems)
-    groups = len(blocks) // 2
+def settle(y, blocks, grad_hbm, side, grad, mover, deep):
+    groups = len(blocks)
     n, half = grad.shape[1], blocks[0].shape[1]
     puts = []
-    for y in range(2):
-        for z in range(groups):
-            block = blocks[y * groups + z][...].astype(f32)
-            at = lax.axis_index("exp") ^ (2 * z + y)
-            k = 2 * z + y
-            grad[k, :, :half] = block[:n]
-            grad[k, :, half:] = block[n : 2 * n]
-            puts.append(mover.start(grad.at[k], grad_hbm.at[at]))
-            side[(at & 1) * groups + (at >> 1)] = joined(block[2 * n : 2 * n + 2 * deep])
+    for z in range(groups):
+        block = blocks[z][...].astype(f32)
+        at = lax.axis_index("exp") ^ (2 * z + y)
+        grad[z, :, :half] = block[:n]
+        grad[z, :, half:] = block[n : 2 * n]
+        puts.append(mover.start(grad.at[z], grad_hbm.at[at]))
+        side[(at & 1) * groups + (at >> 1)] = joined(block[2 * n : 2 * n + 2 * deep])
+    return puts
+
+
+def settle_kernel(deep, *refs):
+    blocks, (grad_hbm, side, grad, sems) = refs[:-4], refs[-4:]
+    for put in settle(0, blocks, grad_hbm, side, grad, Mover(sems), deep):
+        put.wait()
+
+
+def last_kernel(deep, early, *refs):
+    blocks, refs = refs[:-9], refs[-9:]
+    unit_t, slot_norm, _, grad_hbm, slots_hbm, side, grad, slots_out, sems = refs
+    mover = Mover(sems)
+    side[...] = early[...]
+    puts = settle(1, blocks, grad_hbm, side, grad, mover, deep)
     total = jnp.concatenate([side[k] for k in range(side.shape[0])], axis=0)
     total = jnp.concatenate(halves(total), axis=1)
     unit = unit_t[...]
@@ -423,20 +446,23 @@
     deep = proj_weight.shape[0]
     block = (deep, width)
     left = (width // 2, rows)
-    *lefts, near_copy, mixed, ctx, cot = call(
+    early = (1,) + expert_in.shape[1:]
+    *lefts, near_copy, mixed, ctx, cot, early = call(
         functools.partial(prepare_kernel, n_img, n_exp),
         "prepare",
         16,
-        [("hbm", x) for x in (flat_ctx, flat_res, flat_cot, proj_weight)] + [("vmem", near)],
+        [("hbm", x) for x in (flat_ctx, flat_res, flat_cot, proj_weight, expert_in)]
+        + [("vmem", near)],
         [("hbm", left, bf16)] * 4
         + [("hbm", block, bf16), ("vmem", (rows, width), f32)]
-        + [("vmem", (rows, width), bf16)] * 2,
+        + [("vmem", (rows, width), bf16)] * 2
+        + [("vmem", early, bf16)],
         [
             pltpu.VMEM((rows, width), bf16),
             pltpu.VMEM(block, bf16),
             pltpu.VMEM((width, rows), f32),
             pltpu.VMEM((4,) + left, bf16),
-            dma((9,)),
+            dma((10,)),
         ],
     )
     params32 = slot_params.astype(f32).T
@@ -477,27 +503,24 @@
         ],
         [("hbm", block, bf16)]
         + [("vmem", *s) for s in stats]
-        + [("hbm", (message, width), bf16)],
-        [
-            pltpu.VMEM((message, width), bf16),
-            dma((2,)),
-        ],
+        + [("vmem", (message, width), bf16)],
+        [dma((1,))],
     )
 
     got = lax.all_to_all(out.reshape(n_exp, -1, width), "exp", 0, 0, tiled=True)
     got = got.reshape(-1, width)
     got, first, second = lax.optimization_barrier((got, expert_in, expert_out))
     across = swap(got, "img", n_img, 2)
-    near = swap(got, "img", n_img, 1)
     first, second = call(
         fetch_kernel,
         "weights",
         4,
         [("hbm", first), ("hbm", second)],
-        [("vmem", first.shape, bf16), ("vmem", second.shape, bf16)],
+        [("vmem", (owned - 1,) + first.shape[1:], bf16), ("vmem", second.shape, bf16)],
         [dma((2,))],
     )
-    across, first, second = lax.optimization_barrier((across, first, second))
+    got, across, first, second = lax.optimization_barrier((got, across, first, second))
+    near = swap(got, "img", n_img, 1)
     diagonal = swap(across, "img", n_img, 1)
 
     kept = [((owned * 2, count, width), bf16)] + [((owned, count, hidden), bf16)] * 2
@@ -507,7 +530,7 @@
         "experts",
         16,
         [("vmem", x) for x in (got, near, across, diagonal)]
-        + [("free", shuffle), ("vmem", first), ("vmem", second)],
+        + [("free", shuffle), ("vmem", early), ("vmem", first), ("vmem", second)],
         [("hbm", *s) for s in kept] + [("vmem", returned, bf16)] * 2,
         [
             *[pltpu.VMEM(*s) for s in kept],
@@ -524,38 +547,30 @@
         "pair",
         4,
         [("vmem", keep), ("vmem", near)],
-        [("hbm", (far_img,) + got.shape, bf16)],
-        [pltpu.VMEM((far_img,) + got.shape, bf16), dma((far_img,))],
+        [("vmem", (far_img,) + got.shape, bf16)],
     )
     back = back.reshape(far_img * n_exp, -1, width)
     back = lax.all_to_all(
         back, ("img", "exp"), 0, 0, axis_index_groups=groups, tiled=True
     )
 
-    cuts = 4
-    fixed = lambda x: pltpu.with_memory_space_constraint(x, pltpu.HBM)
-    part = lambda s: pl.BlockSpec((1,) + s, lambda j, f: (j, 0, 0))
-    grad_expert_in, grad_expert_out = pl.pallas_call(
-        grads_kernel,
-        grid=(owned, cuts),
-        in_specs=[
-            pl.BlockSpec((2, count, width), lambda j, f: (j, 0, 0)),
-            part((count, hidden)),
-            part((count, hidden)),
+    cuts = 2
+    grad_expert_in, grad_expert_out, left_p, cot = call(
+        functools.partial(grads_kernel, cuts),
+        "expert_grads",
+        20,
+        [("hbm", x) for x in (slot_rows, act, grad_pre, send_left[0], flat_cot)],
+        [("hbm", expert_in.shape, bf16), ("hbm", expert_out.shape, bf16), ("vmem", left, bf16)]
+        + [("vmem", (rows, width), bf16)],
+        [
+            *[pltpu.VMEM(*s) for s in kept],
+            pltpu.VMEM(expert_in.shape, bf16),
+            pltpu.VMEM(expert_out.shape, bf16),
+            dma((5 + 2 * owned * cuts,)),
         ],
-        out_specs=[
-            pl.BlockSpec((1, width // cuts, hidden), lambda j, f: (j, f, 0)),
-            pl.BlockSpec((1, hidden // cuts, width), lambda j, f: (j, f, 0)),
-        ],
-        out_shape=[pltpu.HBM(expert_in.shape, bf16), pltpu.HBM(expert_out.shape, bf16)],
-        compiler_params=pltpu.CompilerParams(vmem_limit_bytes=14 * 1024 * 1024),
-        name="expert_grads",
-    )(fixed(slot_rows), fixed(act), fixed(grad_pre))
-    (left_p,) = call(
-        fetch_kernel, "left", 4, [("hbm", send_left[0])], [("vmem", left, bf16)], [dma((1,))]
-    )
-    back, grad_expert_in, grad_expert_out, left_p = lax.optimization_barrier(
-        (back, grad_expert_in, grad_expert_out, left_p)
+    )
+    back, grad_expert_in, grad_expert_out, left_p, cot = lax.optimization_barrier(
+        (back, grad_expert_in, grad_expert_out, left_p, cot)
     )
 
     n = width // 2
@@ -646,18 +661,28 @@
     )
     held = [held] + [swap(held, "exp", n_exp, 2 * m) for m in range(1, groups)]
     others = [swap(x, "exp", n_exp, 1) for x in held]
+    grad_proj, side = call(
+        functools.partial(settle_kernel, piece),
+        "settle",
+        6,
+        [("vmem", x) for x in held],
+        [("hbm", (n_exp, n, width), f32), ("vmem", (n_exp, piece, half), f32)],
+        [pltpu.VMEM((groups, n, width), f32), dma((groups,))],
+    )
     grad_proj, grad_slots = call(
         functools.partial(last_kernel, piece),
         "last",
         6,
-        [("vmem", x) for x in (*held, *others)] + [("free", unit_t32), ("free", slot_norm)],
+        [("vmem", x) for x in (side, *others)]
+        + [("free", unit_t32), ("free", slot_norm), ("hbm", grad_proj)],
         [("hbm", (n_exp, n, width), f32), ("hbm", (slots, width), f32)],
         [
-            pltpu.VMEM((n_exp, n, width), f32),
             pltpu.VMEM((n_exp, piece, half), f32),
+            pltpu.VMEM((groups, n, width), f32),
             pltpu.VMEM((slots, width), f32),
-            dma((n_exp + 1,)),
+            dma((groups + 1,)),
         ],
+        {groups + 3: 0},
     )
     return (
         grad_context.reshape(images, tokens, width),

time: 108 us -> 107 us (level)
  Pallas kernels: 36.9 us -> 33.9 us
  waiting for transfers between devices: 26.4 us -> 28.8 us
    pallas_call x1 -> x0, Pallas kernels: 7.39 us -> none  [shards(): pl.pallas_call(grads_kernel, grid=(owned, cuts), in_specs=[pl.BlockSpec((...]
    pallas_call x15 -> x16, Pallas kernels: 29.5 us -> 33.9 us  [call(): pl.pallas_call(kernel, in_specs=[pl.BlockSpec(memory_space=spaces[where])...]
    all_to_all x1, waiting for transfers between devices: 1.99 us -> 5.29 us  [shards(): lax.all_to_all(back, ('img', 'exp'), 0, 0, axis_index_groups=groups, tile...]
  transfers between devices with their start and end apart: 23 -> 23, of which waited for: 15 -> 17; matrix products, arithmetic and copies ran while one was open for 3% -> 3% of each run, Pallas kernels for 22% -> 20%
where the time goes in v6:
time: 107 us; the launch traced here: 106 us
  Pallas kernels  33.9 us (32%)
  waiting for transfers between devices  28.8 us (27%)
  starting transfers between devices  26 us (24%)
  blocking collectives  13.2 us (12%)
  other arithmetic  3.24 us (3%)
    pallas_call x16, Pallas kernels, call(): pl.pallas_call(kernel, in_specs=[pl.BlockSpec(memory_space=spaces[where])...  33.9 us
    ppermute x22, waiting for transfers between devices, swap(): return lax.ppermute(x, axis, [(i, i ^ bit) for i in range(size)])  23.5 us
    ppermute x22, starting transfers between devices, swap(): return lax.ppermute(x, axis, [(i, i ^ bit) for i in range(size)])  22.2 us
    all_to_all x1, blocking collectives, shards(): got = lax.all_to_all(out.reshape(n_exp, -1, width), 'exp', 0, 0, tiled=True)  13.2 us
    all_to_all x1, waiting for transfers between devices, shards(): lax.all_to_all(back, ('img', 'exp'), 0, 0, axis_index_groups=groups, tile...  5.29 us
    all_to_all x1, starting transfers between devices, shards(): lax.all_to_all(back, ('img', 'exp'), 0, 0, axis_index_groups=groups, tile...  3.82 us
  transfers between devices with their start and end apart: 23, of which 17 were waited for; matrix products, arithmetic and copies ran while one was open for 3% of the time, Pallas kernels for 20%

profile of v6, /device:TPU:0, one launch (start us, length us, event | category | flops | bytes accessed | tf_op | source)
XLA Modules:
  0.0 106.2 jit_solution(6768547559314442714)
XLA Ops:
  0.6 3.0 %collective-permute-start.1 = (bf16[256,1024]{1,0:T(8,128)(2,1)}, bf16[256,1024]{1,0:T(8,128)(2,1)S(1)}, u32[]{:S(2)}, u32[]{:S(2)}) collective-permute-start(bf16[256,1024]{1,0:T(8,128)(2,1)} %own_hbm.3), channel_id=1, source_target_pairs={{0,16},{8,24},{16,0},{24,8},{1,17},{9,25},{17,1},{25,9},{2,18},{10... | collective-permute-start | bytes 1572872 | tf_op jit(solution)/shard_map/ppermute | solution.py:46
  7.0 4.4 %prepare.1 = (bf16[512,512]{1,0:T(8,128)(2,1)}, bf16[512,512]{1,0:T(8,128)(2,1)}, bf16[512,512]{1,0:T(8,128)(2,1)}, bf16[512,512]{1,0:T(8,128)(2,1)}, bf16[256,1...) custom-call(bf16[512,1024]{1,0:T(8,128)(2,1)} %bitcast.27, ...), custom_call_target="tpu_custom_call" | custom-call | tf_op jit(solution)/shard_map/prepare/pallas_call | solution.py:24
  11.4 4.3 %collective-permute-done.1.block = bf16[256,1024]{1,0:T(8,128)(2,1)S(1)} collective-permute-done((bf16[256,1024]{1,0:T(8,128)(2,1)}, bf16[256,1024]{1,0:T(8,128)(2,1)S(1)}, u32[]{:S(2)}, u32[]{:S(2)}) %collective-permute-start.1) | collective-permute-done | bytes 524320 | tf_op jit(solution)/shard_map/ppermute | solution.py:46
  17.7 2.5 %forward.1 = (bf16[256,1024]{1,0:T(8,128)(2,1)}, bf16[512,1024]{1,0:T(8,128)(2,1)S(1)}, f32[512,16]{1,0:T(8,128)S(1)}, bf16[64,1024]{1,0:T(8,128)(2,1)S(1)}) custom-call(bf16[512,1024]{1,0:T(8,128)(2,1)S(1)} %get-tuple-element.79.ctx, f32[512,1024]{1,0:T(8,128)S(1)} %get-tuple-element.84.start, bf16[512,1024]{1,0:T(8,128)(2,1)S(1)} %get-tuple-element.85.cot, ...), custom_call_target="tpu_custom_call" | custom-call | tf_op jit(solution)/shard_map/forward/pallas_call | solution.py:24
  20.2 13.2 %all_to_all.10 = bf16[8,8,1024]{2,1,0:T(8,128)(2,1)S(1)} all-to-all(bf16[8,8,1024]{2,1,0:T(8,128)(2,1)S(1)} %bitcast.21), channel_id=1, replica_groups=mesh['img'=4,'exp'=8] {'exp'}, dimensions={0} | all-to-all | bytes 262144 | tf_op jit(solution)/shard_map/all_to_all | solution.py:510
  33.4 1.5 %collective-permute-start.3 = (bf16[64,1024]{1,0:T(8,128)(2,1)S(1)}, bf16[64,1024]{1,0:T(8,128)(2,1)S(1)}, u32[]{:S(2)}, u32[]{:S(2)}) collective-permute-start(bf16[64,1024]{1,0:T(8,128)(2,1)S(1)} %bitcast.18), channel_id=1, source_target_pairs={{0,16},{8,24},{16,0},{24,8},{1,17},{9,25},{17,1},{25,9},{2,18},{10... | collective-permute-start | bytes 393224 | tf_op jit(solution)/shard_map/ppermute | solution.py:46
  34.9 2.8 %weights.1 = (bf16[1,1024,1024]{2,1,0:T(8,128)(2,1)S(1)}, bf16[2,1024,1024]{2,1,0:T(8,128)(2,1)S(1)}) custom-call(bf16[2,1024,1024]{2,1,0:T(8,128)(2,1)} %refs_0_, bf16[2,1024,1024]{2,1,0:T(8,128)(2,1)} %refs_1_), custom_call_target="tpu_custom_call" | custom-call | tf_op jit(solution)/shard_map/weights/pallas_call | solution.py:24
  39.9 4.9 %experts.1 = (bf16[4,64,1024]{2,1,0:T(8,128)(2,1)}, bf16[2,64,1024]{2,1,0:T(8,128)(2,1)}, bf16[2,64,1024]{2,1,0:T(8,128)(2,1)}, bf16[128,1024]{1,0:T(8,128)(2,1)S(1)}, bf16[128,1024]{1,0:T(8,128)(2,1)S(1)}) custom-call(bf16[64,1024]{1,0:T(8,128)(2,1)S(1)} %bitcast.20, bf16[64,1024]{1,0:T(8,128)(2,1)S(1)} %collective-permute-done.4.near, ...), custom_call_target="tpu_custom_call" | custom-call | tf_op jit(solution)/shard_map/experts/pallas_call | solution.py:24
  47.2 3.8 %all-to-all-start.1 = ((bf16[16,8,1024]{2,1,0:T(8,128)(2,1)}), bf16[16,8,1024]{2,1,0:T(8,128)(2,1)S(1)}, u32[]{:S(2)}, u32[]{:S(2)}) async-start(bf16[16,8,1024]{2,1,0:T(8,128)(2,1)} %bitcast.6), calls=%async_computation.1 | async-start | bytes 524288 | tf_op jit(solution)/shard_map/all_to_all | solution.py:553
  51.0 5.1 %expert_grads.1 = (bf16[2,1024,1024]{2,1,0:T(8,128)(2,1)}, bf16[2,1024,1024]{2,1,0:T(8,128)(2,1)}, bf16[512,512]{1,0:T(8,128)(2,1)S(1)}, bf16[512,1024]{1,0:T(8,128)(2,1)S(1)}) custom-call(bf16[4,64,1024]{2,1,0:T(8,128)(2,1)} %get-tuple-element.102.rows_hbm, bf16[2,64,1024]{2,1,0:T(8,128)(2,1)} %get-tuple-element.103.act_hbm, ...), custom_call_target="tpu_custom_call" | custom-call | tf_op jit(solution)/shard_map/expert_grads/pallas_call | solution.py:24
  56.1 5.3 %all-to-all-done.1 = bf16[16,8,1024]{2,1,0:T(8,128)(2,1)S(1)} async-done(((bf16[16,8,1024]{2,1,0:T(8,128)(2,1)}), bf16[16,8,1024]{2,1,0:T(8,128)(2,1)S(1)}, u32[]{:S(2)}, u32[]{:S(2)}) %all-to-all-start.1) | async-done | bytes 262176 | tf_op jit(solution)/shard_map/all_to_all | solution.py:553
  61.3 3.1 %backward.1 = (bf16[512,1024]{1,0:T(8,128)(2,1)}, bf16[1088,512]{1,0:T(8,128)(2,1)S(1)}, f32[32,512]{1,0:T(8,128)S(1)}) custom-call(bf16[2,64,1024]{2,1,0:T(8,128)(2,1)S(1)} %bitcast.17, bf16[64,64]{1,0:T(8,128)(2,1)S(1)} %fusion.3.perm, bf16[16,1024]{1,0:T(8,128)(2,1)S(1)} %get-tuple-element.86.unit.unit_t, ...), custom_call_target="tpu_custom_call" | custom-call | tf_op jit(solution)/shard_map/backward/pallas_call | solution.py:24
  64.5 2.3 %keep.1 = bf16[1024,512]{1,0:T(8,128)(2,1)S(1)} custom-call(bf16[512,512]{1,0:T(8,128)(2,1)} %get-tuple-element.77.left_p_hbm, bf16[512,512]{1,0:T(8,128)(2,1)} %get-tuple-element.78.left_q_hbm, bf16[512,1024]{1,0:T(8,128)(2,1)} %get-tuple-element.116.grad_hbm), custom_call_target="tpu_custom_call" | custom-call | tf_op jit(solution)/shard_map/keep/pallas_call | solution.py:24
  69.2 5.0 %context.1 = bf16[512,1024]{1,0:T(8,128)(2,1)} custom-call(bf16[512,1024]{1,0:T(8,128)(2,1)} %get-tuple-element.116.grad_hbm, bf16[256,1024]{1,0:T(8,128)(2,1)} %own_hbm.3, bf16[256,1024]{1,0:T(8,128)(2,1)} %get-tuple-element.121.near_hbm, bf16[256,1024]{1,0:T(8,128)(2,1)} %get-tuple-element.122.far_hbm, bf16[256,1024]{1,0:T(8,128)(2,1)} %get-tuple-element.123.far_near_hbm), custom_call_target="tpu_custom_call" | custom-call | tf_op jit(solution)/shard_map/context/pallas_call | solution.py:24
  74.3 2.1 %collective-permute-done.8.got_p = bf16[256,512]{1,0:T(8,128)(2,1)S(1)} collective-permute-done((bf16[256,512]{1,0:T(8,128)(2,1)S(1)}, bf16[256,512]{1,0:T(8,128)(2,1)S(1)}, u32[]{:S(2)}, u32[]{:S(2)}) %collective-permute-start.8) | collective-permute-done | bytes 262176 | tf_op jit(solution)/shard_map/ppermute | solution.py:46
  78.9 3.9 %collective-permute-done.10.got_p = bf16[128,512]{1,0:T(8,128)(2,1)S(1)} collective-permute-done((bf16[128,512]{1,0:T(8,128)(2,1)S(1)}, bf16[128,512]{1,0:T(8,128)(2,1)S(1)}, u32[]{:S(2)}, u32[]{:S(2)}) %collective-permute-start.10) | collective-permute-done | bytes 131104 | tf_op jit(solution)/shard_map/ppermute | solution.py:46
  83.8 1.3 %collective-permute-start.13 = (bf16[72,512]{1,0:T(8,128)(2,1)S(1)}, bf16[72,512]{1,0:T(8,128)(2,1)S(1)}, u32[]{:S(2)}, u32[]{:S(2)}) collective-permute-start(bf16[72,512]{1,0:T(8,128)(2,1)S(1)} %get-tuple-element.138), channel_id=1, source_target_pairs={{0,4},{1,5},{2,6},{3,7},{4,0},{5,1},{6,2},{7,3},{8,12},{9,13},{10,... | collective-permute-start | bytes 221192 | tf_op jit(solution)/shard_map/ppermute | solution.py:46
  85.0 2.4 %collective-permute-start.14 = (bf16[72,512]{1,0:T(8,128)(2,1)S(1)}, bf16[72,512]{1,0:T(8,128)(2,1)S(1)}, u32[]{:S(2)}, u32[]{:S(2)}) collective-permute-start(bf16[72,512]{1,0:T(8,128)(2,1)S(1)} %get-tuple-element.139), channel_id=1, source_target_pairs={{0,6},{1,7},{2,4},{3,5},{4,2},{5,3},{6,0},{7,1},{8,14},{9,15},{10,... | collective-permute-start | bytes 221192 | tf_op jit(solution)/shard_map/ppermute | solution.py:46
  87.6 2.3 %collective-permute-done.13.refs_1_ = bf16[72,512]{1,0:T(8,128)(2,1)S(1)} collective-permute-done((bf16[72,512]{1,0:T(8,128)(2,1)S(1)}, bf16[72,512]{1,0:T(8,128)(2,1)S(1)}, u32[]{:S(2)}, u32[]{:S(2)}) %collective-permute-start.13) | collective-permute-done | bytes 73760 | tf_op jit(solution)/shard_map/ppermute | solution.py:46
  89.9 1.5 %collective-permute-done.14.refs_2_ = bf16[72,512]{1,0:T(8,128)(2,1)S(1)} collective-permute-done((bf16[72,512]{1,0:T(8,128)(2,1)S(1)}, bf16[72,512]{1,0:T(8,128)(2,1)S(1)}, u32[]{:S(2)}, u32[]{:S(2)}) %collective-permute-start.14) | collective-permute-done | bytes 73760 | tf_op jit(solution)/shard_map/ppermute | solution.py:46
  92.2 2.5 %collective-permute-start.16 = (bf16[72,512]{1,0:T(8,128)(2,1)S(1)}, bf16[72,512]{1,0:T(8,128)(2,1)S(1)}, u32[]{:S(2)}, u32[]{:S(2)}) collective-permute-start(bf16[72,512]{1,0:T(8,128)(2,1)S(1)} %fourth.1.refs_0_), channel_id=1, source_target_pairs={{0,4},{1,5},{2,6},{3,7},{4,0},{5,1},{6,2},{7,3},{8,12},{9,13},{10,... | collective-permute-start | bytes 221192 | tf_op jit(solution)/shard_map/ppermute | solution.py:46
  94.6 1.2 %collective-permute-start.17 = (bf16[72,512]{1,0:T(8,128)(2,1)S(1)}, bf16[72,512]{1,0:T(8,128)(2,1)S(1)}, u32[]{:S(2)}, u32[]{:S(2)}) collective-permute-start(bf16[72,512]{1,0:T(8,128)(2,1)S(1)} %fourth.1.refs_0_), channel_id=1, source_target_pairs={{0,6},{1,7},{2,4},{3,5},{4,2},{5,3},{6,0},{7,1},{8,14},{9,15},{10,... | collective-permute-start | bytes 221192 | tf_op jit(solution)/shard_map/ppermute | solution.py:46
  99.0 1.8 %collective-permute-done.17.refs_3_ = bf16[72,512]{1,0:T(8,128)(2,1)S(1)} collective-permute-done((bf16[72,512]{1,0:T(8,128)(2,1)S(1)}, bf16[72,512]{1,0:T(8,128)(2,1)S(1)}, u32[]{:S(2)}, u32[]{:S(2)}) %collective-permute-start.17) | collective-permute-done | bytes 73760 | tf_op jit(solution)/shard_map/ppermute | solution.py:46
  102.8 2.3 %collective-permute-done.21.refs_3_ = bf16[72,512]{1,0:T(8,128)(2,1)S(1)} collective-permute-done((bf16[72,512]{1,0:T(8,128)(2,1)S(1)}, bf16[72,512]{1,0:T(8,128)(2,1)S(1)}, u32[]{:S(2)}, u32[]{:S(2)}) %collective-permute-start.21) | collective-permute-done | bytes 73760 | tf_op jit(solution)/shard_map/ppermute | solution.py:46
  (45 shorter events, 22.7 us)
Async XLA Ops:
  0.6 15.1 %collective-permute-start.1 = (bf16[256,1024]{1,0:T(8,128)(2,1)}, bf16[256,1024]{1,0:T(8,128)(2,1)S(1)}, u32[]{:S(2)}, u32[]{:S(2)}) collective-permute-start(bf16[256,1024]{1,0:T(8,128)(2,1)} %own_hbm.3), channel_id=1, source_target_pairs={{0,16},{8,24},{16,0},{24,8},{1,17},{9,25},{17,1},{25,9},{2,18},{10... | collective-permute-start | bytes 1572872 | tf_op jit(solution)/shard_map/ppermute | solution.py:46
  4.4 2.6 %collective-permute-start = (bf16[256,1024]{1,0:T(8,128)(2,1)}, bf16[256,1024]{1,0:T(8,128)(2,1)S(1)}, u32[]{:S(2)}, u32[]{:S(2)}) collective-permute-start(bf16[256,1024]{1,0:T(8,128)(2,1)} %own_hbm.3), channel_id=1, source_target_pairs={{0,8},{8,0},{16,24},{24,16},{1,9},{9,1},{17,25},{25,17},{2,10},{10... | collective-permute-start | bytes 1572872 | tf_op jit(solution)/shard_map/ppermute | solution.py:46
  15.8 1.9 %collective-permute-start.2 = (bf16[256,1024]{1,0:T(8,128)(2,1)S(1)}, bf16[256,1024]{1,0:T(8,128)(2,1)S(1)}, u32[]{:S(2)}, u32[]{:S(2)}) collective-permute-start(bf16[256,1024]{1,0:T(8,128)(2,1)S(1)} %collective-permute-done.1.block), channel_id=1, source_target_pairs={{0,8},{8,0},{16,24},{24,16},{1,9},{9,1},{17,25},{25,17},{2,10},{10... | collective-permute-start | bytes 1572872 | tf_op jit(solution)/shard_map/ppermute | solution.py:46
  33.4 5.0 %collective-permute-start.3 = (bf16[64,1024]{1,0:T(8,128)(2,1)S(1)}, bf16[64,1024]{1,0:T(8,128)(2,1)S(1)}, u32[]{:S(2)}, u32[]{:S(2)}) collective-permute-start(bf16[64,1024]{1,0:T(8,128)(2,1)S(1)} %bitcast.18), channel_id=1, source_target_pairs={{0,16},{8,24},{16,0},{24,8},{1,17},{9,25},{17,1},{25,9},{2,18},{10... | collective-permute-start | bytes 393224 | tf_op jit(solution)/shard_map/ppermute | solution.py:46
  38.3 1.3 %collective-permute-start.4 = (bf16[64,1024]{1,0:T(8,128)(2,1)S(1)}, bf16[64,1024]{1,0:T(8,128)(2,1)S(1)}, u32[]{:S(2)}, u32[]{:S(2)}) collective-permute-start(bf16[64,1024]{1,0:T(8,128)(2,1)S(1)} %bitcast.19), channel_id=1, source_target_pairs={{0,8},{8,0},{16,24},{24,16},{1,9},{9,1},{17,25},{25,17},{2,10},{10... | collective-permute-start | bytes 393224 | tf_op jit(solution)/shard_map/ppermute | solution.py:46
  38.4 1.5 %collective-permute-start.5 = (bf16[64,1024]{1,0:T(8,128)(2,1)S(1)}, bf16[64,1024]{1,0:T(8,128)(2,1)S(1)}, u32[]{:S(2)}, u32[]{:S(2)}) collective-permute-start(bf16[64,1024]{1,0:T(8,128)(2,1)S(1)} %collective-permute-done.3.across), channel_id=1, source_target_pairs={{0,8},{8,0},{16,24},{24,16},{1,9},{9,1},{17,25},{25,17},{2,10},{10... | collective-permute-start | bytes 393224 | tf_op jit(solution)/shard_map/ppermute | solution.py:46
  44.8 1.6 %collective-permute-start.6 = (bf16[128,1024]{1,0:T(8,128)(2,1)S(1)}, bf16[128,1024]{1,0:T(8,128)(2,1)S(1)}, u32[]{:S(2)}, u32[]{:S(2)}) collective-permute-start(bf16[128,1024]{1,0:T(8,128)(2,1)S(1)} %get-tuple-element.101), channel_id=1, source_target_pairs={{0,8},{8,0},{16,24},{24,16},{1,9},{9,1},{17,25},{25,17},{2,10},{10... | collective-permute-start | bytes 786440 | tf_op jit(solution)/shard_map/ppermute | solution.py:46
  47.2 14.2 %all-to-all-start.1 = ((bf16[16,8,1024]{2,1,0:T(8,128)(2,1)}), bf16[16,8,1024]{2,1,0:T(8,128)(2,1)S(1)}, u32[]{:S(2)}, u32[]{:S(2)}) async-start(bf16[16,8,1024]{2,1,0:T(8,128)(2,1)} %bitcast.6), calls=%async_computation.1 | async-start | bytes 524288 | tf_op jit(solution)/shard_map/all_to_all | solution.py:553
  64.4 2.8 %collective-permute-start.7 = (bf16[1088,512]{1,0:T(8,128)(2,1)S(1)}, bf16[1088,512]{1,0:T(8,128)(2,1)S(1)}, u32[]{:S(2)}, u32[]{:S(2)}) collective-permute-start(bf16[1088,512]{1,0:T(8,128)(2,1)S(1)} %get-tuple-element.118), channel_id=1, source_target_pairs={{0,8},{8,0},{16,24},{24,16},{1,9},{9,1},{17,25},{25,17},{2,10},{10... | collective-permute-start | bytes 3342344 | tf_op jit(solution)/shard_map/ppermute | solution.py:46
  67.5 9.1 %collective-permute-start.9 = (bf16[288,512]{1,0:T(8,128)(2,1)S(1)}, bf16[288,512]{1,0:T(8,128)(2,1)S(1)}, u32[]{:S(2)}, u32[]{:S(2)}) collective-permute-start(bf16[288,512]{1,0:T(8,128)(2,1)S(1)} %get-tuple-element.120), channel_id=1, source_target_pairs={{0,1},{1,0},{2,3},{3,2},{4,5},{5,4},{6,7},{7,6},{8,9},{9,8},{10,11... | collective-permute-start | bytes 884744 | tf_op jit(solution)/shard_map/ppermute | solution.py:46
  68.3 8.1 %collective-permute-start.8 = (bf16[256,512]{1,0:T(8,128)(2,1)S(1)}, bf16[256,512]{1,0:T(8,128)(2,1)S(1)}, u32[]{:S(2)}, u32[]{:S(2)}) collective-permute-start(bf16[256,512]{1,0:T(8,128)(2,1)S(1)} %get-tuple-element.119), channel_id=1, source_target_pairs={{0,16},{8,24},{16,0},{24,8},{1,17},{9,25},{17,1},{25,9},{2,18},{10... | collective-permute-start | bytes 786440 | tf_op jit(solution)/shard_map/ppermute | solution.py:46
  76.8 6.1 %collective-permute-start.11 = (bf16[160,512]{1,0:T(8,128)(2,1)S(1)}, bf16[160,512]{1,0:T(8,128)(2,1)S(1)}, u32[]{:S(2)}, u32[]{:S(2)}) collective-permute-start(bf16[160,512]{1,0:T(8,128)(2,1)S(1)} %get-tuple-element.134), channel_id=1, source_target_pairs={{0,16},{8,24},{16,0},{24,8},{1,17},{9,25},{17,1},{25,9},{2,18},{10... | collective-permute-start | bytes 491528 | tf_op jit(solution)/shard_map/ppermute | solution.py:46
  77.9 5.0 %collective-permute-start.10 = (bf16[128,512]{1,0:T(8,128)(2,1)S(1)}, bf16[128,512]{1,0:T(8,128)(2,1)S(1)}, u32[]{:S(2)}, u32[]{:S(2)}) collective-permute-start(bf16[128,512]{1,0:T(8,128)(2,1)S(1)} %get-tuple-element.133), channel_id=1, source_target_pairs={{0,1},{1,0},{2,3},{3,2},{4,5},{5,4},{6,7},{7,6},{8,9},{9,8},{10,11... | collective-permute-start | bytes 393224 | tf_op jit(solution)/shard_map/ppermute | solution.py:46
  82.9 4.7 %collective-permute-start.12 = (bf16[72,512]{1,0:T(8,128)(2,1)S(1)}, bf16[72,512]{1,0:T(8,128)(2,1)S(1)}, u32[]{:S(2)}, u32[]{:S(2)}) collective-permute-start(bf16[72,512]{1,0:T(8,128)(2,1)S(1)} %get-tuple-element.137), channel_id=1, source_target_pairs={{0,2},{1,3},{2,0},{3,1},{4,6},{5,7},{6,4},{7,5},{8,10},{9,11},{10,... | collective-permute-start | bytes 221192 | tf_op jit(solution)/shard_map/ppermute | solution.py:46
  83.8 6.1 %collective-permute-start.13 = (bf16[72,512]{1,0:T(8,128)(2,1)S(1)}, bf16[72,512]{1,0:T(8,128)(2,1)S(1)}, u32[]{:S(2)}, u32[]{:S(2)}) collective-permute-start(bf16[72,512]{1,0:T(8,128)(2,1)S(1)} %get-tuple-element.138), channel_id=1, source_target_pairs={{0,4},{1,5},{2,6},{3,7},{4,0},{5,1},{6,2},{7,3},{8,12},{9,13},{10,... | collective-permute-start | bytes 221192 | tf_op jit(solution)/shard_map/ppermute | solution.py:46
  85.0 6.3 %collective-permute-start.14 = (bf16[72,512]{1,0:T(8,128)(2,1)S(1)}, bf16[72,512]{1,0:T(8,128)(2,1)S(1)}, u32[]{:S(2)}, u32[]{:S(2)}) collective-permute-start(bf16[72,512]{1,0:T(8,128)(2,1)S(1)} %get-tuple-element.139), channel_id=1, source_target_pairs={{0,6},{1,7},{2,4},{3,5},{4,2},{5,3},{6,0},{7,1},{8,14},{9,15},{10,... | collective-permute-start | bytes 221192 | tf_op jit(solution)/shard_map/ppermute | solution.py:46
  91.4 5.5 %collective-permute-start.15 = (bf16[72,512]{1,0:T(8,128)(2,1)S(1)}, bf16[72,512]{1,0:T(8,128)(2,1)S(1)}, u32[]{:S(2)}, u32[]{:S(2)}) collective-permute-start(bf16[72,512]{1,0:T(8,128)(2,1)S(1)} %fourth.1.refs_0_), channel_id=1, source_target_pairs={{0,2},{1,3},{2,0},{3,1},{4,6},{5,7},{6,4},{7,5},{8,10},{9,11},{10,... | collective-permute-start | bytes 221192 | tf_op jit(solution)/shard_map/ppermute | solution.py:46
  92.2 6.1 %collective-permute-start.16 = (bf16[72,512]{1,0:T(8,128)(2,1)S(1)}, bf16[72,512]{1,0:T(8,128)(2,1)S(1)}, u32[]{:S(2)}, u32[]{:S(2)}) collective-permute-start(bf16[72,512]{1,0:T(8,128)(2,1)S(1)} %fourth.1.refs_0_), channel_id=1, source_target_pairs={{0,4},{1,5},{2,6},{3,7},{4,0},{5,1},{6,2},{7,3},{8,12},{9,13},{10,... | collective-permute-start | bytes 221192 | tf_op jit(solution)/shard_map/ppermute | solution.py:46
  94.6 6.2 %collective-permute-start.17 = (bf16[72,512]{1,0:T(8,128)(2,1)S(1)}, bf16[72,512]{1,0:T(8,128)(2,1)S(1)}, u32[]{:S(2)}, u32[]{:S(2)}) collective-permute-start(bf16[72,512]{1,0:T(8,128)(2,1)S(1)} %fourth.1.refs_0_), channel_id=1, source_target_pairs={{0,6},{1,7},{2,4},{3,5},{4,2},{5,3},{6,0},{7,1},{8,14},{9,15},{10,... | collective-permute-start | bytes 221192 | tf_op jit(solution)/shard_map/ppermute | solution.py:46
  95.8 7.0 %collective-permute-start.18 = (bf16[72,512]{1,0:T(8,128)(2,1)S(1)}, bf16[72,512]{1,0:T(8,128)(2,1)S(1)}, u32[]{:S(2)}, u32[]{:S(2)}) collective-permute-start(bf16[72,512]{1,0:T(8,128)(2,1)S(1)} %fourth.1.refs_0_), channel_id=1, source_target_pairs={{0,1},{1,0},{2,3},{3,2},{4,5},{5,4},{6,7},{7,6},{8,9},{9,8},{10,11... | collective-permute-start | bytes 221192 | tf_op jit(solution)/shard_map/ppermute | solution.py:46
  96.9 5.9 %collective-permute-start.19 = (bf16[72,512]{1,0:T(8,128)(2,1)S(1)}, bf16[72,512]{1,0:T(8,128)(2,1)S(1)}, u32[]{:S(2)}, u32[]{:S(2)}) collective-permute-start(bf16[72,512]{1,0:T(8,128)(2,1)S(1)} %collective-permute-done.15.refs_1_), channel_id=1, source_target_pairs={{0,1},{1,0},{2,3},{3,2},{4,5},{5,4},{6,7},{7,6},{8,9},{9,8},{10,11... | collective-permute-start | bytes 221192 | tf_op jit(solution)/shard_map/ppermute | solution.py:46
  98.3 4.5 %collective-permute-start.20 = (bf16[72,512]{1,0:T(8,128)(2,1)S(1)}, bf16[72,512]{1,0:T(8,128)(2,1)S(1)}, u32[]{:S(2)}, u32[]{:S(2)}) collective-permute-start(bf16[72,512]{1,0:T(8,128)(2,1)S(1)} %collective-permute-done.16.refs_2_), channel_id=1, source_target_pairs={{0,1},{1,0},{2,3},{3,2},{4,5},{5,4},{6,7},{7,6},{8,9},{9,8},{10,11... | collective-permute-start | bytes 221192 | tf_op jit(solution)/shard_map/ppermute | solution.py:46
  100.8 4.4 %collective-permute-start.21 = (bf16[72,512]{1,0:T(8,128)(2,1)S(1)}, bf16[72,512]{1,0:T(8,128)(2,1)S(1)}, u32[]{:S(2)}, u32[]{:S(2)}) collective-permute-start(bf16[72,512]{1,0:T(8,128)(2,1)S(1)} %collective-permute-done.17.refs_3_), channel_id=1, source_target_pairs={{0,1},{1,0},{2,3},{3,2},{4,5},{5,4},{6,7},{7,6},{8,9},{9,8},{10,11... | collective-permute-start | bytes 221192 | tf_op jit(solution)/shard_map/ppermute | solution.py:46

commit v7 on v6

--- a/solution.py
+++ b/solution.py
@@ -239,16 +239,18 @@
 
 
 def backward_kernel(images, factor, back, perm, unit_t, *refs):
-    stream, expo, cot, left_p, left_q_hbm, grad_hbm, send, side_out, left_q, grad_v, sems = refs
+    stream, expo, cot, left_p, left_q_hbm, *keep_hbm = refs[:7]
+    grad_v, send_p, send_q, side_out, *keep_left = refs[7:13]
+    left_q, sems = refs[13:]
     mover = Mover(sems)
     get = mover.start(left_q_hbm, left_q)
+    gets = [mover.start(*pair) for pair in zip(keep_hbm, keep_left, strict=True)]
     tokens = cot.shape[0] // images
     slots = unit_t.shape[0]
-    half = send.shape[1]
+    half = send_p.shape[1]
     total = tree([back[r].astype(f32) for r in range(back.shape[0])]).astype(bf16)
     parts = dot(perm[...], total).astype(bf16)
     unit_sum = 0.0
-    out = []
     for b in range(images):
         at = pl.ds(b * tokens, tokens)
         slot_out = parts[b * slots : (b + 1) * slots]
@@ -273,51 +275,43 @@
             grad_normed - normed32 * jnp.mean(normed32 * grad_normed, axis=-1, keepdims=True)
         )
         grad_v[at, :] = grad.astype(bf16)
-        out.append(mover.start(grad_v.at[at, :], grad_hbm.at[at, :]))
     n = left_p.shape[0]
-    send[:n, :] = dot(left_p[...], grad_v[:, :half]).astype(bf16)
+    send_p[...] = dot(left_p[...], grad_v[:, :half]).astype(bf16)
     get.wait()
-    send[n : 2 * n, :] = dot(left_q[...], grad_v[:, half:]).astype(bf16)
+    send_q[:n, :] = dot(left_q[...], grad_v[:, half:]).astype(bf16)
     unit_sum = factor * unit_sum
     side = high_low(jnp.concatenate([unit_sum[:, :half], unit_sum[:, half:]], axis=0))
-    send[2 * n :, :] = side.astype(bf16)
+    send_q[n:, :] = side.astype(bf16)
+    for get in gets:
+        get.wait()
     side_out[...] = joined(side)
-    for copy in out:
-        copy.wait()
-
-
-def keep_kernel(left_p_hbm, left_q_hbm, grad_hbm, out, left_p, left_q, grad, sems):
-    mover = Mover(sems)
-    gets = [
-        mover.start(grad_hbm, grad),
-        mover.start(left_p_hbm, left_p),
-        mover.start(left_q_hbm, left_q),
-    ]
-    half = out.shape[1]
-    n = left_p.shape[0]
-    gets[0].wait()
-    gets[1].wait()
-    out[:n, :] = dot(left_p[...], grad[:, :half]).astype(bf16)
-    gets[2].wait()
-    out[n:, :] = dot(left_q[...], grad[:, half:]).astype(bf16)
+
+
+def keep_kernel(left_p, left_q, grad, out_p, out_q):
+    half = out_p.shape[1]
+    out_p[...] = dot(left_p[...], grad[:, :half]).astype(bf16)
+    out_q[...] = dot(left_q[...], grad[:, half:]).astype(bf16)
 
 
 def chosen(bit, low, high):
     return jnp.where(bit == 0, low, high)
 
 
-def first_kernel(keep, side, got, p_out, q_out, side_out, send_p, send_q):
-    n = keep.shape[0] // 2
-    p0, p1 = halves(keep[:n, :].astype(f32) + got[:n, :].astype(f32))
-    q0, q1 = halves(keep[n:, :].astype(f32) + got[n : 2 * n, :].astype(f32))
-    low, high = halves(side[...] + joined(got[2 * n :, :].astype(f32)))
+def first_p_kernel(keep, got, out, send):
+    kept, sent = halves(keep[...].astype(f32) + got[...].astype(f32))
+    out[...], send[...] = kept.astype(bf16), sent.astype(bf16)
+
+
+def first_q_kernel(keep, side, got, out, side_out, send):
+    n = keep.shape[0]
+    got = got[...].astype(f32)
+    kept, sent = halves(keep[...].astype(f32) + got[:n])
+    low, high = halves(side[...] + joined(got[n:]))
     bit = lax.axis_index("exp") & 1
     side_out[...] = chosen(bit, low, high)
-    p_out[...] = p0.astype(bf16)
-    q_out[...] = q0.astype(bf16)
-    send_p[...] = p1.astype(bf16)
+    out[...] = kept.astype(bf16)
     other = high_low(chosen(bit, high, low))
-    send_q[...] = jnp.concatenate([q1, other], axis=0).astype(bf16)
+    send[...] = jnp.concatenate([sent, other], axis=0).astype(bf16)
 
 
 def second_kernel(p_in, q_in, side, got_p, got_q, p_out, q_out, side_out, send_p, send_q):
@@ -372,14 +366,13 @@
     own[...] = total.astype(bf16)
 
 
-def context_kernel(grad_hbm, own_hbm, near_hbm, far_hbm, far_near_hbm, out_hbm, grad, blocks, out, sems):
+def context_kernel(grad, own_hbm, near_hbm, far_hbm, far_near_hbm, *refs):
+    out_hbm, grad_hbm, blocks, out, sems = refs
     mover = Mover(sems)
     deep = blocks.shape[1]
-    get = mover.start(grad_hbm, grad)
     sources = (own_hbm, near_hbm, far_hbm, far_near_hbm)
     gets = [mover.start(source, blocks.at[r]) for r, source in enumerate(sources)]
-    get.wait()
-    puts = []
+    puts = [mover.start(grad, grad_hbm)]
     for r, get in enumerate(gets):
         get.wait()
         columns = pl.ds(pl.multiple_of((lax.axis_index("img") ^ r) * deep, deep), deep)
@@ -574,33 +567,35 @@
     )
 
     n = width // 2
-    grad_residual, send, side = call(
+    grad, send_p, send_q, side, *keep_left = call(
         functools.partial(backward_kernel, images, factor),
         "backward",
         24,
         [("vmem", back.reshape(far_img, -1, width)), ("free", perm), ("free", unit_t)]
         + [("vmem", x) for x in (*kept_stats, cot, left_p)]
-        + [("hbm", send_left[1])],
+        + [("hbm", x) for x in (send_left[1], *keep_left)],
         [
-            ("hbm", (rows, width), bf16),
-            ("vmem", (2 * n + 4 * slots, half), bf16),
+            ("vmem", (rows, width), bf16),
+            ("vmem", (n, half), bf16),
+            ("vmem", (n + 4 * slots, half), bf16),
             ("vmem", (2 * slots, half), f32),
+            ("vmem", left, bf16),
+            ("vmem", left, bf16),
         ],
         [
             pltpu.VMEM(left, bf16),
-            pltpu.VMEM((rows, width), bf16),
-            dma((1 + images,)),
+            dma((3,)),
         ],
     )
 
-    got = swap(send, "img", n_img, 1)
-    (keep,) = call(
+    got_p = swap(send_p, "img", n_img, 1)
+    got_q = swap(send_q, "img", n_img, 1)
+    keep_p, keep_q = call(
         keep_kernel,
         "keep",
-        8,
-        [("hbm", x) for x in (*keep_left, grad_residual)],
-        [("vmem", (2 * n, half), bf16)],
-        [pltpu.VMEM(left, bf16), pltpu.VMEM(left, bf16), pltpu.VMEM((rows, width), bf16), dma((3,))],
+        4,
+        [("vmem", x) for x in (*keep_left, grad)],
+        [("vmem", (n, half), bf16)] * 2,
     )
 
     def after(n):
@@ -608,30 +603,35 @@
         return [*rest, ("vmem", (n, half), bf16), ("vmem", (n + 2 * slots, half), bf16)]
 
     n = n // 2
-    p, q, side, send_p, send_q = call(
-        first_kernel,
-        "first",
-        6,
-        [("vmem", keep), ("vmem", side), ("vmem", got)],
-        after(n),
+    part = ("vmem", (n, half), bf16)
+    p, send_p = call(
+        first_p_kernel, "first_p", 4, [("vmem", keep_p), ("vmem", got_p)], [part, part]
+    )
+    q, side, send_q = call(
+        first_q_kernel,
+        "first_q",
+        4,
+        [("vmem", x) for x in (keep_q, side, got_q)],
+        [part, ("vmem", (slots, half), f32), ("vmem", (n + 2 * slots, half), bf16)],
     )
     got_p = swap(send_p, "img", n_img, 2)
     got_q = swap(send_q, "exp", n_exp, 1)
     projection = (proj_weight, near_copy, far_copy, far_near_copy)
-    (grad_context,) = call(
+    grad_context, grad_residual = call(
         context_kernel,
         "context",
         12,
-        [("hbm", x) for x in (grad_residual, *projection)],
-        [("hbm", (rows, width), bf16)],
+        [("vmem", grad)] + [("hbm", x) for x in projection],
+        [("hbm", (rows, width), bf16)] * 2,
         [
-            pltpu.VMEM((rows, width), bf16),
             pltpu.VMEM((n_img,) + block, bf16),
             pltpu.VMEM((n_img, rows, deep), bf16),
-            dma((1 + 2 * n_img,)),
+            dma((2 * n_img + 1,)),
         ],
     )
-    got_p, got_q, grad_context = lax.optimization_barrier((got_p, got_q, grad_context))
+    got_p, got_q, grad_context, grad_residual = lax.optimization_barrier(
+        (got_p, got_q, grad_context, grad_residual)
+    )
     n = n // 2
     p, q, side, send_p, send_q = call(
         second_kernel, "second", 4, [("vmem", x) for x in (p, q, side, got_p, got_q)], after(n)

time: 107 us -> 106 us (level)
  Pallas kernels: 33.9 us -> 32.3 us
  starting transfers between devices: 26 us -> 27.5 us
    pallas_call x16 -> x17, Pallas kernels: 33.9 us -> 32.3 us  [call(): pl.pallas_call(kernel, in_specs=[pl.BlockSpec(memory_space=spaces[where])...]
    ppermute x22 -> x23, starting transfers between devices: 22.2 us -> 23.7 us  [swap(): return lax.ppermute(x, axis, [(i, i ^ bit) for i in range(size)])]
    ppermute x22 -> x23, waiting for transfers between devices: 23.5 us -> 22.7 us  [swap(): return lax.ppermute(x, axis, [(i, i ^ bit) for i in range(size)])]
  transfers between devices with their start and end apart: 23 -> 24, of which waited for: 17 -> 15; matrix products, arithmetic and copies ran while one was open for 3% -> 3% of each run, Pallas kernels for 20% -> 19%
where the time goes in v7:
time: 106 us; the launch traced here: 105 us
  Pallas kernels  32.3 us (30%)
  waiting for transfers between devices  28 us (26%)
  starting transfers between devices  27.5 us (26%)
  blocking collectives  13.2 us (12%)
  other arithmetic  3.24 us (3%)
    pallas_call x17, Pallas kernels, call(): pl.pallas_call(kernel, in_specs=[pl.BlockSpec(memory_space=spaces[where])...  32.3 us
    ppermute x23, starting transfers between devices, swap(): return lax.ppermute(x, axis, [(i, i ^ bit) for i in range(size)])  23.7 us
    ppermute x23, waiting for transfers between devices, swap(): return lax.ppermute(x, axis, [(i, i ^ bit) for i in range(size)])  22.7 us
    all_to_all x1, blocking collectives, shards(): got = lax.all_to_all(out.reshape(n_exp, -1, width), 'exp', 0, 0, tiled=True)  13.2 us
    all_to_all x1, waiting for transfers between devices, shards(): lax.all_to_all(back, ('img', 'exp'), 0, 0, axis_index_groups=groups, tile...  5.29 us
    all_to_all x1, starting transfers between devices, shards(): lax.all_to_all(back, ('img', 'exp'), 0, 0, axis_index_groups=groups, tile...  3.82 us
  transfers between devices with their start and end apart: 24, of which 15 were waited for; matrix products, arithmetic and copies ran while one was open for 3% of the time, Pallas kernels for 19%

profile of v7, /device:TPU:0, one launch (start us, length us, event | category | flops | bytes accessed | tf_op | source)
XLA Modules:
  0.0 105.3 jit_solution(2832709999369726760)
XLA Ops:
  0.6 3.0 %collective-permute-start.1 = (bf16[256,1024]{1,0:T(8,128)(2,1)}, bf16[256,1024]{1,0:T(8,128)(2,1)S(1)}, u32[]{:S(2)}, u32[]{:S(2)}) collective-permute-start(bf16[256,1024]{1,0:T(8,128)(2,1)} %own_hbm.3), channel_id=1, source_target_pairs={{0,16},{8,24},{16,0},{24,8},{1,17},{9,25},{17,1},{25,9},{2,18},{10... | collective-permute-start | bytes 1572872 | tf_op jit(solution)/shard_map/ppermute | solution.py:46
  7.0 4.4 %prepare.1 = (bf16[512,512]{1,0:T(8,128)(2,1)}, bf16[512,512]{1,0:T(8,128)(2,1)}, bf16[512,512]{1,0:T(8,128)(2,1)}, bf16[512,512]{1,0:T(8,128)(2,1)}, bf16[256,1...) custom-call(bf16[512,1024]{1,0:T(8,128)(2,1)} %bitcast.25, ...), custom_call_target="tpu_custom_call" | custom-call | tf_op jit(solution)/shard_map/prepare/pallas_call | solution.py:24
  11.4 4.3 %collective-permute-done.1.block = bf16[256,1024]{1,0:T(8,128)(2,1)S(1)} collective-permute-done((bf16[256,1024]{1,0:T(8,128)(2,1)}, bf16[256,1024]{1,0:T(8,128)(2,1)S(1)}, u32[]{:S(2)}, u32[]{:S(2)}) %collective-permute-start.1) | collective-permute-done | bytes 524320 | tf_op jit(solution)/shard_map/ppermute | solution.py:46
  17.7 2.5 %forward.1 = (bf16[256,1024]{1,0:T(8,128)(2,1)}, bf16[512,1024]{1,0:T(8,128)(2,1)S(1)}, f32[512,16]{1,0:T(8,128)S(1)}, bf16[64,1024]{1,0:T(8,128)(2,1)S(1)}) custom-call(bf16[512,1024]{1,0:T(8,128)(2,1)S(1)} %get-tuple-element.85.ctx, f32[512,1024]{1,0:T(8,128)S(1)} %get-tuple-element.90.start, bf16[512,1024]{1,0:T(8,128)(2,1)S(1)} %get-tuple-element.91.cot, ...), custom_call_target="tpu_custom_call" | custom-call | tf_op jit(solution)/shard_map/forward/pallas_call | solution.py:24
  20.2 13.2 %all_to_all.10 = bf16[8,8,1024]{2,1,0:T(8,128)(2,1)S(1)} all-to-all(bf16[8,8,1024]{2,1,0:T(8,128)(2,1)S(1)} %bitcast.21), channel_id=1, replica_groups=mesh['img'=4,'exp'=8] {'exp'}, dimensions={0} | all-to-all | bytes 262144 | tf_op jit(solution)/shard_map/all_to_all | solution.py:503
  33.4 1.5 %collective-permute-start.3 = (bf16[64,1024]{1,0:T(8,128)(2,1)S(1)}, bf16[64,1024]{1,0:T(8,128)(2,1)S(1)}, u32[]{:S(2)}, u32[]{:S(2)}) collective-permute-start(bf16[64,1024]{1,0:T(8,128)(2,1)S(1)} %bitcast.18), channel_id=1, source_target_pairs={{0,16},{8,24},{16,0},{24,8},{1,17},{9,25},{17,1},{25,9},{2,18},{10... | collective-permute-start | bytes 393224 | tf_op jit(solution)/shard_map/ppermute | solution.py:46
  34.9 2.8 %weights.1 = (bf16[1,1024,1024]{2,1,0:T(8,128)(2,1)S(1)}, bf16[2,1024,1024]{2,1,0:T(8,128)(2,1)S(1)}) custom-call(bf16[2,1024,1024]{2,1,0:T(8,128)(2,1)} %refs_0_, bf16[2,1024,1024]{2,1,0:T(8,128)(2,1)} %refs_1_), custom_call_target="tpu_custom_call" | custom-call | tf_op jit(solution)/shard_map/weights/pallas_call | solution.py:24
  39.9 4.9 %experts.1 = (bf16[4,64,1024]{2,1,0:T(8,128)(2,1)}, bf16[2,64,1024]{2,1,0:T(8,128)(2,1)}, bf16[2,64,1024]{2,1,0:T(8,128)(2,1)}, bf16[128,1024]{1,0:T(8,128)(2,1)S(1)}, bf16[128,1024]{1,0:T(8,128)(2,1)S(1)}) custom-call(bf16[64,1024]{1,0:T(8,128)(2,1)S(1)} %bitcast.20, bf16[64,1024]{1,0:T(8,128)(2,1)S(1)} %collective-permute-done.4.near, ...), custom_call_target="tpu_custom_call" | custom-call | tf_op jit(solution)/shard_map/experts/pallas_call | solution.py:24
  47.2 3.8 %all-to-all-start.1 = ((bf16[16,8,1024]{2,1,0:T(8,128)(2,1)}), bf16[16,8,1024]{2,1,0:T(8,128)(2,1)S(1)}, u32[]{:S(2)}, u32[]{:S(2)}) async-start(bf16[16,8,1024]{2,1,0:T(8,128)(2,1)} %bitcast.6), calls=%async_computation.1 | async-start | bytes 524288 | tf_op jit(solution)/shard_map/all_to_all | solution.py:546
  51.0 5.1 %expert_grads.1 = (bf16[2,1024,1024]{2,1,0:T(8,128)(2,1)}, bf16[2,1024,1024]{2,1,0:T(8,128)(2,1)}, bf16[512,512]{1,0:T(8,128)(2,1)S(1)}, bf16[512,1024]{1,0:T(8,128)(2,1)S(1)}) custom-call(bf16[4,64,1024]{2,1,0:T(8,128)(2,1)} %get-tuple-element.108.rows_hbm, bf16[2,64,1024]{2,1,0:T(8,128)(2,1)} %get-tuple-element.109.act_hbm, ...), custom_call_target="tpu_custom_call" | custom-call | tf_op jit(solution)/shard_map/expert_grads/pallas_call | solution.py:24
  56.1 5.3 %all-to-all-done.1 = bf16[16,8,1024]{2,1,0:T(8,128)(2,1)S(1)} async-done(((bf16[16,8,1024]{2,1,0:T(8,128)(2,1)}), bf16[16,8,1024]{2,1,0:T(8,128)(2,1)S(1)}, u32[]{:S(2)}, u32[]{:S(2)}) %all-to-all-start.1) | async-done | bytes 262176 | tf_op jit(solution)/shard_map/all_to_all | solution.py:546
  61.3 3.0 %backward.1 = (bf16[512,1024]{1,0:T(8,128)(2,1)S(1)}, bf16[512,512]{1,0:T(8,128)(2,1)S(1)}, bf16[576,512]{1,0:T(8,128)(2,1)S(1)}, f32[32,512]{1,0:T(8,128)S(1)},...) custom-call(bf16[2,64,1024]{2,1,0:T(8,128)(2,1)S(1)} %bitcast.17, bf16[64,64]{1,0:T(8,128)(2,1)S(1)} %fusion.3.perm, ...), custom_call_target="tpu_custom_call" | custom-call | tf_op jit(solution)/shard_map/backward/pallas_call | solution.py:24
  68.5 5.1 %context.1 = (bf16[512,1024]{1,0:T(8,128)(2,1)}, bf16[512,1024]{1,0:T(8,128)(2,1)}) custom-call(bf16[512,1024]{1,0:T(8,128)(2,1)S(1)} %get-tuple-element.126.grad, bf16[256,1024]{1,0:T(8,128)(2,1)} %own_hbm.3, bf16[256,1024]{1,0:T(8,128)(2,1)} %get-tuple-element.134.near_hbm, bf16[256,1024]{1,0:T(8,128)(2,1)} %get-tuple-element.135.far_hbm, ...), custom_call_target="tpu_custom_call" | custom-call | tf_op jit(solution)/shard_map/context/pallas_call | solution.py:24
  73.6 2.1 %collective-permute-done.8.got_p = bf16[256,512]{1,0:T(8,128)(2,1)S(1)} collective-permute-done((bf16[256,512]{1,0:T(8,128)(2,1)S(1)}, bf16[256,512]{1,0:T(8,128)(2,1)S(1)}, u32[]{:S(2)}, u32[]{:S(2)}) %collective-permute-start.8) | collective-permute-done | bytes 262176 | tf_op jit(solution)/shard_map/ppermute | solution.py:46
  78.2 3.8 %collective-permute-done.11.got_p = bf16[128,512]{1,0:T(8,128)(2,1)S(1)} collective-permute-done((bf16[128,512]{1,0:T(8,128)(2,1)S(1)}, bf16[128,512]{1,0:T(8,128)(2,1)S(1)}, u32[]{:S(2)}, u32[]{:S(2)}) %collective-permute-start.11) | collective-permute-done | bytes 131104 | tf_op jit(solution)/shard_map/ppermute | solution.py:46
  82.9 1.3 %collective-permute-start.14 = (bf16[72,512]{1,0:T(8,128)(2,1)S(1)}, bf16[72,512]{1,0:T(8,128)(2,1)S(1)}, u32[]{:S(2)}, u32[]{:S(2)}) collective-permute-start(bf16[72,512]{1,0:T(8,128)(2,1)S(1)} %get-tuple-element.154), channel_id=1, source_target_pairs={{0,4},{1,5},{2,6},{3,7},{4,0},{5,1},{6,2},{7,3},{8,12},{9,13},{10,... | collective-permute-start | bytes 221192 | tf_op jit(solution)/shard_map/ppermute | solution.py:46
  84.1 2.4 %collective-permute-start.15 = (bf16[72,512]{1,0:T(8,128)(2,1)S(1)}, bf16[72,512]{1,0:T(8,128)(2,1)S(1)}, u32[]{:S(2)}, u32[]{:S(2)}) collective-permute-start(bf16[72,512]{1,0:T(8,128)(2,1)S(1)} %get-tuple-element.155), channel_id=1, source_target_pairs={{0,6},{1,7},{2,4},{3,5},{4,2},{5,3},{6,0},{7,1},{8,14},{9,15},{10,... | collective-permute-start | bytes 221192 | tf_op jit(solution)/shard_map/ppermute | solution.py:46
  87.0 1.9 %collective-permute-done.14.refs_1_ = bf16[72,512]{1,0:T(8,128)(2,1)S(1)} collective-permute-done((bf16[72,512]{1,0:T(8,128)(2,1)S(1)}, bf16[72,512]{1,0:T(8,128)(2,1)S(1)}, u32[]{:S(2)}, u32[]{:S(2)}) %collective-permute-start.14) | collective-permute-done | bytes 73760 | tf_op jit(solution)/shard_map/ppermute | solution.py:46
  88.9 1.5 %collective-permute-done.15.refs_2_ = bf16[72,512]{1,0:T(8,128)(2,1)S(1)} collective-permute-done((bf16[72,512]{1,0:T(8,128)(2,1)S(1)}, bf16[72,512]{1,0:T(8,128)(2,1)S(1)}, u32[]{:S(2)}, u32[]{:S(2)}) %collective-permute-start.15) | collective-permute-done | bytes 73760 | tf_op jit(solution)/shard_map/ppermute | solution.py:46
  91.2 2.5 %collective-permute-start.17 = (bf16[72,512]{1,0:T(8,128)(2,1)S(1)}, bf16[72,512]{1,0:T(8,128)(2,1)S(1)}, u32[]{:S(2)}, u32[]{:S(2)}) collective-permute-start(bf16[72,512]{1,0:T(8,128)(2,1)S(1)} %fourth.1.refs_0_), channel_id=1, source_target_pairs={{0,4},{1,5},{2,6},{3,7},{4,0},{5,1},{6,2},{7,3},{8,12},{9,13},{10,... | collective-permute-start | bytes 221192 | tf_op jit(solution)/shard_map/ppermute | solution.py:46
  93.7 1.2 %collective-permute-start.18 = (bf16[72,512]{1,0:T(8,128)(2,1)S(1)}, bf16[72,512]{1,0:T(8,128)(2,1)S(1)}, u32[]{:S(2)}, u32[]{:S(2)}) collective-permute-start(bf16[72,512]{1,0:T(8,128)(2,1)S(1)} %fourth.1.refs_0_), channel_id=1, source_target_pairs={{0,6},{1,7},{2,4},{3,5},{4,2},{5,3},{6,0},{7,1},{8,14},{9,15},{10,... | collective-permute-start | bytes 221192 | tf_op jit(solution)/shard_map/ppermute | solution.py:46
  98.2 1.7 %collective-permute-done.18.refs_3_ = bf16[72,512]{1,0:T(8,128)(2,1)S(1)} collective-permute-done((bf16[72,512]{1,0:T(8,128)(2,1)S(1)}, bf16[72,512]{1,0:T(8,128)(2,1)S(1)}, u32[]{:S(2)}, u32[]{:S(2)}) %collective-permute-start.18) | collective-permute-done | bytes 73760 | tf_op jit(solution)/shard_map/ppermute | solution.py:46
  99.9 1.3 %collective-permute-start.22 = (bf16[72,512]{1,0:T(8,128)(2,1)S(1)}, bf16[72,512]{1,0:T(8,128)(2,1)S(1)}, u32[]{:S(2)}, u32[]{:S(2)}) collective-permute-start(bf16[72,512]{1,0:T(8,128)(2,1)S(1)} %collective-permute-done.18.refs_3_), channel_id=1, source_target_pairs={{0,1},{1,0},{2,3},{3,2},{4,5},{5,4},{6,7},{7,6},{8,9},{9,8},{10,11... | collective-permute-start | bytes 221192 | tf_op jit(solution)/shard_map/ppermute | solution.py:46
  102.1 2.1 %collective-permute-done.22.refs_3_ = bf16[72,512]{1,0:T(8,128)(2,1)S(1)} collective-permute-done((bf16[72,512]{1,0:T(8,128)(2,1)S(1)}, bf16[72,512]{1,0:T(8,128)(2,1)S(1)}, u32[]{:S(2)}, u32[]{:S(2)}) %collective-permute-start.22) | collective-permute-done | bytes 73760 | tf_op jit(solution)/shard_map/ppermute | solution.py:46
  (48 shorter events, 23.6 us)
Async XLA Ops:
  0.6 15.1 %collective-permute-start.1 = (bf16[256,1024]{1,0:T(8,128)(2,1)}, bf16[256,1024]{1,0:T(8,128)(2,1)S(1)}, u32[]{:S(2)}, u32[]{:S(2)}) collective-permute-start(bf16[256,1024]{1,0:T(8,128)(2,1)} %own_hbm.3), channel_id=1, source_target_pairs={{0,16},{8,24},{16,0},{24,8},{1,17},{9,25},{17,1},{25,9},{2,18},{10... | collective-permute-start | bytes 1572872 | tf_op jit(solution)/shard_map/ppermute | solution.py:46
  4.4 2.6 %collective-permute-start = (bf16[256,1024]{1,0:T(8,128)(2,1)}, bf16[256,1024]{1,0:T(8,128)(2,1)S(1)}, u32[]{:S(2)}, u32[]{:S(2)}) collective-permute-start(bf16[256,1024]{1,0:T(8,128)(2,1)} %own_hbm.3), channel_id=1, source_target_pairs={{0,8},{8,0},{16,24},{24,16},{1,9},{9,1},{17,25},{25,17},{2,10},{10... | collective-permute-start | bytes 1572872 | tf_op jit(solution)/shard_map/ppermute | solution.py:46
  15.8 1.9 %collective-permute-start.2 = (bf16[256,1024]{1,0:T(8,128)(2,1)S(1)}, bf16[256,1024]{1,0:T(8,128)(2,1)S(1)}, u32[]{:S(2)}, u32[]{:S(2)}) collective-permute-start(bf16[256,1024]{1,0:T(8,128)(2,1)S(1)} %collective-permute-done.1.block), channel_id=1, source_target_pairs={{0,8},{8,0},{16,24},{24,16},{1,9},{9,1},{17,25},{25,17},{2,10},{10... | collective-permute-start | bytes 1572872 | tf_op jit(solution)/shard_map/ppermute | solution.py:46
  33.4 5.0 %collective-permute-start.3 = (bf16[64,1024]{1,0:T(8,128)(2,1)S(1)}, bf16[64,1024]{1,0:T(8,128)(2,1)S(1)}, u32[]{:S(2)}, u32[]{:S(2)}) collective-permute-start(bf16[64,1024]{1,0:T(8,128)(2,1)S(1)} %bitcast.18), channel_id=1, source_target_pairs={{0,16},{8,24},{16,0},{24,8},{1,17},{9,25},{17,1},{25,9},{2,18},{10... | collective-permute-start | bytes 393224 | tf_op jit(solution)/shard_map/ppermute | solution.py:46
  38.3 1.3 %collective-permute-start.4 = (bf16[64,1024]{1,0:T(8,128)(2,1)S(1)}, bf16[64,1024]{1,0:T(8,128)(2,1)S(1)}, u32[]{:S(2)}, u32[]{:S(2)}) collective-permute-start(bf16[64,1024]{1,0:T(8,128)(2,1)S(1)} %bitcast.19), channel_id=1, source_target_pairs={{0,8},{8,0},{16,24},{24,16},{1,9},{9,1},{17,25},{25,17},{2,10},{10... | collective-permute-start | bytes 393224 | tf_op jit(solution)/shard_map/ppermute | solution.py:46
  38.4 1.5 %collective-permute-start.5 = (bf16[64,1024]{1,0:T(8,128)(2,1)S(1)}, bf16[64,1024]{1,0:T(8,128)(2,1)S(1)}, u32[]{:S(2)}, u32[]{:S(2)}) collective-permute-start(bf16[64,1024]{1,0:T(8,128)(2,1)S(1)} %collective-permute-done.3.across), channel_id=1, source_target_pairs={{0,8},{8,0},{16,24},{24,16},{1,9},{9,1},{17,25},{25,17},{2,10},{10... | collective-permute-start | bytes 393224 | tf_op jit(solution)/shard_map/ppermute | solution.py:46
  44.8 1.6 %collective-permute-start.6 = (bf16[128,1024]{1,0:T(8,128)(2,1)S(1)}, bf16[128,1024]{1,0:T(8,128)(2,1)S(1)}, u32[]{:S(2)}, u32[]{:S(2)}) collective-permute-start(bf16[128,1024]{1,0:T(8,128)(2,1)S(1)} %get-tuple-element.107), channel_id=1, source_target_pairs={{0,8},{8,0},{16,24},{24,16},{1,9},{9,1},{17,25},{25,17},{2,10},{10... | collective-permute-start | bytes 786440 | tf_op jit(solution)/shard_map/ppermute | solution.py:46
  47.2 14.2 %all-to-all-start.1 = ((bf16[16,8,1024]{2,1,0:T(8,128)(2,1)}), bf16[16,8,1024]{2,1,0:T(8,128)(2,1)S(1)}, u32[]{:S(2)}, u32[]{:S(2)}) async-start(bf16[16,8,1024]{2,1,0:T(8,128)(2,1)} %bitcast.6), calls=%async_computation.1 | async-start | bytes 524288 | tf_op jit(solution)/shard_map/all_to_all | solution.py:546
  64.3 2.1 %collective-permute-start.9 = (bf16[576,512]{1,0:T(8,128)(2,1)S(1)}, bf16[576,512]{1,0:T(8,128)(2,1)S(1)}, u32[]{:S(2)}, u32[]{:S(2)}) collective-permute-start(bf16[576,512]{1,0:T(8,128)(2,1)S(1)} %get-tuple-element.132), channel_id=1, source_target_pairs={{0,8},{8,0},{16,24},{24,16},{1,9},{9,1},{17,25},{25,17},{2,10},{10... | collective-permute-start | bytes 1769480 | tf_op jit(solution)/shard_map/ppermute | solution.py:46
  64.4 3.0 %collective-permute-start.7 = (bf16[512,512]{1,0:T(8,128)(2,1)S(1)}, bf16[512,512]{1,0:T(8,128)(2,1)S(1)}, u32[]{:S(2)}, u32[]{:S(2)}) collective-permute-start(bf16[512,512]{1,0:T(8,128)(2,1)S(1)} %get-tuple-element.128), channel_id=1, source_target_pairs={{0,8},{8,0},{16,24},{24,16},{1,9},{9,1},{17,25},{25,17},{2,10},{10... | collective-permute-start | bytes 1572872 | tf_op jit(solution)/shard_map/ppermute | solution.py:46
  66.6 9.2 %collective-permute-start.10 = (bf16[288,512]{1,0:T(8,128)(2,1)S(1)}, bf16[288,512]{1,0:T(8,128)(2,1)S(1)}, u32[]{:S(2)}, u32[]{:S(2)}) collective-permute-start(bf16[288,512]{1,0:T(8,128)(2,1)S(1)} %get-tuple-element.133), channel_id=1, source_target_pairs={{0,1},{1,0},{2,3},{3,2},{4,5},{5,4},{6,7},{7,6},{8,9},{9,8},{10,11... | collective-permute-start | bytes 884744 | tf_op jit(solution)/shard_map/ppermute | solution.py:46
  67.5 8.2 %collective-permute-start.8 = (bf16[256,512]{1,0:T(8,128)(2,1)S(1)}, bf16[256,512]{1,0:T(8,128)(2,1)S(1)}, u32[]{:S(2)}, u32[]{:S(2)}) collective-permute-start(bf16[256,512]{1,0:T(8,128)(2,1)S(1)} %get-tuple-element.129), channel_id=1, source_target_pairs={{0,16},{8,24},{16,0},{24,8},{1,17},{9,25},{17,1},{25,9},{2,18},{10... | collective-permute-start | bytes 786440 | tf_op jit(solution)/shard_map/ppermute | solution.py:46
  75.8 6.1 %collective-permute-start.12 = (bf16[160,512]{1,0:T(8,128)(2,1)S(1)}, bf16[160,512]{1,0:T(8,128)(2,1)S(1)}, u32[]{:S(2)}, u32[]{:S(2)}) collective-permute-start(bf16[160,512]{1,0:T(8,128)(2,1)S(1)} %get-tuple-element.150), channel_id=1, source_target_pairs={{0,16},{8,24},{16,0},{24,8},{1,17},{9,25},{17,1},{25,9},{2,18},{10... | collective-permute-start | bytes 491528 | tf_op jit(solution)/shard_map/ppermute | solution.py:46
  77.0 5.0 %collective-permute-start.11 = (bf16[128,512]{1,0:T(8,128)(2,1)S(1)}, bf16[128,512]{1,0:T(8,128)(2,1)S(1)}, u32[]{:S(2)}, u32[]{:S(2)}) collective-permute-start(bf16[128,512]{1,0:T(8,128)(2,1)S(1)} %get-tuple-element.149), channel_id=1, source_target_pairs={{0,1},{1,0},{2,3},{3,2},{4,5},{5,4},{6,7},{7,6},{8,9},{9,8},{10,11... | collective-permute-start | bytes 393224 | tf_op jit(solution)/shard_map/ppermute | solution.py:46
  82.1 5.0 %collective-permute-start.13 = (bf16[72,512]{1,0:T(8,128)(2,1)S(1)}, bf16[72,512]{1,0:T(8,128)(2,1)S(1)}, u32[]{:S(2)}, u32[]{:S(2)}) collective-permute-start(bf16[72,512]{1,0:T(8,128)(2,1)S(1)} %get-tuple-element.153), channel_id=1, source_target_pairs={{0,2},{1,3},{2,0},{3,1},{4,6},{5,7},{6,4},{7,5},{8,10},{9,11},{10,... | collective-permute-start | bytes 221192 | tf_op jit(solution)/shard_map/ppermute | solution.py:46
  82.9 6.1 %collective-permute-start.14 = (bf16[72,512]{1,0:T(8,128)(2,1)S(1)}, bf16[72,512]{1,0:T(8,128)(2,1)S(1)}, u32[]{:S(2)}, u32[]{:S(2)}) collective-permute-start(bf16[72,512]{1,0:T(8,128)(2,1)S(1)} %get-tuple-element.154), channel_id=1, source_target_pairs={{0,4},{1,5},{2,6},{3,7},{4,0},{5,1},{6,2},{7,3},{8,12},{9,13},{10,... | collective-permute-start | bytes 221192 | tf_op jit(solution)/shard_map/ppermute | solution.py:46
  84.1 6.3 %collective-permute-start.15 = (bf16[72,512]{1,0:T(8,128)(2,1)S(1)}, bf16[72,512]{1,0:T(8,128)(2,1)S(1)}, u32[]{:S(2)}, u32[]{:S(2)}) collective-permute-start(bf16[72,512]{1,0:T(8,128)(2,1)S(1)} %get-tuple-element.155), channel_id=1, source_target_pairs={{0,6},{1,7},{2,4},{3,5},{4,2},{5,3},{6,0},{7,1},{8,14},{9,15},{10,... | collective-permute-start | bytes 221192 | tf_op jit(solution)/shard_map/ppermute | solution.py:46
  90.5 5.7 %collective-permute-start.16 = (bf16[72,512]{1,0:T(8,128)(2,1)S(1)}, bf16[72,512]{1,0:T(8,128)(2,1)S(1)}, u32[]{:S(2)}, u32[]{:S(2)}) collective-permute-start(bf16[72,512]{1,0:T(8,128)(2,1)S(1)} %fourth.1.refs_0_), channel_id=1, source_target_pairs={{0,2},{1,3},{2,0},{3,1},{4,6},{5,7},{6,4},{7,5},{8,10},{9,11},{10,... | collective-permute-start | bytes 221192 | tf_op jit(solution)/shard_map/ppermute | solution.py:46
  91.2 5.8 %collective-permute-start.17 = (bf16[72,512]{1,0:T(8,128)(2,1)S(1)}, bf16[72,512]{1,0:T(8,128)(2,1)S(1)}, u32[]{:S(2)}, u32[]{:S(2)}) collective-permute-start(bf16[72,512]{1,0:T(8,128)(2,1)S(1)} %fourth.1.refs_0_), channel_id=1, source_target_pairs={{0,4},{1,5},{2,6},{3,7},{4,0},{5,1},{6,2},{7,3},{8,12},{9,13},{10,... | collective-permute-start | bytes 221192 | tf_op jit(solution)/shard_map/ppermute | solution.py:46
  93.7 6.2 %collective-permute-start.18 = (bf16[72,512]{1,0:T(8,128)(2,1)S(1)}, bf16[72,512]{1,0:T(8,128)(2,1)S(1)}, u32[]{:S(2)}, u32[]{:S(2)}) collective-permute-start(bf16[72,512]{1,0:T(8,128)(2,1)S(1)} %fourth.1.refs_0_), channel_id=1, source_target_pairs={{0,6},{1,7},{2,4},{3,5},{4,2},{5,3},{6,0},{7,1},{8,14},{9,15},{10,... | collective-permute-start | bytes 221192 | tf_op jit(solution)/shard_map/ppermute | solution.py:46
  95.0 7.1 %collective-permute-start.19 = (bf16[72,512]{1,0:T(8,128)(2,1)S(1)}, bf16[72,512]{1,0:T(8,128)(2,1)S(1)}, u32[]{:S(2)}, u32[]{:S(2)}) collective-permute-start(bf16[72,512]{1,0:T(8,128)(2,1)S(1)} %fourth.1.refs_0_), channel_id=1, source_target_pairs={{0,1},{1,0},{2,3},{3,2},{4,5},{5,4},{6,7},{7,6},{8,9},{9,8},{10,11... | collective-permute-start | bytes 221192 | tf_op jit(solution)/shard_map/ppermute | solution.py:46
  96.2 5.9 %collective-permute-start.20 = (bf16[72,512]{1,0:T(8,128)(2,1)S(1)}, bf16[72,512]{1,0:T(8,128)(2,1)S(1)}, u32[]{:S(2)}, u32[]{:S(2)}) collective-permute-start(bf16[72,512]{1,0:T(8,128)(2,1)S(1)} %collective-permute-done.16.refs_1_), channel_id=1, source_target_pairs={{0,1},{1,0},{2,3},{3,2},{4,5},{5,4},{6,7},{7,6},{8,9},{9,8},{10,11... | collective-permute-start | bytes 221192 | tf_op jit(solution)/shard_map/ppermute | solution.py:46
  97.0 5.1 %collective-permute-start.21 = (bf16[72,512]{1,0:T(8,128)(2,1)S(1)}, bf16[72,512]{1,0:T(8,128)(2,1)S(1)}, u32[]{:S(2)}, u32[]{:S(2)}) collective-permute-start(bf16[72,512]{1,0:T(8,128)(2,1)S(1)} %collective-permute-done.17.refs_2_), channel_id=1, source_target_pairs={{0,1},{1,0},{2,3},{3,2},{4,5},{5,4},{6,7},{7,6},{8,9},{9,8},{10,11... | collective-permute-start | bytes 221192 | tf_op jit(solution)/shard_map/ppermute | solution.py:46
  99.9 4.4 %collective-permute-start.22 = (bf16[72,512]{1,0:T(8,128)(2,1)S(1)}, bf16[72,512]{1,0:T(8,128)(2,1)S(1)}, u32[]{:S(2)}, u32[]{:S(2)}) collective-permute-start(bf16[72,512]{1,0:T(8,128)(2,1)S(1)} %collective-permute-done.18.refs_3_), channel_id=1, source_target_pairs={{0,1},{1,0},{2,3},{3,2},{4,5},{5,4},{6,7},{7,6},{8,9},{9,8},{10,11... | collective-permute-start | bytes 221192 | tf_op jit(solution)/shard_map/ppermute | solution.py:46

commit v8 on v7

--- a/solution.py
+++ b/solution.py
@@ -358,8 +358,9 @@
 
 
 def fourth_kernel(keep, side, *refs):
-    gots, own = refs[:-1], refs[-1]
+    gots, own = list(refs[:-1]), refs[-1]
     n, deep = keep.shape[0], side.shape[0]
+    gots[0], gots[1] = gots[1], gots[0]
     gots = [g[...].astype(f32) for g in gots]
     total = tree([side[...]] + [joined(g[n : n + 2 * deep]) for g in gots])
     total = jnp.concatenate([tree([keep[...]] + [g[:n] for g in gots]), side_rows(total)], axis=0)
@@ -397,7 +398,8 @@
 
 
 def settle_kernel(deep, *refs):
-    blocks, (grad_hbm, side, grad, sems) = refs[:-4], refs[-4:]
+    blocks, (grad_hbm, side, grad, sems) = list(refs[:-4]), refs[-4:]
+    blocks[1], blocks[2] = blocks[2], blocks[1]
     for put in settle(0, blocks, grad_hbm, side, grad, Mover(sems), deep):
         put.wait()
 
@@ -656,7 +658,7 @@
         fourth_kernel,
         "fourth",
         4,
-        [("vmem", x) for x in (keep, side, *gots)],
+        [("vmem", x) for x in (keep, side, gots[1], gots[0], *gots[2:])],
         [("vmem", block, bf16)],
     )
     held = [held] + [swap(held, "exp", n_exp, 2 * m) for m in range(1, groups)]
@@ -665,7 +667,7 @@
         functools.partial(settle_kernel, piece),
         "settle",
         6,
-        [("vmem", x) for x in held],
+        [("vmem", x) for x in (held[0], held[2], held[1], *held[3:])],
         [("hbm", (n_exp, n, width), f32), ("vmem", (n_exp, piece, half), f32)],
         [pltpu.VMEM((groups, n, width), f32), dma((groups,))],
     )

time: 106 us -> 105 us (level)
  no operation moved by 1% of the time
where the time goes in v8:
time: 105 us
  Pallas kernels  32.3 us (31%)
  starting transfers between devices  27.9 us (27%)
  waiting for transfers between devices  27.2 us (26%)
  blocking collectives  13.2 us (13%)
  other arithmetic  3.24 us (3%)
    pallas_call x17, Pallas kernels, call(): pl.pallas_call(kernel, in_specs=[pl.BlockSpec(memory_space=spaces[where])...  32.3 us
    ppermute x23, starting transfers between devices, swap(): return lax.ppermute(x, axis, [(i, i ^ bit) for i in range(size)])  24 us
    ppermute x23, waiting for transfers between devices, swap(): return lax.ppermute(x, axis, [(i, i ^ bit) for i in range(size)])  22 us
    all_to_all x1, blocking collectives, shards(): got = lax.all_to_all(out.reshape(n_exp, -1, width), 'exp', 0, 0, tiled=True)  13.2 us
    all_to_all x1, waiting for transfers between devices, shards(): lax.all_to_all(back, ('img', 'exp'), 0, 0, axis_index_groups=groups, tile...  5.29 us
    all_to_all x1, starting transfers between devices, shards(): lax.all_to_all(back, ('img', 'exp'), 0, 0, axis_index_groups=groups, tile...  3.82 us
  transfers between devices with their start and end apart: 24, of which 15 were waited for; matrix products, arithmetic and copies ran while one was open for 3% of the time, Pallas kernels for 19%

profile of v8, /device:TPU:0, one launch (start us, length us, event | category | flops | bytes accessed | tf_op | source)
XLA Modules:
  0.0 104.9 jit_solution(16099873501596261626)
XLA Ops:
  0.6 3.0 %collective-permute-start.1 = (bf16[256,1024]{1,0:T(8,128)(2,1)}, bf16[256,1024]{1,0:T(8,128)(2,1)S(1)}, u32[]{:S(2)}, u32[]{:S(2)}) collective-permute-start(bf16[256,1024]{1,0:T(8,128)(2,1)} %own_hbm.3), channel_id=1, source_target_pairs={{0,16},{8,24},{16,0},{24,8},{1,17},{9,25},{17,1},{25,9},{2,18},{10... | collective-permute-start | bytes 1572872 | tf_op jit(solution)/shard_map/ppermute | solution.py:46
  7.0 4.4 %prepare.1 = (bf16[512,512]{1,0:T(8,128)(2,1)}, bf16[512,512]{1,0:T(8,128)(2,1)}, bf16[512,512]{1,0:T(8,128)(2,1)}, bf16[512,512]{1,0:T(8,128)(2,1)}, bf16[256,1...) custom-call(bf16[512,1024]{1,0:T(8,128)(2,1)} %bitcast.25, ...), custom_call_target="tpu_custom_call" | custom-call | tf_op jit(solution)/shard_map/prepare/pallas_call | solution.py:24
  11.4 4.3 %collective-permute-done.1.block = bf16[256,1024]{1,0:T(8,128)(2,1)S(1)} collective-permute-done((bf16[256,1024]{1,0:T(8,128)(2,1)}, bf16[256,1024]{1,0:T(8,128)(2,1)S(1)}, u32[]{:S(2)}, u32[]{:S(2)}) %collective-permute-start.1) | collective-permute-done | bytes 524320 | tf_op jit(solution)/shard_map/ppermute | solution.py:46
  17.7 2.5 %forward.1 = (bf16[256,1024]{1,0:T(8,128)(2,1)}, bf16[512,1024]{1,0:T(8,128)(2,1)S(1)}, f32[512,16]{1,0:T(8,128)S(1)}, bf16[64,1024]{1,0:T(8,128)(2,1)S(1)}) custom-call(bf16[512,1024]{1,0:T(8,128)(2,1)S(1)} %get-tuple-element.85.ctx, f32[512,1024]{1,0:T(8,128)S(1)} %get-tuple-element.90.start, bf16[512,1024]{1,0:T(8,128)(2,1)S(1)} %get-tuple-element.91.cot, ...), custom_call_target="tpu_custom_call" | custom-call | tf_op jit(solution)/shard_map/forward/pallas_call | solution.py:24
  20.2 13.2 %all_to_all.10 = bf16[8,8,1024]{2,1,0:T(8,128)(2,1)S(1)} all-to-all(bf16[8,8,1024]{2,1,0:T(8,128)(2,1)S(1)} %bitcast.21), channel_id=1, replica_groups=mesh['img'=4,'exp'=8] {'exp'}, dimensions={0} | all-to-all | bytes 262144 | tf_op jit(solution)/shard_map/all_to_all | solution.py:505
  33.4 1.5 %collective-permute-start.3 = (bf16[64,1024]{1,0:T(8,128)(2,1)S(1)}, bf16[64,1024]{1,0:T(8,128)(2,1)S(1)}, u32[]{:S(2)}, u32[]{:S(2)}) collective-permute-start(bf16[64,1024]{1,0:T(8,128)(2,1)S(1)} %bitcast.18), channel_id=1, source_target_pairs={{0,16},{8,24},{16,0},{24,8},{1,17},{9,25},{17,1},{25,9},{2,18},{10... | collective-permute-start | bytes 393224 | tf_op jit(solution)/shard_map/ppermute | solution.py:46
  34.9 2.8 %weights.1 = (bf16[1,1024,1024]{2,1,0:T(8,128)(2,1)S(1)}, bf16[2,1024,1024]{2,1,0:T(8,128)(2,1)S(1)}) custom-call(bf16[2,1024,1024]{2,1,0:T(8,128)(2,1)} %refs_0_, bf16[2,1024,1024]{2,1,0:T(8,128)(2,1)} %refs_1_), custom_call_target="tpu_custom_call" | custom-call | tf_op jit(solution)/shard_map/weights/pallas_call | solution.py:24
  39.9 4.9 %experts.1 = (bf16[4,64,1024]{2,1,0:T(8,128)(2,1)}, bf16[2,64,1024]{2,1,0:T(8,128)(2,1)}, bf16[2,64,1024]{2,1,0:T(8,128)(2,1)}, bf16[128,1024]{1,0:T(8,128)(2,1)S(1)}, bf16[128,1024]{1,0:T(8,128)(2,1)S(1)}) custom-call(bf16[64,1024]{1,0:T(8,128)(2,1)S(1)} %bitcast.20, bf16[64,1024]{1,0:T(8,128)(2,1)S(1)} %collective-permute-done.4.near, ...), custom_call_target="tpu_custom_call" | custom-call | tf_op jit(solution)/shard_map/experts/pallas_call | solution.py:24
  47.2 3.8 %all-to-all-start.1 = ((bf16[16,8,1024]{2,1,0:T(8,128)(2,1)}), bf16[16,8,1024]{2,1,0:T(8,128)(2,1)S(1)}, u32[]{:S(2)}, u32[]{:S(2)}) async-start(bf16[16,8,1024]{2,1,0:T(8,128)(2,1)} %bitcast.6), calls=%async_computation.1 | async-start | bytes 524288 | tf_op jit(solution)/shard_map/all_to_all | solution.py:548
  51.0 5.1 %expert_grads.1 = (bf16[2,1024,1024]{2,1,0:T(8,128)(2,1)}, bf16[2,1024,1024]{2,1,0:T(8,128)(2,1)}, bf16[512,512]{1,0:T(8,128)(2,1)S(1)}, bf16[512,1024]{1,0:T(8,128)(2,1)S(1)}) custom-call(bf16[4,64,1024]{2,1,0:T(8,128)(2,1)} %get-tuple-element.108.rows_hbm, bf16[2,64,1024]{2,1,0:T(8,128)(2,1)} %get-tuple-element.109.act_hbm, ...), custom_call_target="tpu_custom_call" | custom-call | tf_op jit(solution)/shard_map/expert_grads/pallas_call | solution.py:24
  56.1 5.3 %all-to-all-done.1 = bf16[16,8,1024]{2,1,0:T(8,128)(2,1)S(1)} async-done(((bf16[16,8,1024]{2,1,0:T(8,128)(2,1)}), bf16[16,8,1024]{2,1,0:T(8,128)(2,1)S(1)}, u32[]{:S(2)}, u32[]{:S(2)}) %all-to-all-start.1) | async-done | bytes 262176 | tf_op jit(solution)/shard_map/all_to_all | solution.py:548
  61.3 3.0 %backward.1 = (bf16[512,1024]{1,0:T(8,128)(2,1)S(1)}, bf16[512,512]{1,0:T(8,128)(2,1)S(1)}, bf16[576,512]{1,0:T(8,128)(2,1)S(1)}, f32[32,512]{1,0:T(8,128)S(1)},...) custom-call(bf16[2,64,1024]{2,1,0:T(8,128)(2,1)S(1)} %bitcast.17, bf16[64,64]{1,0:T(8,128)(2,1)S(1)} %fusion.3.perm, ...), custom_call_target="tpu_custom_call" | custom-call | tf_op jit(solution)/shard_map/backward/pallas_call | solution.py:24
  68.5 5.1 %context.1 = (bf16[512,1024]{1,0:T(8,128)(2,1)}, bf16[512,1024]{1,0:T(8,128)(2,1)}) custom-call(bf16[512,1024]{1,0:T(8,128)(2,1)S(1)} %get-tuple-element.126.grad, bf16[256,1024]{1,0:T(8,128)(2,1)} %own_hbm.3, bf16[256,1024]{1,0:T(8,128)(2,1)} %get-tuple-element.134.near_hbm, bf16[256,1024]{1,0:T(8,128)(2,1)} %get-tuple-element.135.far_hbm, ...), custom_call_target="tpu_custom_call" | custom-call | tf_op jit(solution)/shard_map/context/pallas_call | solution.py:24
  73.6 2.1 %collective-permute-done.8.got_p = bf16[256,512]{1,0:T(8,128)(2,1)S(1)} collective-permute-done((bf16[256,512]{1,0:T(8,128)(2,1)S(1)}, bf16[256,512]{1,0:T(8,128)(2,1)S(1)}, u32[]{:S(2)}, u32[]{:S(2)}) %collective-permute-start.8) | collective-permute-done | bytes 262176 | tf_op jit(solution)/shard_map/ppermute | solution.py:46
  78.2 3.8 %collective-permute-done.11.got_p = bf16[128,512]{1,0:T(8,128)(2,1)S(1)} collective-permute-done((bf16[128,512]{1,0:T(8,128)(2,1)S(1)}, bf16[128,512]{1,0:T(8,128)(2,1)S(1)}, u32[]{:S(2)}, u32[]{:S(2)}) %collective-permute-start.11) | collective-permute-done | bytes 131104 | tf_op jit(solution)/shard_map/ppermute | solution.py:46
  82.6 1.5 %collective-permute-start.14 = (bf16[72,512]{1,0:T(8,128)(2,1)S(1)}, bf16[72,512]{1,0:T(8,128)(2,1)S(1)}, u32[]{:S(2)}, u32[]{:S(2)}) collective-permute-start(bf16[72,512]{1,0:T(8,128)(2,1)S(1)} %get-tuple-element.154), channel_id=1, source_target_pairs={{0,2},{1,3},{2,0},{3,1},{4,6},{5,7},{6,4},{7,5},{8,10},{9,11},{10,... | collective-permute-start | bytes 221192 | tf_op jit(solution)/shard_map/ppermute | solution.py:46
  84.1 2.4 %collective-permute-start.15 = (bf16[72,512]{1,0:T(8,128)(2,1)S(1)}, bf16[72,512]{1,0:T(8,128)(2,1)S(1)}, u32[]{:S(2)}, u32[]{:S(2)}) collective-permute-start(bf16[72,512]{1,0:T(8,128)(2,1)S(1)} %get-tuple-element.155), channel_id=1, source_target_pairs={{0,6},{1,7},{2,4},{3,5},{4,2},{5,3},{6,0},{7,1},{8,14},{9,15},{10,... | collective-permute-start | bytes 221192 | tf_op jit(solution)/shard_map/ppermute | solution.py:46
  86.5 2.0 %collective-permute-done.13.refs_0_ = bf16[72,512]{1,0:T(8,128)(2,1)S(1)} collective-permute-done((bf16[72,512]{1,0:T(8,128)(2,1)S(1)}, bf16[72,512]{1,0:T(8,128)(2,1)S(1)}, u32[]{:S(2)}, u32[]{:S(2)}) %collective-permute-start.13) | collective-permute-done | bytes 73760 | tf_op jit(solution)/shard_map/ppermute | solution.py:46
  88.5 1.9 %collective-permute-done.15.refs_2_ = bf16[72,512]{1,0:T(8,128)(2,1)S(1)} collective-permute-done((bf16[72,512]{1,0:T(8,128)(2,1)S(1)}, bf16[72,512]{1,0:T(8,128)(2,1)S(1)}, u32[]{:S(2)}, u32[]{:S(2)}) %collective-permute-start.15) | collective-permute-done | bytes 73760 | tf_op jit(solution)/shard_map/ppermute | solution.py:46
  90.5 2.9 %collective-permute-start.16 = (bf16[72,512]{1,0:T(8,128)(2,1)S(1)}, bf16[72,512]{1,0:T(8,128)(2,1)S(1)}, u32[]{:S(2)}, u32[]{:S(2)}) collective-permute-start(bf16[72,512]{1,0:T(8,128)(2,1)S(1)} %fourth.1.refs_0_), channel_id=1, source_target_pairs={{0,4},{1,5},{2,6},{3,7},{4,0},{5,1},{6,2},{7,3},{8,12},{9,13},{10,... | collective-permute-start | bytes 221192 | tf_op jit(solution)/shard_map/ppermute | solution.py:46
  93.4 1.5 %collective-permute-start.18 = (bf16[72,512]{1,0:T(8,128)(2,1)S(1)}, bf16[72,512]{1,0:T(8,128)(2,1)S(1)}, u32[]{:S(2)}, u32[]{:S(2)}) collective-permute-start(bf16[72,512]{1,0:T(8,128)(2,1)S(1)} %fourth.1.refs_0_), channel_id=1, source_target_pairs={{0,6},{1,7},{2,4},{3,5},{4,2},{5,3},{6,0},{7,1},{8,14},{9,15},{10,... | collective-permute-start | bytes 221192 | tf_op jit(solution)/shard_map/ppermute | solution.py:46
  96.9 1.5 %collective-permute-start.21 = (bf16[72,512]{1,0:T(8,128)(2,1)S(1)}, bf16[72,512]{1,0:T(8,128)(2,1)S(1)}, u32[]{:S(2)}, u32[]{:S(2)}) collective-permute-start(bf16[72,512]{1,0:T(8,128)(2,1)S(1)} %collective-permute-done.16.refs_1_), channel_id=1, source_target_pairs={{0,1},{1,0},{2,3},{3,2},{4,5},{5,4},{6,7},{7,6},{8,9},{9,8},{10,11... | collective-permute-start | bytes 221192 | tf_op jit(solution)/shard_map/ppermute | solution.py:46
  99.5 1.7 %collective-permute-start.22 = (bf16[72,512]{1,0:T(8,128)(2,1)S(1)}, bf16[72,512]{1,0:T(8,128)(2,1)S(1)}, u32[]{:S(2)}, u32[]{:S(2)}) collective-permute-start(bf16[72,512]{1,0:T(8,128)(2,1)S(1)} %collective-permute-done.18.refs_3_), channel_id=1, source_target_pairs={{0,1},{1,0},{2,3},{3,2},{4,5},{5,4},{6,7},{7,6},{8,9},{9,8},{10,11... | collective-permute-start | bytes 221192 | tf_op jit(solution)/shard_map/ppermute | solution.py:46
  102.2 1.7 %collective-permute-done.22.refs_3_ = bf16[72,512]{1,0:T(8,128)(2,1)S(1)} collective-permute-done((bf16[72,512]{1,0:T(8,128)(2,1)S(1)}, bf16[72,512]{1,0:T(8,128)(2,1)S(1)}, u32[]{:S(2)}, u32[]{:S(2)}) %collective-permute-start.22) | collective-permute-done | bytes 73760 | tf_op jit(solution)/shard_map/ppermute | solution.py:46
  (48 shorter events, 22.0 us)
Async XLA Ops:
  0.6 15.1 %collective-permute-start.1 = (bf16[256,1024]{1,0:T(8,128)(2,1)}, bf16[256,1024]{1,0:T(8,128)(2,1)S(1)}, u32[]{:S(2)}, u32[]{:S(2)}) collective-permute-start(bf16[256,1024]{1,0:T(8,128)(2,1)} %own_hbm.3), channel_id=1, source_target_pairs={{0,16},{8,24},{16,0},{24,8},{1,17},{9,25},{17,1},{25,9},{2,18},{10... | collective-permute-start | bytes 1572872 | tf_op jit(solution)/shard_map/ppermute | solution.py:46
  4.4 2.6 %collective-permute-start = (bf16[256,1024]{1,0:T(8,128)(2,1)}, bf16[256,1024]{1,0:T(8,128)(2,1)S(1)}, u32[]{:S(2)}, u32[]{:S(2)}) collective-permute-start(bf16[256,1024]{1,0:T(8,128)(2,1)} %own_hbm.3), channel_id=1, source_target_pairs={{0,8},{8,0},{16,24},{24,16},{1,9},{9,1},{17,25},{25,17},{2,10},{10... | collective-permute-start | bytes 1572872 | tf_op jit(solution)/shard_map/ppermute | solution.py:46
  15.8 1.9 %collective-permute-start.2 = (bf16[256,1024]{1,0:T(8,128)(2,1)S(1)}, bf16[256,1024]{1,0:T(8,128)(2,1)S(1)}, u32[]{:S(2)}, u32[]{:S(2)}) collective-permute-start(bf16[256,1024]{1,0:T(8,128)(2,1)S(1)} %collective-permute-done.1.block), channel_id=1, source_target_pairs={{0,8},{8,0},{16,24},{24,16},{1,9},{9,1},{17,25},{25,17},{2,10},{10... | collective-permute-start | bytes 1572872 | tf_op jit(solution)/shard_map/ppermute | solution.py:46
  33.4 5.0 %collective-permute-start.3 = (bf16[64,1024]{1,0:T(8,128)(2,1)S(1)}, bf16[64,1024]{1,0:T(8,128)(2,1)S(1)}, u32[]{:S(2)}, u32[]{:S(2)}) collective-permute-start(bf16[64,1024]{1,0:T(8,128)(2,1)S(1)} %bitcast.18), channel_id=1, source_target_pairs={{0,16},{8,24},{16,0},{24,8},{1,17},{9,25},{17,1},{25,9},{2,18},{10... | collective-permute-start | bytes 393224 | tf_op jit(solution)/shard_map/ppermute | solution.py:46
  38.3 1.3 %collective-permute-start.4 = (bf16[64,1024]{1,0:T(8,128)(2,1)S(1)}, bf16[64,1024]{1,0:T(8,128)(2,1)S(1)}, u32[]{:S(2)}, u32[]{:S(2)}) collective-permute-start(bf16[64,1024]{1,0:T(8,128)(2,1)S(1)} %bitcast.19), channel_id=1, source_target_pairs={{0,8},{8,0},{16,24},{24,16},{1,9},{9,1},{17,25},{25,17},{2,10},{10... | collective-permute-start | bytes 393224 | tf_op jit(solution)/shard_map/ppermute | solution.py:46
  38.4 1.5 %collective-permute-start.5 = (bf16[64,1024]{1,0:T(8,128)(2,1)S(1)}, bf16[64,1024]{1,0:T(8,128)(2,1)S(1)}, u32[]{:S(2)}, u32[]{:S(2)}) collective-permute-start(bf16[64,1024]{1,0:T(8,128)(2,1)S(1)} %collective-permute-done.3.across), channel_id=1, source_target_pairs={{0,8},{8,0},{16,24},{24,16},{1,9},{9,1},{17,25},{25,17},{2,10},{10... | collective-permute-start | bytes 393224 | tf_op jit(solution)/shard_map/ppermute | solution.py:46
  44.8 1.6 %collective-permute-start.6 = (bf16[128,1024]{1,0:T(8,128)(2,1)S(1)}, bf16[128,1024]{1,0:T(8,128)(2,1)S(1)}, u32[]{:S(2)}, u32[]{:S(2)}) collective-permute-start(bf16[128,1024]{1,0:T(8,128)(2,1)S(1)} %get-tuple-element.107), channel_id=1, source_target_pairs={{0,8},{8,0},{16,24},{24,16},{1,9},{9,1},{17,25},{25,17},{2,10},{10... | collective-permute-start | bytes 786440 | tf_op jit(solution)/shard_map/ppermute | solution.py:46
  47.2 14.2 %all-to-all-start.1 = ((bf16[16,8,1024]{2,1,0:T(8,128)(2,1)}), bf16[16,8,1024]{2,1,0:T(8,128)(2,1)S(1)}, u32[]{:S(2)}, u32[]{:S(2)}) async-start(bf16[16,8,1024]{2,1,0:T(8,128)(2,1)} %bitcast.6), calls=%async_computation.1 | async-start | bytes 524288 | tf_op jit(solution)/shard_map/all_to_all | solution.py:548
  64.3 2.1 %collective-permute-start.9 = (bf16[576,512]{1,0:T(8,128)(2,1)S(1)}, bf16[576,512]{1,0:T(8,128)(2,1)S(1)}, u32[]{:S(2)}, u32[]{:S(2)}) collective-permute-start(bf16[576,512]{1,0:T(8,128)(2,1)S(1)} %get-tuple-element.132), channel_id=1, source_target_pairs={{0,8},{8,0},{16,24},{24,16},{1,9},{9,1},{17,25},{25,17},{2,10},{10... | collective-permute-start | bytes 1769480 | tf_op jit(solution)/shard_map/ppermute | solution.py:46
  64.4 3.0 %collective-permute-start.7 = (bf16[512,512]{1,0:T(8,128)(2,1)S(1)}, bf16[512,512]{1,0:T(8,128)(2,1)S(1)}, u32[]{:S(2)}, u32[]{:S(2)}) collective-permute-start(bf16[512,512]{1,0:T(8,128)(2,1)S(1)} %get-tuple-element.128), channel_id=1, source_target_pairs={{0,8},{8,0},{16,24},{24,16},{1,9},{9,1},{17,25},{25,17},{2,10},{10... | collective-permute-start | bytes 1572872 | tf_op jit(solution)/shard_map/ppermute | solution.py:46
  66.6 9.2 %collective-permute-start.10 = (bf16[288,512]{1,0:T(8,128)(2,1)S(1)}, bf16[288,512]{1,0:T(8,128)(2,1)S(1)}, u32[]{:S(2)}, u32[]{:S(2)}) collective-permute-start(bf16[288,512]{1,0:T(8,128)(2,1)S(1)} %get-tuple-element.133), channel_id=1, source_target_pairs={{0,1},{1,0},{2,3},{3,2},{4,5},{5,4},{6,7},{7,6},{8,9},{9,8},{10,11... | collective-permute-start | bytes 884744 | tf_op jit(solution)/shard_map/ppermute | solution.py:46
  67.5 8.2 %collective-permute-start.8 = (bf16[256,512]{1,0:T(8,128)(2,1)S(1)}, bf16[256,512]{1,0:T(8,128)(2,1)S(1)}, u32[]{:S(2)}, u32[]{:S(2)}) collective-permute-start(bf16[256,512]{1,0:T(8,128)(2,1)S(1)} %get-tuple-element.129), channel_id=1, source_target_pairs={{0,16},{8,24},{16,0},{24,8},{1,17},{9,25},{17,1},{25,9},{2,18},{10... | collective-permute-start | bytes 786440 | tf_op jit(solution)/shard_map/ppermute | solution.py:46
  75.8 6.1 %collective-permute-start.12 = (bf16[160,512]{1,0:T(8,128)(2,1)S(1)}, bf16[160,512]{1,0:T(8,128)(2,1)S(1)}, u32[]{:S(2)}, u32[]{:S(2)}) collective-permute-start(bf16[160,512]{1,0:T(8,128)(2,1)S(1)} %get-tuple-element.150), channel_id=1, source_target_pairs={{0,16},{8,24},{16,0},{24,8},{1,17},{9,25},{17,1},{25,9},{2,18},{10... | collective-permute-start | bytes 491528 | tf_op jit(solution)/shard_map/ppermute | solution.py:46
  77.0 5.0 %collective-permute-start.11 = (bf16[128,512]{1,0:T(8,128)(2,1)S(1)}, bf16[128,512]{1,0:T(8,128)(2,1)S(1)}, u32[]{:S(2)}, u32[]{:S(2)}) collective-permute-start(bf16[128,512]{1,0:T(8,128)(2,1)S(1)} %get-tuple-element.149), channel_id=1, source_target_pairs={{0,1},{1,0},{2,3},{3,2},{4,5},{5,4},{6,7},{7,6},{8,9},{9,8},{10,11... | collective-permute-start | bytes 393224 | tf_op jit(solution)/shard_map/ppermute | solution.py:46
  82.1 6.4 %collective-permute-start.13 = (bf16[72,512]{1,0:T(8,128)(2,1)S(1)}, bf16[72,512]{1,0:T(8,128)(2,1)S(1)}, u32[]{:S(2)}, u32[]{:S(2)}) collective-permute-start(bf16[72,512]{1,0:T(8,128)(2,1)S(1)} %get-tuple-element.153), channel_id=1, source_target_pairs={{0,4},{1,5},{2,6},{3,7},{4,0},{5,1},{6,2},{7,3},{8,12},{9,13},{10,... | collective-permute-start | bytes 221192 | tf_op jit(solution)/shard_map/ppermute | solution.py:46
  82.6 5.9 %collective-permute-start.14 = (bf16[72,512]{1,0:T(8,128)(2,1)S(1)}, bf16[72,512]{1,0:T(8,128)(2,1)S(1)}, u32[]{:S(2)}, u32[]{:S(2)}) collective-permute-start(bf16[72,512]{1,0:T(8,128)(2,1)S(1)} %get-tuple-element.154), channel_id=1, source_target_pairs={{0,2},{1,3},{2,0},{3,1},{4,6},{5,7},{6,4},{7,5},{8,10},{9,11},{10,... | collective-permute-start | bytes 221192 | tf_op jit(solution)/shard_map/ppermute | solution.py:46
  84.1 6.3 %collective-permute-start.15 = (bf16[72,512]{1,0:T(8,128)(2,1)S(1)}, bf16[72,512]{1,0:T(8,128)(2,1)S(1)}, u32[]{:S(2)}, u32[]{:S(2)}) collective-permute-start(bf16[72,512]{1,0:T(8,128)(2,1)S(1)} %get-tuple-element.155), channel_id=1, source_target_pairs={{0,6},{1,7},{2,4},{3,5},{4,2},{5,3},{6,0},{7,1},{8,14},{9,15},{10,... | collective-permute-start | bytes 221192 | tf_op jit(solution)/shard_map/ppermute | solution.py:46
  90.5 5.9 %collective-permute-start.17 = (bf16[72,512]{1,0:T(8,128)(2,1)S(1)}, bf16[72,512]{1,0:T(8,128)(2,1)S(1)}, u32[]{:S(2)}, u32[]{:S(2)}) collective-permute-start(bf16[72,512]{1,0:T(8,128)(2,1)S(1)} %fourth.1.refs_0_), channel_id=1, source_target_pairs={{0,2},{1,3},{2,0},{3,1},{4,6},{5,7},{6,4},{7,5},{8,10},{9,11},{10,... | collective-permute-start | bytes 221192 | tf_op jit(solution)/shard_map/ppermute | solution.py:46
  90.5 6.4 %collective-permute-start.16 = (bf16[72,512]{1,0:T(8,128)(2,1)S(1)}, bf16[72,512]{1,0:T(8,128)(2,1)S(1)}, u32[]{:S(2)}, u32[]{:S(2)}) collective-permute-start(bf16[72,512]{1,0:T(8,128)(2,1)S(1)} %fourth.1.refs_0_), channel_id=1, source_target_pairs={{0,4},{1,5},{2,6},{3,7},{4,0},{5,1},{6,2},{7,3},{8,12},{9,13},{10,... | collective-permute-start | bytes 221192 | tf_op jit(solution)/shard_map/ppermute | solution.py:46
  93.4 6.2 %collective-permute-start.18 = (bf16[72,512]{1,0:T(8,128)(2,1)S(1)}, bf16[72,512]{1,0:T(8,128)(2,1)S(1)}, u32[]{:S(2)}, u32[]{:S(2)}) collective-permute-start(bf16[72,512]{1,0:T(8,128)(2,1)S(1)} %fourth.1.refs_0_), channel_id=1, source_target_pairs={{0,6},{1,7},{2,4},{3,5},{4,2},{5,3},{6,0},{7,1},{8,14},{9,15},{10,... | collective-permute-start | bytes 221192 | tf_op jit(solution)/shard_map/ppermute | solution.py:46
  94.9 7.3 %collective-permute-start.19 = (bf16[72,512]{1,0:T(8,128)(2,1)S(1)}, bf16[72,512]{1,0:T(8,128)(2,1)S(1)}, u32[]{:S(2)}, u32[]{:S(2)}) collective-permute-start(bf16[72,512]{1,0:T(8,128)(2,1)S(1)} %fourth.1.refs_0_), channel_id=1, source_target_pairs={{0,1},{1,0},{2,3},{3,2},{4,5},{5,4},{6,7},{7,6},{8,9},{9,8},{10,11... | collective-permute-start | bytes 221192 | tf_op jit(solution)/shard_map/ppermute | solution.py:46
  96.4 5.8 %collective-permute-start.20 = (bf16[72,512]{1,0:T(8,128)(2,1)S(1)}, bf16[72,512]{1,0:T(8,128)(2,1)S(1)}, u32[]{:S(2)}, u32[]{:S(2)}) collective-permute-start(bf16[72,512]{1,0:T(8,128)(2,1)S(1)} %collective-permute-done.17.refs_2_), channel_id=1, source_target_pairs={{0,1},{1,0},{2,3},{3,2},{4,5},{5,4},{6,7},{7,6},{8,9},{9,8},{10,11... | collective-permute-start | bytes 221192 | tf_op jit(solution)/shard_map/ppermute | solution.py:46
  96.9 5.3 %collective-permute-start.21 = (bf16[72,512]{1,0:T(8,128)(2,1)S(1)}, bf16[72,512]{1,0:T(8,128)(2,1)S(1)}, u32[]{:S(2)}, u32[]{:S(2)}) collective-permute-start(bf16[72,512]{1,0:T(8,128)(2,1)S(1)} %collective-permute-done.16.refs_1_), channel_id=1, source_target_pairs={{0,1},{1,0},{2,3},{3,2},{4,5},{5,4},{6,7},{7,6},{8,9},{9,8},{10,11... | collective-permute-start | bytes 221192 | tf_op jit(solution)/shard_map/ppermute | solution.py:46
  99.5 4.4 %collective-permute-start.22 = (bf16[72,512]{1,0:T(8,128)(2,1)S(1)}, bf16[72,512]{1,0:T(8,128)(2,1)S(1)}, u32[]{:S(2)}, u32[]{:S(2)}) collective-permute-start(bf16[72,512]{1,0:T(8,128)(2,1)S(1)} %collective-permute-done.18.refs_3_), channel_id=1, source_target_pairs={{0,1},{1,0},{2,3},{3,2},{4,5},{5,4},{6,7},{7,6},{8,9},{9,8},{10,11... | collective-permute-start | bytes 221192 | tf_op jit(solution)/shard_map/ppermute | solution.py:46

commit v9 on v8

--- a/solution.py
+++ b/solution.py
@@ -405,7 +405,8 @@
 
 
 def last_kernel(deep, early, *refs):
-    blocks, refs = refs[:-9], refs[-9:]
+    blocks, refs = list(refs[:-9]), refs[-9:]
+    blocks[1], blocks[2] = blocks[2], blocks[1]
     unit_t, slot_norm, _, grad_hbm, slots_hbm, side, grad, slots_out, sems = refs
     mover = Mover(sems)
     side[...] = early[...]
@@ -675,7 +676,7 @@
         functools.partial(last_kernel, piece),
         "last",
         6,
-        [("vmem", x) for x in (side, *others)]
+        [("vmem", x) for x in (side, others[0], others[2], others[1], *others[3:])]
         + [("free", unit_t32), ("free", slot_norm), ("hbm", grad_proj)],
         [("hbm", (n_exp, n, width), f32), ("hbm", (slots, width), f32)],
         [

time: 105 us -> 106 us (level)
  transfers between devices with their start and end apart: 24 -> 24, of which waited for: 15 -> 16; matrix products, arithmetic and copies ran while one was open for 3% -> 3% of each run, Pallas kernels for 19% -> 19%
where the time goes in v9:
time: 106 us; the launch traced here: 105 us
  Pallas kernels  32.3 us (30%)
  waiting for transfers between devices  28.2 us (27%)
  starting transfers between devices  27.2 us (26%)
  blocking collectives  13.2 us (12%)
  other arithmetic  3.24 us (3%)
    pallas_call x17, Pallas kernels, call(): pl.pallas_call(kernel, in_specs=[pl.BlockSpec(memory_space=spaces[where])...  32.3 us
    ppermute x23, starting transfers between devices, swap(): return lax.ppermute(x, axis, [(i, i ^ bit) for i in range(size)])  23.4 us
    ppermute x23, waiting for transfers between devices, swap(): return lax.ppermute(x, axis, [(i, i ^ bit) for i in range(size)])  22.9 us
    all_to_all x1, blocking collectives, shards(): got = lax.all_to_all(out.reshape(n_exp, -1, width), 'exp', 0, 0, tiled=True)  13.2 us
    all_to_all x1, waiting for transfers between devices, shards(): lax.all_to_all(back, ('img', 'exp'), 0, 0, axis_index_groups=groups, tile...  5.29 us
    all_to_all x1, starting transfers between devices, shards(): lax.all_to_all(back, ('img', 'exp'), 0, 0, axis_index_groups=groups, tile...  3.82 us
  transfers between devices with their start and end apart: 24, of which 16 were waited for; matrix products, arithmetic and copies ran while one was open for 3% of the time, Pallas kernels for 19%

profile of v9, /device:TPU:0, one launch (start us, length us, event | category | flops | bytes accessed | tf_op | source)
XLA Modules:
  0.0 105.3 jit_solution(11905241455622865879)
XLA Ops:
  0.6 3.0 %collective-permute-start.1 = (bf16[256,1024]{1,0:T(8,128)(2,1)}, bf16[256,1024]{1,0:T(8,128)(2,1)S(1)}, u32[]{:S(2)}, u32[]{:S(2)}) collective-permute-start(bf16[256,1024]{1,0:T(8,128)(2,1)} %own_hbm.3), channel_id=1, source_target_pairs={{0,16},{8,24},{16,0},{24,8},{1,17},{9,25},{17,1},{25,9},{2,18},{10... | collective-permute-start | bytes 1572872 | tf_op jit(solution)/shard_map/ppermute | solution.py:46
  7.0 4.4 %prepare.1 = (bf16[512,512]{1,0:T(8,128)(2,1)}, bf16[512,512]{1,0:T(8,128)(2,1)}, bf16[512,512]{1,0:T(8,128)(2,1)}, bf16[512,512]{1,0:T(8,128)(2,1)}, bf16[256,1...) custom-call(bf16[512,1024]{1,0:T(8,128)(2,1)} %bitcast.25, ...), custom_call_target="tpu_custom_call" | custom-call | tf_op jit(solution)/shard_map/prepare/pallas_call | solution.py:24
  11.4 4.3 %collective-permute-done.1.block = bf16[256,1024]{1,0:T(8,128)(2,1)S(1)} collective-permute-done((bf16[256,1024]{1,0:T(8,128)(2,1)}, bf16[256,1024]{1,0:T(8,128)(2,1)S(1)}, u32[]{:S(2)}, u32[]{:S(2)}) %collective-permute-start.1) | collective-permute-done | bytes 524320 | tf_op jit(solution)/shard_map/ppermute | solution.py:46
  17.7 2.5 %forward.1 = (bf16[256,1024]{1,0:T(8,128)(2,1)}, bf16[512,1024]{1,0:T(8,128)(2,1)S(1)}, f32[512,16]{1,0:T(8,128)S(1)}, bf16[64,1024]{1,0:T(8,128)(2,1)S(1)}) custom-call(bf16[512,1024]{1,0:T(8,128)(2,1)S(1)} %get-tuple-element.85.ctx, f32[512,1024]{1,0:T(8,128)S(1)} %get-tuple-element.90.start, bf16[512,1024]{1,0:T(8,128)(2,1)S(1)} %get-tuple-element.91.cot, ...), custom_call_target="tpu_custom_call" | custom-call | tf_op jit(solution)/shard_map/forward/pallas_call | solution.py:24
  20.2 13.2 %all_to_all.10 = bf16[8,8,1024]{2,1,0:T(8,128)(2,1)S(1)} all-to-all(bf16[8,8,1024]{2,1,0:T(8,128)(2,1)S(1)} %bitcast.21), channel_id=1, replica_groups=mesh['img'=4,'exp'=8] {'exp'}, dimensions={0} | all-to-all | bytes 262144 | tf_op jit(solution)/shard_map/all_to_all | solution.py:506
  33.4 1.5 %collective-permute-start.3 = (bf16[64,1024]{1,0:T(8,128)(2,1)S(1)}, bf16[64,1024]{1,0:T(8,128)(2,1)S(1)}, u32[]{:S(2)}, u32[]{:S(2)}) collective-permute-start(bf16[64,1024]{1,0:T(8,128)(2,1)S(1)} %bitcast.18), channel_id=1, source_target_pairs={{0,16},{8,24},{16,0},{24,8},{1,17},{9,25},{17,1},{25,9},{2,18},{10... | collective-permute-start | bytes 393224 | tf_op jit(solution)/shard_map/ppermute | solution.py:46
  34.9 2.8 %weights.1 = (bf16[1,1024,1024]{2,1,0:T(8,128)(2,1)S(1)}, bf16[2,1024,1024]{2,1,0:T(8,128)(2,1)S(1)}) custom-call(bf16[2,1024,1024]{2,1,0:T(8,128)(2,1)} %refs_0_, bf16[2,1024,1024]{2,1,0:T(8,128)(2,1)} %refs_1_), custom_call_target="tpu_custom_call" | custom-call | tf_op jit(solution)/shard_map/weights/pallas_call | solution.py:24
  39.9 4.9 %experts.1 = (bf16[4,64,1024]{2,1,0:T(8,128)(2,1)}, bf16[2,64,1024]{2,1,0:T(8,128)(2,1)}, bf16[2,64,1024]{2,1,0:T(8,128)(2,1)}, bf16[128,1024]{1,0:T(8,128)(2,1)S(1)}, bf16[128,1024]{1,0:T(8,128)(2,1)S(1)}) custom-call(bf16[64,1024]{1,0:T(8,128)(2,1)S(1)} %bitcast.20, bf16[64,1024]{1,0:T(8,128)(2,1)S(1)} %collective-permute-done.4.near, ...), custom_call_target="tpu_custom_call" | custom-call | tf_op jit(solution)/shard_map/experts/pallas_call | solution.py:24
  45.2 1.2 %collective-permute-done.6.got = bf16[128,1024]{1,0:T(8,128)(2,1)S(1)} collective-permute-done((bf16[128,1024]{1,0:T(8,128)(2,1)S(1)}, bf16[128,1024]{1,0:T(8,128)(2,1)S(1)}, u32[]{:S(2)}, u32[]{:S(2)}) %collective-permute-start.6) | collective-permute-done | bytes 262176 | tf_op jit(solution)/shard_map/ppermute | solution.py:46
  47.2 3.8 %all-to-all-start.1 = ((bf16[16,8,1024]{2,1,0:T(8,128)(2,1)}), bf16[16,8,1024]{2,1,0:T(8,128)(2,1)S(1)}, u32[]{:S(2)}, u32[]{:S(2)}) async-start(bf16[16,8,1024]{2,1,0:T(8,128)(2,1)} %bitcast.6), calls=%async_computation.1 | async-start | bytes 524288 | tf_op jit(solution)/shard_map/all_to_all | solution.py:549
  51.0 5.1 %expert_grads.1 = (bf16[2,1024,1024]{2,1,0:T(8,128)(2,1)}, bf16[2,1024,1024]{2,1,0:T(8,128)(2,1)}, bf16[512,512]{1,0:T(8,128)(2,1)S(1)}, bf16[512,1024]{1,0:T(8,128)(2,1)S(1)}) custom-call(bf16[4,64,1024]{2,1,0:T(8,128)(2,1)} %get-tuple-element.108.rows_hbm, bf16[2,64,1024]{2,1,0:T(8,128)(2,1)} %get-tuple-element.109.act_hbm, ...), custom_call_target="tpu_custom_call" | custom-call | tf_op jit(solution)/shard_map/expert_grads/pallas_call | solution.py:24
  56.1 5.3 %all-to-all-done.1 = bf16[16,8,1024]{2,1,0:T(8,128)(2,1)S(1)} async-done(((bf16[16,8,1024]{2,1,0:T(8,128)(2,1)}), bf16[16,8,1024]{2,1,0:T(8,128)(2,1)S(1)}, u32[]{:S(2)}, u32[]{:S(2)}) %all-to-all-start.1) | async-done | bytes 262176 | tf_op jit(solution)/shard_map/all_to_all | solution.py:549
  61.3 3.0 %backward.1 = (bf16[512,1024]{1,0:T(8,128)(2,1)S(1)}, bf16[512,512]{1,0:T(8,128)(2,1)S(1)}, bf16[576,512]{1,0:T(8,128)(2,1)S(1)}, f32[32,512]{1,0:T(8,128)S(1)},...) custom-call(bf16[2,64,1024]{2,1,0:T(8,128)(2,1)S(1)} %bitcast.17, bf16[64,64]{1,0:T(8,128)(2,1)S(1)} %fusion.3.perm, ...), custom_call_target="tpu_custom_call" | custom-call | tf_op jit(solution)/shard_map/backward/pallas_call | solution.py:24
  68.5 5.1 %context.1 = (bf16[512,1024]{1,0:T(8,128)(2,1)}, bf16[512,1024]{1,0:T(8,128)(2,1)}) custom-call(bf16[512,1024]{1,0:T(8,128)(2,1)S(1)} %get-tuple-element.126.grad, bf16[256,1024]{1,0:T(8,128)(2,1)} %own_hbm.3, bf16[256,1024]{1,0:T(8,128)(2,1)} %get-tuple-element.134.near_hbm, bf16[256,1024]{1,0:T(8,128)(2,1)} %get-tuple-element.135.far_hbm, ...), custom_call_target="tpu_custom_call" | custom-call | tf_op jit(solution)/shard_map/context/pallas_call | solution.py:24
  73.6 2.1 %collective-permute-done.8.got_p = bf16[256,512]{1,0:T(8,128)(2,1)S(1)} collective-permute-done((bf16[256,512]{1,0:T(8,128)(2,1)S(1)}, bf16[256,512]{1,0:T(8,128)(2,1)S(1)}, u32[]{:S(2)}, u32[]{:S(2)}) %collective-permute-start.8) | collective-permute-done | bytes 262176 | tf_op jit(solution)/shard_map/ppermute | solution.py:46
  78.2 3.8 %collective-permute-done.11.got_p = bf16[128,512]{1,0:T(8,128)(2,1)S(1)} collective-permute-done((bf16[128,512]{1,0:T(8,128)(2,1)S(1)}, bf16[128,512]{1,0:T(8,128)(2,1)S(1)}, u32[]{:S(2)}, u32[]{:S(2)}) %collective-permute-start.11) | collective-permute-done | bytes 131104 | tf_op jit(solution)/shard_map/ppermute | solution.py:46
  82.6 1.5 %collective-permute-start.14 = (bf16[72,512]{1,0:T(8,128)(2,1)S(1)}, bf16[72,512]{1,0:T(8,128)(2,1)S(1)}, u32[]{:S(2)}, u32[]{:S(2)}) collective-permute-start(bf16[72,512]{1,0:T(8,128)(2,1)S(1)} %get-tuple-element.154), channel_id=1, source_target_pairs={{0,2},{1,3},{2,0},{3,1},{4,6},{5,7},{6,4},{7,5},{8,10},{9,11},{10,... | collective-permute-start | bytes 221192 | tf_op jit(solution)/shard_map/ppermute | solution.py:46
  84.1 2.4 %collective-permute-start.15 = (bf16[72,512]{1,0:T(8,128)(2,1)S(1)}, bf16[72,512]{1,0:T(8,128)(2,1)S(1)}, u32[]{:S(2)}, u32[]{:S(2)}) collective-permute-start(bf16[72,512]{1,0:T(8,128)(2,1)S(1)} %get-tuple-element.155), channel_id=1, source_target_pairs={{0,6},{1,7},{2,4},{3,5},{4,2},{5,3},{6,0},{7,1},{8,14},{9,15},{10,... | collective-permute-start | bytes 221192 | tf_op jit(solution)/shard_map/ppermute | solution.py:46
  86.5 2.0 %collective-permute-done.13.refs_0_ = bf16[72,512]{1,0:T(8,128)(2,1)S(1)} collective-permute-done((bf16[72,512]{1,0:T(8,128)(2,1)S(1)}, bf16[72,512]{1,0:T(8,128)(2,1)S(1)}, u32[]{:S(2)}, u32[]{:S(2)}) %collective-permute-start.13) | collective-permute-done | bytes 73760 | tf_op jit(solution)/shard_map/ppermute | solution.py:46
  88.5 1.8 %collective-permute-done.15.refs_2_ = bf16[72,512]{1,0:T(8,128)(2,1)S(1)} collective-permute-done((bf16[72,512]{1,0:T(8,128)(2,1)S(1)}, bf16[72,512]{1,0:T(8,128)(2,1)S(1)}, u32[]{:S(2)}, u32[]{:S(2)}) %collective-permute-start.15) | collective-permute-done | bytes 73760 | tf_op jit(solution)/shard_map/ppermute | solution.py:46
  90.4 3.3 %collective-permute-start.17 = (bf16[72,512]{1,0:T(8,128)(2,1)S(1)}, bf16[72,512]{1,0:T(8,128)(2,1)S(1)}, u32[]{:S(2)}, u32[]{:S(2)}) collective-permute-start(bf16[72,512]{1,0:T(8,128)(2,1)S(1)} %fourth.1.refs_0_), channel_id=1, source_target_pairs={{0,2},{1,3},{2,0},{3,1},{4,6},{5,7},{6,4},{7,5},{8,10},{9,11},{10,... | collective-permute-start | bytes 221192 | tf_op jit(solution)/shard_map/ppermute | solution.py:46
  94.8 1.3 %collective-permute-start.19 = (bf16[72,512]{1,0:T(8,128)(2,1)S(1)}, bf16[72,512]{1,0:T(8,128)(2,1)S(1)}, u32[]{:S(2)}, u32[]{:S(2)}) collective-permute-start(bf16[72,512]{1,0:T(8,128)(2,1)S(1)} %fourth.1.refs_0_), channel_id=1, source_target_pairs={{0,1},{1,0},{2,3},{3,2},{4,5},{5,4},{6,7},{7,6},{8,9},{9,8},{10,11... | collective-permute-start | bytes 221192 | tf_op jit(solution)/shard_map/ppermute | solution.py:46
  98.5 1.3 %collective-permute-done.18.refs_3_ = bf16[72,512]{1,0:T(8,128)(2,1)S(1)} collective-permute-done((bf16[72,512]{1,0:T(8,128)(2,1)S(1)}, bf16[72,512]{1,0:T(8,128)(2,1)S(1)}, u32[]{:S(2)}, u32[]{:S(2)}) %collective-permute-start.18) | collective-permute-done | bytes 73760 | tf_op jit(solution)/shard_map/ppermute | solution.py:46
  101.8 2.4 %collective-permute-done.22.refs_3_ = bf16[72,512]{1,0:T(8,128)(2,1)S(1)} collective-permute-done((bf16[72,512]{1,0:T(8,128)(2,1)S(1)}, bf16[72,512]{1,0:T(8,128)(2,1)S(1)}, u32[]{:S(2)}, u32[]{:S(2)}) %collective-permute-start.22) | collective-permute-done | bytes 73760 | tf_op jit(solution)/shard_map/ppermute | solution.py:46
  (48 shorter events, 22.2 us)
Async XLA Ops:
  0.6 15.1 %collective-permute-start.1 = (bf16[256,1024]{1,0:T(8,128)(2,1)}, bf16[256,1024]{1,0:T(8,128)(2,1)S(1)}, u32[]{:S(2)}, u32[]{:S(2)}) collective-permute-start(bf16[256,1024]{1,0:T(8,128)(2,1)} %own_hbm.3), channel_id=1, source_target_pairs={{0,16},{8,24},{16,0},{24,8},{1,17},{9,25},{17,1},{25,9},{2,18},{10... | collective-permute-start | bytes 1572872 | tf_op jit(solution)/shard_map/ppermute | solution.py:46
  4.4 2.6 %collective-permute-start = (bf16[256,1024]{1,0:T(8,128)(2,1)}, bf16[256,1024]{1,0:T(8,128)(2,1)S(1)}, u32[]{:S(2)}, u32[]{:S(2)}) collective-permute-start(bf16[256,1024]{1,0:T(8,128)(2,1)} %own_hbm.3), channel_id=1, source_target_pairs={{0,8},{8,0},{16,24},{24,16},{1,9},{9,1},{17,25},{25,17},{2,10},{10... | collective-permute-start | bytes 1572872 | tf_op jit(solution)/shard_map/ppermute | solution.py:46
  15.8 1.9 %collective-permute-start.2 = (bf16[256,1024]{1,0:T(8,128)(2,1)S(1)}, bf16[256,1024]{1,0:T(8,128)(2,1)S(1)}, u32[]{:S(2)}, u32[]{:S(2)}) collective-permute-start(bf16[256,1024]{1,0:T(8,128)(2,1)S(1)} %collective-permute-done.1.block), channel_id=1, source_target_pairs={{0,8},{8,0},{16,24},{24,16},{1,9},{9,1},{17,25},{25,17},{2,10},{10... | collective-permute-start | bytes 1572872 | tf_op jit(solution)/shard_map/ppermute | solution.py:46
  33.4 5.0 %collective-permute-start.3 = (bf16[64,1024]{1,0:T(8,128)(2,1)S(1)}, bf16[64,1024]{1,0:T(8,128)(2,1)S(1)}, u32[]{:S(2)}, u32[]{:S(2)}) collective-permute-start(bf16[64,1024]{1,0:T(8,128)(2,1)S(1)} %bitcast.18), channel_id=1, source_target_pairs={{0,16},{8,24},{16,0},{24,8},{1,17},{9,25},{17,1},{25,9},{2,18},{10... | collective-permute-start | bytes 393224 | tf_op jit(solution)/shard_map/ppermute | solution.py:46
  38.3 1.3 %collective-permute-start.4 = (bf16[64,1024]{1,0:T(8,128)(2,1)S(1)}, bf16[64,1024]{1,0:T(8,128)(2,1)S(1)}, u32[]{:S(2)}, u32[]{:S(2)}) collective-permute-start(bf16[64,1024]{1,0:T(8,128)(2,1)S(1)} %bitcast.19), channel_id=1, source_target_pairs={{0,8},{8,0},{16,24},{24,16},{1,9},{9,1},{17,25},{25,17},{2,10},{10... | collective-permute-start | bytes 393224 | tf_op jit(solution)/shard_map/ppermute | solution.py:46
  38.4 1.5 %collective-permute-start.5 = (bf16[64,1024]{1,0:T(8,128)(2,1)S(1)}, bf16[64,1024]{1,0:T(8,128)(2,1)S(1)}, u32[]{:S(2)}, u32[]{:S(2)}) collective-permute-start(bf16[64,1024]{1,0:T(8,128)(2,1)S(1)} %collective-permute-done.3.across), channel_id=1, source_target_pairs={{0,8},{8,0},{16,24},{24,16},{1,9},{9,1},{17,25},{25,17},{2,10},{10... | collective-permute-start | bytes 393224 | tf_op jit(solution)/shard_map/ppermute | solution.py:46
  44.8 1.6 %collective-permute-start.6 = (bf16[128,1024]{1,0:T(8,128)(2,1)S(1)}, bf16[128,1024]{1,0:T(8,128)(2,1)S(1)}, u32[]{:S(2)}, u32[]{:S(2)}) collective-permute-start(bf16[128,1024]{1,0:T(8,128)(2,1)S(1)} %get-tuple-element.107), channel_id=1, source_target_pairs={{0,8},{8,0},{16,24},{24,16},{1,9},{9,1},{17,25},{25,17},{2,10},{10... | collective-permute-start | bytes 786440 | tf_op jit(solution)/shard_map/ppermute | solution.py:46
  47.2 14.2 %all-to-all-start.1 = ((bf16[16,8,1024]{2,1,0:T(8,128)(2,1)}), bf16[16,8,1024]{2,1,0:T(8,128)(2,1)S(1)}, u32[]{:S(2)}, u32[]{:S(2)}) async-start(bf16[16,8,1024]{2,1,0:T(8,128)(2,1)} %bitcast.6), calls=%async_computation.1 | async-start | bytes 524288 | tf_op jit(solution)/shard_map/all_to_all | solution.py:549
  64.3 2.1 %collective-permute-start.9 = (bf16[576,512]{1,0:T(8,128)(2,1)S(1)}, bf16[576,512]{1,0:T(8,128)(2,1)S(1)}, u32[]{:S(2)}, u32[]{:S(2)}) collective-permute-start(bf16[576,512]{1,0:T(8,128)(2,1)S(1)} %get-tuple-element.132), channel_id=1, source_target_pairs={{0,8},{8,0},{16,24},{24,16},{1,9},{9,1},{17,25},{25,17},{2,10},{10... | collective-permute-start | bytes 1769480 | tf_op jit(solution)/shard_map/ppermute | solution.py:46
  64.4 3.0 %collective-permute-start.7 = (bf16[512,512]{1,0:T(8,128)(2,1)S(1)}, bf16[512,512]{1,0:T(8,128)(2,1)S(1)}, u32[]{:S(2)}, u32[]{:S(2)}) collective-permute-start(bf16[512,512]{1,0:T(8,128)(2,1)S(1)} %get-tuple-element.128), channel_id=1, source_target_pairs={{0,8},{8,0},{16,24},{24,16},{1,9},{9,1},{17,25},{25,17},{2,10},{10... | collective-permute-start | bytes 1572872 | tf_op jit(solution)/shard_map/ppermute | solution.py:46
  66.6 9.2 %collective-permute-start.10 = (bf16[288,512]{1,0:T(8,128)(2,1)S(1)}, bf16[288,512]{1,0:T(8,128)(2,1)S(1)}, u32[]{:S(2)}, u32[]{:S(2)}) collective-permute-start(bf16[288,512]{1,0:T(8,128)(2,1)S(1)} %get-tuple-element.133), channel_id=1, source_target_pairs={{0,1},{1,0},{2,3},{3,2},{4,5},{5,4},{6,7},{7,6},{8,9},{9,8},{10,11... | collective-permute-start | bytes 884744 | tf_op jit(solution)/shard_map/ppermute | solution.py:46
  67.5 8.2 %collective-permute-start.8 = (bf16[256,512]{1,0:T(8,128)(2,1)S(1)}, bf16[256,512]{1,0:T(8,128)(2,1)S(1)}, u32[]{:S(2)}, u32[]{:S(2)}) collective-permute-start(bf16[256,512]{1,0:T(8,128)(2,1)S(1)} %get-tuple-element.129), channel_id=1, source_target_pairs={{0,16},{8,24},{16,0},{24,8},{1,17},{9,25},{17,1},{25,9},{2,18},{10... | collective-permute-start | bytes 786440 | tf_op jit(solution)/shard_map/ppermute | solution.py:46
  75.8 6.1 %collective-permute-start.12 = (bf16[160,512]{1,0:T(8,128)(2,1)S(1)}, bf16[160,512]{1,0:T(8,128)(2,1)S(1)}, u32[]{:S(2)}, u32[]{:S(2)}) collective-permute-start(bf16[160,512]{1,0:T(8,128)(2,1)S(1)} %get-tuple-element.150), channel_id=1, source_target_pairs={{0,16},{8,24},{16,0},{24,8},{1,17},{9,25},{17,1},{25,9},{2,18},{10... | collective-permute-start | bytes 491528 | tf_op jit(solution)/shard_map/ppermute | solution.py:46
  77.0 5.0 %collective-permute-start.11 = (bf16[128,512]{1,0:T(8,128)(2,1)S(1)}, bf16[128,512]{1,0:T(8,128)(2,1)S(1)}, u32[]{:S(2)}, u32[]{:S(2)}) collective-permute-start(bf16[128,512]{1,0:T(8,128)(2,1)S(1)} %get-tuple-element.149), channel_id=1, source_target_pairs={{0,1},{1,0},{2,3},{3,2},{4,5},{5,4},{6,7},{7,6},{8,9},{9,8},{10,11... | collective-permute-start | bytes 393224 | tf_op jit(solution)/shard_map/ppermute | solution.py:46
  82.1 6.4 %collective-permute-start.13 = (bf16[72,512]{1,0:T(8,128)(2,1)S(1)}, bf16[72,512]{1,0:T(8,128)(2,1)S(1)}, u32[]{:S(2)}, u32[]{:S(2)}) collective-permute-start(bf16[72,512]{1,0:T(8,128)(2,1)S(1)} %get-tuple-element.153), channel_id=1, source_target_pairs={{0,4},{1,5},{2,6},{3,7},{4,0},{5,1},{6,2},{7,3},{8,12},{9,13},{10,... | collective-permute-start | bytes 221192 | tf_op jit(solution)/shard_map/ppermute | solution.py:46
  82.6 5.9 %collective-permute-start.14 = (bf16[72,512]{1,0:T(8,128)(2,1)S(1)}, bf16[72,512]{1,0:T(8,128)(2,1)S(1)}, u32[]{:S(2)}, u32[]{:S(2)}) collective-permute-start(bf16[72,512]{1,0:T(8,128)(2,1)S(1)} %get-tuple-element.154), channel_id=1, source_target_pairs={{0,2},{1,3},{2,0},{3,1},{4,6},{5,7},{6,4},{7,5},{8,10},{9,11},{10,... | collective-permute-start | bytes 221192 | tf_op jit(solution)/shard_map/ppermute | solution.py:46
  84.1 6.2 %collective-permute-start.15 = (bf16[72,512]{1,0:T(8,128)(2,1)S(1)}, bf16[72,512]{1,0:T(8,128)(2,1)S(1)}, u32[]{:S(2)}, u32[]{:S(2)}) collective-permute-start(bf16[72,512]{1,0:T(8,128)(2,1)S(1)} %get-tuple-element.155), channel_id=1, source_target_pairs={{0,6},{1,7},{2,4},{3,5},{4,2},{5,3},{6,0},{7,1},{8,14},{9,15},{10,... | collective-permute-start | bytes 221192 | tf_op jit(solution)/shard_map/ppermute | solution.py:46
  90.3 6.2 %collective-permute-start.16 = (bf16[72,512]{1,0:T(8,128)(2,1)S(1)}, bf16[72,512]{1,0:T(8,128)(2,1)S(1)}, u32[]{:S(2)}, u32[]{:S(2)}) collective-permute-start(bf16[72,512]{1,0:T(8,128)(2,1)S(1)} %fourth.1.refs_0_), channel_id=1, source_target_pairs={{0,4},{1,5},{2,6},{3,7},{4,0},{5,1},{6,2},{7,3},{8,12},{9,13},{10,... | collective-permute-start | bytes 221192 | tf_op jit(solution)/shard_map/ppermute | solution.py:46
  90.4 7.1 %collective-permute-start.17 = (bf16[72,512]{1,0:T(8,128)(2,1)S(1)}, bf16[72,512]{1,0:T(8,128)(2,1)S(1)}, u32[]{:S(2)}, u32[]{:S(2)}) collective-permute-start(bf16[72,512]{1,0:T(8,128)(2,1)S(1)} %fourth.1.refs_0_), channel_id=1, source_target_pairs={{0,2},{1,3},{2,0},{3,1},{4,6},{5,7},{6,4},{7,5},{8,10},{9,11},{10,... | collective-permute-start | bytes 221192 | tf_op jit(solution)/shard_map/ppermute | solution.py:46
  93.7 6.2 %collective-permute-start.18 = (bf16[72,512]{1,0:T(8,128)(2,1)S(1)}, bf16[72,512]{1,0:T(8,128)(2,1)S(1)}, u32[]{:S(2)}, u32[]{:S(2)}) collective-permute-start(bf16[72,512]{1,0:T(8,128)(2,1)S(1)} %fourth.1.refs_0_), channel_id=1, source_target_pairs={{0,6},{1,7},{2,4},{3,5},{4,2},{5,3},{6,0},{7,1},{8,14},{9,15},{10,... | collective-permute-start | bytes 221192 | tf_op jit(solution)/shard_map/ppermute | solution.py:46
  94.8 7.0 %collective-permute-start.19 = (bf16[72,512]{1,0:T(8,128)(2,1)S(1)}, bf16[72,512]{1,0:T(8,128)(2,1)S(1)}, u32[]{:S(2)}, u32[]{:S(2)}) collective-permute-start(bf16[72,512]{1,0:T(8,128)(2,1)S(1)} %fourth.1.refs_0_), channel_id=1, source_target_pairs={{0,1},{1,0},{2,3},{3,2},{4,5},{5,4},{6,7},{7,6},{8,9},{9,8},{10,11... | collective-permute-start | bytes 221192 | tf_op jit(solution)/shard_map/ppermute | solution.py:46
  96.5 5.3 %collective-permute-start.20 = (bf16[72,512]{1,0:T(8,128)(2,1)S(1)}, bf16[72,512]{1,0:T(8,128)(2,1)S(1)}, u32[]{:S(2)}, u32[]{:S(2)}) collective-permute-start(bf16[72,512]{1,0:T(8,128)(2,1)S(1)} %collective-permute-done.16.refs_1_), channel_id=1, source_target_pairs={{0,1},{1,0},{2,3},{3,2},{4,5},{5,4},{6,7},{7,6},{8,9},{9,8},{10,11... | collective-permute-start | bytes 221192 | tf_op jit(solution)/shard_map/ppermute | solution.py:46
  97.5 4.4 %collective-permute-start.21 = (bf16[72,512]{1,0:T(8,128)(2,1)S(1)}, bf16[72,512]{1,0:T(8,128)(2,1)S(1)}, u32[]{:S(2)}, u32[]{:S(2)}) collective-permute-start(bf16[72,512]{1,0:T(8,128)(2,1)S(1)} %collective-permute-done.17.refs_2_), channel_id=1, source_target_pairs={{0,1},{1,0},{2,3},{3,2},{4,5},{5,4},{6,7},{7,6},{8,9},{9,8},{10,11... | collective-permute-start | bytes 221192 | tf_op jit(solution)/shard_map/ppermute | solution.py:46
  99.9 4.4 %collective-permute-start.22 = (bf16[72,512]{1,0:T(8,128)(2,1)S(1)}, bf16[72,512]{1,0:T(8,128)(2,1)S(1)}, u32[]{:S(2)}, u32[]{:S(2)}) collective-permute-start(bf16[72,512]{1,0:T(8,128)(2,1)S(1)} %collective-permute-done.18.refs_3_), channel_id=1, source_target_pairs={{0,1},{1,0},{2,3},{3,2},{4,5},{5,4},{6,7},{7,6},{8,9},{9,8},{10,11... | collective-permute-start | bytes 221192 | tf_op jit(solution)/shard_map/ppermute | solution.py:46
